TPU v7x, 32 devices: a whole 2x2x4 slice. The times are simulated.
32 devices in a mesh: dp: 16 (over z, x, core), seq: 2 (over y).
Axes of the slice: x: 2, y: 2, z: 4, core: 2. Of those that a mesh axis runs over, the one named last changes fastest.
Arguments:
- q_proj: bfloat16 [16, 256, 4096], P('dp', 'seq'), may hold values from -200 to 200
- k_proj: bfloat16 [16, 256, 512], P('dp', 'seq'), may hold values from -6 to 6
- v_proj: bfloat16 [16, 256, 512], P('dp', 'seq'), may hold values from -6 to 6
- cache_k: bfloat16 [16, 1024, 512], P('dp', 'seq'), may hold values from -6 to 6
- cache_v: bfloat16 [16, 1024, 512], P('dp', 'seq'), may hold values from -6 to 6
- bias_q: bfloat16 [4096], replicated, may hold values from -3 to 3
- bias_k: bfloat16 [512], replicated, may hold values from -3 to 3
- bias_v: bfloat16 [512], replicated, may hold values from -3 to 3
- start: int32 [16], P('dp'), may hold values from 256 to 1024, as said below
- dout: bfloat16 [16, 256, 4096], P('dp', 'seq'), may hold values from -6 to 6
Outputs:
- attn_out: bfloat16 [16, 256, 4096], P('dp', 'seq')
- grad_q: bfloat16 [16, 256, 4096], P('dp', 'seq')
- grad_k: bfloat16 [16, 256, 512], P('dp', 'seq')
- grad_v: bfloat16 [16, 256, 512], P('dp', 'seq')
- grad_bias_q: float32 [4096], replicated
- grad_bias_k: float32 [512], replicated
- grad_bias_v: float32 [512], replicated
Inputs may be any that keep to these rules, and one draw needn't show every extreme that they name: Cache slots at and beyond start hold no prefix; some sequence has a full prefix of 1024 slots.
All inputs are finite; a program needn't handle non-finite values.
Results may differ from a plain program's by a relative error of at most 0.04.
The roundings to bfloat16 on the way count: a program that leaves them out, or rounds other values in their place, can miss the bound.
Values may be sent and summed in bfloat16 or wider, within the bound.
No kernel may reach another device: no remote copies, remote signals or barrier semaphores. Data moves between devices by JAX's collectives and lax.ppermute only.
A program may use at most 128 MiB of HBM per device.

v0:
```python
import jax
import jax.numpy as jnp
from jax import lax
from jax.sharding import PartitionSpec as P

HQ = 32
KV = 4
HD = 128
GROUP = 8


def rotary_tables(positions, width):
    half = width // 2
    freqs = jnp.exp(
        -(2.0 * jnp.arange(half, dtype=jnp.float32) / width) * jnp.log(jnp.float32(1000000.0))
    )
    angles = positions.astype(jnp.float32)[:, None] * freqs[None, :]
    cosine = jnp.concatenate([jnp.cos(angles), jnp.cos(angles)], axis=1)
    sine = jnp.concatenate([jnp.sin(angles), jnp.sin(angles)], axis=1)
    return (cosine[:, None, :], sine[:, None, :])


def rotary(values, positions):
    cosine, sine = rotary_tables(positions, values.shape[2])
    half = values.shape[2] // 2
    turned = jnp.concatenate([-values[:, :, half:], values[:, :, :half]], axis=2)
    return values * cosine + turned * sine


def rotary_back(grads, positions):
    cosine, sine = rotary_tables(positions, grads.shape[2])
    half = grads.shape[2] // 2
    scaled = grads * sine
    turned = jnp.concatenate([scaled[:, :, half:], -scaled[:, :, :half]], axis=2)
    return grads * cosine + turned


def attend(queries, cotangent, keys, values, first, row_zero, prefix):
    rows, heads, width = queries.shape
    key_count = keys.shape[0]
    slab = key_count - prefix
    head_block = max(1, min(512 // rows, GROUP, heads))
    row_block = min(rows, 512)
    scale = width ** (-0.5)
    key_index = jnp.arange(key_count, dtype=jnp.int32)

    def head_step(carry, head_slot):
        key_acc, value_acc = carry
        head_zero = head_slot * head_block
        owner = head_zero // GROUP
        key_one = lax.dynamic_index_in_dim(keys, owner, 1, keepdims=False)
        value_one = lax.dynamic_index_in_dim(values, owner, 1, keepdims=False)
        query_part = lax.dynamic_slice_in_dim(queries, head_zero, head_block, 1)
        cot_part = lax.dynamic_slice_in_dim(cotangent, head_zero, head_block, 1)

        def row_step(inner, row_slot):
            grad_key, grad_value = inner
            offset = row_slot * row_block
            query_rows = lax.dynamic_slice_in_dim(query_part, offset, row_block, 0)
            cot_rows = lax.dynamic_slice_in_dim(cot_part, offset, row_block, 0)
            query_index = row_zero + offset + jnp.arange(row_block, dtype=jnp.int32)
            allowed = jnp.where(
                key_index[None, :] < prefix,
                key_index[None, :] < first,
                key_index[None, :] - prefix <= query_index[:, None],
            )
            scores = (
                jnp.einsum("rhd,kd->hrk", query_rows, key_one, preferred_element_type=jnp.float32)
                * scale
            )
            scores = jnp.where(allowed[None], scores, -1e30)
            highest = jnp.max(scores, axis=-1, keepdims=True)
            expo = jnp.exp(scores - highest)
            probs = expo / jnp.sum(expo, axis=-1, keepdims=True)
            probs_b = probs.astype(jnp.bfloat16)
            output = jnp.einsum(
                "hrk,kd->rhd", probs_b, value_one, preferred_element_type=jnp.float32
            ).astype(jnp.bfloat16)
            delta = jnp.sum(cot_rows.astype(jnp.float32) * output.astype(jnp.float32), axis=-1).T
            dprobs = jnp.einsum(
                "rhd,kd->hrk", cot_rows, value_one, preferred_element_type=jnp.float32
            )
            dscore = (probs * (dprobs - delta[:, :, None])).astype(jnp.bfloat16)
            grad_query = (
                jnp.einsum("hrk,kd->rhd", dscore, key_one, preferred_element_type=jnp.float32)
                * scale
            ).astype(jnp.bfloat16)
            grad_key = (
                grad_key
                + jnp.einsum(
                    "hrk,rhd->kd",
                    dscore[:, :, prefix:],
                    query_rows,
                    preferred_element_type=jnp.float32,
                )
                * scale
            )
            grad_value = grad_value + jnp.einsum(
                "hrk,rhd->kd", probs_b[:, :, prefix:], cot_rows, preferred_element_type=jnp.float32
            )
            return ((grad_key, grad_value), (output, grad_query))

        empty = jnp.zeros((slab, width), jnp.float32)
        (grad_key, grad_value), (outputs, grads) = lax.scan(
            row_step, (empty, empty), jnp.arange(rows // row_block, dtype=jnp.int32)
        )
        outputs = outputs.reshape(rows, head_block, width)
        grads = grads.reshape(rows, head_block, width)
        old_key = lax.dynamic_index_in_dim(key_acc, owner, 1, keepdims=False)
        old_value = lax.dynamic_index_in_dim(value_acc, owner, 1, keepdims=False)
        key_acc = lax.dynamic_update_index_in_dim(key_acc, old_key + grad_key, owner, 1)
        value_acc = lax.dynamic_update_index_in_dim(value_acc, old_value + grad_value, owner, 1)
        return ((key_acc, value_acc), (outputs, grads))

    zeros_kv = jnp.zeros((slab, keys.shape[1], width), jnp.float32)
    (key_acc, value_acc), (outputs, grads) = lax.scan(
        head_step, (zeros_kv, zeros_kv), jnp.arange(heads // head_block, dtype=jnp.int32)
    )
    outputs = jnp.transpose(outputs, (1, 0, 2, 3)).reshape(rows, heads, width)
    grads = jnp.transpose(grads, (1, 0, 2, 3)).reshape(rows, heads, width)
    return (outputs, grads, key_acc, value_acc)


def body(q_proj, k_proj, v_proj, cache_k, cache_v, bias_q, bias_k, bias_v, start, dout):
    devices = lax.axis_size("seq")
    rank = lax.axis_index("seq")
    tokens = q_proj.shape[1]
    first = start[0]
    positions = first + rank * tokens + jnp.arange(tokens, dtype=jnp.int32)
    queries = rotary(
        (q_proj[0].astype(jnp.float32) + bias_q.astype(jnp.float32)).reshape(tokens, HQ, HD),
        positions,
    ).astype(jnp.bfloat16)
    keys = rotary(
        (k_proj[0].astype(jnp.float32) + bias_k.astype(jnp.float32)).reshape(tokens, KV, HD),
        positions,
    ).astype(jnp.bfloat16)
    values = (
        (v_proj[0].astype(jnp.float32) + bias_v.astype(jnp.float32))
        .astype(jnp.bfloat16)
        .reshape(tokens, KV, HD)
    )
    cotangent = dout[0].reshape(tokens, HQ, HD)
    cached_keys = cache_k[0].reshape(cache_k.shape[1], KV, HD)
    cached_values = cache_v[0].reshape(cache_v.shape[1], KV, HD)
    copies = max(devices // KV, 1)
    keys_wide = jnp.repeat(keys, copies, axis=1)
    values_wide = jnp.repeat(values, copies, axis=1)
    cache_keys_wide = jnp.repeat(cached_keys, copies, axis=1)
    cache_values_wide = jnp.repeat(cached_values, copies, axis=1)
    head_queries, head_keys, head_values, head_cot = (
        lax.all_to_all(queries, "seq", split_axis=1, concat_axis=0, tiled=True),
        lax.all_to_all(keys_wide, "seq", split_axis=1, concat_axis=0, tiled=True),
        lax.all_to_all(values_wide, "seq", split_axis=1, concat_axis=0, tiled=True),
        lax.all_to_all(cotangent, "seq", split_axis=1, concat_axis=0, tiled=True),
    )
    head_cache_keys, head_cache_values = (
        lax.all_to_all(cache_keys_wide, "seq", split_axis=1, concat_axis=0, tiled=True),
        lax.all_to_all(cache_values_wide, "seq", split_axis=1, concat_axis=0, tiled=True),
    )
    prefix = head_cache_keys.shape[0]
    all_keys = jnp.concatenate([head_cache_keys, head_keys], axis=0)
    all_values = jnp.concatenate([head_cache_values, head_values], axis=0)
    outputs, dq_rot, dk_rot, dv_all = attend(
        head_queries, head_cot, all_keys, all_values, first, 0, prefix
    )
    out_tokens, dq_tokens = (
        lax.all_to_all(outputs, "seq", split_axis=0, concat_axis=1, tiled=True),
        lax.all_to_all(dq_rot, "seq", split_axis=0, concat_axis=1, tiled=True),
    )
    dk_copies, dv_copies = (
        lax.all_to_all(
            dk_rot.astype(jnp.bfloat16), "seq", split_axis=0, concat_axis=1, tiled=True
        ).astype(dk_rot.dtype),
        lax.all_to_all(
            dv_all.astype(jnp.bfloat16), "seq", split_axis=0, concat_axis=1, tiled=True
        ).astype(dv_all.dtype),
    )
    dk_tokens = jnp.sum(dk_copies.reshape(tokens, KV, copies, HD), axis=2)
    dv_tokens = jnp.sum(dv_copies.reshape(tokens, KV, copies, HD), axis=2)
    grad_query = rotary_back(dq_tokens.astype(jnp.float32), positions)
    grad_key = rotary_back(dk_tokens, positions)
    sums_query, sums_key, sums_value = lax.psum(
        (
            jnp.sum(grad_query, axis=0).reshape(HQ * HD),
            jnp.sum(grad_key, axis=0).reshape(KV * HD),
            jnp.sum(dv_tokens, axis=0).reshape(KV * HD),
        ),
        ("dp", "seq"),
    )
    return (
        out_tokens.reshape(1, tokens, HQ * HD),
        grad_query.astype(jnp.bfloat16).reshape(1, tokens, HQ * HD),
        grad_key.astype(jnp.bfloat16).reshape(1, tokens, KV * HD),
        dv_tokens.astype(jnp.bfloat16).reshape(1, tokens, KV * HD),
        sums_query,
        sums_key,
        sums_value,
    )


def solution(mesh):
    placed = (
        P("dp", "seq", None),
        P("dp", "seq", None),
        P("dp", "seq", None),
        P("dp", "seq", None),
        P("dp", "seq", None),
        P(),
        P(),
        P(),
        P("dp"),
        P("dp", "seq", None),
    )
    return jax.shard_map(
        body,
        mesh=mesh,
        in_specs=placed,
        out_specs=(
            P("dp", "seq", None),
            P("dp", "seq", None),
            P("dp", "seq", None),
            P("dp", "seq", None),
            P(),
            P(),
            P(),
        ),
        check_vma=False,
    )
```

profile of v0, /device:TPU:0, one launch (start us, length us, event | category | flops | bytes accessed | tf_op | source)
XLA Modules:
  0.0 352.3 jit_solution(13515698020719961795)
XLA Ops:
  4.3 4.4 %all-to-all-start.1 = ((bf16[128,4,128]{0,2,1:T(8,128)(2,1)}), bf16[128,4,128]{0,2,1:T(8,128)(2,1)S(1)}, u32[]{:S(2)}, u32[]{:S(2)}) async-start(bf16[128,4,128]{0,2,1:T(8,128)(2,1)} %fusion.57), calls=%async_computation.1 | async-start | bytes 262144 | tf_op jit(solution)/shard_map/all_to_all | solution.py:153
  11.2 2.0 copy.275
  13.3 4.0 %all-to-all-start.4 = ((bf16[128,4,128]{0,2,1:T(8,128)(2,1)}), bf16[128,4,128]{0,2,1:T(8,128)(2,1)}, u32[]{:S(2)}, u32[]{:S(2)}) async-start(bf16[128,4,128]{0,2,1:T(8,128)(2,1)} %fusion.59), calls=%async_computation.4 | async-start | bytes 262144 | tf_op jit(solution)/shard_map/all_to_all | solution.py:154
  21.9 3.5 all-to-all-start
  25.4 4.9 %slice_negate_fusion.1 = (f32[128,32,64]{2,1,0:T(8,128)}, f32[128,32,64]{2,1,0:T(8,128)}) fusion(f32[128,32,128]{2,1,0:T(8,128)} %bitcast_add_fusion), kind=kLoop, calls=%fused_computation.64 | loop fusion | flops 262144 | bytes 4194304 | tf_op jit(solution)/shard_map/neg | solution.py:26
  30.3 2.9 all-to-all-done
  33.2 3.5 all-to-all-start.3
  36.7 3.0 fusion.54
  41.1 2.5 all-to-all-done.3
  43.6 3.6 %all-to-all-start.2 = ((bf16[128,32,128]{2,0,1:T(8,128)(2,1)}), bf16[128,32,128]{2,0,1:T(8,128)(2,1)S(1)}, u32[]{:S(2)}, u32[]{:S(2)}) async-start(bf16[128,32,128]{2,0,1:T(8,128)(2,1)} %copy.213), calls=%async_computation.2 | async-start | bytes 2097152 | tf_op jit(solution)/shard_map/all_to_all | solution.py:152
  50.1 8.7 %all-to-all-done.2 = bf16[128,32,128]{2,0,1:T(8,128)(2,1)S(1)} async-done(((bf16[128,32,128]{2,0,1:T(8,128)(2,1)}), bf16[128,32,128]{2,0,1:T(8,128)(2,1)S(1)}, u32[]{:S(2)}, u32[]{:S(2)}) %all-to-all-start.2) | async-done | bytes 1048608 | tf_op jit(solution)/shard_map/all_to_all | solution.py:152
  58.8 4.6 %all-to-all-start.5 = ((bf16[128,32,128]{2,0,1:T(8,128)(2,1)}), bf16[128,32,128]{2,0,1:T(8,128)(2,1)}, u32[]{:S(2)}, u32[]{:S(2)}) async-start(bf16[128,32,128]{2,0,1:T(8,128)(2,1)} %copy.222), calls=%async_computation.5 | async-start | bytes 2097152 | tf_op jit(solution)/shard_map/all_to_all | solution.py:155
  66.3 7.7 %all-to-all-done.5 = bf16[128,32,128]{2,0,1:T(8,128)(2,1)} async-done(((bf16[128,32,128]{2,0,1:T(8,128)(2,1)}), bf16[128,32,128]{2,0,1:T(8,128)(2,1)}, u32[]{:S(2)}, u32[]{:S(2)}) %all-to-all-start.5) | async-done | bytes 1048608 | tf_op jit(solution)/shard_map/all_to_all | solution.py:155
  74.0 2.9 copy.224
  77.7 172.1 %while.20 = (s32[]{:T(128)}, f32[256,2,128]{2,1,0:T(2,128)S(1)}, f32[256,2,128]{2,1,0:T(2,128)}, bf16[8,256,2,128]{3,1,2,0:T(8,128)(2,1)}, bf16[8,256,2,128]{1,3...) while((s32[]{:T(128)}, f32[256,2,128]{2,1,0:T(2,128)S(1)}, ...), condition=%wide.region_4.5_spmd.clone.clone, body=%wide.region_0.4_spmd.clone.clone.sunk | while | flops 745968128 | bytes 30173688 | solution.py:116
  80.7 3.4 fusion.100
  84.1 2.1 fusion.101
  91.1 2.9 dynamic_update_slice.47
  94.9 4.4 %dynamic_update_slice.48 = f32[256,2,128]{2,1,0:T(2,128)} dynamic-update-slice(f32[256,2,128]{2,1,0:T(2,128)} %get-tuple-element.519, f32[256,1,128]{2,1,0:T(1,128)S(1)} %bitcast.228, s32[]{:T(128)} %constant.141.clone.1..sunk, s32[]{:T(128)S(6)} %select_n.78, s32[]{:T(128)} %constant.141.clone.1..sunk) | dynamic-update-slice | bytes 262148 | tf_op jit(solution)/shard_map/while/body/eval_jaxpr/jit(dynamic_update_index_in_dim)/dynamic_update_slice | solution.py:112
  102.2 3.4 fusion.100
  105.6 2.1 fusion.101
  112.6 2.9 dynamic_update_slice.47
  116.4 4.4 %dynamic_update_slice.48 = f32[256,2,128]{2,1,0:T(2,128)} dynamic-update-slice(f32[256,2,128]{2,1,0:T(2,128)} %get-tuple-element.519, f32[256,1,128]{2,1,0:T(1,128)S(1)} %bitcast.228, s32[]{:T(128)} %constant.141.clone.1..sunk, s32[]{:T(128)S(6)} %select_n.78, s32[]{:T(128)} %constant.141.clone.1..sunk) | dynamic-update-slice | bytes 262148 | tf_op jit(solution)/shard_map/while/body/eval_jaxpr/jit(dynamic_update_index_in_dim)/dynamic_update_slice | solution.py:112
  123.7 3.4 fusion.100
  127.1 2.1 fusion.101
  134.1 2.9 dynamic_update_slice.47
  137.9 4.4 %dynamic_update_slice.48 = f32[256,2,128]{2,1,0:T(2,128)} dynamic-update-slice(f32[256,2,128]{2,1,0:T(2,128)} %get-tuple-element.519, f32[256,1,128]{2,1,0:T(1,128)S(1)} %bitcast.228, s32[]{:T(128)} %constant.141.clone.1..sunk, s32[]{:T(128)S(6)} %select_n.78, s32[]{:T(128)} %constant.141.clone.1..sunk) | dynamic-update-slice | bytes 262148 | tf_op jit(solution)/shard_map/while/body/eval_jaxpr/jit(dynamic_update_index_in_dim)/dynamic_update_slice | solution.py:112
  145.3 3.4 fusion.100
  148.6 2.1 fusion.101
  155.6 2.9 dynamic_update_slice.47
  159.4 4.4 %dynamic_update_slice.48 = f32[256,2,128]{2,1,0:T(2,128)} dynamic-update-slice(f32[256,2,128]{2,1,0:T(2,128)} %get-tuple-element.519, f32[256,1,128]{2,1,0:T(1,128)S(1)} %bitcast.228, s32[]{:T(128)} %constant.141.clone.1..sunk, s32[]{:T(128)S(6)} %select_n.78, s32[]{:T(128)} %constant.141.clone.1..sunk) | dynamic-update-slice | bytes 262148 | tf_op jit(solution)/shard_map/while/body/eval_jaxpr/jit(dynamic_update_index_in_dim)/dynamic_update_slice | solution.py:112
  166.8 3.4 fusion.100
  170.1 2.1 fusion.101
  177.1 2.9 dynamic_update_slice.47
  180.9 4.4 %dynamic_update_slice.48 = f32[256,2,128]{2,1,0:T(2,128)} dynamic-update-slice(f32[256,2,128]{2,1,0:T(2,128)} %get-tuple-element.519, f32[256,1,128]{2,1,0:T(1,128)S(1)} %bitcast.228, s32[]{:T(128)} %constant.141.clone.1..sunk, s32[]{:T(128)S(6)} %select_n.78, s32[]{:T(128)} %constant.141.clone.1..sunk) | dynamic-update-slice | bytes 262148 | tf_op jit(solution)/shard_map/while/body/eval_jaxpr/jit(dynamic_update_index_in_dim)/dynamic_update_slice | solution.py:112
  188.3 3.4 fusion.100
  191.6 2.1 fusion.101
  198.7 2.9 dynamic_update_slice.47
  202.4 4.4 %dynamic_update_slice.48 = f32[256,2,128]{2,1,0:T(2,128)} dynamic-update-slice(f32[256,2,128]{2,1,0:T(2,128)} %get-tuple-element.519, f32[256,1,128]{2,1,0:T(1,128)S(1)} %bitcast.228, s32[]{:T(128)} %constant.141.clone.1..sunk, s32[]{:T(128)S(6)} %select_n.78, s32[]{:T(128)} %constant.141.clone.1..sunk) | dynamic-update-slice | bytes 262148 | tf_op jit(solution)/shard_map/while/body/eval_jaxpr/jit(dynamic_update_index_in_dim)/dynamic_update_slice | solution.py:112
  209.8 3.4 fusion.100
  213.2 2.1 fusion.101
  220.2 2.9 dynamic_update_slice.47
  223.9 4.4 %dynamic_update_slice.48 = f32[256,2,128]{2,1,0:T(2,128)} dynamic-update-slice(f32[256,2,128]{2,1,0:T(2,128)} %get-tuple-element.519, f32[256,1,128]{2,1,0:T(1,128)S(1)} %bitcast.228, s32[]{:T(128)} %constant.141.clone.1..sunk, s32[]{:T(128)S(6)} %select_n.78, s32[]{:T(128)} %constant.141.clone.1..sunk) | dynamic-update-slice | bytes 262148 | tf_op jit(solution)/shard_map/while/body/eval_jaxpr/jit(dynamic_update_index_in_dim)/dynamic_update_slice | solution.py:112
  231.3 3.4 fusion.100
  234.7 2.1 fusion.101
  241.7 2.9 dynamic_update_slice.47
  245.5 4.4 %dynamic_update_slice.48 = f32[256,2,128]{2,1,0:T(2,128)} dynamic-update-slice(f32[256,2,128]{2,1,0:T(2,128)} %get-tuple-element.519, f32[256,1,128]{2,1,0:T(1,128)S(1)} %bitcast.228, s32[]{:T(128)} %constant.141.clone.1..sunk, s32[]{:T(128)S(6)} %select_n.78, s32[]{:T(128)} %constant.141.clone.1..sunk) | dynamic-update-slice | bytes 262148 | tf_op jit(solution)/shard_map/while/body/eval_jaxpr/jit(dynamic_update_index_in_dim)/dynamic_update_slice | solution.py:112
  250.6 3.4 all-to-all-start.8
  254.0 3.7 %copy.229 = bf16[256,8,2,128]{3,2,1,0:T(2,128)(2,1)} copy(bf16[256,8,2,128]{0,3,2,1:T(8,128)(2,1)} %bitcast.249) | data formatting | bytes 2097152 | tf_op jit(solution)/shard_map/transpose | solution.py:120
  258.5 2.0 copy.227
  260.5 3.4 all-to-all-start.9
  264.0 4.3 %all-to-all-done.9 = bf16[256,2,128]{2,1,0:T(2,128)(2,1)S(1)} async-done(((bf16[256,2,128]{2,1,0:T(2,128)(2,1)}), bf16[256,2,128]{2,1,0:T(2,128)(2,1)S(1)}, u32[]{:S(2)}, u32[]{:S(2)}) %all-to-all-start.9) | async-done | bytes 131104 | tf_op jit(solution)/shard_map/all_to_all | solution.py:175
  268.4 3.6 %all-to-all-start.7 = ((bf16[256,16,128]{2,1,0:T(8,128)(2,1)}), bf16[256,16,128]{2,1,0:T(8,128)(2,1)S(1)}, u32[]{:S(2)}, u32[]{:S(2)}) async-start(bf16[256,16,128]{2,1,0:T(8,128)(2,1)} %bitcast.38), calls=%async_computation.7 | async-start | bytes 2097152 | tf_op jit(solution)/shard_map/all_to_all | solution.py:169
  273.9 7.4 %all-to-all-done.7 = bf16[256,16,128]{2,1,0:T(8,128)(2,1)S(1)} async-done(((bf16[256,16,128]{2,1,0:T(8,128)(2,1)}), bf16[256,16,128]{2,1,0:T(8,128)(2,1)S(1)}, u32[]{:S(2)}, u32[]{:S(2)}) %all-to-all-start.7) | async-done | bytes 1048608 | tf_op jit(solution)/shard_map/all_to_all | solution.py:169
  281.3 4.7 %all-to-all-start.6 = ((bf16[256,16,128]{2,1,0:T(8,128)(2,1)}), bf16[256,16,128]{2,1,0:T(8,128)(2,1)}, u32[]{:S(2)}, u32[]{:S(2)}) async-start(bf16[256,16,128]{2,1,0:T(8,128)(2,1)} %bitcast.33), calls=%async_computation.6 | async-start | bytes 2097152 | tf_op jit(solution)/shard_map/all_to_all | solution.py:168
  289.7 1.9 bitcast_multiply_fusion
  293.8 2.0 pad_maximum_fusion
  295.8 3.0 copy.233
  298.8 3.4 fusion.55
  302.2 2.3 copy.245
  304.4 2.7 copy.228
  307.1 2.3 copy.244
  309.4 2.2 fusion.52
  311.6 40.7 %all-reduce = (f32[4096]{0:T(1024)}, f32[512]{0:T(512)}, f32[512]{0:T(512)}) all-reduce(f32[4096]{0:T(1024)S(1)} %bitcast.255, f32[512]{0:T(512)S(1)} %bitcast.258, f32[512]{0:T(512)S(1)} %bitcast.257), channel_id=1, replica_groups=mesh['dp'=16,'seq'=2] {'dp','seq'}, use_global_device_ids=true, to_apply=%region_6.7 | all-reduce | flops 5120 | bytes 40960 | tf_op jit(solution)/shard_map/psum | solution.py:183
  (212 shorter events, 91.6 us)
Async XLA Ops:
  0.6 8.1 %copy-start.4 = (bf16[1,128,4096]{2,1,0:T(8,128)(2,1)S(1)}, bf16[1,128,4096]{2,1,0:T(8,128)(2,1)}, u32[]{:S(2)}) copy-start(bf16[1,128,4096]{2,1,0:T(8,128)(2,1)} %param.12) | copy-start | bytes 3145732
  3.5 6.8 %copy-start.14 = (bf16[1,128,512]{2,1,0:T(8,128)(2,1)S(1)}, bf16[1,128,512]{2,1,0:T(8,128)(2,1)}, u32[]{:S(2)}) copy-start(bf16[1,128,512]{2,1,0:T(8,128)(2,1)} %param.14) | copy-start | bytes 393220
  3.5 6.9 %copy-start.16 = (bf16[512]{0:T(512)(128)(2,1)S(1)}, bf16[512]{0:T(512)(128)(2,1)}, u32[]{:S(2)}) copy-start(bf16[512]{0:T(512)(128)(2,1)} %param.19) | copy-start | bytes 3076
  4.3 6.9 %copy-start.15 = (bf16[4096]{0:T(1024)(128)(2,1)S(1)}, bf16[4096]{0:T(1024)(128)(2,1)}, u32[]{:S(2)}) copy-start(bf16[4096]{0:T(1024)(128)(2,1)} %param.17) | copy-start | bytes 24580
  4.3 8.9 %all-to-all-start.1 = ((bf16[128,4,128]{0,2,1:T(8,128)(2,1)}), bf16[128,4,128]{0,2,1:T(8,128)(2,1)S(1)}, u32[]{:S(2)}, u32[]{:S(2)}) async-start(bf16[128,4,128]{0,2,1:T(8,128)(2,1)} %fusion.57), calls=%async_computation.1 | async-start | bytes 262144 | tf_op jit(solution)/shard_map/all_to_all | solution.py:153
  13.3 5.7 %copy-start.12 = (bf16[128,4,128]{0,2,1:T(8,128)(2,1)}, bf16[128,4,128]{0,2,1:T(8,128)(2,1)S(1)}, u32[]{:S(2)}) copy-start(bf16[128,4,128]{0,2,1:T(8,128)(2,1)S(1)} %all-to-all-done.1) | copy-start | bytes 393220
  13.3 8.6 %all-to-all-start.4 = ((bf16[128,4,128]{0,2,1:T(8,128)(2,1)}), bf16[128,4,128]{0,2,1:T(8,128)(2,1)}, u32[]{:S(2)}, u32[]{:S(2)}) async-start(bf16[128,4,128]{0,2,1:T(8,128)(2,1)} %fusion.59), calls=%async_computation.4 | async-start | bytes 262144 | tf_op jit(solution)/shard_map/all_to_all | solution.py:154
  17.3 1.8 copy-start.10
  17.3 2.9 copy-start.11
  19.0 17.7 %copy-start.8 = (f32[128,128]{1,0:T(8,128)}, f32[128,128]{1,0:T(8,128)S(1)}, u32[]{:S(2)}) copy-start(f32[128,128]{1,0:T(8,128)S(1)} %copy.211) | copy-start | bytes 196612
  19.1 17.6 %copy-start.6 = (f32[128,128]{1,0:T(8,128)}, f32[128,128]{1,0:T(8,128)S(1)}, u32[]{:S(2)}) copy-start(f32[128,128]{1,0:T(8,128)S(1)} %copy.212) | copy-start | bytes 196612
  21.9 11.3 %all-to-all-start = ((bf16[512,4,128]{0,2,1:T(8,128)(2,1)}), bf16[512,4,128]{0,2,1:T(8,128)(2,1)S(1)}, u32[]{:S(2)}, u32[]{:S(2)}) async-start(bf16[512,4,128]{0,2,1:T(8,128)(2,1)} %bitcast.1), calls=%async_computation | async-start | bytes 1048576 | tf_op jit(solution)/shard_map/all_to_all | solution.py:158
  33.2 10.4 %all-to-all-start.3 = ((bf16[512,4,128]{0,2,1:T(8,128)(2,1)}), bf16[512,4,128]{0,2,1:T(8,128)(2,1)S(1)}, u32[]{:S(2)}, u32[]{:S(2)}) async-start(bf16[512,4,128]{0,2,1:T(8,128)(2,1)} %bitcast.240), calls=%async_computation.3 | async-start | bytes 1048576 | tf_op jit(solution)/shard_map/all_to_all | solution.py:159
  43.6 15.2 %all-to-all-start.2 = ((bf16[128,32,128]{2,0,1:T(8,128)(2,1)}), bf16[128,32,128]{2,0,1:T(8,128)(2,1)S(1)}, u32[]{:S(2)}, u32[]{:S(2)}) async-start(bf16[128,32,128]{2,0,1:T(8,128)(2,1)} %copy.213), calls=%async_computation.2 | async-start | bytes 2097152 | tf_op jit(solution)/shard_map/all_to_all | solution.py:152
  48.8 14.6 %copy-start.13 = (bf16[128,4,128]{0,2,1:T(8,128)(2,1)S(1)}, bf16[128,4,128]{0,2,1:T(8,128)(2,1)}, u32[]{:S(2)}) copy-start(bf16[128,4,128]{0,2,1:T(8,128)(2,1)} %copy-done.12) | copy-start | bytes 393220
  58.8 15.2 %all-to-all-start.5 = ((bf16[128,32,128]{2,0,1:T(8,128)(2,1)}), bf16[128,32,128]{2,0,1:T(8,128)(2,1)}, u32[]{:S(2)}, u32[]{:S(2)}) async-start(bf16[128,32,128]{2,0,1:T(8,128)(2,1)} %copy.222), calls=%async_computation.5 | async-start | bytes 2097152 | tf_op jit(solution)/shard_map/all_to_all | solution.py:155
  84.1 4.0 %copy-start = (f32[2,256,1280]{1,2,0:T(8,128)S(1)}, f32[2,256,1280]{1,2,0:T(8,128)}, u32[]{:S(2)}) copy-start(f32[2,256,1280]{1,2,0:T(8,128)} %get-tuple-element.493) | copy-start | bytes 7864324 | tf_op jit(solution)/shard_map/while
  88.1 1.6 copy-start.2
  105.6 4.0 %copy-start = (f32[2,256,1280]{1,2,0:T(8,128)S(1)}, f32[2,256,1280]{1,2,0:T(8,128)}, u32[]{:S(2)}) copy-start(f32[2,256,1280]{1,2,0:T(8,128)} %get-tuple-element.493) | copy-start | bytes 7864324 | tf_op jit(solution)/shard_map/while
  109.6 1.6 copy-start.2
  127.1 4.0 %copy-start = (f32[2,256,1280]{1,2,0:T(8,128)S(1)}, f32[2,256,1280]{1,2,0:T(8,128)}, u32[]{:S(2)}) copy-start(f32[2,256,1280]{1,2,0:T(8,128)} %get-tuple-element.493) | copy-start | bytes 7864324 | tf_op jit(solution)/shard_map/while
  131.1 1.6 copy-start.2
  148.6 4.0 %copy-start = (f32[2,256,1280]{1,2,0:T(8,128)S(1)}, f32[2,256,1280]{1,2,0:T(8,128)}, u32[]{:S(2)}) copy-start(f32[2,256,1280]{1,2,0:T(8,128)} %get-tuple-element.493) | copy-start | bytes 7864324 | tf_op jit(solution)/shard_map/while
  152.6 1.6 copy-start.2
  170.1 4.0 %copy-start = (f32[2,256,1280]{1,2,0:T(8,128)S(1)}, f32[2,256,1280]{1,2,0:T(8,128)}, u32[]{:S(2)}) copy-start(f32[2,256,1280]{1,2,0:T(8,128)} %get-tuple-element.493) | copy-start | bytes 7864324 | tf_op jit(solution)/shard_map/while
  174.1 1.6 copy-start.2
  191.6 4.0 %copy-start = (f32[2,256,1280]{1,2,0:T(8,128)S(1)}, f32[2,256,1280]{1,2,0:T(8,128)}, u32[]{:S(2)}) copy-start(f32[2,256,1280]{1,2,0:T(8,128)} %get-tuple-element.493) | copy-start | bytes 7864324 | tf_op jit(solution)/shard_map/while
  195.7 1.6 copy-start.2
  213.2 4.0 %copy-start = (f32[2,256,1280]{1,2,0:T(8,128)S(1)}, f32[2,256,1280]{1,2,0:T(8,128)}, u32[]{:S(2)}) copy-start(f32[2,256,1280]{1,2,0:T(8,128)} %get-tuple-element.493) | copy-start | bytes 7864324 | tf_op jit(solution)/shard_map/while
  217.2 1.6 copy-start.2
  234.7 4.0 %copy-start = (f32[2,256,1280]{1,2,0:T(8,128)S(1)}, f32[2,256,1280]{1,2,0:T(8,128)}, u32[]{:S(2)}) copy-start(f32[2,256,1280]{1,2,0:T(8,128)} %get-tuple-element.493) | copy-start | bytes 7864324 | tf_op jit(solution)/shard_map/while
  238.7 1.6 copy-start.2
  249.8 7.9 %copy-start.3 = (f32[256,2,128]{2,1,0:T(2,128)S(1)}, f32[256,2,128]{2,1,0:T(2,128)}, u32[]{:S(2)}) copy-start(f32[256,2,128]{2,1,0:T(2,128)} %get-tuple-element.204) | copy-start | bytes 786436
  249.9 8.6 %copy-start.5 = (bf16[8,256,2,128]{3,1,2,0:T(8,128)(2,1)S(1)}, bf16[8,256,2,128]{3,1,2,0:T(8,128)(2,1)}, u32[]{:S(2)}) copy-start(bf16[8,256,2,128]{3,1,2,0:T(8,128)(2,1)} %get-tuple-element.201) | copy-start | bytes 3145732
  250.6 9.9 %all-to-all-start.8 = ((bf16[256,2,128]{2,1,0:T(2,128)(2,1)}), bf16[256,2,128]{2,1,0:T(2,128)(2,1)S(1)}, u32[]{:S(2)}, u32[]{:S(2)}) async-start(bf16[256,2,128]{2,1,0:T(2,128)(2,1)} %convert_element_type.206), calls=%async_computation.8 | async-start | bytes 262144 | tf_op jit(solution)/shard_map/all_to_all | solution.py:172
  260.5 7.8 %all-to-all-start.9 = ((bf16[256,2,128]{2,1,0:T(2,128)(2,1)}), bf16[256,2,128]{2,1,0:T(2,128)(2,1)S(1)}, u32[]{:S(2)}, u32[]{:S(2)}) async-start(bf16[256,2,128]{2,1,0:T(2,128)(2,1)} %convert_element_type.214), calls=%async_computation.9 | async-start | bytes 262144 | tf_op jit(solution)/shard_map/all_to_all | solution.py:175
  268.4 13.0 %all-to-all-start.7 = ((bf16[256,16,128]{2,1,0:T(8,128)(2,1)}), bf16[256,16,128]{2,1,0:T(8,128)(2,1)S(1)}, u32[]{:S(2)}, u32[]{:S(2)}) async-start(bf16[256,16,128]{2,1,0:T(8,128)(2,1)} %bitcast.38), calls=%async_computation.7 | async-start | bytes 2097152 | tf_op jit(solution)/shard_map/all_to_all | solution.py:169
  281.3 23.1 %all-to-all-start.6 = ((bf16[256,16,128]{2,1,0:T(8,128)(2,1)}), bf16[256,16,128]{2,1,0:T(8,128)(2,1)}, u32[]{:S(2)}, u32[]{:S(2)}) async-start(bf16[256,16,128]{2,1,0:T(8,128)(2,1)} %bitcast.33), calls=%async_computation.6 | async-start | bytes 2097152 | tf_op jit(solution)/shard_map/all_to_all | solution.py:168
  287.9 1.9 copy-start.7
  292.4 1.3 copy-start.1
  304.4 5.0 %copy-start.9 = (f32[128,128]{1,0:T(8,128)S(1)}, f32[128,128]{1,0:T(8,128)}, u32[]{:S(2)}) copy-start(f32[128,128]{1,0:T(8,128)} %copy-done.8) | copy-start | bytes 196612
where the time goes:
time: 356 us; the launch traced here: 352 us
  local copies, waits for them, and re-layouts  118 us (33%)
  other arithmetic  56.7 us (16%)
  matrix products  55.8 us (16%)
  blocking collectives  40.7 us (11%)
  starting transfers between devices  38.6 us (11%)
  waiting for transfers between devices  34.3 us (10%)
  loops' own time  6.03 us (2%)
    psum x1, blocking collectives, body(): lax.psum((jnp.sum(grad_query, axis=0).reshape(HQ * HD), jnp.sum(grad_key,...  40.7 us
    dynamic_update_slice x8, local copies, waits for them, and re-layouts, head_step(): lax.dynamic_update_index_in_dim(value_acc, old_value + grad_value, owner, 1)  35.1 us
    sub x8, matrix products, row_step(): expo = jnp.exp(scores - highest)  26.9 us
    dynamic_update_slice x8, local copies, waits for them, and re-layouts, head_step(): lax.dynamic_update_index_in_dim(key_acc, old_key + grad_key, owner, 1)  23 us
    convert_element_type x8, other arithmetic, row_step(): probs_b = probs.astype(jnp.bfloat16)  16.8 us
    unnamed x39, local copies, waits for them, and re-layouts  13.4 us
    dynamic_slice x8, local copies, waits for them, and re-layouts, head_step(): cot_part = lax.dynamic_slice_in_dim(cotangent, head_zero, head_block, 1)  9.49 us
    dot_general x8, matrix products, row_step(): jnp.einsum('hrk,rhd->kd', dscore[:, :, prefix:], query_rows, preferred_el...  9 us
  transfers between devices with their start and end apart: 10, of which 8 were waited for; matrix products, arithmetic and copies ran while one was open for 14% of the time, Pallas kernels for 0%

commit v1 on v0

v1 whole, which is shorter than its diff:
```python
import functools
import math

import jax
import jax.numpy as jnp
from jax import lax
from jax.experimental import pallas as pl
from jax.experimental.pallas import tpu as pltpu
from jax.sharding import PartitionSpec as P

HQ = 32
KV = 4
HD = 128
GROUP = 8
HEADS = 4
NEG = -1e30


def turn(x):
    return pltpu.roll(x, HD // 2, 1)


def dot(a, b, dims):
    return lax.dot_general(a, b, (dims, ((), ())), preferred_element_type=jnp.float32)


NT = ((1,), (1,))
NN = ((1,), (0,))
TN = ((0,), (0,))


def pack_kernel(groups, ck_ref, cv_ref, *rest):
    outs, sems = rest[:-1], rest[-1]
    rows = ck_ref.shape[0]
    copies = []
    for slot, (g, out) in enumerate(zip(groups, outs)):
        for half, src in enumerate((ck_ref, cv_ref)):
            copy = pltpu.make_async_copy(
                src.at[:, pl.ds(g * HD, HD)],
                out.at[pl.ds(half * rows, rows)],
                sems.at[2 * slot + half],
            )
            copy.start()
            copies.append(copy)
    for copy in copies:
        copy.wait()


def pack(groups, ck, cv):
    rows = ck.shape[0]
    any_spec = pl.BlockSpec(memory_space=pl.ANY)
    return pl.pallas_call(
        functools.partial(pack_kernel, groups),
        out_shape=[jax.ShapeDtypeStruct((2 * rows, HD), ck.dtype) for _ in groups],
        in_specs=[any_spec] * 2,
        out_specs=[any_spec] * len(groups),
        scratch_shapes=[pltpu.SemaphoreType.DMA((2 * len(groups),))],
        cost_estimate=pl.CostEstimate(
            flops=0, bytes_accessed=8 * rows * HD * len(groups), transcendentals=0
        ),
        name="pack",
    )(ck, cv)


def attend_kernel(
    shards, chained,
    at_ref, q_ref, do_ref, bq_ref, cos_ref, sin_ref,
    ck_ref, cv_ref, kp_ref, vp_ref, bk_ref, bv_ref, *rest,
):
    far, rest = rest[: 2 * (shards - 1)], rest[2 * (shards - 1):]
    rest = rest[2 if chained else 0:]
    (out_ref, gq_ref, sq_ref, dk_ref, dv_ref, send_ref, sk_ref, sv_ref,
     keys, values, dkt, dvt) = rest
    step = pl.program_id(0)
    tokens = q_ref.shape[0]
    slots = ck_ref.shape[0]
    prefix = shards * slots
    slab = shards * tokens
    first = at_ref[0]
    rank = at_ref[1]

    @pl.when(step == 0)
    def _():
        keys[pl.ds(0, slots)] = ck_ref[...]
        values[pl.ds(0, slots)] = cv_ref[...]
        for s in range(1, shards):
            keys[pl.ds(s * slots, slots)] = far[s - 1][pl.ds(0, slots)]
            values[pl.ds(s * slots, slots)] = far[s - 1][pl.ds(slots, slots)]
        for s in range(shards):
            rows = pl.ds(s * tokens, tokens)
            if s == 0:
                kp, vp = kp_ref[...], vp_ref[...]
            else:
                block = far[shards - 1 + s - 1]
                kp, vp = block[0], block[1]
            k = kp.astype(jnp.float32) + bk_ref[...].astype(jnp.float32)
            k = k * cos_ref[rows, :] + turn(k) * sin_ref[rows, :]
            v = vp.astype(jnp.float32) + bv_ref[...].astype(jnp.float32)
            place = pl.ds(prefix + s * tokens, tokens)
            keys[place] = k.astype(jnp.bfloat16)
            values[place] = v.astype(jnp.bfloat16)
        dkt[...] = jnp.zeros_like(dkt)
        dvt[...] = jnp.zeros_like(dvt)

    cosine = cos_ref[pl.ds(0, tokens), :]
    sine = sin_ref[pl.ds(0, tokens), :]
    queries = []
    cots = []
    for h in range(HEADS):
        cols = pl.ds(h * HD, HD)
        x = q_ref[:, cols].astype(jnp.float32) + bq_ref[:, cols].astype(jnp.float32)
        x = x * cosine + turn(x) * sine
        queries.append(x.astype(jnp.bfloat16))
        cots.append(do_ref[:, cols])
    q = jnp.concatenate(queries, axis=0)
    do = jnp.concatenate(cots, axis=0)
    rows = HEADS * tokens

    scale = HD ** -0.5
    s = dot(q, keys[...], NT)
    parts = []
    col = lax.broadcasted_iota(jnp.int32, (1, slots), 1)
    for j in range(shards):
        owner = lax.rem(rank - j + shards, shards)
        part = s[:, j * slots:(j + 1) * slots]
        parts.append(jnp.where(col < first - owner * slots, part, NEG))
    part = s[:, prefix:prefix + tokens]
    token = lax.broadcasted_iota(jnp.int32, (rows, tokens), 0) & (tokens - 1)
    parts.append(jnp.where(lax.broadcasted_iota(jnp.int32, (rows, tokens), 1) <= token, part, NEG))
    for j in range(1, shards):
        part = s[:, prefix + j * tokens:prefix + (j + 1) * tokens]
        parts.append(jnp.where(rank >= j, part, NEG))
    s = jnp.concatenate(parts, axis=1)
    top = jnp.max(s, axis=1, keepdims=True)
    e = jnp.exp2((s - top) * (scale * math.log2(math.e)))
    p = e * (1.0 / jnp.sum(e, axis=1, keepdims=True))
    pb = p.astype(jnp.bfloat16)
    o = dot(pb, values[...], NN).astype(jnp.bfloat16)
    delta = jnp.sum(do.astype(jnp.float32) * o.astype(jnp.float32), axis=1, keepdims=True)
    dp = dot(do, values[...], NT)
    ds = (p * (dp - delta)).astype(jnp.bfloat16)
    dq = (dot(ds, keys[...], NN) * scale).astype(jnp.bfloat16).astype(jnp.float32)
    for h in range(HEADS):
        cols = pl.ds(h * HD, HD)
        part = slice(h * tokens, (h + 1) * tokens)
        out_ref[:, cols] = o[part]
        g = dq[part]
        g = g * cosine - turn(g) * sine
        gq_ref[:, cols] = g.astype(jnp.bfloat16)
        sq_ref[:, cols] = jnp.sum(g, axis=0, keepdims=True)
    dkt[...] += dot(q, ds[:, prefix:], TN)
    dvt[...] += dot(do, pb[:, prefix:], TN)

    @pl.when(step == pl.num_programs(0) - 1)
    def _():
        dk = dkt[...].T * scale
        dv = dvt[...].T
        gk = dk * cos_ref[...] - turn(dk) * sin_ref[...]
        dk_ref[...] = dk[:tokens]
        dv_ref[...] = dv[:tokens]
        for j in range(1, shards):
            block = slice(j * tokens, (j + 1) * tokens)
            send_ref[2 * (j - 1)] = dk[block].astype(jnp.bfloat16)
            send_ref[2 * (j - 1) + 1] = dv[block].astype(jnp.bfloat16)
        sk_ref[...] = jnp.sum(gk, axis=0, keepdims=True)
        sv_ref[...] = jnp.sum(dv, axis=0, keepdims=True)


def attend(g, shards, at, q, do, bq, cosine, sine, ck, cv, kp, vp, bk, bv, far, slabs, before):
    tokens, slots = q.shape[0], ck.shape[0]
    slab = shards * tokens
    total = slab + shards * slots
    steps = GROUP // HEADS
    width = HEADS * HD

    def wide(rows):
        return pl.BlockSpec((rows, width), lambda i: (0, g * steps + i))

    def column(rows):
        return pl.BlockSpec((rows, HD), lambda i: (0, g))

    def whole(shape):
        return pl.BlockSpec(shape, lambda i: (0,) * len(shape))

    in_specs = [
        pl.BlockSpec(memory_space=pltpu.SMEM),
        wide(tokens), wide(tokens), wide(1),
        whole((slab, HD)), whole((slab, HD)),
        column(slots), column(slots), column(tokens), column(tokens), column(1), column(1),
    ]
    in_specs += [whole(a.shape) for a in far]
    in_specs += [pl.BlockSpec((2, tokens, HD), lambda i: (0, 0, g)) for _ in slabs]
    aliases = {}
    if before is not None:
        aliases = {len(in_specs): 0, len(in_specs) + 1: 1}
        in_specs += [pl.BlockSpec(memory_space=pl.ANY)] * 2
    f32, b16 = jnp.float32, jnp.bfloat16
    flops = 2 * GROUP * tokens * HD * (4 * total + 2 * slab)
    return pl.pallas_call(
        functools.partial(attend_kernel, shards, before is not None),
        grid=(steps,),
        in_specs=in_specs,
        out_shape=[
            jax.ShapeDtypeStruct((tokens, HQ * HD), b16),
            jax.ShapeDtypeStruct((tokens, HQ * HD), b16),
            jax.ShapeDtypeStruct((1, GROUP * HD), f32),
            jax.ShapeDtypeStruct((tokens, HD), f32),
            jax.ShapeDtypeStruct((tokens, HD), f32),
            jax.ShapeDtypeStruct((max(2 * (shards - 1), 1), tokens, HD), b16),
            jax.ShapeDtypeStruct((1, HD), f32),
            jax.ShapeDtypeStruct((1, HD), f32),
        ],
        out_specs=[
            wide(tokens), wide(tokens),
            pl.BlockSpec((1, width), lambda i: (0, i)),
            whole((tokens, HD)), whole((tokens, HD)),
            whole((max(2 * (shards - 1), 1), tokens, HD)),
            whole((1, HD)), whole((1, HD)),
        ],
        scratch_shapes=[
            pltpu.VMEM((total, HD), b16), pltpu.VMEM((total, HD), b16),
            pltpu.VMEM((HD, slab), f32), pltpu.VMEM((HD, slab), f32),
        ],
        input_output_aliases=aliases,
        compiler_params=pltpu.CompilerParams(
            dimension_semantics=("arbitrary",), vmem_limit_bytes=40 * 1024 * 1024
        ),
        cost_estimate=pl.CostEstimate(
            flops=flops,
            bytes_accessed=8 * tokens * GROUP * HD + 8 * total * HD,
            transcendentals=GROUP * tokens * total,
        ),
        name="attend",
    )(at, q, do, bq, cosine, sine, ck, cv, kp, vp, bk, bv, *far, *slabs, *(before or ()))


def body(q_proj, k_proj, v_proj, cache_k, cache_v, bias_q, bias_k, bias_v, start, dout):
    shards = lax.axis_size("seq")
    rank = lax.axis_index("seq")
    tokens = q_proj.shape[1]
    first = start[0]
    ck, cv = cache_k[0], cache_v[0]

    def ring(x, s):
        return lax.ppermute(x, "seq", [(i, (i + s) % shards) for i in range(shards)])

    def later(x, s):
        return lax.ppermute(x, "seq", [(i, i + s) for i in range(shards - s)])

    def earlier(x, s):
        return lax.ppermute(x, "seq", [(i + s, i) for i in range(shards - s)])

    chunks = pack((0,), ck, cv) + pack(tuple(range(1, KV)), ck, cv)
    own = jnp.stack([k_proj[0], v_proj[0]])
    slabs = [later(own, s) for s in range(1, shards)]
    far = [[ring(chunk, s) for s in range(1, shards)] for chunk in chunks]

    owners = lax.rem(rank - jnp.arange(shards, dtype=jnp.int32) + shards, shards)
    positions = first + owners[:, None] * tokens + jnp.arange(tokens, dtype=jnp.int32)[None]
    freqs = jnp.exp(
        -(2.0 * jnp.arange(HD // 2, dtype=jnp.float32) / HD) * jnp.log(jnp.float32(1000000.0))
    )
    angles = positions.reshape(-1).astype(jnp.float32)[:, None] * freqs[None, :]
    c, n = jnp.cos(angles), jnp.sin(angles)
    cosine = jnp.concatenate([c, c], axis=1)
    sine = jnp.concatenate([-n, n], axis=1)
    at = jnp.stack([first, rank.astype(jnp.int32)])

    before = None
    sums_q, sums_k, sums_v, grads_k, grads_v = [], [], [], [], []
    for g in range(KV):
        out, gq, sq, dk, dv, send, sk, sv = attend(
            g, shards, at, q_proj[0], dout[0], bias_q[None], cosine, sine, ck, cv,
            k_proj[0], v_proj[0], bias_k[None], bias_v[None], far[g], slabs, before,
        )
        before = (out, gq)
        sums_q.append(sq[0])
        sums_k.append(sk[0])
        sums_v.append(sv[0])
        for s in range(1, shards):
            back = earlier(send[2 * (s - 1):2 * s], s).astype(jnp.float32)
            dk = dk + back[0]
            dv = dv + back[1]
        turned = jnp.concatenate([dk[:, HD // 2:], dk[:, :HD // 2]], axis=1)
        grads_k.append(dk * cosine[:tokens] - turned * sine[:tokens])
        grads_v.append(dv)
    sums = lax.psum(jnp.concatenate(sums_q + sums_k + sums_v), ("dp", "seq"))
    wide, narrow = HQ * HD, KV * HD
    return (
        out[None],
        gq[None],
        jnp.concatenate(grads_k, axis=1).astype(jnp.bfloat16)[None],
        jnp.concatenate(grads_v, axis=1).astype(jnp.bfloat16)[None],
        sums[:wide],
        sums[wide:wide + narrow],
        sums[wide + narrow:],
    )


def solution(mesh):
    split = P("dp", "seq", None)
    return jax.shard_map(
        body,
        mesh=mesh,
        in_specs=(split,) * 5 + (P(), P(), P(), P("dp"), split),
        out_specs=(split,) * 4 + (P(), P(), P()),
        check_vma=False,
    )
```

time: 356 us -> 155 us (0.44)
  local copies, waits for them, and re-layouts: 118 us -> 19.3 us
  Pallas kernels: 0 us -> 64.9 us
  matrix products: 55.8 us -> 0 us
  other arithmetic: 56.7 us -> 4.26 us
  waiting for transfers between devices: 34.3 us -> 8.39 us
  starting transfers between devices: 38.6 us -> 14.2 us
  loops' own time: 6.03 us -> 0 us
    pallas_call x0 -> x6, Pallas kernels: none -> 64.9 us  [the longest x2 34 us: pack(): pl.pallas_call(functools.partial(pack_kernel, groups), out_shape=[jax.Sha...]
    dynamic_update_slice x24 -> x0, local copies, waits for them, and re-layouts: 63.5 us -> none  [the longest x8 35.1 us: head_step(): lax.dynamic_update_index_in_dim(value_acc, old_value + grad_value, owner, 1)]
    all_to_all x10 -> x0, starting transfers between devices: 38.6 us -> none  [the longest x1 4.71 us: body(): lax.all_to_all(outputs, 'seq', split_axis=0, concat_axis=1, tiled=True)]
    all_to_all x10 -> x0, waiting for transfers between devices: 34.3 us -> none  [the longest x1 8.66 us: body(): lax.all_to_all(queries, 'seq', split_axis=1, concat_axis=0, tiled=True)]
    dot_general x40 -> x0, matrix products: 28.9 us -> none  [the longest x8 9 us: row_step(): jnp.einsum('hrk,rhd->kd', dscore[:, :, prefix:], query_rows, preferred_el...]
    sub x8 -> x0, matrix products: 26.9 us -> none  [row_step(): expo = jnp.exp(scores - highest)]
    convert_element_type x17 -> x5, other arithmetic: 26.5 us -> 0.12 us  [the longest x1 0.07 us: body(): angles = positions.reshape(-1).astype(jnp.float32)[:, None] * freqs[None, :]]
    dynamic_slice x24 -> x0, local copies, waits for them, and re-layouts: 16.3 us -> none  [the longest x8 9.49 us: head_step(): cot_part = lax.dynamic_slice_in_dim(cotangent, head_zero, head_block, 1)]
  transfers between devices with their start and end apart: 10 -> 9, of which waited for: 8 -> 2; matrix products, arithmetic and copies ran while one was open for 14% -> 3% of each run, Pallas kernels for 0% -> 37%
where the time goes in v1:
time: 155 us; the launch traced here: 154 us
  Pallas kernels  64.9 us (42%)
  blocking collectives  41.1 us (27%)
  local copies, waits for them, and re-layouts  19.3 us (12%)
  starting transfers between devices  14.2 us (9%)
  waiting for transfers between devices  8.39 us (5%)
  other arithmetic  4.26 us (3%)
  between operations  1.7 us (1%)
    psum x1, blocking collectives, body(): sums = lax.psum(jnp.concatenate(sums_q + sums_k + sums_v), ('dp', 'seq'))  41.1 us
    pallas_call x2, Pallas kernels, pack(): pl.pallas_call(functools.partial(pack_kernel, groups), out_shape=[jax.Sha...  34 us
    pallas_call x4, Pallas kernels, attend(): pl.pallas_call(functools.partial(attend_kernel, shards, before is not Non...  30.9 us
    unnamed x63, local copies, waits for them, and re-layouts  16.5 us
    ppermute x4, starting transfers between devices, earlier(): return lax.ppermute(x, 'seq', [(i + s, i) for i in range(shards - s)])  5.15 us
    ppermute x1, starting transfers between devices, later(): return lax.ppermute(x, 'seq', [(i, i + s) for i in range(shards - s)])  4.87 us
    ppermute x4, waiting for transfers between devices, earlier(): return lax.ppermute(x, 'seq', [(i + s, i) for i in range(shards - s)])  4.72 us
    ppermute x4, starting transfers between devices, ring(): lax.ppermute(x, 'seq', [(i, (i + s) % shards) for i in range(shards)])  4.17 us
  transfers between devices with their start and end apart: 9, of which 2 were waited for; matrix products, arithmetic and copies ran while one was open for 3% of the time, Pallas kernels for 37%

profile of v1, /device:TPU:0, one launch (start us, length us, event | category | flops | bytes accessed | tf_op | source)
XLA Modules:
  0.0 153.8 jit_solution(16462241596118581219)
XLA Ops:
  0.6 1.7 %pad_maximum_fusion = bf16[2,128,512]{2,1,0:T(8,128)(2,1)} fusion(bf16[1,128,512]{2,1,0:T(8,128)(2,1)} %param.12, bf16[1,128,512]{2,1,0:T(8,128)(2,1)} %param.11), kind=kLoop, calls=%fused_computation | loop fusion | flops 131072 | bytes 524288 | tf_op jit(solution)/shard_map/stack | solution.py:254
  2.3 4.9 %collective-permute-start.1 = (bf16[2,128,512]{2,1,0:T(8,128)(2,1)}, bf16[2,128,512]{2,1,0:T(8,128)(2,1)S(1)}, u32[]{:S(2)}, u32[]{:S(2)}) collective-permute-start(bf16[2,128,512]{2,1,0:T(8,128)(2,1)} %pad_maximum_fusion), channel_id=1, source_target_pairs={{0,1},{2,3},{4,5},{6,7},{8,9},{10,11},{12,13},{14,15},{16,17},{18,... | collective-permute-start | bytes 786440 | tf_op jit(solution)/shard_map/ppermute | solution.py:248
  7.2 0.0 copy-start.3
  7.2 0.0 copy-start.4
  7.2 0.0 copy-start.5
  7.2 9.1 %pack.3 = bf16[1024,128]{1,0:T(8,128)(2,1)} custom-call(bf16[512,512]{1,0:T(8,128)(2,1)} %bitcast.97, bf16[512,512]{1,0:T(8,128)(2,1)} %bitcast.103), custom_call_target="tpu_custom_call" | custom-call | bytes 524288 | tf_op jit(solution)/shard_map/pack/pallas_call | solution.py:52
  16.3 0.0 copy-start.2
  16.3 0.1 collective-permute-start.4
  16.4 25.0 %pack.2 = (bf16[1024,128]{1,0:T(8,128)(2,1)}, bf16[1024,128]{1,0:T(8,128)(2,1)}, bf16[1024,128]{1,0:T(8,128)(2,1)}) custom-call(bf16[512,512]{1,0:T(8,128)(2,1)} %bitcast.98, bf16[512,512]{1,0:T(8,128)(2,1)} %bitcast.104), custom_call_target="tpu_custom_call" | custom-call | bytes 1572864 | tf_op jit(solution)/shard_map/pack/pallas_call | solution.py:52
  41.4 2.1 %collective-permute-start = (bf16[1024,128]{1,0:T(8,128)(2,1)}, bf16[1024,128]{1,0:T(8,128)(2,1)S(1)}, u32[]{:S(2)}, u32[]{:S(2)}) collective-permute-start(bf16[1024,128]{1,0:T(8,128)(2,1)} %get-tuple-element.42), channel_id=1, source_target_pairs={{0,1},{1,0},{2,3},{3,2},{4,5},{5,4},{6,7},{7,6},{8,9},{9,8},{10,11... | collective-permute-start | bytes 786440 | tf_op jit(solution)/shard_map/ppermute | solution.py:245
  43.5 0.1 collective-permute-start.2
  43.5 1.9 %collective-permute-start.3 = (bf16[1024,128]{1,0:T(8,128)(2,1)}, bf16[1024,128]{1,0:T(8,128)(2,1)S(1)}, u32[]{:S(2)}, u32[]{:S(2)}) collective-permute-start(bf16[1024,128]{1,0:T(8,128)(2,1)} %get-tuple-element.44), channel_id=1, source_target_pairs={{0,1},{1,0},{2,3},{3,2},{4,5},{5,4},{6,7},{7,6},{8,9},{9,8},{10,11... | collective-permute-start | bytes 786440 | tf_op jit(solution)/shard_map/ppermute | solution.py:245
  46.2 0.1 convert_bitcast_fusion
  46.3 0.5 fusion.22
  46.8 0.0 copy-start.19
  46.8 0.0 copy-start.25
  46.9 0.1 pad_maximum_fusion.3
  47.0 0.5 copy-done.17
  47.5 0.0 copy-done.19
  47.5 0.0 copy-done.21
  47.5 0.1 pad_add_fusion.at_ref
  47.6 0.6 copy-done.23
  48.3 8.1 %attend.4 = (bf16[128,4096]{1,0:T(8,128)(2,1)}, bf16[128,4096]{1,0:T(8,128)(2,1)}, f32[1,1024]{1,0:T(1,128)S(1)}, f32[128,128]{1,0:T(8,128)S(1)}, f32[128,128]{1...) custom-call(s32[2]{0:T(128)S(1)} %pad_add_fusion.at_ref, ...), custom_call_target="tpu_custom_call" | custom-call | flops 1476395008 | bytes 2359296 | tf_op jit(solution)/shard_map/attend/pallas_call | solution.py:199
  56.4 0.6 constant_dynamic-update-slice_fusion.11
  57.0 3.7 %collective-permute-done.3.rest_0_ = bf16[1024,128]{1,0:T(8,128)(2,1)S(1)} collective-permute-done((bf16[1024,128]{1,0:T(8,128)(2,1)}, bf16[1024,128]{1,0:T(8,128)(2,1)S(1)}, u32[]{:S(2)}, u32[]{:S(2)}) %collective-permute-start.3) | collective-permute-done | bytes 262176 | tf_op jit(solution)/shard_map/ppermute | solution.py:245
  60.7 7.5 %attend.5 = (bf16[128,4096]{1,0:T(8,128)(2,1)}, bf16[128,4096]{1,0:T(8,128)(2,1)}, f32[1,1024]{1,0:T(1,128)S(1)}, f32[128,128]{1,0:T(8,128)S(1)}, f32[128,128]{1...) custom-call(s32[2]{0:T(128)S(1)} %pad_add_fusion.at_ref, ...), custom_call_target="tpu_custom_call", output_to_operand_aliasing={{0}: (14, {}), {1}: (15, {})} | custom-call | flops 1476395008 | bytes 2359296 | tf_op jit(solution)/shard_map/attend/pallas_call | solution.py:199
  68.2 0.6 copy-done.6
  68.8 0.6 copy-done.8
  69.5 0.6 copy-done.12
  70.1 0.6 constant_dynamic-update-slice_fusion.10
  70.7 7.5 %attend.6 = (bf16[128,4096]{1,0:T(8,128)(2,1)}, bf16[128,4096]{1,0:T(8,128)(2,1)}, f32[1,1024]{1,0:T(1,128)S(1)}, f32[128,128]{1,0:T(8,128)S(1)}, f32[128,128]{1...) custom-call(s32[2]{0:T(128)S(1)} %pad_add_fusion.at_ref, ...), custom_call_target="tpu_custom_call", output_to_operand_aliasing={{0}: (14, {}), {1}: (15, {})} | custom-call | flops 1476395008 | bytes 2359296 | tf_op jit(solution)/shard_map/attend/pallas_call | solution.py:199
  78.2 0.6 copy-done.14
  78.8 0.6 constant_dynamic-update-slice_fusion.9
  79.4 7.7 %attend.7 = (bf16[128,4096]{1,0:T(8,128)(2,1)}, bf16[128,4096]{1,0:T(8,128)(2,1)}, f32[1,1024]{1,0:T(1,128)S(1)}, f32[128,128]{1,0:T(8,128)S(1)}, f32[128,128]{1...) custom-call(s32[2]{0:T(128)S(1)} %pad_add_fusion.at_ref, ...), custom_call_target="tpu_custom_call", output_to_operand_aliasing={{0}: (14, {}), {1}: (15, {})} | custom-call | flops 1476395008 | bytes 2359296 | tf_op jit(solution)/shard_map/attend/pallas_call | solution.py:199
  87.2 0.6 copy-done.16
  87.8 0.6 constant_dynamic-update-slice_fusion.8
  88.4 1.3 constant_dynamic-update-slice_fusion.7
  89.7 1.3 constant_dynamic-update-slice_fusion.6
  90.9 1.3 constant_dynamic-update-slice_fusion.5
  92.2 1.3 constant_dynamic-update-slice_fusion.4
  93.4 1.3 constant_dynamic-update-slice_fusion.3
  94.7 1.3 constant_dynamic-update-slice_fusion.2
  96.0 1.3 constant_dynamic-update-slice_fusion.1
  97.2 1.3 constant_dynamic-update-slice_fusion
  98.5 41.1 %psum.7 = f32[5120]{0:T(1024)S(1)} all-reduce(f32[5120]{0:T(1024)} %constant_dynamic-update-slice_fusion), channel_id=1, replica_groups=mesh['dp'=16,'seq'=2] {'dp','seq'}, use_global_device_ids=true, to_apply=%region_0.0 | all-reduce | flops 5120 | bytes 40960 | tf_op jit(solution)/shard_map/psum | solution.py:287
  139.6 1.3 collective-permute-start.5
  140.8 0.6 fusion.40
  141.4 0.6 slice.110
  142.0 1.3 collective-permute-start.8
  143.3 1.3 collective-permute-start.7
  144.7 1.3 collective-permute-start.6
  146.0 0.1 fusion.39
  146.1 4.7 %collective-permute-done.6 = bf16[2,128,128]{2,1,0:T(8,128)(2,1)S(1)} collective-permute-done((bf16[2,128,128]{2,1,0:T(8,128)(2,1)S(1)}, bf16[2,128,128]{2,1,0:T(8,128)(2,1)S(1)}, u32[]{:S(2)}, u32[]{:S(2)}) %collective-permute-start.6) | collective-permute-done | bytes 65568 | tf_op jit(solution)/shard_map/ppermute | solution.py:251
  150.9 0.1 fusion.36
  151.0 0.1 fusion.37
  151.1 0.0 copy-start.22
  151.2 0.1 fusion.38
  151.3 0.8 copy-done.22
  152.0 0.1 copy-done.18
  152.1 0.1 copy-done.20
  152.2 0.1 fusion.26
  152.3 0.7 pad_maximum_fusion.2
  153.0 0.1 fusion.25
  153.1 0.7 pad_maximum_fusion.1
  (53 shorter events, 0.3 us)
Async XLA Ops:
  2.3 45.9 %collective-permute-start.1 = (bf16[2,128,512]{2,1,0:T(8,128)(2,1)}, bf16[2,128,512]{2,1,0:T(8,128)(2,1)S(1)}, u32[]{:S(2)}, u32[]{:S(2)}) collective-permute-start(bf16[2,128,512]{2,1,0:T(8,128)(2,1)} %pad_maximum_fusion), channel_id=1, source_target_pairs={{0,1},{2,3},{4,5},{6,7},{8,9},{10,11},{12,13},{14,15},{16,17},{18,... | collective-permute-start | bytes 786440 | tf_op jit(solution)/shard_map/ppermute | solution.py:248
  7.2 41.1 %copy-start.3 = (bf16[1,128,4096]{2,1,0:T(8,128)(2,1)S(1)}, bf16[1,128,4096]{2,1,0:T(8,128)(2,1)}, u32[]{:S(2)}) copy-start(bf16[1,128,4096]{2,1,0:T(8,128)(2,1)} %param.19) | copy-start | bytes 3145732
  7.2 41.1 %copy-start.4 = (bf16[1,128,512]{2,1,0:T(8,128)(2,1)S(1)}, bf16[1,128,512]{2,1,0:T(8,128)(2,1)}, u32[]{:S(2)}) copy-start(bf16[1,128,512]{2,1,0:T(8,128)(2,1)} %param.11) | copy-start | bytes 393220
  7.2 41.1 %copy-start.5 = (bf16[1,128,512]{2,1,0:T(8,128)(2,1)S(1)}, bf16[1,128,512]{2,1,0:T(8,128)(2,1)}, u32[]{:S(2)}) copy-start(bf16[1,128,512]{2,1,0:T(8,128)(2,1)} %param.12) | copy-start | bytes 393220
  16.3 32.0 %copy-start.2 = (bf16[1,128,4096]{2,1,0:T(8,128)(2,1)S(1)}, bf16[1,128,4096]{2,1,0:T(8,128)(2,1)}, u32[]{:S(2)}) copy-start(bf16[1,128,4096]{2,1,0:T(8,128)(2,1)} %param.10) | copy-start | bytes 3145732
  16.3 31.9 %collective-permute-start.4 = (bf16[1024,128]{1,0:T(8,128)(2,1)}, bf16[1024,128]{1,0:T(8,128)(2,1)}, u32[]{:S(2)}, u32[]{:S(2)}) collective-permute-start(bf16[1024,128]{1,0:T(8,128)(2,1)} %pack.3), channel_id=1, source_target_pairs={{0,1},{1,0},{2,3},{3,2},{4,5},{5,4},{6,7},{7,6},{8,9},{9,8},{10,11... | collective-permute-start | bytes 786440 | tf_op jit(solution)/shard_map/ppermute | solution.py:245
  41.4 38.0 %collective-permute-start = (bf16[1024,128]{1,0:T(8,128)(2,1)}, bf16[1024,128]{1,0:T(8,128)(2,1)S(1)}, u32[]{:S(2)}, u32[]{:S(2)}) collective-permute-start(bf16[1024,128]{1,0:T(8,128)(2,1)} %get-tuple-element.42), channel_id=1, source_target_pairs={{0,1},{1,0},{2,3},{3,2},{4,5},{5,4},{6,7},{7,6},{8,9},{9,8},{10,11... | collective-permute-start | bytes 786440 | tf_op jit(solution)/shard_map/ppermute | solution.py:245
  43.5 27.2 %collective-permute-start.2 = (bf16[1024,128]{1,0:T(8,128)(2,1)}, bf16[1024,128]{1,0:T(8,128)(2,1)S(1)}, u32[]{:S(2)}, u32[]{:S(2)}) collective-permute-start(bf16[1024,128]{1,0:T(8,128)(2,1)} %get-tuple-element.43), channel_id=1, source_target_pairs={{0,1},{1,0},{2,3},{3,2},{4,5},{5,4},{6,7},{7,6},{8,9},{9,8},{10,11... | collective-permute-start | bytes 786440 | tf_op jit(solution)/shard_map/ppermute | solution.py:245
  43.5 17.1 %collective-permute-start.3 = (bf16[1024,128]{1,0:T(8,128)(2,1)}, bf16[1024,128]{1,0:T(8,128)(2,1)S(1)}, u32[]{:S(2)}, u32[]{:S(2)}) collective-permute-start(bf16[1024,128]{1,0:T(8,128)(2,1)} %get-tuple-element.44), channel_id=1, source_target_pairs={{0,1},{1,0},{2,3},{3,2},{4,5},{5,4},{6,7},{7,6},{8,9},{9,8},{10,11... | collective-permute-start | bytes 786440 | tf_op jit(solution)/shard_map/ppermute | solution.py:245
  46.3 2.1 %copy-start = (bf16[1,512,512]{2,1,0:T(8,128)(2,1)S(1)}, bf16[1,512,512]{2,1,0:T(8,128)(2,1)}, u32[]{:S(2)}) copy-start(bf16[1,512,512]{2,1,0:T(8,128)(2,1)} %param.13) | copy-start | bytes 1572868
  46.3 2.1 %copy-start.1 = (bf16[1,512,512]{2,1,0:T(8,128)(2,1)S(1)}, bf16[1,512,512]{2,1,0:T(8,128)(2,1)}, u32[]{:S(2)}) copy-start(bf16[1,512,512]{2,1,0:T(8,128)(2,1)} %param.14) | copy-start | bytes 1572868
  46.8 0.7 copy-start.17
  46.8 0.7 copy-start.19
  46.8 0.7 copy-start.21
  46.8 0.8 copy-start.24
  46.8 0.8 copy-start.25
  47.5 0.7 copy-start.23
  56.4 11.8 %copy-start.10 = (bf16[2,128,128]{2,1,0:T(8,128)(2,1)}, bf16[2,128,128]{2,1,0:T(8,128)(2,1)S(1)}, u32[]{:S(2)}) copy-start(bf16[2,128,128]{2,1,0:T(8,128)(2,1)S(1)} %get-tuple-element.54) | copy-start | bytes 196612
  68.2 0.6 copy-start.6
  68.8 0.6 copy-start.8
  69.5 0.6 copy-start.12
  78.2 0.6 copy-start.14
  79.4 63.9 %copy-start.15 = (bf16[2,128,128]{2,1,0:T(8,128)(2,1)S(1)}, bf16[2,128,128]{2,1,0:T(8,128)(2,1)}, u32[]{:S(2)}) copy-start(bf16[2,128,128]{2,1,0:T(8,128)(2,1)} %copy-done.14) | copy-start | bytes 196612
  87.2 0.6 copy-start.16
  87.8 51.8 %copy-start.11 = (bf16[2,128,128]{2,1,0:T(8,128)(2,1)S(1)}, bf16[2,128,128]{2,1,0:T(8,128)(2,1)}, u32[]{:S(2)}) copy-start(bf16[2,128,128]{2,1,0:T(8,128)(2,1)} %copy-done.10) | copy-start | bytes 196612
  87.8 56.8 %copy-start.13 = (bf16[2,128,128]{2,1,0:T(8,128)(2,1)S(1)}, bf16[2,128,128]{2,1,0:T(8,128)(2,1)}, u32[]{:S(2)}) copy-start(bf16[2,128,128]{2,1,0:T(8,128)(2,1)} %copy-done.12) | copy-start | bytes 196612
  139.6 6.4 %collective-permute-start.5 = (bf16[2,128,128]{2,1,0:T(8,128)(2,1)S(1)}, bf16[2,128,128]{2,1,0:T(8,128)(2,1)S(1)}, u32[]{:S(2)}, u32[]{:S(2)}) collective-permute-start(bf16[2,128,128]{2,1,0:T(8,128)(2,1)S(1)} %copy-done.11), channel_id=1, source_target_pairs={{1,0},{3,2},{5,4},{7,6},{9,8},{11,10},{13,12},{15,14},{17,16},{19,... | collective-permute-start | bytes 196616 | tf_op jit(solution)/shard_map/ppermute | solution.py:251
  142.0 9.0 %collective-permute-start.8 = (bf16[2,128,128]{2,1,0:T(8,128)(2,1)}, bf16[2,128,128]{2,1,0:T(8,128)(2,1)S(1)}, u32[]{:S(2)}, u32[]{:S(2)}) collective-permute-start(bf16[2,128,128]{2,1,0:T(8,128)(2,1)} %copy-done.16), channel_id=1, source_target_pairs={{1,0},{3,2},{5,4},{7,6},{9,8},{11,10},{13,12},{15,14},{17,16},{19,... | collective-permute-start | bytes 196616 | tf_op jit(solution)/shard_map/ppermute | solution.py:251
  143.3 7.6 %collective-permute-start.7 = (bf16[2,128,128]{2,1,0:T(8,128)(2,1)S(1)}, bf16[2,128,128]{2,1,0:T(8,128)(2,1)S(1)}, u32[]{:S(2)}, u32[]{:S(2)}) collective-permute-start(bf16[2,128,128]{2,1,0:T(8,128)(2,1)S(1)} %copy-done.15), channel_id=1, source_target_pairs={{1,0},{3,2},{5,4},{7,6},{9,8},{11,10},{13,12},{15,14},{17,16},{19,... | collective-permute-start | bytes 196616 | tf_op jit(solution)/shard_map/ppermute | solution.py:251
  144.7 6.2 %collective-permute-start.6 = (bf16[2,128,128]{2,1,0:T(8,128)(2,1)S(1)}, bf16[2,128,128]{2,1,0:T(8,128)(2,1)S(1)}, u32[]{:S(2)}, u32[]{:S(2)}) collective-permute-start(bf16[2,128,128]{2,1,0:T(8,128)(2,1)S(1)} %copy-done.13), channel_id=1, source_target_pairs={{1,0},{3,2},{5,4},{7,6},{9,8},{11,10},{13,12},{15,14},{17,16},{19,... | collective-permute-start | bytes 196616 | tf_op jit(solution)/shard_map/ppermute | solution.py:251
  146.1 4.7 %copy-start.7 = (f32[128,128]{1,0:T(8,128)S(1)}, f32[128,128]{1,0:T(8,128)}, u32[]{:S(2)}) copy-start(f32[128,128]{1,0:T(8,128)} %copy-done.6) | copy-start | bytes 196612
  146.1 4.7 %copy-start.9 = (f32[128,128]{1,0:T(8,128)S(1)}, f32[128,128]{1,0:T(8,128)}, u32[]{:S(2)}) copy-start(f32[128,128]{1,0:T(8,128)} %copy-done.8) | copy-start | bytes 196612
  151.1 0.9 copy-start.22
  151.2 0.9 copy-start.18
  151.2 1.0 copy-start.20

commit v2 on v1

v2 whole, which is shorter than its diff:
```python
import functools
import math

import jax
import jax.numpy as jnp
from jax import lax
from jax.experimental import pallas as pl
from jax.experimental.pallas import tpu as pltpu
from jax.sharding import PartitionSpec as P

HQ = 32
KV = 4
HD = 128
GROUP = 8
HEADS = 2
NEG = -1e30
SUMS = (GROUP + 2) * HD
VMEM = 56 * 1024 * 1024
F32, B16 = jnp.float32, jnp.bfloat16


def turn(x):
    return pltpu.roll(x, HD // 2, 1)


def dot(a, b, dims):
    return lax.dot_general(a, b, (dims, ((), ())), preferred_element_type=F32)


NT = ((1,), (1,))
NN = ((1,), (0,))
TN = ((0,), (0,))


def whole(shape):
    return pl.BlockSpec(shape, lambda i: (0,) * len(shape))


def column(rows, g):
    return pl.BlockSpec((rows, HD), lambda i: (0, g))


def params():
    return pltpu.CompilerParams(dimension_semantics=("arbitrary",), vmem_limit_bytes=VMEM)


def pack_kernel(ck_ref, cv_ref, *rest):
    out_ref = rest[-1] if len(rest) == 1 else rest[2]
    rows = ck_ref.shape[0]
    out_ref[pl.ds(0, rows)] = ck_ref[...]
    out_ref[pl.ds(rows, rows)] = cv_ref[...]
    if len(rest) > 1:
        kp_ref, vp_ref, _, slab_ref = rest
        slab_ref[0] = kp_ref[...]
        slab_ref[1] = vp_ref[...]


def pack(g, ck, cv, slab=()):
    rows = ck.shape[0]
    out_shape = [jax.ShapeDtypeStruct((2 * rows, HD), B16)]
    if slab:
        out_shape.append(jax.ShapeDtypeStruct((2,) + slab[0].shape, B16))
    return pl.pallas_call(
        pack_kernel,
        grid=(1,),
        in_specs=[column(rows, g)] * 2 + [whole(a.shape) for a in slab],
        out_specs=[whole(a.shape) for a in out_shape],
        out_shape=out_shape,
        compiler_params=params(),
        cost_estimate=pl.CostEstimate(flops=0, bytes_accessed=8 * rows * HD, transcendentals=0),
        name="pack",
    )(ck, cv, *slab)


def attend_kernel(
    shards, chained,
    at_ref, q_ref, do_ref, bq_ref, cos_ref, sin_ref,
    ck_ref, cv_ref, kp_ref, vp_ref, bk_ref, bv_ref, *rest,
):
    far, rest = rest[: 2 * (shards - 1)], rest[2 * (shards - 1):]
    rest = rest[chained:]
    out_ref, gq_ref, sums_ref, dk_ref, dv_ref, send_ref, keys, values = rest
    tokens = q_ref.shape[0]
    slots = ck_ref.shape[0]
    prefix = shards * slots
    slab = shards * tokens
    first = at_ref[0]
    rank = at_ref[1]
    cosine = cos_ref[pl.ds(0, tokens), :]
    sine = sin_ref[pl.ds(0, tokens), :]

    keys[pl.ds(0, slots)] = ck_ref[...]
    values[pl.ds(0, slots)] = cv_ref[...]
    for s in range(1, shards):
        keys[pl.ds(s * slots, slots)] = far[s - 1][pl.ds(0, slots)]
        values[pl.ds(s * slots, slots)] = far[s - 1][pl.ds(slots, slots)]
    for s in range(shards):
        rows = pl.ds(s * tokens, tokens)
        if s == 0:
            kp, vp = kp_ref[...], vp_ref[...]
        else:
            block = far[shards - 1 + s - 1]
            kp, vp = block[0], block[1]
        k = kp.astype(F32) + bk_ref[...].astype(F32)
        k = k * cos_ref[rows, :] + turn(k) * sin_ref[rows, :]
        v = vp.astype(F32) + bv_ref[...].astype(F32)
        place = pl.ds(prefix + s * tokens, tokens)
        keys[place] = k.astype(B16)
        values[place] = v.astype(B16)

    rows = HEADS * tokens
    scale = HD ** -0.5
    col = lax.broadcasted_iota(jnp.int32, (1, slots), 1)
    seen = [col < first - lax.rem(rank - j + shards, shards) * slots for j in range(shards)]
    token = lax.broadcasted_iota(jnp.int32, (rows, tokens), 0) & (tokens - 1)
    causal = lax.broadcasted_iota(jnp.int32, (rows, tokens), 1) <= token

    def scores(c):
        queries = []
        for h in range(c * HEADS, (c + 1) * HEADS):
            cols = pl.ds(h * HD, HD)
            x = q_ref[:, cols].astype(F32) + bq_ref[:, cols].astype(F32)
            x = x * cosine + turn(x) * sine
            queries.append(x.astype(B16))
        q = jnp.concatenate(queries, axis=0)
        do = jnp.concatenate(
            [do_ref[:, pl.ds(h * HD, HD)] for h in range(c * HEADS, (c + 1) * HEADS)], axis=0
        )
        s = dot(q, keys[...], NT)
        parts = []
        for j in range(shards):
            parts.append(jnp.where(seen[j], s[:, j * slots:(j + 1) * slots], NEG))
        parts.append(jnp.where(causal, s[:, prefix:prefix + tokens], NEG))
        for j in range(1, shards):
            part = s[:, prefix + j * tokens:prefix + (j + 1) * tokens]
            parts.append(jnp.where(rank >= j, part, NEG))
        return q, do, jnp.concatenate(parts, axis=1)

    def softmax(s):
        top = jnp.max(s, axis=1, keepdims=True)
        e = jnp.exp2((s - top) * (scale * math.log2(math.e)))
        return e * (1.0 / jnp.sum(e, axis=1, keepdims=True))

    def backward(c, q, do, p, dp):
        pb = p.astype(B16)
        o = dot(pb, values[...], NN).astype(B16)
        delta = jnp.sum(do.astype(F32) * o.astype(F32), axis=1, keepdims=True)
        ds = (p * (dp - delta)).astype(B16)
        dq = (dot(ds, keys[...], NN) * scale).astype(B16).astype(F32)
        for i in range(HEADS):
            h = c * HEADS + i
            cols = pl.ds(h * HD, HD)
            part = slice(i * tokens, (i + 1) * tokens)
            out_ref[:, cols] = o[part]
            g = dq[part]
            g = g * cosine - turn(g) * sine
            gq_ref[:, cols] = g.astype(B16)
            sums_ref[0, :, cols] = jnp.sum(g, axis=0, keepdims=True)
        return dot(q, ds[:, prefix:], TN), dot(do, pb[:, prefix:], TN)

    chains = GROUP // HEADS
    dkt = jnp.zeros((HD, slab), F32)
    dvt = jnp.zeros((HD, slab), F32)
    ready = scores(0)
    for c in range(chains):
        q, do, s = ready
        if c + 1 < chains:
            ready = scores(c + 1)
        dp = dot(do, values[...], NT)
        dk_part, dv_part = backward(c, q, do, softmax(s), dp)
        dkt += dk_part
        dvt += dv_part

    dk = dkt.T * scale
    dv = dvt.T
    gk = dk * cos_ref[...] - turn(dk) * sin_ref[...]
    dk_ref[...] = dk[:tokens]
    dv_ref[...] = dv[:tokens]
    for j in range(1, shards):
        block = slice(j * tokens, (j + 1) * tokens)
        send_ref[2 * (j - 1)] = dk[block].astype(B16)
        send_ref[2 * (j - 1) + 1] = dv[block].astype(B16)
    sums_ref[0, :, pl.ds(GROUP * HD, HD)] = jnp.sum(gk, axis=0, keepdims=True)
    sums_ref[0, :, pl.ds((GROUP + 1) * HD, HD)] = jnp.sum(dv, axis=0, keepdims=True)


def attend(g, shards, at, q, do, bq, cosine, sine, ck, cv, kp, vp, bk, bv, far, slabs, before):
    tokens, slots = q.shape[0], ck.shape[0]
    slab = shards * tokens
    total = slab + shards * slots
    width = GROUP * HD
    last = g == KV - 1
    sends = max(2 * (shards - 1), 1)

    def wide(rows):
        return pl.BlockSpec((rows, width), lambda i: (0, g))

    in_specs = [
        pl.BlockSpec(memory_space=pltpu.SMEM),
        wide(tokens), wide(tokens), wide(1),
        whole((slab, HD)), whole((slab, HD)),
        column(slots, g), column(slots, g), column(tokens, g), column(tokens, g),
        column(1, g), column(1, g),
    ]
    in_specs += [whole(a.shape) for a in far]
    in_specs += [pl.BlockSpec((2, tokens, HD), lambda i: (0, 0, g)) for _ in slabs]
    send_heads, send_place = (1, 0) if last else (KV - 1, g)
    out_shape = [
        jax.ShapeDtypeStruct((tokens, HQ * HD), B16),
        jax.ShapeDtypeStruct((tokens, HQ * HD), B16),
        jax.ShapeDtypeStruct((KV, 1, SUMS), F32),
        jax.ShapeDtypeStruct((tokens, KV * HD), F32),
        jax.ShapeDtypeStruct((tokens, KV * HD), F32),
        jax.ShapeDtypeStruct((sends, tokens, send_heads * HD), B16),
    ]
    out_specs = [
        wide(tokens), wide(tokens),
        pl.BlockSpec((1, 1, SUMS), lambda i: (g, 0, 0)),
        column(tokens, g), column(tokens, g),
        pl.BlockSpec((sends, tokens, HD), lambda i: (0, 0, send_place)),
    ]
    handed = [] if before is None else list(before[:5] if last else before)
    aliases = {len(in_specs) + i: i for i in range(len(handed))}
    in_specs += [pl.BlockSpec(memory_space=pl.ANY)] * len(handed)
    return pl.pallas_call(
        functools.partial(attend_kernel, shards, len(handed)),
        grid=(1,),
        in_specs=in_specs,
        out_shape=out_shape,
        out_specs=out_specs,
        scratch_shapes=[pltpu.VMEM((total, HD), B16), pltpu.VMEM((total, HD), B16)],
        input_output_aliases=aliases,
        compiler_params=params(),
        cost_estimate=pl.CostEstimate(
            flops=2 * GROUP * tokens * HD * (4 * total + 2 * slab),
            bytes_accessed=8 * tokens * GROUP * HD + 8 * total * HD,
            transcendentals=GROUP * tokens * total,
        ),
        name="attend",
    )(at, q, do, bq, cosine, sine, ck, cv, kp, vp, bk, bv, *far, *slabs, *handed)


def finish_kernel(shards, dk_ref, dv_ref, cos_ref, sin_ref, *rest):
    early, late = rest[: shards - 1], rest[shards - 1: 2 * (shards - 1)]
    gk_ref, gv_ref = rest[-2:]
    for g in range(KV):
        cols = pl.ds(g * HD, HD)
        dk = dk_ref[:, cols]
        dv = dv_ref[:, cols]
        for s in range(shards - 1):
            back, place = (late[s], pl.ds(0, HD)) if g == KV - 1 else (early[s], cols)
            dk = dk + back[0, :, place].astype(F32)
            dv = dv + back[1, :, place].astype(F32)
        gk_ref[:, cols] = (dk * cos_ref[...] - turn(dk) * sin_ref[...]).astype(B16)
        gv_ref[:, cols] = dv.astype(B16)


def finish(shards, dk, dv, cosine, sine, early, late):
    tokens = dk.shape[0]
    return pl.pallas_call(
        functools.partial(finish_kernel, shards),
        grid=(1,),
        in_specs=[whole(dk.shape)] * 2 + [whole((tokens, HD))] * 2
        + [whole(a.shape) for a in early + late],
        out_specs=[whole(dk.shape)] * 2,
        out_shape=[jax.ShapeDtypeStruct(dk.shape, B16)] * 2,
        compiler_params=params(),
        cost_estimate=pl.CostEstimate(flops=0, bytes_accessed=1 << 20, transcendentals=0),
        name="finish",
    )(dk, dv, cosine, sine, *early, *late)


def sum_over(x, axis):
    size = lax.axis_size(axis)
    if size & (size - 1):
        return lax.psum(x, axis)
    step = 1
    while step < size:
        x = x + lax.ppermute(x, axis, [(i, i ^ step) for i in range(size)])
        step *= 2
    return x


def body(q_proj, k_proj, v_proj, cache_k, cache_v, bias_q, bias_k, bias_v, start, dout):
    shards = lax.axis_size("seq")
    rank = lax.axis_index("seq")
    tokens = q_proj.shape[1]
    first = start[0]
    ck, cv, kp, vp = cache_k[0], cache_v[0], k_proj[0], v_proj[0]

    def ring(x, s):
        return lax.ppermute(x, "seq", [(i, (i + s) % shards) for i in range(shards)])

    def later(x, s):
        return lax.ppermute(x, "seq", [(i, i + s) for i in range(shards - s)])

    def earlier(x, s):
        return lax.ppermute(x, "seq", [(i + s, i) for i in range(shards - s)])

    chunk, own = pack(0, ck, cv, (kp, vp))
    chunks = [chunk] + [pack(g, ck, cv)[0] for g in range(1, KV)]
    slabs = [later(own, s) for s in range(1, shards)]
    far = [[ring(chunk, s) for s in range(1, shards)] for chunk in chunks]

    owners = lax.rem(rank - jnp.arange(shards, dtype=jnp.int32) + shards, shards)
    positions = first + owners[:, None] * tokens + jnp.arange(tokens, dtype=jnp.int32)[None]
    freqs = jnp.exp(
        -(2.0 * jnp.arange(HD // 2, dtype=F32) / HD) * jnp.log(jnp.float32(1000000.0))
    )
    angles = positions.reshape(-1).astype(F32)[:, None] * freqs[None, :]
    c, n = jnp.cos(angles), jnp.sin(angles)
    cosine = jnp.concatenate([c, c], axis=1)
    sine = jnp.concatenate([-n, n], axis=1)
    at = jnp.stack([first, rank.astype(jnp.int32)])

    before = None
    for g in range(KV):
        if g == KV - 1:
            early = [earlier(before[5][2 * (s - 1):2 * s], s) for s in range(1, shards)]
        before = attend(
            g, shards, at, q_proj[0], dout[0], bias_q[None], cosine, sine, ck, cv,
            kp, vp, bias_k[None], bias_v[None], far[g], slabs, before,
        )
    out, gq, sums, dk, dv, send = before
    late = [earlier(send[2 * (s - 1):2 * s], s) for s in range(1, shards)]
    sums = sum_over(sum_over(sums, "seq"), "dp")[:, 0]
    gk, gv = finish(shards, dk, dv, cosine, sine, early, late)
    wide = GROUP * HD
    return (
        out[None],
        gq[None],
        gk[None],
        gv[None],
        sums[:, :wide].reshape(-1),
        sums[:, wide:wide + HD].reshape(-1),
        sums[:, wide + HD:].reshape(-1),
    )


def solution(mesh):
    split = P("dp", "seq", None)
    return jax.shard_map(
        body,
        mesh=mesh,
        in_specs=(split,) * 5 + (P(), P(), P(), P("dp"), split),
        out_specs=(split,) * 4 + (P(), P(), P()),
        check_vma=False,
    )
```

time: 155 us -> 80.7 us (0.52)
  blocking collectives: 41.1 us -> 0 us
  Pallas kernels: 64.9 us -> 36.9 us
  local copies, waits for them, and re-layouts: 19.3 us -> 6.74 us
  waiting for transfers between devices: 8.39 us -> 13.7 us
  starting transfers between devices: 14.2 us -> 18.5 us
    psum x1 -> x0, blocking collectives: 41.1 us -> none  [body(): sums = lax.psum(jnp.concatenate(sums_q + sums_k + sums_v), ('dp', 'seq'))]
    pallas_call x6 -> x9, Pallas kernels: 64.9 us -> 36.9 us  [the longest x4 27.9 us: attend(): pl.pallas_call(functools.partial(attend_kernel, shards, len(handed)), gri...]
    unnamed x63 -> x25, local copies, waits for them, and re-layouts: 16.5 us -> 4.38 us
    ppermute x0 -> x5, waiting for transfers between devices: none -> 8.7 us  [sum_over(): x = x + lax.ppermute(x, axis, [(i, i ^ step) for i in range(size)])]
    ppermute x0 -> x5, starting transfers between devices: none -> 6.96 us  [sum_over(): x = x + lax.ppermute(x, axis, [(i, i ^ step) for i in range(size)])]
    ppermute x4, waiting for transfers between devices: 3.67 us -> 0.01 us  [ring(): lax.ppermute(x, 'seq', [(i, (i + s) % shards) for i in range(shards)])]
    ppermute x4 -> x2, starting transfers between devices: 5.15 us -> 2.57 us  [earlier(): return lax.ppermute(x, 'seq', [(i + s, i) for i in range(shards - s)])]
    another operation x1 -> x0, other arithmetic: 1.7 us -> none  [body(): own = jnp.stack([k_proj[0], v_proj[0]])]
  transfers between devices with their start and end apart: 9 -> 12, of which waited for: 2 -> 6; matrix products, arithmetic and copies ran while one was open for 3% -> 6% of each run, Pallas kernels for 37% -> 33%
where the time goes in v2:
time: 80.7 us; the launch traced here: 80.2 us
  Pallas kernels  36.9 us (46%)
  starting transfers between devices  18.5 us (23%)
  waiting for transfers between devices  13.7 us (17%)
  local copies, waits for them, and re-layouts  6.74 us (8%)
  other arithmetic  2.93 us (4%)
  between operations  1.46 us (2%)
    pallas_call x4, Pallas kernels, attend(): pl.pallas_call(functools.partial(attend_kernel, shards, len(handed)), gri...  27.9 us
    ppermute x5, waiting for transfers between devices, sum_over(): x = x + lax.ppermute(x, axis, [(i, i ^ step) for i in range(size)])  8.7 us
    pallas_call x4, Pallas kernels, pack(): pl.pallas_call(pack_kernel, grid=(1,), in_specs=[column(rows, g)] * 2 + [...  7.03 us
    ppermute x5, starting transfers between devices, sum_over(): x = x + lax.ppermute(x, axis, [(i, i ^ step) for i in range(size)])  6.96 us
    ppermute x2, waiting for transfers between devices, earlier(): return lax.ppermute(x, 'seq', [(i + s, i) for i in range(shards - s)])  5 us
    ppermute x1, starting transfers between devices, later(): return lax.ppermute(x, 'seq', [(i, i + s) for i in range(shards - s)])  4.87 us
    unnamed x25, local copies, waits for them, and re-layouts  4.38 us
    ppermute x4, starting transfers between devices, ring(): lax.ppermute(x, 'seq', [(i, (i + s) % shards) for i in range(shards)])  4.11 us
  transfers between devices with their start and end apart: 12, of which 6 were waited for; matrix products, arithmetic and copies ran while one was open for 6% of the time, Pallas kernels for 33%

profile of v2, /device:TPU:0, one launch (start us, length us, event | category | flops | bytes accessed | tf_op | source)
XLA Modules:
  0.0 80.2 jit_solution(12179098425389122300)
XLA Ops:
  0.6 1.9 %pack.5 = (bf16[1024,128]{1,0:T(8,128)(2,1)}, bf16[2,128,512]{2,1,0:T(8,128)(2,1)}) custom-call(bf16[512,512]{1,0:T(8,128)(2,1)} %bitcast.27, bf16[512,512]{1,0:T(8,128)(2,1)} %bitcast.35, bf16[128,512]{1,0:T(8,128)(2,1)} %bitcast.53, bf16[128,512]{1,0:T(8,128)(2,1)} %bitcast.58), custom_call_target="tpu_custom_call" | custom-call | bytes 524288 | tf_op jit(solution)/shard_map/pack/pallas_call | solution.py:63
  2.5 4.9 %collective-permute-start.1 = (bf16[2,128,512]{2,1,0:T(8,128)(2,1)}, bf16[2,128,512]{2,1,0:T(8,128)(2,1)S(1)}, u32[]{:S(2)}, u32[]{:S(2)}) collective-permute-start(bf16[2,128,512]{2,1,0:T(8,128)(2,1)} %get-tuple-element.35), channel_id=1, source_target_pairs={{0,1},{2,3},{4,5},{6,7},{8,9},{10,11},{12,13},{14,15},{16,17},{18,... | collective-permute-start | bytes 786440 | tf_op jit(solution)/shard_map/ppermute | solution.py:295
  7.4 0.1 collective-permute-start.4
  7.5 1.7 %pack.7 = bf16[1024,128]{1,0:T(8,128)(2,1)} custom-call(bf16[512,512]{1,0:T(8,128)(2,1)} %bitcast.28, bf16[512,512]{1,0:T(8,128)(2,1)} %bitcast.36), custom_call_target="tpu_custom_call" | custom-call | bytes 524288 | tf_op jit(solution)/shard_map/pack/pallas_call | solution.py:63
  9.2 2.0 %collective-permute-start.3 = (bf16[1024,128]{1,0:T(8,128)(2,1)}, bf16[1024,128]{1,0:T(8,128)(2,1)S(1)}, u32[]{:S(2)}, u32[]{:S(2)}) collective-permute-start(bf16[1024,128]{1,0:T(8,128)(2,1)} %pack.7), channel_id=1, source_target_pairs={{0,1},{1,0},{2,3},{3,2},{4,5},{5,4},{6,7},{7,6},{8,9},{9,8},{10,11... | collective-permute-start | bytes 786440 | tf_op jit(solution)/shard_map/ppermute | solution.py:292
  11.2 1.7 %pack.6 = bf16[1024,128]{1,0:T(8,128)(2,1)} custom-call(bf16[512,512]{1,0:T(8,128)(2,1)} %bitcast.29, bf16[512,512]{1,0:T(8,128)(2,1)} %bitcast.37), custom_call_target="tpu_custom_call" | custom-call | bytes 524288 | tf_op jit(solution)/shard_map/pack/pallas_call | solution.py:63
  12.9 0.0 collective-permute-start.2
  12.9 1.7 %pack.4 = bf16[1024,128]{1,0:T(8,128)(2,1)} custom-call(bf16[512,512]{1,0:T(8,128)(2,1)} %bitcast.30, bf16[512,512]{1,0:T(8,128)(2,1)} %bitcast.38), custom_call_target="tpu_custom_call" | custom-call | bytes 524288 | tf_op jit(solution)/shard_map/pack/pallas_call | solution.py:63
  14.6 2.0 %collective-permute-start = (bf16[1024,128]{1,0:T(8,128)(2,1)}, bf16[1024,128]{1,0:T(8,128)(2,1)S(1)}, u32[]{:S(2)}, u32[]{:S(2)}) collective-permute-start(bf16[1024,128]{1,0:T(8,128)(2,1)} %pack.4), channel_id=1, source_target_pairs={{0,1},{1,0},{2,3},{3,2},{4,5},{5,4},{6,7},{7,6},{8,9},{9,8},{10,11... | collective-permute-start | bytes 786440 | tf_op jit(solution)/shard_map/ppermute | solution.py:292
  17.3 0.1 convert_bitcast_fusion
  17.4 0.0 copy-start.7
  17.4 0.5 fusion
  18.0 0.6 pad_add_fusion.at_ref
  18.6 0.0 copy-done.7
  18.6 0.0 copy-start.8
  18.6 0.6 broadcast_in_dim.14.bq_ref
  19.2 0.1 copy-done.8
  19.3 0.0 copy-start.9
  19.3 0.6 broadcast_in_dim.15.bk_ref
  19.8 0.1 copy-done.9
  19.9 0.6 broadcast_in_dim.16.bv_ref
  20.5 0.8 %pad_maximum_fusion = (f32[256,128]{1,0:T(8,128)}, f32[256,128]{1,0:T(8,128)}) fusion(f32[256,64]{1,0:T(8,128)S(1)} %get-tuple-element.67, f32[256,64]{1,0:T(8,128)S(1)} %get-tuple-element.66, f32[256,64]{1,0:T(8,128)S(1)} %get-tuple-element.65), kind=kLoop, calls=%fused_computation.2 | loop fusion | flops 65536 | bytes 458752 | tf_op jit(solution)/shard_map/concatenate | solution.py:312
  21.4 0.0 collective-permute-done.1.rest_1_
  21.4 0.0 copy-start
  21.4 0.0 collective-permute-done.4.rest_0_
  21.4 0.0 copy-start.10
  21.4 0.7 copy-done
  22.1 0.1 copy-done.10
  22.2 6.9 %attend.4 = (bf16[128,4096]{1,0:T(8,128)(2,1)}, bf16[128,4096]{1,0:T(8,128)(2,1)}, f32[4,1,1280]{2,1,0:T(1,128)}, f32[128,512]{1,0:T(8,128)}, f32[128,512]{1,0:T(8,128)}, /*index=5*/bf16[2,128,384]{2,1,0:T(8,128)(2,1)}) custom-call(s32[2]{0:T(128)} %pad_add_fusion.at_ref, bf16[128,4096]{1,0:T(8,128)(2,1)} %bitcast.43, bf16[128,4096]{1,0:T(8,128)(2,1)} %bitcast.47, ...), custom_call_target="tpu_custom_call" | custom-call | flops 1476395008 | bytes 2359296 | tf_op jit(solution)/shard_map/attend/pallas_call | solution.py:225
  29.1 0.0 collective-permute-done.3.rest_0_
  29.1 0.0 copy-start.4
  29.1 0.7 copy-done.4
  29.8 6.9 %attend.5 = (bf16[128,4096]{1,0:T(8,128)(2,1)}, bf16[128,4096]{1,0:T(8,128)(2,1)}, f32[4,1,1280]{2,1,0:T(1,128)}, f32[128,512]{1,0:T(8,128)}, f32[128,512]{1,0:T(8,128)}, /*index=5*/bf16[2,128,384]{2,1,0:T(8,128)(2,1)}) custom-call(s32[2]{0:T(128)} %pad_add_fusion.at_ref, ...), custom_call_target="tpu_custom_call", output_to_operand_aliasing={{0}: (14, {}), {1}: (15, {}), {2}: (16, {}), {3}: (17, {}),... | custom-call | flops 1476395008 | bytes 2359296 | tf_op jit(solution)/shard_map/attend/pallas_call | solution.py:225
  36.8 0.0 collective-permute-done.2.rest_0_
  36.8 0.0 copy-start.3
  36.8 0.7 copy-done.3
  37.5 7.1 %attend.6 = (bf16[128,4096]{1,0:T(8,128)(2,1)}, bf16[128,4096]{1,0:T(8,128)(2,1)}, f32[4,1,1280]{2,1,0:T(1,128)}, f32[128,512]{1,0:T(8,128)}, f32[128,512]{1,0:T(8,128)}, /*index=5*/bf16[2,128,384]{2,1,0:T(8,128)(2,1)}) custom-call(s32[2]{0:T(128)} %pad_add_fusion.at_ref, ...), custom_call_target="tpu_custom_call", output_to_operand_aliasing={{0}: (14, {}), {1}: (15, {}), {2}: (16, {}), {3}: (17, {}),... | custom-call | flops 1476395008 | bytes 2359296 | tf_op jit(solution)/shard_map/attend/pallas_call | solution.py:225
  44.6 0.0 collective-permute-done.rest_0_
  44.6 0.0 copy-start.2
  44.6 0.7 copy-done.2
  45.3 6.9 %attend.7 = (bf16[128,4096]{1,0:T(8,128)(2,1)}, bf16[128,4096]{1,0:T(8,128)(2,1)}, f32[4,1,1280]{2,1,0:T(1,128)}, f32[128,512]{1,0:T(8,128)}, f32[128,512]{1,0:T(8,128)}, /*index=5*/bf16[2,128,128]{2,1,0:T(8,128)(2,1)}) custom-call(s32[2]{0:T(128)} %pad_add_fusion.at_ref, ...), custom_call_target="tpu_custom_call", output_to_operand_aliasing={{0}: (14, {}), {1}: (15, {}), {2}: (16, {}), {3}: (17, {}),... | custom-call | flops 1476395008 | bytes 2359296 | tf_op jit(solution)/shard_map/attend/pallas_call | solution.py:225
  52.2 0.0 copy-start.1
  52.2 1.0 %collective-permute-start.7 = (f32[4,1,1280]{2,1,0:T(1,128)}, f32[4,1,1280]{2,1,0:T(1,128)S(1)}, u32[]{:S(2)}, u32[]{:S(2)}) collective-permute-start(f32[4,1,1280]{2,1,0:T(1,128)} %get-tuple-element.62), channel_id=1, source_target_pairs={{0,1},{1,0},{2,3},{3,2},{4,5},{5,4},{6,7},{7,6},{8,9},{9,8},{10,11... | collective-permute-start | bytes 61448 | tf_op jit(solution)/shard_map/ppermute | solution.py:279
  53.3 3.0 %collective-permute-done.7 = f32[4,1,1280]{2,1,0:T(1,128)S(1)} collective-permute-done((f32[4,1,1280]{2,1,0:T(1,128)}, f32[4,1,1280]{2,1,0:T(1,128)S(1)}, u32[]{:S(2)}, u32[]{:S(2)}) %collective-permute-start.7) | collective-permute-done | bytes 20512 | tf_op jit(solution)/shard_map/ppermute | solution.py:279
  56.3 0.7 add.58
  57.0 0.1 collective-permute-start.8
  57.1 1.2 %collective-permute-done.8 = f32[4,1,1280]{2,1,0:T(1,128)S(1)} collective-permute-done((f32[4,1,1280]{2,1,0:T(1,128)S(1)}, f32[4,1,1280]{2,1,0:T(1,128)S(1)}, u32[]{:S(2)}, u32[]{:S(2)}) %collective-permute-start.8) | collective-permute-done | bytes 20512 | tf_op jit(solution)/shard_map/ppermute | solution.py:279
  58.3 1.6 %collective-permute-start.9 = (f32[4,1,1280]{2,1,0:T(1,128)S(1)}, f32[4,1,1280]{2,1,0:T(1,128)S(1)}, u32[]{:S(2)}, u32[]{:S(2)}) collective-permute-start(f32[4,1,1280]{2,1,0:T(1,128)S(1)} %add.59), channel_id=1, source_target_pairs={{0,4},{2,6},{4,0},{6,2},{8,12},{10,14},{12,8},{14,10},{16,20},{18,... | collective-permute-start | bytes 61448 | tf_op jit(solution)/shard_map/ppermute | solution.py:279
  59.9 2.3 %collective-permute-done.9 = f32[4,1,1280]{2,1,0:T(1,128)S(1)} collective-permute-done((f32[4,1,1280]{2,1,0:T(1,128)S(1)}, f32[4,1,1280]{2,1,0:T(1,128)S(1)}, u32[]{:S(2)}, u32[]{:S(2)}) %collective-permute-start.9) | collective-permute-done | bytes 20512 | tf_op jit(solution)/shard_map/ppermute | solution.py:279
  62.2 1.6 %collective-permute-start.10 = (f32[4,1,1280]{2,1,0:T(1,128)S(1)}, f32[4,1,1280]{2,1,0:T(1,128)S(1)}, u32[]{:S(2)}, u32[]{:S(2)}) collective-permute-start(f32[4,1,1280]{2,1,0:T(1,128)S(1)} %add.60), channel_id=1, source_target_pairs={{0,8},{2,10},{4,12},{6,14},{8,0},{10,2},{12,4},{14,6},{16,24},{18,... | collective-permute-start | bytes 61448 | tf_op jit(solution)/shard_map/ppermute | solution.py:279
  63.8 2.2 %collective-permute-done.10 = f32[4,1,1280]{2,1,0:T(1,128)S(1)} collective-permute-done((f32[4,1,1280]{2,1,0:T(1,128)S(1)}, f32[4,1,1280]{2,1,0:T(1,128)S(1)}, u32[]{:S(2)}, u32[]{:S(2)}) %collective-permute-start.10) | collective-permute-done | bytes 20512 | tf_op jit(solution)/shard_map/ppermute | solution.py:279
  66.1 2.7 %collective-permute-start.11 = (f32[4,1,1280]{2,1,0:T(1,128)S(1)}, f32[4,1,1280]{2,1,0:T(1,128)S(1)}, u32[]{:S(2)}, u32[]{:S(2)}) collective-permute-start(f32[4,1,1280]{2,1,0:T(1,128)S(1)} %add.61), channel_id=1, source_target_pairs={{0,16},{2,18},{4,20},{6,22},{8,24},{10,26},{12,28},{14,30},{16,0},... | collective-permute-start | bytes 61448 | tf_op jit(solution)/shard_map/ppermute | solution.py:279
  68.7 1.3 %collective-permute-start.6 = (bf16[2,128,128]{2,1,0:T(8,128)(2,1)}, bf16[2,128,128]{2,1,0:T(8,128)(2,1)S(1)}, u32[]{:S(2)}, u32[]{:S(2)}) collective-permute-start(bf16[2,128,128]{2,1,0:T(8,128)(2,1)} %get-tuple-element.59), channel_id=1, source_target_pairs={{1,0},{3,2},{5,4},{7,6},{9,8},{11,10},{13,12},{15,14},{17,16},{19,... | collective-permute-start | bytes 196616 | tf_op jit(solution)/shard_map/ppermute | solution.py:298
  70.0 0.0 copy-done.1
  70.0 1.3 %collective-permute-start.5 = (bf16[2,128,384]{2,1,0:T(8,128)(2,1)S(1)}, bf16[2,128,384]{2,1,0:T(8,128)(2,1)S(1)}, u32[]{:S(2)}, u32[]{:S(2)}) collective-permute-start(bf16[2,128,384]{2,1,0:T(8,128)(2,1)S(1)} %copy-done.1), channel_id=1, source_target_pairs={{1,0},{3,2},{5,4},{7,6},{9,8},{11,10},{13,12},{15,14},{17,16},{19,... | collective-permute-start | bytes 589832 | tf_op jit(solution)/shard_map/ppermute | solution.py:298
  71.3 0.0 collective-permute-done.11
  71.4 0.6 slice_bitcast_fusion.1
  72.0 0.6 copy.39
  72.6 2.5 %collective-permute-done.6.rest_1_ = bf16[2,128,128]{2,1,0:T(8,128)(2,1)S(1)} collective-permute-done((bf16[2,128,128]{2,1,0:T(8,128)(2,1)}, bf16[2,128,128]{2,1,0:T(8,128)(2,1)S(1)}, u32[]{:S(2)}, u32[]{:S(2)}) %collective-permute-start.6) | collective-permute-done | bytes 65568 | tf_op jit(solution)/shard_map/ppermute | solution.py:298
  75.1 0.0 copy-start.6
  75.1 2.5 %collective-permute-done.5.rest_0_ = bf16[2,128,384]{2,1,0:T(8,128)(2,1)S(1)} collective-permute-done((bf16[2,128,384]{2,1,0:T(8,128)(2,1)S(1)}, bf16[2,128,384]{2,1,0:T(8,128)(2,1)S(1)}, u32[]{:S(2)}, u32[]{:S(2)}) %collective-permute-start.5) | collective-permute-done | bytes 196640 | tf_op jit(solution)/shard_map/ppermute | solution.py:298
  77.6 0.0 copy-done.6
  77.6 0.7 copy-done.5
  78.3 1.9 %finish.1 = (bf16[128,512]{1,0:T(8,128)(2,1)}, bf16[128,512]{1,0:T(8,128)(2,1)}) custom-call(f32[128,512]{1,0:T(8,128)} %get-tuple-element.56.dk_ref, f32[128,512]{1,0:T(8,128)} %get-tuple-element.57.dv_ref, f32[256,128]{1,0:T(8,128)} %get-tuple-element.68.cos_ref, f32[256,128]{1,0:T(8,128)} %get-tuple-element.69.sin_ref, bf16[2,128,384]{2,1,0:T(8,128)(2,1)} %copy-done.5, ...), custom_call_target="tpu_custom_call" | custom-call | bytes 1048576 | tf_op jit(solution)/shard_map/finish/pallas_call | solution.py:260
  (9 shorter events, 0.1 us)
Async XLA Ops:
  2.5 18.8 %collective-permute-start.1 = (bf16[2,128,512]{2,1,0:T(8,128)(2,1)}, bf16[2,128,512]{2,1,0:T(8,128)(2,1)S(1)}, u32[]{:S(2)}, u32[]{:S(2)}) collective-permute-start(bf16[2,128,512]{2,1,0:T(8,128)(2,1)} %get-tuple-element.35), channel_id=1, source_target_pairs={{0,1},{2,3},{4,5},{6,7},{8,9},{10,11},{12,13},{14,15},{16,17},{18,... | collective-permute-start | bytes 786440 | tf_op jit(solution)/shard_map/ppermute | solution.py:295
  7.4 13.9 %collective-permute-start.4 = (bf16[1024,128]{1,0:T(8,128)(2,1)}, bf16[1024,128]{1,0:T(8,128)(2,1)S(1)}, u32[]{:S(2)}, u32[]{:S(2)}) collective-permute-start(bf16[1024,128]{1,0:T(8,128)(2,1)} %get-tuple-element.36), channel_id=1, source_target_pairs={{0,1},{1,0},{2,3},{3,2},{4,5},{5,4},{6,7},{7,6},{8,9},{9,8},{10,11... | collective-permute-start | bytes 786440 | tf_op jit(solution)/shard_map/ppermute | solution.py:292
  9.2 19.9 %collective-permute-start.3 = (bf16[1024,128]{1,0:T(8,128)(2,1)}, bf16[1024,128]{1,0:T(8,128)(2,1)S(1)}, u32[]{:S(2)}, u32[]{:S(2)}) collective-permute-start(bf16[1024,128]{1,0:T(8,128)(2,1)} %pack.7), channel_id=1, source_target_pairs={{0,1},{1,0},{2,3},{3,2},{4,5},{5,4},{6,7},{7,6},{8,9},{9,8},{10,11... | collective-permute-start | bytes 786440 | tf_op jit(solution)/shard_map/ppermute | solution.py:292
  12.9 23.8 %collective-permute-start.2 = (bf16[1024,128]{1,0:T(8,128)(2,1)}, bf16[1024,128]{1,0:T(8,128)(2,1)S(1)}, u32[]{:S(2)}, u32[]{:S(2)}) collective-permute-start(bf16[1024,128]{1,0:T(8,128)(2,1)} %pack.6), channel_id=1, source_target_pairs={{0,1},{1,0},{2,3},{3,2},{4,5},{5,4},{6,7},{7,6},{8,9},{9,8},{10,11... | collective-permute-start | bytes 786440 | tf_op jit(solution)/shard_map/ppermute | solution.py:292
  14.6 29.9 %collective-permute-start = (bf16[1024,128]{1,0:T(8,128)(2,1)}, bf16[1024,128]{1,0:T(8,128)(2,1)S(1)}, u32[]{:S(2)}, u32[]{:S(2)}) collective-permute-start(bf16[1024,128]{1,0:T(8,128)(2,1)} %pack.4), channel_id=1, source_target_pairs={{0,1},{1,0},{2,3},{3,2},{4,5},{5,4},{6,7},{7,6},{8,9},{9,8},{10,11... | collective-permute-start | bytes 786440 | tf_op jit(solution)/shard_map/ppermute | solution.py:292
  17.4 1.2 %copy-start.7 = (bf16[4096]{0:T(1024)(128)(2,1)S(1)}, bf16[4096]{0:T(1024)(128)(2,1)}, u32[]{:S(2)}) copy-start(bf16[4096]{0:T(1024)(128)(2,1)} %param.15) | copy-start | bytes 24580
  18.6 0.7 copy-start.8
  19.3 0.7 copy-start.9
  21.4 0.7 copy-start
  21.4 0.8 copy-start.10
  29.1 0.7 copy-start.4
  36.8 0.7 copy-start.3
  44.6 0.7 copy-start.2
  52.2 17.8 %copy-start.1 = (bf16[2,128,384]{2,1,0:T(8,128)(2,1)S(1)}, bf16[2,128,384]{2,1,0:T(8,128)(2,1)}, u32[]{:S(2)}) copy-start(bf16[2,128,384]{2,1,0:T(8,128)(2,1)} %get-tuple-element.58) | copy-start | bytes 589828
  52.2 4.1 %collective-permute-start.7 = (f32[4,1,1280]{2,1,0:T(1,128)}, f32[4,1,1280]{2,1,0:T(1,128)S(1)}, u32[]{:S(2)}, u32[]{:S(2)}) collective-permute-start(f32[4,1,1280]{2,1,0:T(1,128)} %get-tuple-element.62), channel_id=1, source_target_pairs={{0,1},{1,0},{2,3},{3,2},{4,5},{5,4},{6,7},{7,6},{8,9},{9,8},{10,11... | collective-permute-start | bytes 61448 | tf_op jit(solution)/shard_map/ppermute | solution.py:279
  57.0 1.3 %collective-permute-start.8 = (f32[4,1,1280]{2,1,0:T(1,128)S(1)}, f32[4,1,1280]{2,1,0:T(1,128)S(1)}, u32[]{:S(2)}, u32[]{:S(2)}) collective-permute-start(f32[4,1,1280]{2,1,0:T(1,128)S(1)} %add.58), channel_id=1, source_target_pairs={{0,2},{2,0},{4,6},{6,4},{8,10},{10,8},{12,14},{14,12},{16,18},{18,... | collective-permute-start | bytes 61448 | tf_op jit(solution)/shard_map/ppermute | solution.py:279
  58.3 3.8 %collective-permute-start.9 = (f32[4,1,1280]{2,1,0:T(1,128)S(1)}, f32[4,1,1280]{2,1,0:T(1,128)S(1)}, u32[]{:S(2)}, u32[]{:S(2)}) collective-permute-start(f32[4,1,1280]{2,1,0:T(1,128)S(1)} %add.59), channel_id=1, source_target_pairs={{0,4},{2,6},{4,0},{6,2},{8,12},{10,14},{12,8},{14,10},{16,20},{18,... | collective-permute-start | bytes 61448 | tf_op jit(solution)/shard_map/ppermute | solution.py:279
  62.2 3.8 %collective-permute-start.10 = (f32[4,1,1280]{2,1,0:T(1,128)S(1)}, f32[4,1,1280]{2,1,0:T(1,128)S(1)}, u32[]{:S(2)}, u32[]{:S(2)}) collective-permute-start(f32[4,1,1280]{2,1,0:T(1,128)S(1)} %add.60), channel_id=1, source_target_pairs={{0,8},{2,10},{4,12},{6,14},{8,0},{10,2},{12,4},{14,6},{16,24},{18,... | collective-permute-start | bytes 61448 | tf_op jit(solution)/shard_map/ppermute | solution.py:279
  66.1 5.3 %collective-permute-start.11 = (f32[4,1,1280]{2,1,0:T(1,128)S(1)}, f32[4,1,1280]{2,1,0:T(1,128)S(1)}, u32[]{:S(2)}, u32[]{:S(2)}) collective-permute-start(f32[4,1,1280]{2,1,0:T(1,128)S(1)} %add.61), channel_id=1, source_target_pairs={{0,16},{2,18},{4,20},{6,22},{8,24},{10,26},{12,28},{14,30},{16,0},... | collective-permute-start | bytes 61448 | tf_op jit(solution)/shard_map/ppermute | solution.py:279
  68.7 6.4 %collective-permute-start.6 = (bf16[2,128,128]{2,1,0:T(8,128)(2,1)}, bf16[2,128,128]{2,1,0:T(8,128)(2,1)S(1)}, u32[]{:S(2)}, u32[]{:S(2)}) collective-permute-start(bf16[2,128,128]{2,1,0:T(8,128)(2,1)} %get-tuple-element.59), channel_id=1, source_target_pairs={{1,0},{3,2},{5,4},{7,6},{9,8},{11,10},{13,12},{15,14},{17,16},{19,... | collective-permute-start | bytes 196616 | tf_op jit(solution)/shard_map/ppermute | solution.py:298
  70.0 7.6 %collective-permute-start.5 = (bf16[2,128,384]{2,1,0:T(8,128)(2,1)S(1)}, bf16[2,128,384]{2,1,0:T(8,128)(2,1)S(1)}, u32[]{:S(2)}, u32[]{:S(2)}) collective-permute-start(bf16[2,128,384]{2,1,0:T(8,128)(2,1)S(1)} %copy-done.1), channel_id=1, source_target_pairs={{1,0},{3,2},{5,4},{7,6},{9,8},{11,10},{13,12},{15,14},{17,16},{19,... | collective-permute-start | bytes 589832 | tf_op jit(solution)/shard_map/ppermute | solution.py:298
  75.1 2.5 %copy-start.6 = (bf16[2,128,128]{2,1,0:T(8,128)(2,1)}, bf16[2,128,128]{2,1,0:T(8,128)(2,1)S(1)}, u32[]{:S(2)}) copy-start(bf16[2,128,128]{2,1,0:T(8,128)(2,1)S(1)} %collective-permute-done.6.rest_1_) | copy-start | bytes 196612
  77.6 0.7 copy-start.5

commit v3 on v2

v3 whole, which is shorter than its diff:
```python
import functools
import math

import jax
import jax.numpy as jnp
from jax import lax
from jax.experimental import pallas as pl
from jax.experimental.pallas import tpu as pltpu
from jax.sharding import PartitionSpec as P

HQ = 32
KV = 4
HD = 128
GROUP = 8
HEADS = 2
NEG = -1e30
SUMS = HQ + 2 * KV
VMEM = 28 * 1024 * 1024
F32, B16 = jnp.float32, jnp.bfloat16


def turn(x):
    return pltpu.roll(x, HD // 2, 1)


def dot(a, b, dims):
    return lax.dot_general(a, b, (dims, ((), ())), preferred_element_type=F32)


NT = ((1,), (1,))
NN = ((1,), (0,))
TN = ((0,), (0,))


def whole(shape):
    return pl.BlockSpec(shape, lambda i: (0,) * len(shape))


def column(rows, g):
    return pl.BlockSpec((rows, HD), lambda i: (0, g))


def params():
    return pltpu.CompilerParams(dimension_semantics=("arbitrary",), vmem_limit_bytes=VMEM)


def pack_kernel(groups, ck_ref, cv_ref, *rest):
    outs = rest[len(rest) - len(groups) - (len(rest) > len(groups)):]
    rows = ck_ref.shape[0]
    width = ck_ref.shape[1] // len(groups)
    for i in range(len(groups)):
        cols = pl.ds(i * width, width)
        outs[i][pl.ds(0, rows)] = ck_ref[:, cols]
        outs[i][pl.ds(rows, rows)] = cv_ref[:, cols]
    if len(rest) > len(groups):
        kp_ref, vp_ref = rest[:2]
        outs[-1][0] = kp_ref[...]
        outs[-1][1] = vp_ref[...]


def pack(first, count, ck, cv, slab=()):
    rows = ck.shape[0]
    shapes = [(2 * rows, HD)] * count
    if slab:
        shapes.append((2,) + slab[0].shape)
    chunk = pl.BlockSpec((pl.Element(rows), pl.Element(count * HD)), lambda i: (0, first * HD))
    return pl.pallas_call(
        functools.partial(pack_kernel, range(count)),
        grid=(1,),
        in_specs=[chunk] * 2 + [whole(a.shape) for a in slab],
        out_specs=[pl.BlockSpec(memory_space=pltpu.VMEM)] * len(shapes),
        out_shape=[pltpu.VMEM(shape, B16) for shape in shapes],
        compiler_params=params(),
        cost_estimate=pl.CostEstimate(
            flops=0, bytes_accessed=8 * rows * HD * count, transcendentals=0
        ),
        name="pack",
    )(ck, cv, *slab)


def attend_kernel(
    g, shards, chained,
    first_ref, rank_ref, q_ref, do_ref, bq_ref, cos_ref, sin_ref,
    ck_ref, cv_ref, kp_ref, vp_ref, bk_ref, bv_ref, *rest,
):
    far, rest = rest[: 2 * (shards - 1)], rest[2 * (shards - 1):]
    old_sums_ref = rest[0] if g else None
    rest = rest[chained:]
    (out_ref, gq_ref, sums_ref, dk_ref, dv_ref, send_ref,
     keys, values, bias, dkt, dvt) = rest
    tokens = q_ref.shape[0]
    slots = ck_ref.shape[0]
    prefix = shards * slots
    slab = shards * tokens
    first = first_ref[0]
    rank = rank_ref[0]

    keys[pl.ds(0, slots)] = ck_ref[...]
    values[pl.ds(0, slots)] = cv_ref[...]
    for s in range(1, shards):
        keys[pl.ds(s * slots, slots)] = far[s - 1][pl.ds(0, slots)]
        values[pl.ds(s * slots, slots)] = far[s - 1][pl.ds(slots, slots)]
    bias_k = bk_ref[...].astype(F32)[g:g + 1]
    bias_v = bv_ref[...].astype(F32)[g:g + 1]
    for s in range(shards):
        rows = pl.ds(s * tokens, tokens)
        if s == 0:
            kp, vp = kp_ref[...], vp_ref[...]
        else:
            block = far[shards - 1 + s - 1]
            kp, vp = block[0], block[1]
        k = kp.astype(F32) + bias_k
        k = k * cos_ref[rows, :] + turn(k) * sin_ref[rows, :]
        v = vp.astype(F32) + bias_v
        place = pl.ds(prefix + s * tokens, tokens)
        keys[place] = k.astype(B16)
        values[place] = v.astype(B16)
    bias[...] = bq_ref[...].astype(F32)
    sums_ref[...] = jnp.zeros_like(sums_ref) if old_sums_ref is None else old_sums_ref[...]
    dkt[...] = jnp.zeros_like(dkt)
    dvt[...] = jnp.zeros_like(dvt)

    rows = HEADS * tokens
    scale = HD ** -0.5

    def scores(head):
        cosine = cos_ref[pl.ds(0, tokens), :]
        sine = sin_ref[pl.ds(0, tokens), :]
        queries, cots = [], []
        for h in range(HEADS):
            cols = pl.ds(pl.multiple_of((head + h) * HD, HD), HD)
            x = q_ref[:, cols].astype(F32) + bias[pl.ds(head + h, 1), :]
            x = x * cosine + turn(x) * sine
            queries.append(x.astype(B16))
            cots.append(do_ref[:, cols])
        q = jnp.concatenate(queries, axis=0)
        do = jnp.concatenate(cots, axis=0)
        s = dot(q, keys[...], NT)
        col = lax.broadcasted_iota(jnp.int32, (1, slots), 1)
        parts = []
        for j in range(shards):
            seen = col < first - lax.rem(rank - j + shards, shards) * slots
            parts.append(jnp.where(seen, s[:, j * slots:(j + 1) * slots], NEG))
        token = lax.broadcasted_iota(jnp.int32, (rows, tokens), 0) & (tokens - 1)
        causal = lax.broadcasted_iota(jnp.int32, (rows, tokens), 1) <= token
        parts.append(jnp.where(causal, s[:, prefix:prefix + tokens], NEG))
        for j in range(1, shards):
            part = s[:, prefix + j * tokens:prefix + (j + 1) * tokens]
            parts.append(jnp.where(rank >= j, part, NEG))
        return q, do, jnp.concatenate(parts, axis=1)

    def softmax(s):
        top = jnp.max(s, axis=1, keepdims=True)
        e = jnp.exp2((s - top) * (scale * math.log2(math.e)))
        return e * (1.0 / jnp.sum(e, axis=1, keepdims=True))

    def weigh(pb, do):
        o = dot(pb, values[...], NN).astype(B16)
        return o, jnp.sum(do.astype(F32) * o.astype(F32), axis=1, keepdims=True)

    def store(head, o, dq):
        cosine = cos_ref[pl.ds(0, tokens), :]
        sine = sin_ref[pl.ds(0, tokens), :]
        for h in range(HEADS):
            cols = pl.ds(pl.multiple_of((head + h) * HD, HD), HD)
            part = slice(h * tokens, (h + 1) * tokens)
            out_ref[:, cols] = o[part]
            x = dq[part]
            x = x * cosine - turn(x) * sine
            gq_ref[:, cols] = x.astype(B16)
            sums_ref[pl.ds(g * GROUP + head + h, 1), :] = jnp.sum(x, axis=0, keepdims=True)

    def query_grad(ds):
        return (dot(ds, keys[...], NN) * scale).astype(B16).astype(F32)

    def pair(i, carry):
        head_a = i * 2 * HEADS
        head_b = head_a + HEADS
        q_a, do_a, s_a = scores(head_a)
        q_b, do_b, s_b = scores(head_b)
        dp_a = dot(do_a, values[...], NT)
        p_a = softmax(s_a)
        pb_a = p_a.astype(B16)
        dp_b = dot(do_b, values[...], NT)
        o_a, delta_a = weigh(pb_a, do_a)
        p_b = softmax(s_b)
        pb_b = p_b.astype(B16)
        ds_a = (p_a * (dp_a - delta_a)).astype(B16)
        o_b, delta_b = weigh(pb_b, do_b)
        dq_a = query_grad(ds_a)
        dkt[...] += dot(q_a, ds_a[:, prefix:], TN)
        dvt[...] += dot(do_a, pb_a[:, prefix:], TN)
        ds_b = (p_b * (dp_b - delta_b)).astype(B16)
        store(head_a, o_a, dq_a)
        dq_b = query_grad(ds_b)
        dkt[...] += dot(q_b, ds_b[:, prefix:], TN)
        dvt[...] += dot(do_b, pb_b[:, prefix:], TN)
        store(head_b, o_b, dq_b)
        return carry

    lax.fori_loop(0, GROUP // (2 * HEADS), pair, 0)

    dk = dkt[...].T * scale
    dv = dvt[...].T
    gk = dk * cos_ref[...] - turn(dk) * sin_ref[...]
    dk_ref[...] = dk[:tokens]
    dv_ref[...] = dv[:tokens]
    for j in range(1, shards):
        block = slice(j * tokens, (j + 1) * tokens)
        send_ref[2 * (j - 1)] = dk[block].astype(B16)
        send_ref[2 * (j - 1) + 1] = dv[block].astype(B16)
    sums_ref[pl.ds(HQ + g, 1), :] = jnp.sum(gk, axis=0, keepdims=True)
    sums_ref[pl.ds(HQ + KV + g, 1), :] = jnp.sum(dv, axis=0, keepdims=True)


def attend(
    g, shards, first, rank, q, do, bq, cosine, sine, ck, cv, kp, vp, bk, bv, far, slabs, before
):
    tokens, slots = q.shape[0], ck.shape[0]
    slab = shards * tokens
    total = slab + shards * slots
    width = GROUP * HD
    last = g == KV - 1
    sends = max(2 * (shards - 1), 1)
    smem = pl.BlockSpec(memory_space=pltpu.SMEM)

    def wide(rows):
        return pl.BlockSpec((rows, width), lambda i: (0, g))

    in_specs = [
        smem, smem, wide(tokens), wide(tokens), pl.BlockSpec((GROUP, HD), lambda i: (g, 0)),
        whole((slab, HD)), whole((slab, HD)),
        column(slots, g), column(slots, g), column(tokens, g), column(tokens, g),
        whole((KV, HD)), whole((KV, HD)),
    ]
    in_specs += [whole(a.shape) for a in far]
    in_specs += [pl.BlockSpec((2, tokens, HD), lambda i: (0, 0, g)) for _ in slabs]
    send_heads, send_place = (1, 0) if last else (KV - 1, g)
    out_shape = [
        pltpu.HBM((tokens, HQ * HD), B16),
        pltpu.HBM((tokens, HQ * HD), B16),
        jax.ShapeDtypeStruct((SUMS, HD), F32),
        pltpu.HBM((tokens, KV * HD), F32),
        pltpu.HBM((tokens, KV * HD), F32),
        pltpu.HBM((sends, tokens, send_heads * HD), B16),
    ]
    out_specs = [
        wide(tokens), wide(tokens), whole((SUMS, HD)),
        column(tokens, g), column(tokens, g),
        pl.BlockSpec((sends, tokens, HD), lambda i: (0, 0, send_place)),
    ]
    handed = []
    aliases = {}
    if before is not None:
        out, gq, sums, dk, dv, send = before
        handed = [sums, out, gq, dk, dv] + ([] if last else [send])
        aliases = {len(in_specs) + 1 + i: j for i, j in enumerate((0, 1, 3, 4, 5)[:len(handed) - 1])}
        in_specs += [whole((SUMS, HD))] + [pl.BlockSpec(memory_space=pl.ANY)] * (len(handed) - 1)
    return pl.pallas_call(
        functools.partial(attend_kernel, g, shards, len(handed)),
        grid=(1,),
        in_specs=in_specs,
        out_shape=out_shape,
        out_specs=out_specs,
        scratch_shapes=[
            pltpu.VMEM((total, HD), B16), pltpu.VMEM((total, HD), B16),
            pltpu.VMEM((GROUP, HD), F32),
            pltpu.VMEM((HD, slab), F32), pltpu.VMEM((HD, slab), F32),
        ],
        input_output_aliases=aliases,
        compiler_params=params(),
        cost_estimate=pl.CostEstimate(
            flops=2 * GROUP * tokens * HD * (4 * total + 2 * slab),
            bytes_accessed=8 * tokens * GROUP * HD + 8 * total * HD,
            transcendentals=GROUP * tokens * total,
        ),
        name="attend",
    )(first, rank, q, do, bq, cosine, sine, ck, cv, kp, vp, bk, bv, *far, *slabs, *handed)


def finish_kernel(shards, dk_ref, dv_ref, cos_ref, sin_ref, *rest):
    early, late = rest[: shards - 1], rest[shards - 1: 2 * (shards - 1)]
    gk_ref, gv_ref = rest[-2:]
    for g in range(KV):
        cols = pl.ds(g * HD, HD)
        dk = dk_ref[:, cols]
        dv = dv_ref[:, cols]
        for s in range(shards - 1):
            back, place = (late[s], pl.ds(0, HD)) if g == KV - 1 else (early[s], cols)
            dk = dk + back[0, :, place].astype(F32)
            dv = dv + back[1, :, place].astype(F32)
        gk_ref[:, cols] = (dk * cos_ref[...] - turn(dk) * sin_ref[...]).astype(B16)
        gv_ref[:, cols] = dv.astype(B16)


def finish(shards, dk, dv, cosine, sine, early, late):
    tokens = dk.shape[0]
    return pl.pallas_call(
        functools.partial(finish_kernel, shards),
        grid=(1,),
        in_specs=[whole(dk.shape)] * 2 + [whole((tokens, HD))] * 2
        + [whole(a.shape) for a in early + late],
        out_specs=[whole(dk.shape)] * 2,
        out_shape=[jax.ShapeDtypeStruct(dk.shape, B16)] * 2,
        compiler_params=params(),
        cost_estimate=pl.CostEstimate(flops=0, bytes_accessed=1 << 20, transcendentals=0),
        name="finish",
    )(dk, dv, cosine, sine, *early, *late)


def body(q_proj, k_proj, v_proj, cache_k, cache_v, bias_q, bias_k, bias_v, start, dout):
    shards = lax.axis_size("seq")
    rank = lax.axis_index("seq").astype(jnp.int32)
    tokens = q_proj.shape[1]
    ck, cv, kp, vp = cache_k[0], cache_v[0], k_proj[0], v_proj[0]

    def ring(x, s):
        return lax.ppermute(x, "seq", [(i, (i + s) % shards) for i in range(shards)])

    def later(x, s):
        return lax.ppermute(x, "seq", [(i, i + s) for i in range(shards - s)])

    def earlier(x, s):
        return lax.ppermute(x, "seq", [(i + s, i) for i in range(shards - s)])

    chunk, own = pack(0, 1, ck, cv, (kp, vp))
    chunks = [chunk] + list(pack(1, KV - 1, ck, cv))
    slabs = [later(own, s) for s in range(1, shards)]
    far = [[ring(chunk, s) for s in range(1, shards)] for chunk in chunks]

    owners = lax.rem(rank - jnp.arange(shards, dtype=jnp.int32) + shards, shards)
    positions = start[0] + owners[:, None] * tokens + jnp.arange(tokens, dtype=jnp.int32)[None]
    lane = jnp.arange(HD, dtype=jnp.int32)
    freqs = jnp.exp(
        -(2.0 * (lane % (HD // 2)).astype(F32) / HD) * jnp.log(jnp.float32(1000000.0))
    )
    angles = positions.reshape(-1).astype(F32)[:, None] * freqs[None, :]
    cosine = jnp.cos(angles)
    sine = jnp.sin(angles) * jnp.where(lane < HD // 2, -1.0, 1.0).astype(F32)[None]

    before = None
    for g in range(KV):
        if g == KV - 1:
            early = [earlier(before[5][2 * (s - 1):2 * s], s) for s in range(1, shards)]
        before = attend(
            g, shards, start, rank.reshape(1), q_proj[0], dout[0], bias_q.reshape(HQ, HD),
            cosine, sine, ck, cv, kp, vp, bias_k.reshape(KV, HD), bias_v.reshape(KV, HD),
            far[g], slabs, before,
        )
    out, gq, sums, dk, dv, send = before
    late = [earlier(send[2 * (s - 1):2 * s], s) for s in range(1, shards)]
    gk, gv = finish(shards, dk, dv, cosine, sine, early, late)
    sums = jnp.sum(lax.all_gather(sums, ("dp", "seq")), axis=0)
    return (
        out[None],
        gq[None],
        gk[None],
        gv[None],
        sums[:HQ].reshape(-1),
        sums[HQ:HQ + KV].reshape(-1),
        sums[HQ + KV:].reshape(-1),
    )


def solution(mesh):
    split = P("dp", "seq", None)
    return jax.shard_map(
        body,
        mesh=mesh,
        in_specs=(split,) * 5 + (P(), P(), P(), P("dp"), split),
        out_specs=(split,) * 4 + (P(), P(), P()),
        check_vma=False,
    )
```

time: 80.7 us -> 132 us (1.64)
  blocking collectives: 0 us -> 72 us
  Pallas kernels: 36.9 us -> 25.1 us
  starting transfers between devices: 18.5 us -> 11.6 us
  other arithmetic: 2.93 us -> 0.68 us
    all_gather x0 -> x1, blocking collectives: none -> 72 us  [body(): sums = jnp.sum(lax.all_gather(sums, ('dp', 'seq')), axis=0)]
    ppermute x4, waiting for transfers between devices: 0.01 us -> 13.1 us  [ring(): lax.ppermute(x, 'seq', [(i, (i + s) % shards) for i in range(shards)])]
    pallas_call x8 -> x6, Pallas kernels: 34.9 us -> 24.3 us  [the longest x4 22.4 us: attend(): pl.pallas_call(functools.partial(attend_kernel, g, shards, len(handed)),...]
    ppermute x5 -> x0, waiting for transfers between devices: 8.7 us -> none  [sum_over(): x = x + lax.ppermute(x, axis, [(i, i ^ step) for i in range(size)])]
    ppermute x5 -> x0, starting transfers between devices: 6.96 us -> none  [sum_over(): x = x + lax.ppermute(x, axis, [(i, i ^ step) for i in range(size)])]
    ppermute x2, waiting for transfers between devices: 5 us -> 0.01 us  [earlier(): return lax.ppermute(x, 'seq', [(i + s, i) for i in range(shards - s)])]
    broadcast_in_dim x3 -> x0, local copies, waits for them, and re-layouts: 1.78 us -> none  [the longest x1 0.62 us: body(): bias_q[None]]
    unnamed x25 -> x32, local copies, waits for them, and re-layouts: 4.38 us -> 5.79 us
  transfers between devices with their start and end apart: 12 -> 7, of which waited for: 6 -> 3; matrix products, arithmetic and copies ran while one was open for 6% -> 1% of each run, Pallas kernels for 33% -> 14%
where the time goes in v3:
time: 132 us; the launch traced here: 131 us
  blocking collectives  72 us (55%)
  Pallas kernels  25.1 us (19%)
  waiting for transfers between devices  13.6 us (10%)
  starting transfers between devices  11.6 us (9%)
  local copies, waits for them, and re-layouts  6.98 us (5%)
  between operations  1.45 us (1%)
    all_gather x1, blocking collectives, body(): sums = jnp.sum(lax.all_gather(sums, ('dp', 'seq')), axis=0)  72 us
    pallas_call x4, Pallas kernels, attend(): pl.pallas_call(functools.partial(attend_kernel, g, shards, len(handed)),...  22.4 us
    ppermute x4, waiting for transfers between devices, ring(): lax.ppermute(x, 'seq', [(i, (i + s) % shards) for i in range(shards)])  13.1 us
    unnamed x32, local copies, waits for them, and re-layouts  5.79 us
    ppermute x1, starting transfers between devices, later(): return lax.ppermute(x, 'seq', [(i, i + s) for i in range(shards - s)])  4.87 us
    ppermute x4, starting transfers between devices, ring(): lax.ppermute(x, 'seq', [(i, (i + s) % shards) for i in range(shards)])  4.11 us
  transfers between devices with their start and end apart: 7, of which 3 were waited for; matrix products, arithmetic and copies ran while one was open for 1% of the time, Pallas kernels for 14%

profile of v3, /device:TPU:0, one launch (start us, length us, event | category | flops | bytes accessed | tf_op | source)
XLA Modules:
  0.0 131.4 jit_solution(3916746504569641877)
XLA Ops:
  0.6 0.0 copy-start
  0.6 1.0 copy-done
  1.7 0.0 copy-start.2
  1.7 1.0 copy-done.2
  2.7 0.0 copy-start.8
  2.7 0.9 copy-done.8
  3.6 0.0 copy-start.10
  3.6 0.9 copy-done.10
  4.5 0.0 copy-start.4
  4.5 0.9 pack.3
  5.4 4.9 %collective-permute-start.1 = (bf16[2,128,512]{2,1,0:T(8,128)(2,1)}, bf16[2,128,512]{2,1,0:T(8,128)(2,1)S(1)}, u32[]{:S(2)}, u32[]{:S(2)}) collective-permute-start(bf16[2,128,512]{2,1,0:T(8,128)(2,1)} %get-tuple-element.39), channel_id=1, source_target_pairs={{0,1},{2,3},{4,5},{6,7},{8,9},{10,11},{12,13},{14,15},{16,17},{18,... | collective-permute-start | bytes 786440 | tf_op jit(solution)/shard_map/ppermute | solution.py:321
  10.3 0.0 copy-start.1
  10.3 0.0 copy-start.3
  10.3 0.1 collective-permute-start.4
  10.4 1.0 pack.2
  11.4 2.0 %collective-permute-start = (bf16[1024,128]{1,0:T(8,128)(2,1)}, bf16[1024,128]{1,0:T(8,128)(2,1)S(1)}, u32[]{:S(2)}, u32[]{:S(2)}) collective-permute-start(bf16[1024,128]{1,0:T(8,128)(2,1)} %get-tuple-element.38), channel_id=1, source_target_pairs={{0,1},{1,0},{2,3},{3,2},{4,5},{5,4},{6,7},{7,6},{8,9},{9,8},{10,11... | collective-permute-start | bytes 786440 | tf_op jit(solution)/shard_map/ppermute | solution.py:318
  13.4 0.0 collective-permute-start.2
  13.4 2.0 %collective-permute-start.3 = (bf16[1024,128]{1,0:T(8,128)(2,1)}, bf16[1024,128]{1,0:T(8,128)(2,1)S(1)}, u32[]{:S(2)}, u32[]{:S(2)}) collective-permute-start(bf16[1024,128]{1,0:T(8,128)(2,1)} %get-tuple-element.41), channel_id=1, source_target_pairs={{0,1},{1,0},{2,3},{3,2},{4,5},{5,4},{6,7},{7,6},{8,9},{9,8},{10,11... | collective-permute-start | bytes 786440 | tf_op jit(solution)/shard_map/ppermute | solution.py:318
  16.1 0.1 convert_bitcast_fusion
  16.2 0.0 copy-start.9
  16.2 0.0 copy-start.11
  16.2 0.0 copy-start.14
  16.2 0.5 fusion
  16.7 0.0 copy-start.12
  16.8 0.5 collective-permute-done.1.rest_1_
  17.3 5.6 %collective-permute-done.4.rest_0_ = bf16[1024,128]{1,0:T(8,128)(2,1)} collective-permute-done((bf16[1024,128]{1,0:T(8,128)(2,1)}, bf16[1024,128]{1,0:T(8,128)(2,1)}, u32[]{:S(2)}, u32[]{:S(2)}) %collective-permute-start.4) | collective-permute-done | bytes 262176 | tf_op jit(solution)/shard_map/ppermute | solution.py:318
  22.9 0.0 copy-start.13
  22.9 0.0 copy-done.4
  22.9 0.0 copy-done.1
  22.9 0.0 copy-done.3
  22.9 0.0 copy-done.9
  22.9 0.0 copy-done.11
  22.9 0.0 copy-done.14
  22.9 0.0 copy-done.12
  22.9 0.6 copy-done.13
  23.6 0.0 copy-start.5
  23.6 1.2 copy-done.5
  24.8 6.3 %attend.4 = (bf16[128,4096]{1,0:T(8,128)(2,1)}, bf16[128,4096]{1,0:T(8,128)(2,1)}, f32[40,128]{1,0:T(8,128)S(1)}, f32[128,512]{1,0:T(8,128)}, f32[128,512]{1,0:T(8,128)}, /*index=5*/bf16[2,128,384]{2,1,0:T(8,128)(2,1)}) custom-call(s32[1]{0:T(128)} %copy.45.first_ref, s32[1]{0:T(128)} %bitcast.rank_ref, bf16[128,4096]{1,0:T(8,128)(2,1)S(1)} %bitcast.37, ...), custom_call_target="tpu_custom_call" | custom-call | flops 1476395008 | bytes 2359296 | tf_op jit(solution)/shard_map/attend/pallas_call | solution.py:259
  31.1 7.5 %collective-permute-done.3.rest_0_ = bf16[1024,128]{1,0:T(8,128)(2,1)S(1)} collective-permute-done((bf16[1024,128]{1,0:T(8,128)(2,1)}, bf16[1024,128]{1,0:T(8,128)(2,1)S(1)}, u32[]{:S(2)}, u32[]{:S(2)}) %collective-permute-start.3) | collective-permute-done | bytes 262176 | tf_op jit(solution)/shard_map/ppermute | solution.py:318
  38.6 5.4 %attend.5 = (bf16[128,4096]{1,0:T(8,128)(2,1)}, bf16[128,4096]{1,0:T(8,128)(2,1)}, f32[40,128]{1,0:T(8,128)S(1)}, f32[128,512]{1,0:T(8,128)}, f32[128,512]{1,0:T(8,128)}, /*index=5*/bf16[2,128,384]{2,1,0:T(8,128)(2,1)}) custom-call(s32[1]{0:T(128)} %copy.45.first_ref, ...), custom_call_target="tpu_custom_call", output_to_operand_aliasing={{0}: (16, {}), {1}: (17, {}), {3}: (18, {}), {4}: (19, {}),... | custom-call | flops 1476395008 | bytes 2359296 | tf_op jit(solution)/shard_map/attend/pallas_call | solution.py:259
  44.0 0.0 collective-permute-done.2.rest_0_
  44.0 5.4 %attend.6 = (bf16[128,4096]{1,0:T(8,128)(2,1)}, bf16[128,4096]{1,0:T(8,128)(2,1)}, f32[40,128]{1,0:T(8,128)S(1)}, f32[128,512]{1,0:T(8,128)}, f32[128,512]{1,0:T(8,128)}, /*index=5*/bf16[2,128,384]{2,1,0:T(8,128)(2,1)}) custom-call(s32[1]{0:T(128)} %copy.45.first_ref, ...), custom_call_target="tpu_custom_call", output_to_operand_aliasing={{0}: (16, {}), {1}: (17, {}), {3}: (18, {}), {4}: (19, {}),... | custom-call | flops 1476395008 | bytes 2359296 | tf_op jit(solution)/shard_map/attend/pallas_call | solution.py:259
  49.4 0.0 collective-permute-done.rest_0_
  49.4 0.0 copy-start.15
  49.4 5.3 %attend.7 = (bf16[128,4096]{1,0:T(8,128)(2,1)}, bf16[128,4096]{1,0:T(8,128)(2,1)}, f32[40,128]{1,0:T(8,128)S(1)}, f32[128,512]{1,0:T(8,128)}, f32[128,512]{1,0:T(8,128)}, /*index=5*/bf16[2,128,128]{2,1,0:T(8,128)(2,1)}) custom-call(s32[1]{0:T(128)} %copy.45.first_ref, ...), custom_call_target="tpu_custom_call", output_to_operand_aliasing={{0}: (16, {}), {1}: (17, {}), {3}: (18, {}), {4}: (19, {})} | custom-call | flops 1476395008 | bytes 2359296 | tf_op jit(solution)/shard_map/attend/pallas_call | solution.py:259
  54.7 1.3 collective-permute-start.6
  56.0 0.0 copy-done.15
  56.0 1.3 collective-permute-start.5
  57.3 72.0 %all-gather = f32[1280,128]{1,0:T(8,128)S(1)} all-gather(f32[40,128]{1,0:T(8,128)S(1)} %get-tuple-element.68), channel_id=2, replica_groups=mesh['dp'=16,'seq'=2] {'dp','seq'}, dimensions={0}, use_global_device_ids=true | all-gather | bytes 675840 | tf_op jit(solution)/shard_map/all_gather | solution.py:353
  129.3 0.0 copy-start.6
  129.3 0.0 copy-start.7
  129.3 0.1 reduce_sum.9
  129.4 0.6 slice_bitcast_fusion
  130.0 0.6 slice_bitcast_fusion.1
  130.6 0.0 collective-permute-done.6.rest_1_
  130.6 0.0 collective-permute-done.5.rest_0_
  130.6 0.0 copy-done.6
  130.6 0.0 copy-done.7
  130.6 0.8 finish.1
  (2 shorter events, 0.0 us)
Async XLA Ops:
  0.6 1.0 copy-start
  1.7 1.0 copy-start.2
  2.7 0.9 copy-start.8
  3.6 0.9 copy-start.10
  4.5 18.4 %copy-start.4 = (bf16[1,128,4096]{2,1,0:T(8,128)(2,1)S(1)}, bf16[1,128,4096]{2,1,0:T(8,128)(2,1)}, u32[]{:S(2)}) copy-start(bf16[1,128,4096]{2,1,0:T(8,128)(2,1)} %param.10) | copy-start | bytes 3145732
  5.4 11.9 %collective-permute-start.1 = (bf16[2,128,512]{2,1,0:T(8,128)(2,1)}, bf16[2,128,512]{2,1,0:T(8,128)(2,1)S(1)}, u32[]{:S(2)}, u32[]{:S(2)}) collective-permute-start(bf16[2,128,512]{2,1,0:T(8,128)(2,1)} %get-tuple-element.39), channel_id=1, source_target_pairs={{0,1},{2,3},{4,5},{6,7},{8,9},{10,11},{12,13},{14,15},{16,17},{18,... | collective-permute-start | bytes 786440 | tf_op jit(solution)/shard_map/ppermute | solution.py:321
  10.3 12.6 %copy-start.1 = (bf16[1,512,512]{2,1,0:T(8,128)(2,1)S(1)}, bf16[1,512,512]{2,1,0:T(8,128)(2,1)}, u32[]{:S(2)}) copy-start(bf16[1,512,512]{2,1,0:T(8,128)(2,1)} %param.13) | copy-start | bytes 1572868
  10.3 12.6 %copy-start.3 = (bf16[1,512,512]{2,1,0:T(8,128)(2,1)S(1)}, bf16[1,512,512]{2,1,0:T(8,128)(2,1)}, u32[]{:S(2)}) copy-start(bf16[1,512,512]{2,1,0:T(8,128)(2,1)} %param.14) | copy-start | bytes 1572868
  10.3 12.6 %collective-permute-start.4 = (bf16[1024,128]{1,0:T(8,128)(2,1)}, bf16[1024,128]{1,0:T(8,128)(2,1)}, u32[]{:S(2)}, u32[]{:S(2)}) collective-permute-start(bf16[1024,128]{1,0:T(8,128)(2,1)} %get-tuple-element.42), channel_id=1, source_target_pairs={{0,1},{1,0},{2,3},{3,2},{4,5},{5,4},{6,7},{7,6},{8,9},{9,8},{10,11... | collective-permute-start | bytes 786440 | tf_op jit(solution)/shard_map/ppermute | solution.py:318
  11.4 38.0 %collective-permute-start = (bf16[1024,128]{1,0:T(8,128)(2,1)}, bf16[1024,128]{1,0:T(8,128)(2,1)S(1)}, u32[]{:S(2)}, u32[]{:S(2)}) collective-permute-start(bf16[1024,128]{1,0:T(8,128)(2,1)} %get-tuple-element.38), channel_id=1, source_target_pairs={{0,1},{1,0},{2,3},{3,2},{4,5},{5,4},{6,7},{7,6},{8,9},{9,8},{10,11... | collective-permute-start | bytes 786440 | tf_op jit(solution)/shard_map/ppermute | solution.py:318
  13.4 30.6 %collective-permute-start.2 = (bf16[1024,128]{1,0:T(8,128)(2,1)}, bf16[1024,128]{1,0:T(8,128)(2,1)S(1)}, u32[]{:S(2)}, u32[]{:S(2)}) collective-permute-start(bf16[1024,128]{1,0:T(8,128)(2,1)} %get-tuple-element.40), channel_id=1, source_target_pairs={{0,1},{1,0},{2,3},{3,2},{4,5},{5,4},{6,7},{7,6},{8,9},{9,8},{10,11... | collective-permute-start | bytes 786440 | tf_op jit(solution)/shard_map/ppermute | solution.py:318
  13.4 25.2 %collective-permute-start.3 = (bf16[1024,128]{1,0:T(8,128)(2,1)}, bf16[1024,128]{1,0:T(8,128)(2,1)S(1)}, u32[]{:S(2)}, u32[]{:S(2)}) collective-permute-start(bf16[1024,128]{1,0:T(8,128)(2,1)} %get-tuple-element.41), channel_id=1, source_target_pairs={{0,1},{1,0},{2,3},{3,2},{4,5},{5,4},{6,7},{7,6},{8,9},{9,8},{10,11... | collective-permute-start | bytes 786440 | tf_op jit(solution)/shard_map/ppermute | solution.py:318
  16.2 6.7 %copy-start.9 = (bf16[1,128,512]{2,1,0:T(8,128)(2,1)S(1)}, bf16[1,128,512]{2,1,0:T(8,128)(2,1)}, u32[]{:S(2)}) copy-start(bf16[1,128,512]{2,1,0:T(8,128)(2,1)} %param.11) | copy-start | bytes 393220
  16.2 6.7 %copy-start.11 = (bf16[1,128,512]{2,1,0:T(8,128)(2,1)S(1)}, bf16[1,128,512]{2,1,0:T(8,128)(2,1)}, u32[]{:S(2)}) copy-start(bf16[1,128,512]{2,1,0:T(8,128)(2,1)} %param.12) | copy-start | bytes 393220
  16.2 6.7 %copy-start.14 = (bf16[512]{0:T(512)(128)(2,1)S(1)}, bf16[512]{0:T(512)(128)(2,1)}, u32[]{:S(2)}) copy-start(bf16[512]{0:T(512)(128)(2,1)} %param.17) | copy-start | bytes 3076
  16.7 6.2 %copy-start.12 = (bf16[4096]{0:T(1024)(128)(2,1)S(1)}, bf16[4096]{0:T(1024)(128)(2,1)}, u32[]{:S(2)}) copy-start(bf16[4096]{0:T(1024)(128)(2,1)} %param.15) | copy-start | bytes 24580
  22.9 0.7 copy-start.13
  23.6 1.2 copy-start.5
  49.4 6.6 %copy-start.15 = (bf16[2,128,384]{2,1,0:T(8,128)(2,1)S(1)}, bf16[2,128,384]{2,1,0:T(8,128)(2,1)}, u32[]{:S(2)}) copy-start(bf16[2,128,384]{2,1,0:T(8,128)(2,1)} %get-tuple-element.64) | copy-start | bytes 589828
  54.7 75.9 %collective-permute-start.6 = (bf16[2,128,128]{2,1,0:T(8,128)(2,1)}, bf16[2,128,128]{2,1,0:T(8,128)(2,1)S(1)}, u32[]{:S(2)}, u32[]{:S(2)}) collective-permute-start(bf16[2,128,128]{2,1,0:T(8,128)(2,1)} %get-tuple-element.65), channel_id=1, source_target_pairs={{1,0},{3,2},{5,4},{7,6},{9,8},{11,10},{13,12},{15,14},{17,16},{19,... | collective-permute-start | bytes 196616 | tf_op jit(solution)/shard_map/ppermute | solution.py:324
  56.0 74.6 %collective-permute-start.5 = (bf16[2,128,384]{2,1,0:T(8,128)(2,1)S(1)}, bf16[2,128,384]{2,1,0:T(8,128)(2,1)S(1)}, u32[]{:S(2)}, u32[]{:S(2)}) collective-permute-start(bf16[2,128,384]{2,1,0:T(8,128)(2,1)S(1)} %copy-done.15), channel_id=1, source_target_pairs={{1,0},{3,2},{5,4},{7,6},{9,8},{11,10},{13,12},{15,14},{17,16},{19,... | collective-permute-start | bytes 589832 | tf_op jit(solution)/shard_map/ppermute | solution.py:324
  129.3 1.3 copy-start.6
  129.3 1.3 copy-start.7

commit v4 on v3

v4 whole, which is shorter than its diff:
```python
import functools
import math

import jax
import jax.numpy as jnp
from jax import lax
from jax.experimental import pallas as pl
from jax.experimental.pallas import tpu as pltpu
from jax.sharding import PartitionSpec as P

HQ = 32
KV = 4
HD = 128
GROUP = 8
HEADS = 2
NEG = -1e30
SUMS = HQ + 2 * KV
VMEM = 28 * 1024 * 1024
F32, B16 = jnp.float32, jnp.bfloat16


def turn(x):
    return pltpu.roll(x, HD // 2, 1)


def dot(a, b, dims):
    return lax.dot_general(a, b, (dims, ((), ())), preferred_element_type=F32)


NT = ((1,), (1,))
NN = ((1,), (0,))
TN = ((0,), (0,))


def whole(shape):
    return pl.BlockSpec(shape, lambda i: (0,) * len(shape))


def column(rows, g):
    return pl.BlockSpec((rows, HD), lambda i: (0, g))


def params():
    return pltpu.CompilerParams(dimension_semantics=("arbitrary",), vmem_limit_bytes=VMEM)


def copy_chunk(g, ck_ref, cv_ref, out_ref):
    rows = ck_ref.shape[0]
    cols = pl.ds(g * HD, HD)
    out_ref[pl.ds(0, rows)] = ck_ref[:, cols]
    out_ref[pl.ds(rows, rows)] = cv_ref[:, cols]


def pack_kernel(ck_ref, cv_ref, *rest):
    copy_chunk(0, ck_ref, cv_ref, rest[-1])


def pack(g, ck, cv, *after):
    rows = ck.shape[0]
    return pl.pallas_call(
        pack_kernel,
        grid=(1,),
        in_specs=[column(rows, g)] * 2 + [pl.BlockSpec(memory_space=pl.ANY)] * len(after),
        out_specs=pl.BlockSpec(memory_space=pltpu.VMEM),
        out_shape=pltpu.VMEM((2 * rows, HD), B16),
        compiler_params=params(),
        cost_estimate=pl.CostEstimate(flops=0, bytes_accessed=8 * rows * HD, transcendentals=0),
        name="pack",
    )(ck, cv, *after)


def turn_back(x, cosine, sine):
    return x * cosine - turn(x) * sine


def finish_heads(heads, shards, tables, owns, backs, gk_ref, gv_ref):
    tokens = gk_ref.shape[0]
    cosine, sine = (t[pl.ds(0, tokens), :] for t in tables)
    for i in range(heads):
        dk, dv = owns[i][0], owns[i][1]
        for s in range(shards - 1):
            dk = dk + backs[s][2 * i].astype(F32)
            dv = dv + backs[s][2 * i + 1].astype(F32)
        cols = pl.ds(i * HD, HD)
        gk_ref[:, cols] = turn_back(dk, cosine, sine).astype(B16)
        gv_ref[:, cols] = dv.astype(B16)


def attend_kernel(g, shards, *refs):
    refs = list(refs)

    def take(count):
        taken = refs[:count]
        del refs[:count]
        return taken

    (first_ref, rank_ref, q_ref, do_ref, bq_ref, cos_ref, sin_ref,
     ck_ref, cv_ref, kp_ref, vp_ref, bk_ref, bv_ref) = take(13)
    far = take(shards - 1)
    far_k = take(shards - 1)
    far_v = take(shards - 1)
    old_sums_ref = take(1)[0] if g else None
    old_send = take(shards - 1) if g % 2 else []
    owns = take(2) if g == KV - 1 else []
    backs = take(shards - 1) if g == KV - 1 else []
    if g:
        take(2)
    out_ref, gq_ref, sums_ref, own_ref = take(4)
    send = take(shards - 1)
    pack_ref = take(1)[0] if g + 2 < KV else None
    gk_ref, gv_ref = take(2) if g == KV - 1 else (None, None)
    keys, values, keys_t, values_t, bias, dkt, dvt = refs
    tokens = q_ref.shape[0]
    slots = ck_ref.shape[0]
    prefix = shards * slots
    slab = shards * tokens
    first = first_ref[0]
    rank = rank_ref[0]
    mine = pl.ds(g * HD, HD)

    if pack_ref is not None:
        copy_chunk(g + 2, ck_ref, cv_ref, pack_ref)
    keys[pl.ds(0, slots)] = ck_ref[:, mine]
    values[pl.ds(0, slots)] = cv_ref[:, mine]
    for s in range(1, shards):
        keys[pl.ds(s * slots, slots)] = far[s - 1][pl.ds(0, slots)]
        values[pl.ds(s * slots, slots)] = far[s - 1][pl.ds(slots, slots)]
    bias_k = bk_ref[...].astype(F32)[g:g + 1]
    bias_v = bv_ref[...].astype(F32)[g:g + 1]
    for s in range(shards):
        rows = pl.ds(s * tokens, tokens)
        kp, vp = (kp_ref, vp_ref) if s == 0 else (far_k[s - 1], far_v[s - 1])
        k = kp[:, mine].astype(F32) + bias_k
        k = k * cos_ref[rows, :] + turn(k) * sin_ref[rows, :]
        v = vp[:, mine].astype(F32) + bias_v
        place = pl.ds(prefix + s * tokens, tokens)
        keys[place] = k.astype(B16)
        values[place] = v.astype(B16)
    keys_t[...] = keys[...].T
    values_t[...] = values[...].T
    bias[...] = bq_ref[...].astype(F32)[g * GROUP:(g + 1) * GROUP]
    sums_ref[...] = jnp.zeros_like(sums_ref) if old_sums_ref is None else old_sums_ref[...]
    dkt[...] = jnp.zeros_like(dkt)
    dvt[...] = jnp.zeros_like(dvt)

    rows = HEADS * tokens
    scale = HD ** -0.5

    def scores(head):
        cosine = cos_ref[pl.ds(0, tokens), :]
        sine = sin_ref[pl.ds(0, tokens), :]
        queries, cots = [], []
        for h in range(HEADS):
            cols = pl.ds(pl.multiple_of((g * GROUP + head + h) * HD, HD), HD)
            x = q_ref[:, cols].astype(F32) + bias[pl.ds(head + h, 1), :]
            x = x * cosine + turn(x) * sine
            queries.append(x.astype(B16))
            cots.append(do_ref[:, cols])
        q = jnp.concatenate(queries, axis=0)
        do = jnp.concatenate(cots, axis=0)
        s = dot(q, keys_t[...], NN)
        col = lax.broadcasted_iota(jnp.int32, (1, slots), 1)
        parts = []
        for j in range(shards):
            seen = col < first - lax.rem(rank - j + shards, shards) * slots
            parts.append(jnp.where(seen, s[:, j * slots:(j + 1) * slots], NEG))
        token = lax.broadcasted_iota(jnp.int32, (rows, tokens), 0) & (tokens - 1)
        causal = lax.broadcasted_iota(jnp.int32, (rows, tokens), 1) <= token
        parts.append(jnp.where(causal, s[:, prefix:prefix + tokens], NEG))
        for j in range(1, shards):
            part = s[:, prefix + j * tokens:prefix + (j + 1) * tokens]
            parts.append(jnp.where(rank >= j, part, NEG))
        return q, do, jnp.concatenate(parts, axis=1)

    def softmax(s):
        top = jnp.max(s, axis=1, keepdims=True)
        e = jnp.exp2((s - top) * (scale * math.log2(math.e)))
        return e * (1.0 / jnp.sum(e, axis=1, keepdims=True))

    def weigh(pb, do):
        o = dot(pb, values[...], NN).astype(B16)
        return o, jnp.sum(do.astype(F32) * o.astype(F32), axis=1, keepdims=True)

    def store(head, o, dq):
        cosine = cos_ref[pl.ds(0, tokens), :]
        sine = sin_ref[pl.ds(0, tokens), :]
        for h in range(HEADS):
            cols = pl.ds(pl.multiple_of((head + h) * HD, HD), HD)
            part = slice(h * tokens, (h + 1) * tokens)
            out_ref[:, cols] = o[part]
            x = turn_back(dq[part], cosine, sine)
            gq_ref[:, cols] = x.astype(B16)
            sums_ref[pl.ds(g * GROUP + head + h, 1), :] = jnp.sum(x, axis=0, keepdims=True)

    def query_grad(ds):
        return (dot(ds, keys[...], NN) * scale).astype(B16).astype(F32)

    def pair(i, carry):
        head_a = i * 2 * HEADS
        head_b = head_a + HEADS
        q_a, do_a, s_a = scores(head_a)
        q_b, do_b, s_b = scores(head_b)
        dp_a = dot(do_a, values_t[...], NN)
        p_a = softmax(s_a)
        pb_a = p_a.astype(B16)
        dp_b = dot(do_b, values_t[...], NN)
        o_a, delta_a = weigh(pb_a, do_a)
        p_b = softmax(s_b)
        pb_b = p_b.astype(B16)
        ds_a = (p_a * (dp_a - delta_a)).astype(B16)
        o_b, delta_b = weigh(pb_b, do_b)
        dq_a = query_grad(ds_a)
        dkt[...] += dot(q_a, ds_a[:, prefix:], TN)
        dvt[...] += dot(do_a, pb_a[:, prefix:], TN)
        ds_b = (p_b * (dp_b - delta_b)).astype(B16)
        store(head_a, o_a, dq_a)
        dq_b = query_grad(ds_b)
        dkt[...] += dot(q_b, ds_b[:, prefix:], TN)
        dvt[...] += dot(do_b, pb_b[:, prefix:], TN)
        store(head_b, o_b, dq_b)
        return carry

    lax.fori_loop(0, GROUP // (2 * HEADS), pair, 0)

    dk = dkt[...].T * scale
    dv = dvt[...].T
    gk = turn_back(dk, cos_ref[...], sin_ref[...])
    own_ref[0] = dk[:tokens]
    own_ref[1] = dv[:tokens]
    at = 2 * (g % 2)
    for j in range(1, shards):
        block = slice(j * tokens, (j + 1) * tokens)
        send[j - 1][at] = dk[block].astype(B16)
        send[j - 1][at + 1] = dv[block].astype(B16)
        if at:
            send[j - 1][pl.ds(0, at)] = old_send[j - 1][...]
    sums_ref[pl.ds(HQ + g, 1), :] = jnp.sum(gk, axis=0, keepdims=True)
    sums_ref[pl.ds(HQ + KV + g, 1), :] = jnp.sum(dv, axis=0, keepdims=True)
    if gk_ref is not None:
        finish_heads(2, shards, (cos_ref, sin_ref), owns, backs, gk_ref, gv_ref)


def attend(
    g, shards, first, rank, q, do, bq, cosine, sine, ck, cv, kp, vp, bk, bv, far, far_k, far_v,
    before, owns, backs,
):
    tokens, slots = q.shape[0], ck.shape[0]
    slab = shards * tokens
    total = slab + shards * slots
    last = g == KV - 1
    smem = pl.BlockSpec(memory_space=pltpu.SMEM)
    vmem = pl.BlockSpec(memory_space=pltpu.VMEM)
    anywhere = pl.BlockSpec(memory_space=pl.ANY)
    wide = pl.BlockSpec((tokens, GROUP * HD), lambda i: (0, g))
    half = pl.BlockSpec((tokens, 2 * HD), lambda i: (0, 0))

    args = [first, rank]
    placed = [q, do, bq, cosine, sine, ck, cv, kp, vp, bk, bv, *far, *far_k, *far_v]
    aliases = {}
    if before is not None:
        out, gq, sums, send = before
        placed.append(sums)
        if g % 2:
            placed += send
        if last:
            placed += [*owns[:2], *backs]
    args += placed
    in_specs = [smem] * 2 + [vmem] * len(placed)
    if before is not None:
        aliases = {len(args): 0, len(args) + 1: 1}
        args += [out, gq]
        in_specs += [anywhere] * 2
    out_shape = [
        pltpu.HBM((tokens, HQ * HD), B16),
        pltpu.HBM((tokens, HQ * HD), B16),
        pltpu.VMEM((SUMS, HD), F32),
        pltpu.VMEM((2, tokens, HD), F32),
    ]
    out_specs = [wide, wide, vmem, vmem]
    out_shape += [pltpu.VMEM((2 + 2 * (g % 2), tokens, HD), B16)] * (shards - 1)
    out_specs += [vmem] * (shards - 1)
    if g + 2 < KV:
        out_shape.append(pltpu.VMEM((2 * slots, HD), B16))
        out_specs.append(vmem)
    if last:
        out_shape += [pltpu.HBM((tokens, KV * HD), B16)] * 2
        out_specs += [half] * 2
    results = pl.pallas_call(
        functools.partial(attend_kernel, g, shards),
        grid=(1,),
        in_specs=in_specs,
        out_shape=out_shape,
        out_specs=out_specs,
        scratch_shapes=[
            pltpu.VMEM((total, HD), B16), pltpu.VMEM((total, HD), B16),
            pltpu.VMEM((HD, total), B16), pltpu.VMEM((HD, total), B16),
            pltpu.VMEM((GROUP, HD), F32),
            pltpu.VMEM((HD, slab), F32), pltpu.VMEM((HD, slab), F32),
        ],
        input_output_aliases=aliases,
        compiler_params=params(),
        cost_estimate=pl.CostEstimate(
            flops=2 * GROUP * tokens * HD * (4 * total + 2 * slab),
            bytes_accessed=8 * tokens * GROUP * HD + 8 * total * HD,
            transcendentals=GROUP * tokens * total,
        ),
        name="attend",
    )(*args)
    out, gq, sums, own = results[:4]
    send = results[4:4 + shards - 1]
    return (out, gq, sums, send), own, results[4 + shards - 1:]


def finish_kernel(shards, *refs):
    owns, backs = refs[2:4], refs[4:4 + shards - 1]
    finish_heads(2, shards, refs[:2], owns, backs, *refs[-2:])


def finish(shards, cosine, sine, owns, backs, gk, gv):
    tokens = gk.shape[0]
    vmem = pl.BlockSpec(memory_space=pltpu.VMEM)
    args = [cosine, sine, *owns, *backs]
    return pl.pallas_call(
        functools.partial(finish_kernel, shards),
        grid=(1,),
        in_specs=[vmem] * len(args) + [pl.BlockSpec(memory_space=pl.ANY)] * 2,
        out_specs=[pl.BlockSpec((tokens, 2 * HD), lambda i: (0, 1))] * 2,
        out_shape=[pltpu.HBM(gk.shape, B16)] * 2,
        input_output_aliases={len(args): 0, len(args) + 1: 1},
        compiler_params=params(),
        cost_estimate=pl.CostEstimate(flops=0, bytes_accessed=1 << 19, transcendentals=0),
        name="finish",
    )(*args, gk, gv)


def sum_everywhere(x, axes):
    devices = lax.axis_size(axes)
    copies = jnp.broadcast_to(x[None], (devices,) + x.shape)
    return jnp.sum(lax.all_to_all(copies, axes, 0, 0, tiled=True), axis=0)


def body(q_proj, k_proj, v_proj, cache_k, cache_v, bias_q, bias_k, bias_v, start, dout):
    shards = lax.axis_size("seq")
    rank = lax.axis_index("seq").astype(jnp.int32)
    tokens = q_proj.shape[1]
    ck, cv, kp, vp = cache_k[0], cache_v[0], k_proj[0], v_proj[0]

    def ring(x, s):
        return lax.ppermute(x, "seq", [(i, (i + s) % shards) for i in range(shards)])

    def later(x, s):
        return lax.ppermute(x, "seq", [(i, i + s) for i in range(shards - s)])

    def earlier(x, s):
        return lax.ppermute(x, "seq", [(i + s, i) for i in range(shards - s)])

    shifts = range(1, shards)
    far_k = [later(kp, s) for s in shifts]
    far_v = [later(vp, s) for s in shifts]
    hbm = functools.partial(pltpu.with_memory_space_constraint, memory_space=pltpu.HBM)
    chunk = pack(0, hbm(ck), hbm(cv))
    far = [[ring(chunk, s) for s in shifts]]

    owners = lax.rem(rank - jnp.arange(shards, dtype=jnp.int32) + shards, shards)
    positions = start[0] + owners[:, None] * tokens + jnp.arange(tokens, dtype=jnp.int32)[None]
    lane = jnp.arange(HD, dtype=jnp.int32)
    freqs = jnp.exp(
        -(2.0 * (lane % (HD // 2)).astype(F32) / HD) * jnp.log(jnp.float32(1000000.0))
    )
    angles = positions.reshape(-1).astype(F32)[:, None] * freqs[None, :]
    cosine = jnp.cos(angles)
    sine = jnp.sin(angles) * jnp.where(lane < HD // 2, -1.0, 1.0).astype(F32)[None]

    far.append([ring(pack(1, ck, cv, cosine), s) for s in shifts])
    before, owns, backs = None, [], []
    for g in range(KV):
        before, own, more = attend(
            g, shards, start, rank.reshape(1), q_proj[0], dout[0], bias_q.reshape(HQ, HD),
            cosine, sine, ck, cv, kp, vp, bias_k.reshape(KV, HD), bias_v.reshape(KV, HD),
            far[g], far_k, far_v, before, owns, backs,
        )
        owns.append(own)
        if g + 2 < KV:
            far.append([ring(more[0], s) for s in shifts])
        if g % 2:
            backs = [earlier(x, s) for s, x in zip(shifts, before[3])]
    out, gq, sums, _ = before
    gk, gv = finish(shards, cosine, sine, owns[2:], backs, *more)
    sums = sum_everywhere(sums, ("dp", "seq"))
    return (
        out[None],
        gq[None],
        gk[None],
        gv[None],
        sums[:HQ].reshape(-1),
        sums[HQ:HQ + KV].reshape(-1),
        sums[HQ + KV:].reshape(-1),
    )


def solution(mesh):
    split = P("dp", "seq", None)
    return jax.shard_map(
        body,
        mesh=mesh,
        in_specs=(split,) * 5 + (P(), P(), P(), P("dp"), split),
        out_specs=(split,) * 4 + (P(), P(), P()),
        check_vma=False,
    )
```

time: 132 us -> 73.4 us (0.56)
  blocking collectives: 72 us -> 0 us
  waiting for transfers between devices: 13.6 us -> 24 us
  starting transfers between devices: 11.6 us -> 18.6 us
  local copies, waits for them, and re-layouts: 6.98 us -> 4.01 us
    all_gather x1 -> x0, blocking collectives: 72 us -> none  [body(): sums = jnp.sum(lax.all_gather(sums, ('dp', 'seq')), axis=0)]
    ppermute x2, waiting for transfers between devices: 0.01 us -> 11.3 us  [earlier(): return lax.ppermute(x, 'seq', [(i + s, i) for i in range(shards - s)])]
    ppermute x4, waiting for transfers between devices: 13.1 us -> 5.52 us  [ring(): lax.ppermute(x, 'seq', [(i, (i + s) % shards) for i in range(shards)])]
    all_to_all x0 -> x1, waiting for transfers between devices: none -> 6.24 us  [sum_everywhere(): return jnp.sum(lax.all_to_all(copies, axes, 0, 0, tiled=True), axis=0)]
    all_to_all x0 -> x1, starting transfers between devices: none -> 5.31 us  [sum_everywhere(): return jnp.sum(lax.all_to_all(copies, axes, 0, 0, tiled=True), axis=0)]
    unnamed x32 -> x18, local copies, waits for them, and re-layouts: 5.79 us -> 1.91 us
    ppermute x1 -> x2, starting transfers between devices: 4.87 us -> 6.18 us  [later(): return lax.ppermute(x, 'seq', [(i, i + s) for i in range(shards - s)])]
  transfers between devices with their start and end apart: 7 -> 9, of which waited for: 3 -> 5; matrix products, arithmetic and copies ran while one was open for 1% -> 1% of each run, Pallas kernels for 14% -> 25%
where the time goes in v4:
time: 73.4 us; the launch traced here: 72.7 us
  waiting for transfers between devices  24 us (33%)
  Pallas kernels  23.8 us (32%)
  starting transfers between devices  18.6 us (25%)
  local copies, waits for them, and re-layouts  4.01 us (5%)
  between operations  1.54 us (2%)
    pallas_call x4, Pallas kernels, attend(): pl.pallas_call(functools.partial(attend_kernel, g, shards), grid=(1,), in...  21.9 us
    ppermute x2, waiting for transfers between devices, earlier(): return lax.ppermute(x, 'seq', [(i + s, i) for i in range(shards - s)])  11.3 us
    all_to_all x1, waiting for transfers between devices, sum_everywhere(): return jnp.sum(lax.all_to_all(copies, axes, 0, 0, tiled=True), axis=0)  6.24 us
    ppermute x2, starting transfers between devices, later(): return lax.ppermute(x, 'seq', [(i, i + s) for i in range(shards - s)])  6.18 us
    ppermute x4, waiting for transfers between devices, ring(): lax.ppermute(x, 'seq', [(i, (i + s) % shards) for i in range(shards)])  5.52 us
    all_to_all x1, starting transfers between devices, sum_everywhere(): return jnp.sum(lax.all_to_all(copies, axes, 0, 0, tiled=True), axis=0)  5.31 us
    ppermute x4, starting transfers between devices, ring(): lax.ppermute(x, 'seq', [(i, (i + s) % shards) for i in range(shards)])  4.56 us
    ppermute x2, starting transfers between devices, earlier(): return lax.ppermute(x, 'seq', [(i + s, i) for i in range(shards - s)])  2.57 us
  transfers between devices with their start and end apart: 9, of which 5 were waited for; matrix products, arithmetic and copies ran while one was open for 1% of the time, Pallas kernels for 25%

profile of v4, /device:TPU:0, one launch (start us, length us, event | category | flops | bytes accessed | tf_op | source)
XLA Modules:
  0.0 72.7 jit_solution(12972077239031903215)
XLA Ops:
  0.6 4.9 %collective-permute-start.1 = (bf16[128,512]{1,0:T(8,128)(2,1)}, bf16[128,512]{1,0:T(8,128)(2,1)S(1)}, u32[]{:S(2)}, u32[]{:S(2)}) collective-permute-start(bf16[128,512]{1,0:T(8,128)(2,1)} %bitcast.44), channel_id=1, source_target_pairs={{0,1},{2,3},{4,5},{6,7},{8,9},{10,11},{12,13},{14,15},{16,17},{18,... | collective-permute-start | bytes 393224 | tf_op jit(solution)/shard_map/ppermute | solution.py:352
  5.5 1.3 %collective-permute-start.2 = (bf16[128,512]{1,0:T(8,128)(2,1)}, bf16[128,512]{1,0:T(8,128)(2,1)S(1)}, u32[]{:S(2)}, u32[]{:S(2)}) collective-permute-start(bf16[128,512]{1,0:T(8,128)(2,1)} %bitcast.49), channel_id=1, source_target_pairs={{0,1},{2,3},{4,5},{6,7},{8,9},{10,11},{12,13},{14,15},{16,17},{18,... | collective-permute-start | bytes 393224 | tf_op jit(solution)/shard_map/ppermute | solution.py:352
  6.8 0.0 copy-start
  6.8 0.0 copy-start.1
  6.8 1.1 %pack.3 = bf16[1024,128]{1,0:T(8,128)(2,1)S(1)} custom-call(bf16[512,512]{1,0:T(8,128)(2,1)} %bitcast.24, bf16[512,512]{1,0:T(8,128)(2,1)} %bitcast.30), custom_call_target="tpu_custom_call" | custom-call | bytes 524288 | tf_op jit(solution)/shard_map/pack/pallas_call | solution.py:60
  7.9 0.0 copy-start.2
  7.9 0.1 collective-permute-start.3
  8.8 0.1 convert_bitcast_fusion
  8.8 0.5 fusion
  9.4 0.0 copy-done
  9.4 0.0 copy-done.1
  9.4 0.0 copy-start.4
  9.4 0.0 copy-start.5
  9.4 0.0 copy-start.8
  9.4 0.1 pack.2
  9.5 0.0 copy-start.6
  9.5 2.0 %collective-permute-start = (bf16[1024,128]{1,0:T(8,128)(2,1)S(1)}, bf16[1024,128]{1,0:T(8,128)(2,1)S(1)}, u32[]{:S(2)}, u32[]{:S(2)}) collective-permute-start(bf16[1024,128]{1,0:T(8,128)(2,1)S(1)} %pack.2), channel_id=1, source_target_pairs={{0,1},{1,0},{2,3},{3,2},{4,5},{5,4},{6,7},{7,6},{8,9},{9,8},{10,11... | collective-permute-start | bytes 786440 | tf_op jit(solution)/shard_map/ppermute | solution.py:349
  11.5 0.0 collective-permute-done.1.refs_14_
  11.5 1.0 %collective-permute-done.2.refs_15_ = bf16[128,512]{1,0:T(8,128)(2,1)S(1)} collective-permute-done((bf16[128,512]{1,0:T(8,128)(2,1)}, bf16[128,512]{1,0:T(8,128)(2,1)S(1)}, u32[]{:S(2)}, u32[]{:S(2)}) %collective-permute-start.2) | collective-permute-done | bytes 131104 | tf_op jit(solution)/shard_map/ppermute | solution.py:352
  12.5 5.5 %collective-permute-done.3.refs_13_ = bf16[1024,128]{1,0:T(8,128)(2,1)S(1)} collective-permute-done((bf16[1024,128]{1,0:T(8,128)(2,1)S(1)}, bf16[1024,128]{1,0:T(8,128)(2,1)S(1)}, u32[]{:S(2)}, u32[]{:S(2)}) %collective-permute-start.3) | collective-permute-done | bytes 262176 | tf_op jit(solution)/shard_map/ppermute | solution.py:349
  18.0 0.0 copy-start.7
  18.0 0.0 copy-done.2
  18.0 0.0 copy-done.4
  18.0 0.0 copy-done.5
  18.0 0.0 copy-done.8
  18.1 0.0 copy-done.6
  18.1 0.6 copy-done.7
  18.7 0.0 copy-start.3
  18.7 1.2 %copy-done.3 = bf16[1,128,4096]{2,1,0:T(8,128)(2,1)S(1)} copy-done((bf16[1,128,4096]{2,1,0:T(8,128)(2,1)S(1)}, bf16[1,128,4096]{2,1,0:T(8,128)(2,1)}, u32[]{:S(2)}) %copy-start.3) | copy-done | bytes 1048600
  19.9 5.5 %attend.4 = (bf16[128,4096]{1,0:T(8,128)(2,1)}, bf16[128,4096]{1,0:T(8,128)(2,1)}, f32[40,128]{1,0:T(8,128)S(1)}, f32[2,128,128]{2,1,0:T(8,128)S(1)}, bf16[2,128...) custom-call(s32[1]{0:T(128)} %copy.33.refs_0_, s32[1]{0:T(128)} %bitcast.refs_1_, bf16[128,4096]{1,0:T(8,128)(2,1)S(1)} %bitcast.36, ...), custom_call_target="tpu_custom_call" | custom-call | flops 1476395008 | bytes 2359296 | tf_op jit(solution)/shard_map/attend/pallas_call | solution.py:288
  25.4 2.5 %collective-permute-start.5 = (bf16[1024,128]{1,0:T(8,128)(2,1)S(1)}, bf16[1024,128]{1,0:T(8,128)(2,1)S(1)}, u32[]{:S(2)}, u32[]{:S(2)}) collective-permute-start(bf16[1024,128]{1,0:T(8,128)(2,1)S(1)} %get-tuple-element.38), channel_id=1, source_target_pairs={{0,1},{1,0},{2,3},{3,2},{4,5},{5,4},{6,7},{7,6},{8,9},{9,8},{10,11... | collective-permute-start | bytes 786440 | tf_op jit(solution)/shard_map/ppermute | solution.py:349
  27.9 0.0 collective-permute-done.refs_13_
  27.9 5.4 %attend.5 = (bf16[128,4096]{1,0:T(8,128)(2,1)}, bf16[128,4096]{1,0:T(8,128)(2,1)}, f32[40,128]{1,0:T(8,128)S(1)}, f32[2,128,128]{2,1,0:T(8,128)S(1)}, bf16[4,128...) custom-call(s32[1]{0:T(128)} %copy.33.refs_0_, ...), custom_call_target="tpu_custom_call", output_to_operand_aliasing={{0}: (18, {}), {1}: (19, {})} | custom-call | flops 1476395008 | bytes 2359296 | tf_op jit(solution)/shard_map/attend/pallas_call | solution.py:288
  33.3 0.0 collective-permute-start.4
  33.3 1.3 %collective-permute-start.6 = (bf16[4,128,128]{2,1,0:T(8,128)(2,1)S(1)}, bf16[4,128,128]{2,1,0:T(8,128)(2,1)S(1)}, u32[]{:S(2)}, u32[]{:S(2)}) collective-permute-start(bf16[4,128,128]{2,1,0:T(8,128)(2,1)S(1)} %get-tuple-element.46), channel_id=1, source_target_pairs={{1,0},{3,2},{5,4},{7,6},{9,8},{11,10},{13,12},{15,14},{17,16},{19,... | collective-permute-start | bytes 393224 | tf_op jit(solution)/shard_map/ppermute | solution.py:355
  34.6 0.0 collective-permute-done.5.refs_13_
  34.6 5.5 %attend.6 = (bf16[128,4096]{1,0:T(8,128)(2,1)}, bf16[128,4096]{1,0:T(8,128)(2,1)}, f32[40,128]{1,0:T(8,128)S(1)}, f32[2,128,128]{2,1,0:T(8,128)S(1)}, bf16[2,128,128]{2,1,0:T(8,128)(2,1)S(1)}) custom-call(s32[1]{0:T(128)} %copy.33.refs_0_, s32[1]{0:T(128)} %bitcast.refs_1_, ...), custom_call_target="tpu_custom_call", output_to_operand_aliasing={{0}: (17, {}), {1}: (18, {})} | custom-call | flops 1476395008 | bytes 2359296 | tf_op jit(solution)/shard_map/attend/pallas_call | solution.py:288
  40.1 1.7 %collective-permute-done.6.refs_20_ = bf16[4,128,128]{2,1,0:T(8,128)(2,1)S(1)} collective-permute-done((bf16[4,128,128]{2,1,0:T(8,128)(2,1)S(1)}, bf16[4,128,128]{2,1,0:T(8,128)(2,1)S(1)}, u32[]{:S(2)}, u32[]{:S(2)}) %collective-permute-start.6) | collective-permute-done | bytes 131104 | tf_op jit(solution)/shard_map/ppermute | solution.py:355
  41.8 0.0 collective-permute-done.4.refs_13_
  41.8 5.6 %attend.7 = (bf16[128,4096]{1,0:T(8,128)(2,1)}, bf16[128,4096]{1,0:T(8,128)(2,1)}, f32[40,128]{1,0:T(8,128)S(1)}, f32[2,128,128]{2,1,0:T(8,128)S(1)}, bf16[4,128...) custom-call(s32[1]{0:T(128)} %copy.33.refs_0_, ...), custom_call_target="tpu_custom_call", output_to_operand_aliasing={{0}: (21, {}), {1}: (22, {})} | custom-call | flops 1476395008 | bytes 2359296 | tf_op jit(solution)/shard_map/attend/pallas_call | solution.py:288
  47.4 0.9 %broadcast_in_dim.37 = f32[32,40,128]{2,1,0:T(8,128)} broadcast(f32[40,128]{1,0:T(8,128)S(1)} %get-tuple-element.58), dimensions={1,2} | broadcast | bytes 675840 | tf_op jit(solution)/shard_map/broadcast_in_dim | solution.py:338
  48.3 5.3 %all-to-all-start = ((f32[32,40,128]{2,1,0:T(8,128)}), f32[32,40,128]{2,1,0:T(8,128)S(1)}, u32[]{:S(2)}, u32[]{:S(2)}) async-start(f32[32,40,128]{2,1,0:T(8,128)} %broadcast_in_dim.37), calls=%async_computation | async-start | bytes 1310720 | tf_op jit(solution)/shard_map/all_to_all | solution.py:339
  53.6 1.3 %collective-permute-start.7 = (bf16[4,128,128]{2,1,0:T(8,128)(2,1)S(1)}, bf16[4,128,128]{2,1,0:T(8,128)(2,1)S(1)}, u32[]{:S(2)}, u32[]{:S(2)}) collective-permute-start(bf16[4,128,128]{2,1,0:T(8,128)(2,1)S(1)} %get-tuple-element.53), channel_id=1, source_target_pairs={{1,0},{3,2},{5,4},{7,6},{9,8},{11,10},{13,12},{15,14},{17,16},{19,... | collective-permute-start | bytes 393224 | tf_op jit(solution)/shard_map/ppermute | solution.py:355
  54.9 9.5 %collective-permute-done.7.refs_4_ = bf16[4,128,128]{2,1,0:T(8,128)(2,1)S(1)} collective-permute-done((bf16[4,128,128]{2,1,0:T(8,128)(2,1)S(1)}, bf16[4,128,128]{2,1,0:T(8,128)(2,1)S(1)}, u32[]{:S(2)}, u32[]{:S(2)}) %collective-permute-start.7) | collective-permute-done | bytes 131104 | tf_op jit(solution)/shard_map/ppermute | solution.py:355
  64.5 0.7 %finish.1 = (bf16[128,512]{1,0:T(8,128)(2,1)}, bf16[128,512]{1,0:T(8,128)(2,1)}) custom-call(f32[256,128]{1,0:T(8,128)S(1)} %get-tuple-element.62.rest_0_.refs_5_.refs_0_, f32[256,128]{1,0:T(8,128)S(1)} %get-tuple-element.61.refs_6_.refs_1_, f32[2,128,128]{2,1,0:T(8,128)S(1)} %get-tuple-element.51.refs_2_, ...), custom_call_target="tpu_custom_call", output_to_operand_aliasing={{0}: (5, {}), {1}: (6, {})} | custom-call | bytes 524288 | tf_op jit(solution)/shard_map/finish/pallas_call | solution.py:323
  65.2 6.2 %all-to-all-done = f32[32,40,128]{2,1,0:T(8,128)S(1)} async-done(((f32[32,40,128]{2,1,0:T(8,128)}), f32[32,40,128]{2,1,0:T(8,128)S(1)}, u32[]{:S(2)}, u32[]{:S(2)}) %all-to-all-start) | async-done | bytes 655392 | tf_op jit(solution)/shard_map/all_to_all | solution.py:339
  71.4 0.1 reduce_sum.9
  71.5 0.6 slice_bitcast_fusion.1
  72.1 0.6 slice_bitcast_fusion
  (2 shorter events, 0.0 us)
Async XLA Ops:
  0.6 10.9 %collective-permute-start.1 = (bf16[128,512]{1,0:T(8,128)(2,1)}, bf16[128,512]{1,0:T(8,128)(2,1)S(1)}, u32[]{:S(2)}, u32[]{:S(2)}) collective-permute-start(bf16[128,512]{1,0:T(8,128)(2,1)} %bitcast.44), channel_id=1, source_target_pairs={{0,1},{2,3},{4,5},{6,7},{8,9},{10,11},{12,13},{14,15},{16,17},{18,... | collective-permute-start | bytes 393224 | tf_op jit(solution)/shard_map/ppermute | solution.py:352
  5.5 7.0 %collective-permute-start.2 = (bf16[128,512]{1,0:T(8,128)(2,1)}, bf16[128,512]{1,0:T(8,128)(2,1)S(1)}, u32[]{:S(2)}, u32[]{:S(2)}) collective-permute-start(bf16[128,512]{1,0:T(8,128)(2,1)} %bitcast.49), channel_id=1, source_target_pairs={{0,1},{2,3},{4,5},{6,7},{8,9},{10,11},{12,13},{14,15},{16,17},{18,... | collective-permute-start | bytes 393224 | tf_op jit(solution)/shard_map/ppermute | solution.py:352
  6.8 2.6 %copy-start = (bf16[1,512,512]{2,1,0:T(8,128)(2,1)S(1)}, bf16[1,512,512]{2,1,0:T(8,128)(2,1)}, u32[]{:S(2)}) copy-start(bf16[1,512,512]{2,1,0:T(8,128)(2,1)} %param.13) | copy-start | bytes 1572868
  6.8 2.6 %copy-start.1 = (bf16[1,512,512]{2,1,0:T(8,128)(2,1)S(1)}, bf16[1,512,512]{2,1,0:T(8,128)(2,1)}, u32[]{:S(2)}) copy-start(bf16[1,512,512]{2,1,0:T(8,128)(2,1)} %param.14) | copy-start | bytes 1572868
  7.9 10.1 %copy-start.2 = (bf16[1,128,4096]{2,1,0:T(8,128)(2,1)S(1)}, bf16[1,128,4096]{2,1,0:T(8,128)(2,1)}, u32[]{:S(2)}) copy-start(bf16[1,128,4096]{2,1,0:T(8,128)(2,1)} %param.10) | copy-start | bytes 3145732
  7.9 10.1 %collective-permute-start.3 = (bf16[1024,128]{1,0:T(8,128)(2,1)S(1)}, bf16[1024,128]{1,0:T(8,128)(2,1)S(1)}, u32[]{:S(2)}, u32[]{:S(2)}) collective-permute-start(bf16[1024,128]{1,0:T(8,128)(2,1)S(1)} %pack.3), channel_id=1, source_target_pairs={{0,1},{1,0},{2,3},{3,2},{4,5},{5,4},{6,7},{7,6},{8,9},{9,8},{10,11... | collective-permute-start | bytes 786440 | tf_op jit(solution)/shard_map/ppermute | solution.py:349
  9.4 8.6 %copy-start.4 = (bf16[1,128,512]{2,1,0:T(8,128)(2,1)S(1)}, bf16[1,128,512]{2,1,0:T(8,128)(2,1)}, u32[]{:S(2)}) copy-start(bf16[1,128,512]{2,1,0:T(8,128)(2,1)} %param.11) | copy-start | bytes 393220
  9.4 8.6 %copy-start.5 = (bf16[1,128,512]{2,1,0:T(8,128)(2,1)S(1)}, bf16[1,128,512]{2,1,0:T(8,128)(2,1)}, u32[]{:S(2)}) copy-start(bf16[1,128,512]{2,1,0:T(8,128)(2,1)} %param.12) | copy-start | bytes 393220
  9.4 8.6 %copy-start.8 = (bf16[512]{0:T(512)(128)(2,1)S(1)}, bf16[512]{0:T(512)(128)(2,1)}, u32[]{:S(2)}) copy-start(bf16[512]{0:T(512)(128)(2,1)} %param.17) | copy-start | bytes 3076
  9.5 8.5 %copy-start.6 = (bf16[4096]{0:T(1024)(128)(2,1)S(1)}, bf16[4096]{0:T(1024)(128)(2,1)}, u32[]{:S(2)}) copy-start(bf16[4096]{0:T(1024)(128)(2,1)} %param.15) | copy-start | bytes 24580
  9.5 18.4 %collective-permute-start = (bf16[1024,128]{1,0:T(8,128)(2,1)S(1)}, bf16[1024,128]{1,0:T(8,128)(2,1)S(1)}, u32[]{:S(2)}, u32[]{:S(2)}) collective-permute-start(bf16[1024,128]{1,0:T(8,128)(2,1)S(1)} %pack.2), channel_id=1, source_target_pairs={{0,1},{1,0},{2,3},{3,2},{4,5},{5,4},{6,7},{7,6},{8,9},{9,8},{10,11... | collective-permute-start | bytes 786440 | tf_op jit(solution)/shard_map/ppermute | solution.py:349
  18.0 0.7 copy-start.7
  18.7 1.2 %copy-start.3 = (bf16[1,128,4096]{2,1,0:T(8,128)(2,1)S(1)}, bf16[1,128,4096]{2,1,0:T(8,128)(2,1)}, u32[]{:S(2)}) copy-start(bf16[1,128,4096]{2,1,0:T(8,128)(2,1)} %param.19) | copy-start | bytes 3145732
  25.4 9.2 %collective-permute-start.5 = (bf16[1024,128]{1,0:T(8,128)(2,1)S(1)}, bf16[1024,128]{1,0:T(8,128)(2,1)S(1)}, u32[]{:S(2)}, u32[]{:S(2)}) collective-permute-start(bf16[1024,128]{1,0:T(8,128)(2,1)S(1)} %get-tuple-element.38), channel_id=1, source_target_pairs={{0,1},{1,0},{2,3},{3,2},{4,5},{5,4},{6,7},{7,6},{8,9},{9,8},{10,11... | collective-permute-start | bytes 786440 | tf_op jit(solution)/shard_map/ppermute | solution.py:349
  33.3 8.6 %collective-permute-start.4 = (bf16[1024,128]{1,0:T(8,128)(2,1)S(1)}, bf16[1024,128]{1,0:T(8,128)(2,1)S(1)}, u32[]{:S(2)}, u32[]{:S(2)}) collective-permute-start(bf16[1024,128]{1,0:T(8,128)(2,1)S(1)} %get-tuple-element.37), channel_id=1, source_target_pairs={{0,1},{1,0},{2,3},{3,2},{4,5},{5,4},{6,7},{7,6},{8,9},{9,8},{10,11... | collective-permute-start | bytes 786440 | tf_op jit(solution)/shard_map/ppermute | solution.py:349
  33.3 8.5 %collective-permute-start.6 = (bf16[4,128,128]{2,1,0:T(8,128)(2,1)S(1)}, bf16[4,128,128]{2,1,0:T(8,128)(2,1)S(1)}, u32[]{:S(2)}, u32[]{:S(2)}) collective-permute-start(bf16[4,128,128]{2,1,0:T(8,128)(2,1)S(1)} %get-tuple-element.46), channel_id=1, source_target_pairs={{1,0},{3,2},{5,4},{7,6},{9,8},{11,10},{13,12},{15,14},{17,16},{19,... | collective-permute-start | bytes 393224 | tf_op jit(solution)/shard_map/ppermute | solution.py:355
  48.3 23.1 %all-to-all-start = ((f32[32,40,128]{2,1,0:T(8,128)}), f32[32,40,128]{2,1,0:T(8,128)S(1)}, u32[]{:S(2)}, u32[]{:S(2)}) async-start(f32[32,40,128]{2,1,0:T(8,128)} %broadcast_in_dim.37), calls=%async_computation | async-start | bytes 1310720 | tf_op jit(solution)/shard_map/all_to_all | solution.py:339
  53.6 10.8 %collective-permute-start.7 = (bf16[4,128,128]{2,1,0:T(8,128)(2,1)S(1)}, bf16[4,128,128]{2,1,0:T(8,128)(2,1)S(1)}, u32[]{:S(2)}, u32[]{:S(2)}) collective-permute-start(bf16[4,128,128]{2,1,0:T(8,128)(2,1)S(1)} %get-tuple-element.53), channel_id=1, source_target_pairs={{1,0},{3,2},{5,4},{7,6},{9,8},{11,10},{13,12},{15,14},{17,16},{19,... | collective-permute-start | bytes 393224 | tf_op jit(solution)/shard_map/ppermute | solution.py:355

commit v5 on v4

--- a/solution.py
+++ b/solution.py
@@ -1,4 +1,5 @@
 import functools
+import itertools
 import math
 
 import jax
@@ -86,6 +87,76 @@
         gv_ref[:, cols] = dv.astype(B16)
 
 
+def prep_kernel(
+    tokens, q_ref, do_ref, bq_ref, bk_ref, bv_ref, cos_ref, sin_ref, ck_ref, cv_ref,
+    qs_ref, dos_ref, dot_ref, bias_ref, cos_t_ref, sin_t_ref, pack_ref,
+):
+    g = pl.program_id(0)
+    cosine, sine = cos_ref[pl.ds(0, tokens), :], sin_ref[pl.ds(0, tokens), :]
+    bias_q = bq_ref[...].astype(F32)
+
+    @pl.when(g == 0)
+    def _():
+        bias_ref[pl.ds(0, KV), :] = bk_ref[...].astype(F32)
+        bias_ref[pl.ds(KV, KV), :] = bv_ref[...].astype(F32)
+        cos_t_ref[...] = cosine.T
+        sin_t_ref[...] = sine.T
+        copy_chunk(1, ck_ref, cv_ref, pack_ref)
+
+    for h in range(GROUP):
+        cols = pl.ds(h * HD, HD)
+        rows = pl.ds(pl.multiple_of((g * GROUP + h) * tokens, tokens), tokens)
+        x = q_ref[:, cols].astype(F32) + bias_q[h:h + 1]
+        qs_ref[rows, :] = (x * cosine + turn(x) * sine).astype(B16)
+        do = do_ref[:, cols]
+        dos_ref[rows, :] = do
+        chain, part = h // HEADS, h % HEADS
+        place = pl.ds(pl.multiple_of((g * (GROUP // HEADS) + chain) * HD, HD), HD)
+        dot_ref[place, pl.ds(part * tokens, tokens)] = do.T
+
+
+def prep(q, do, bq, bk, bv, cosine, sine, ck, cv):
+    tokens, slots = q.shape[0], ck.shape[0]
+    vmem = pl.BlockSpec(memory_space=pltpu.VMEM)
+    wide = pl.BlockSpec((tokens, GROUP * HD), lambda i: (0, i))
+    out_shape = [
+        pltpu.VMEM((HQ * tokens, HD), B16),
+        pltpu.VMEM((HQ * tokens, HD), B16),
+        pltpu.VMEM((HQ // HEADS * HD, HEADS * tokens), B16),
+        pltpu.VMEM((2 * KV, HD), F32),
+        pltpu.VMEM((HD, tokens), F32),
+        pltpu.VMEM((HD, tokens), F32),
+        pltpu.VMEM((2 * slots, HD), B16),
+    ]
+    return pl.pallas_call(
+        functools.partial(prep_kernel, tokens),
+        grid=(KV,),
+        in_specs=[
+            wide, wide, pl.BlockSpec((GROUP, HD), lambda i: (i, 0)),
+            whole((KV, HD)), whole((KV, HD)), vmem, vmem, vmem, vmem,
+        ],
+        out_specs=[vmem] * len(out_shape),
+        out_shape=out_shape,
+        compiler_params=params(),
+        cost_estimate=pl.CostEstimate(
+            flops=4 * tokens * HQ * HD, bytes_accessed=12 * tokens * HQ * HD, transcendentals=0
+        ),
+        name="prep",
+    )(q, do, bq, bk, bv, cosine, sine, ck, cv)
+
+
+def alternate(first, second):
+    pieces = [iter(first), iter(second)]
+    while pieces:
+        for piece in list(pieces):
+            if next(piece, pieces) is pieces:
+                pieces.remove(piece)
+
+
+def fold(x, op):
+    return op(x.reshape(x.shape[0] // 8, 8, x.shape[1]), axis=0)
+
+
 def attend_kernel(g, shards, *refs):
     refs = list(refs)
 
@@ -94,8 +165,8 @@
         del refs[:count]
         return taken
 
-    (first_ref, rank_ref, q_ref, do_ref, bq_ref, cos_ref, sin_ref,
-     ck_ref, cv_ref, kp_ref, vp_ref, bk_ref, bv_ref) = take(13)
+    (first_ref, rank_ref, qs_ref, dos_ref, dot_ref, bias_ref, cos_t_ref, sin_t_ref,
+     cos_ref, sin_ref, ck_ref, cv_ref, kp_ref, vp_ref) = take(14)
     far = take(shards - 1)
     far_k = take(shards - 1)
     far_v = take(shards - 1)
@@ -109,11 +180,13 @@
     send = take(shards - 1)
     pack_ref = take(1)[0] if g + 2 < KV else None
     gk_ref, gv_ref = take(2) if g == KV - 1 else (None, None)
-    keys, values, keys_t, values_t, bias, dkt, dvt = refs
-    tokens = q_ref.shape[0]
+    keys, values, keys_t, values_t, dk_acc, dv_acc = take(6)
+    chains = [take(3), take(3)]
+    tokens = kp_ref.shape[0]
     slots = ck_ref.shape[0]
     prefix = shards * slots
     slab = shards * tokens
+    total = prefix + slab
     first = first_ref[0]
     rank = rank_ref[0]
     mine = pl.ds(g * HD, HD)
@@ -125,105 +198,130 @@
     for s in range(1, shards):
         keys[pl.ds(s * slots, slots)] = far[s - 1][pl.ds(0, slots)]
         values[pl.ds(s * slots, slots)] = far[s - 1][pl.ds(slots, slots)]
-    bias_k = bk_ref[...].astype(F32)[g:g + 1]
-    bias_v = bv_ref[...].astype(F32)[g:g + 1]
     for s in range(shards):
         rows = pl.ds(s * tokens, tokens)
         kp, vp = (kp_ref, vp_ref) if s == 0 else (far_k[s - 1], far_v[s - 1])
-        k = kp[:, mine].astype(F32) + bias_k
+        k = kp[:, mine].astype(F32) + bias_ref[g:g + 1, :]
         k = k * cos_ref[rows, :] + turn(k) * sin_ref[rows, :]
-        v = vp[:, mine].astype(F32) + bias_v
+        v = vp[:, mine].astype(F32) + bias_ref[KV + g:KV + g + 1, :]
         place = pl.ds(prefix + s * tokens, tokens)
         keys[place] = k.astype(B16)
         values[place] = v.astype(B16)
     keys_t[...] = keys[...].T
     values_t[...] = values[...].T
-    bias[...] = bq_ref[...].astype(F32)[g * GROUP:(g + 1) * GROUP]
     sums_ref[...] = jnp.zeros_like(sums_ref) if old_sums_ref is None else old_sums_ref[...]
-    dkt[...] = jnp.zeros_like(dkt)
-    dvt[...] = jnp.zeros_like(dvt)
-
-    rows = HEADS * tokens
+    dk_acc[...] = jnp.zeros_like(dk_acc)
+    dv_acc[...] = jnp.zeros_like(dv_acc)
+
+    width = HEADS * tokens
     scale = HD ** -0.5
-
-    def scores(head):
-        cosine = cos_ref[pl.ds(0, tokens), :]
-        sine = sin_ref[pl.ds(0, tokens), :]
-        queries, cots = [], []
-        for h in range(HEADS):
-            cols = pl.ds(pl.multiple_of((g * GROUP + head + h) * HD, HD), HD)
-            x = q_ref[:, cols].astype(F32) + bias[pl.ds(head + h, 1), :]
-            x = x * cosine + turn(x) * sine
-            queries.append(x.astype(B16))
-            cots.append(do_ref[:, cols])
-        q = jnp.concatenate(queries, axis=0)
-        do = jnp.concatenate(cots, axis=0)
-        s = dot(q, keys_t[...], NN)
-        col = lax.broadcasted_iota(jnp.int32, (1, slots), 1)
-        parts = []
-        for j in range(shards):
-            seen = col < first - lax.rem(rank - j + shards, shards) * slots
-            parts.append(jnp.where(seen, s[:, j * slots:(j + 1) * slots], NEG))
-        token = lax.broadcasted_iota(jnp.int32, (rows, tokens), 0) & (tokens - 1)
-        causal = lax.broadcasted_iota(jnp.int32, (rows, tokens), 1) <= token
-        parts.append(jnp.where(causal, s[:, prefix:prefix + tokens], NEG))
-        for j in range(1, shards):
-            part = s[:, prefix + j * tokens:prefix + (j + 1) * tokens]
-            parts.append(jnp.where(rank >= j, part, NEG))
-        return q, do, jnp.concatenate(parts, axis=1)
-
-    def softmax(s):
-        top = jnp.max(s, axis=1, keepdims=True)
-        e = jnp.exp2((s - top) * (scale * math.log2(math.e)))
-        return e * (1.0 / jnp.sum(e, axis=1, keepdims=True))
-
-    def weigh(pb, do):
-        o = dot(pb, values[...], NN).astype(B16)
-        return o, jnp.sum(do.astype(F32) * o.astype(F32), axis=1, keepdims=True)
-
-    def store(head, o, dq):
-        cosine = cos_ref[pl.ds(0, tokens), :]
-        sine = sin_ref[pl.ds(0, tokens), :]
-        for h in range(HEADS):
-            cols = pl.ds(pl.multiple_of((head + h) * HD, HD), HD)
-            part = slice(h * tokens, (h + 1) * tokens)
-            out_ref[:, cols] = o[part]
-            x = turn_back(dq[part], cosine, sine)
-            gq_ref[:, cols] = x.astype(B16)
-            sums_ref[pl.ds(g * GROUP + head + h, 1), :] = jnp.sum(x, axis=0, keepdims=True)
-
-    def query_grad(ds):
-        return (dot(ds, keys[...], NN) * scale).astype(B16).astype(F32)
+    blocks = range(0, total, tokens)
+    tile = 2 * tokens
+    tiles = range(0, total, tile)
+
+    def allowed(start, s):
+        row = lax.broadcasted_iota(jnp.int32, s.shape, 0)
+        if start < prefix:
+            owner = lax.rem(rank - start // slots + shards, shards)
+            return row < first - owner * slots - start % slots
+        if start < prefix + tokens:
+            return row <= (lax.broadcasted_iota(jnp.int32, s.shape, 1) & (tokens - 1))
+        return row < jnp.where(rank >= (start - prefix) // tokens, tokens, 0)
+
+    class Chain:
+        def __init__(self, index, scratch):
+            self.index = index
+            self.s, self.pb, self.ds = scratch
+            self.rows = pl.ds(pl.multiple_of(index * width, width), width)
+            self.top = jnp.full((8, width), NEG, F32)
+
+        def scores(self):
+            q = qs_ref[self.rows, :]
+            for start in tiles:
+                s = dot(keys[pl.ds(start, tile), :], q, NT)
+                for i in range(0, tile, tokens):
+                    part = s[i:i + tokens]
+                    part = jnp.where(allowed(start + i, part), part, NEG)
+                    self.s[pl.ds(start + i, tokens), :] = part
+                    self.top = jnp.maximum(self.top, fold(part, jnp.max))
+                yield
+
+        def softmax(self):
+            top = jnp.max(self.top, axis=0, keepdims=True)
+            total_e = jnp.zeros((8, width), F32)
+            for start in blocks:
+                rows = pl.ds(start, tokens)
+                e = jnp.exp2((self.s[rows, :] - top) * (scale * math.log2(math.e)))
+                self.s[rows, :] = e
+                total_e = total_e + fold(e, jnp.sum)
+                yield
+            self.inverse = 1.0 / jnp.sum(total_e, axis=0, keepdims=True)
+            for start in blocks:
+                rows = pl.ds(start, tokens)
+                self.pb[rows, :] = (self.s[rows, :] * self.inverse).astype(B16)
+                yield
+
+        def heads(self):
+            for i in range(HEADS):
+                head = self.index * HEADS + i
+                yield (
+                    slice(i * tokens, (i + 1) * tokens),
+                    pl.ds(pl.multiple_of((head - g * GROUP) * HD, HD), HD),
+                    head,
+                )
+
+        def output(self):
+            o = dot(values_t[...], self.pb[...], NN).astype(B16)
+            place = pl.ds(pl.multiple_of(self.index * HD, HD), HD)
+            do = dot_ref[place, :].astype(F32)
+            self.delta = jnp.sum(do * o.astype(F32), axis=0, keepdims=True)
+            yield
+            for part, cols, _ in self.heads():
+                out_ref[:, cols] = o[:, part].T
+            yield
+
+        def dscore(self):
+            do = dos_ref[self.rows, :]
+            for start in tiles:
+                rows = pl.ds(start, tile)
+                dp = dot(values[rows, :], do, NT)
+                p = self.s[rows, :] * self.inverse
+                self.ds[rows, :] = (p * (dp - self.delta)).astype(B16)
+                yield
+
+        def grads(self):
+            last = pl.ds(prefix, slab)
+            dk_acc[...] += dot(self.ds[last, :], qs_ref[self.rows, :], NN)
+            dv_acc[...] += dot(self.pb[last, :], dos_ref[self.rows, :], NN)
+            yield
+            dq = (dot(keys_t[...], self.ds[...], NN) * scale).astype(B16).astype(F32)
+            yield
+            for part, cols, head in self.heads():
+                x = dq[:, part]
+                other = jnp.concatenate([x[HD // 2:], x[:HD // 2]], axis=0)
+                x = (x * cos_t_ref[...] - other * sin_t_ref[...]).T
+                gq_ref[:, cols] = x.astype(B16)
+                sums_ref[pl.ds(head, 1), :] = jnp.sum(x, axis=0, keepdims=True)
+            yield
 
     def pair(i, carry):
-        head_a = i * 2 * HEADS
-        head_b = head_a + HEADS
-        q_a, do_a, s_a = scores(head_a)
-        q_b, do_b, s_b = scores(head_b)
-        dp_a = dot(do_a, values_t[...], NN)
-        p_a = softmax(s_a)
-        pb_a = p_a.astype(B16)
-        dp_b = dot(do_b, values_t[...], NN)
-        o_a, delta_a = weigh(pb_a, do_a)
-        p_b = softmax(s_b)
-        pb_b = p_b.astype(B16)
-        ds_a = (p_a * (dp_a - delta_a)).astype(B16)
-        o_b, delta_b = weigh(pb_b, do_b)
-        dq_a = query_grad(ds_a)
-        dkt[...] += dot(q_a, ds_a[:, prefix:], TN)
-        dvt[...] += dot(do_a, pb_a[:, prefix:], TN)
-        ds_b = (p_b * (dp_b - delta_b)).astype(B16)
-        store(head_a, o_a, dq_a)
-        dq_b = query_grad(ds_b)
-        dkt[...] += dot(q_b, ds_b[:, prefix:], TN)
-        dvt[...] += dot(do_b, pb_b[:, prefix:], TN)
-        store(head_b, o_b, dq_b)
+        index = g * (GROUP // HEADS) + 2 * i
+        a, b = Chain(index, chains[0]), Chain(index + 1, chains[1])
+        for _ in a.scores():
+            pass
+        alternate(b.scores(), a.softmax())
+        alternate(itertools.chain(a.output(), a.dscore()), b.softmax())
+        alternate(b.output(), a.grads())
+        for _ in b.dscore():
+            pass
+        for _ in b.grads():
+            pass
         return carry
 
     lax.fori_loop(0, GROUP // (2 * HEADS), pair, 0)
 
-    dk = dkt[...].T * scale
-    dv = dvt[...].T
+    dk = dk_acc[...] * scale
+    dv = dv_acc[...]
     gk = turn_back(dk, cos_ref[...], sin_ref[...])
     own_ref[0] = dk[:tokens]
     own_ref[1] = dv[:tokens]
@@ -241,10 +339,10 @@
 
 
 def attend(
-    g, shards, first, rank, q, do, bq, cosine, sine, ck, cv, kp, vp, bk, bv, far, far_k, far_v,
+    g, shards, first, rank, prepared, cosine, sine, ck, cv, kp, vp, far, far_k, far_v,
     before, owns, backs,
 ):
-    tokens, slots = q.shape[0], ck.shape[0]
+    tokens, slots = kp.shape[0], ck.shape[0]
     slab = shards * tokens
     total = slab + shards * slots
     last = g == KV - 1
@@ -255,7 +353,7 @@
     half = pl.BlockSpec((tokens, 2 * HD), lambda i: (0, 0))
 
     args = [first, rank]
-    placed = [q, do, bq, cosine, sine, ck, cv, kp, vp, bk, bv, *far, *far_k, *far_v]
+    placed = [*prepared, cosine, sine, ck, cv, kp, vp, *far, *far_k, *far_v]
     aliases = {}
     if before is not None:
         out, gq, sums, send = before
@@ -294,8 +392,9 @@
         scratch_shapes=[
             pltpu.VMEM((total, HD), B16), pltpu.VMEM((total, HD), B16),
             pltpu.VMEM((HD, total), B16), pltpu.VMEM((HD, total), B16),
-            pltpu.VMEM((GROUP, HD), F32),
-            pltpu.VMEM((HD, slab), F32), pltpu.VMEM((HD, slab), F32),
+            pltpu.VMEM((slab, HD), F32), pltpu.VMEM((slab, HD), F32),
+        ] + [
+            pltpu.VMEM((total, HEADS * tokens), kind) for kind in (F32, B16, B16) * 2
         ],
         input_output_aliases=aliases,
         compiler_params=params(),
@@ -313,19 +412,28 @@
 
 def finish_kernel(shards, *refs):
     owns, backs = refs[2:4], refs[4:4 + shards - 1]
-    finish_heads(2, shards, refs[:2], owns, backs, *refs[-2:])
-
-
-def finish(shards, cosine, sine, owns, backs, gk, gv):
+    sums, other = refs[4 + shards - 1:4 + shards + 1]
+    gk_ref, gv_ref, *parts = refs[-5:]
+    finish_heads(2, shards, refs[:2], owns, backs, gk_ref, gv_ref)
+    start = 0
+    for part in parts:
+        rows = pl.ds(start, part.shape[0])
+        part[...] = sums[rows, :] + other[rows, :]
+        start += part.shape[0]
+
+
+def finish(shards, cosine, sine, owns, backs, sums, other, gk, gv):
     tokens = gk.shape[0]
     vmem = pl.BlockSpec(memory_space=pltpu.VMEM)
-    args = [cosine, sine, *owns, *backs]
+    args = [cosine, sine, *owns, *backs, sums, other]
+    heads = [(HQ, HD), (KV, HD), (KV, HD)]
     return pl.pallas_call(
         functools.partial(finish_kernel, shards),
         grid=(1,),
         in_specs=[vmem] * len(args) + [pl.BlockSpec(memory_space=pl.ANY)] * 2,
-        out_specs=[pl.BlockSpec((tokens, 2 * HD), lambda i: (0, 1))] * 2,
-        out_shape=[pltpu.HBM(gk.shape, B16)] * 2,
+        out_specs=[pl.BlockSpec((tokens, 2 * HD), lambda i: (0, 1))] * 2
+        + [whole(shape) for shape in heads],
+        out_shape=[pltpu.HBM(gk.shape, B16)] * 2 + [pltpu.HBM(shape, F32) for shape in heads],
         input_output_aliases={len(args): 0, len(args) + 1: 1},
         compiler_params=params(),
         cost_estimate=pl.CostEstimate(flops=0, bytes_accessed=1 << 19, transcendentals=0),
@@ -333,10 +441,21 @@
     )(*args, gk, gv)
 
 
-def sum_everywhere(x, axes):
-    devices = lax.axis_size(axes)
-    copies = jnp.broadcast_to(x[None], (devices,) + x.shape)
-    return jnp.sum(lax.all_to_all(copies, axes, 0, 0, tiled=True), axis=0)
+def exchanges(axis):
+    size = lax.axis_size(axis)
+    step = 1
+    while step < size:
+        yield axis, [(i, i ^ step) for i in range(size)]
+        step *= 2
+
+
+def sum_but_last(x, axes):
+    other = None
+    for axis in axes:
+        for name, perm in exchanges(axis):
+            x = x if other is None else x + other
+            other = lax.ppermute(x, name, perm)
+    return x, other
 
 
 def body(q_proj, k_proj, v_proj, cache_k, cache_v, bias_q, bias_k, bias_v, start, dout):
@@ -371,12 +490,15 @@
     cosine = jnp.cos(angles)
     sine = jnp.sin(angles) * jnp.where(lane < HD // 2, -1.0, 1.0).astype(F32)[None]
 
-    far.append([ring(pack(1, ck, cv, cosine), s) for s in shifts])
+    *prepared, chunk = prep(
+        hbm(q_proj[0]), hbm(dout[0]), hbm(bias_q.reshape(HQ, HD)),
+        hbm(bias_k.reshape(KV, HD)), hbm(bias_v.reshape(KV, HD)), cosine, sine, ck, cv,
+    )
+    far.append([ring(chunk, s) for s in shifts])
     before, owns, backs = None, [], []
     for g in range(KV):
         before, own, more = attend(
-            g, shards, start, rank.reshape(1), q_proj[0], dout[0], bias_q.reshape(HQ, HD),
-            cosine, sine, ck, cv, kp, vp, bias_k.reshape(KV, HD), bias_v.reshape(KV, HD),
+            g, shards, start, rank.reshape(1), prepared, cosine, sine, ck, cv, kp, vp,
             far[g], far_k, far_v, before, owns, backs,
         )
         owns.append(own)
@@ -385,17 +507,9 @@
         if g % 2:
             backs = [earlier(x, s) for s, x in zip(shifts, before[3])]
     out, gq, sums, _ = before
-    gk, gv = finish(shards, cosine, sine, owns[2:], backs, *more)
-    sums = sum_everywhere(sums, ("dp", "seq"))
-    return (
-        out[None],
-        gq[None],
-        gk[None],
-        gv[None],
-        sums[:HQ].reshape(-1),
-        sums[HQ:HQ + KV].reshape(-1),
-        sums[HQ + KV:].reshape(-1),
-    )
+    sums, other = sum_but_last(sums, ("dp", "seq"))
+    gk, gv, *sums = finish(shards, cosine, sine, owns[2:], backs, sums, other, *more)
+    return (out[None], gq[None], gk[None], gv[None], *[x.reshape(-1) for x in sums])
 
 
 def solution(mesh):

time: 73.4 us -> 65.9 us (0.90)
  waiting for transfers between devices: 24 us -> 14.5 us
  local copies, waits for them, and re-layouts: 4.01 us -> 0.02 us
  Pallas kernels: 23.8 us -> 27.3 us
  starting transfers between devices: 18.6 us -> 21.8 us
    ppermute x2, waiting for transfers between devices: 11.3 us -> 1.68 us  [earlier(): return lax.ppermute(x, 'seq', [(i + s, i) for i in range(shards - s)])]
    ppermute x0 -> x5, waiting for transfers between devices: none -> 9.52 us  [sum_but_last(): other = lax.ppermute(x, name, perm)]
    ppermute x0 -> x5, starting transfers between devices: none -> 8.38 us  [sum_but_last(): other = lax.ppermute(x, name, perm)]
    all_to_all x1 -> x0, waiting for transfers between devices: 6.24 us -> none  [sum_everywhere(): return jnp.sum(lax.all_to_all(copies, axes, 0, 0, tiled=True), axis=0)]
    all_to_all x1 -> x0, starting transfers between devices: 5.31 us -> none  [sum_everywhere(): return jnp.sum(lax.all_to_all(copies, axes, 0, 0, tiled=True), axis=0)]
    pallas_call x0 -> x1, Pallas kernels: none -> 3.3 us  [prep(): pl.pallas_call(functools.partial(prep_kernel, tokens), grid=(KV,), in_spe...]
    ppermute x4, waiting for transfers between devices: 5.52 us -> 3.3 us  [ring(): lax.ppermute(x, 'seq', [(i, (i + s) % shards) for i in range(shards)])]
    unnamed x18 -> x8, local copies, waits for them, and re-layouts: 1.91 us -> 0.02 us
  transfers between devices with their start and end apart: 9 -> 13, of which waited for: 5 -> 7; matrix products, arithmetic and copies ran while one was open for 1% -> 1% of each run, Pallas kernels for 25% -> 32%
where the time goes in v5:
time: 65.9 us; the launch traced here: 65.7 us
  Pallas kernels  27.3 us (41%)
  starting transfers between devices  21.8 us (33%)
  waiting for transfers between devices  14.5 us (22%)
  between operations  1.43 us (2%)
    pallas_call x4, Pallas kernels, attend(): pl.pallas_call(functools.partial(attend_kernel, g, shards), grid=(1,), in...  22.2 us
    ppermute x5, waiting for transfers between devices, sum_but_last(): other = lax.ppermute(x, name, perm)  9.52 us
    ppermute x5, starting transfers between devices, sum_but_last(): other = lax.ppermute(x, name, perm)  8.38 us
    ppermute x2, starting transfers between devices, later(): return lax.ppermute(x, 'seq', [(i, i + s) for i in range(shards - s)])  6.18 us
    ppermute x4, starting transfers between devices, ring(): lax.ppermute(x, 'seq', [(i, (i + s) % shards) for i in range(shards)])  4.64 us
    pallas_call x1, Pallas kernels, prep(): pl.pallas_call(functools.partial(prep_kernel, tokens), grid=(KV,), in_spe...  3.3 us
    ppermute x4, waiting for transfers between devices, ring(): lax.ppermute(x, 'seq', [(i, (i + s) % shards) for i in range(shards)])  3.3 us
    ppermute x2, starting transfers between devices, earlier(): return lax.ppermute(x, 'seq', [(i + s, i) for i in range(shards - s)])  2.56 us
  transfers between devices with their start and end apart: 13, of which 7 were waited for; matrix products, arithmetic and copies ran while one was open for 1% of the time, Pallas kernels for 32%

profile of v5, /device:TPU:0, one launch (start us, length us, event | category | flops | bytes accessed | tf_op | source)
XLA Modules:
  0.0 65.7 jit_solution(9055724401250408021)
XLA Ops:
  0.6 4.9 %collective-permute-start.1 = (bf16[128,512]{1,0:T(8,128)(2,1)}, bf16[128,512]{1,0:T(8,128)(2,1)S(1)}, u32[]{:S(2)}, u32[]{:S(2)}) collective-permute-start(bf16[128,512]{1,0:T(8,128)(2,1)} %bitcast.33), channel_id=1, source_target_pairs={{0,1},{2,3},{4,5},{6,7},{8,9},{10,11},{12,13},{14,15},{16,17},{18,... | collective-permute-start | bytes 393224 | tf_op jit(solution)/shard_map/ppermute | solution.py:471
  5.5 1.3 %collective-permute-start.2 = (bf16[128,512]{1,0:T(8,128)(2,1)}, bf16[128,512]{1,0:T(8,128)(2,1)S(1)}, u32[]{:S(2)}, u32[]{:S(2)}) collective-permute-start(bf16[128,512]{1,0:T(8,128)(2,1)} %bitcast.38), channel_id=1, source_target_pairs={{0,1},{2,3},{4,5},{6,7},{8,9},{10,11},{12,13},{14,15},{16,17},{18,... | collective-permute-start | bytes 393224 | tf_op jit(solution)/shard_map/ppermute | solution.py:471
  6.8 0.0 copy-start
  6.8 0.0 copy-start.1
  6.8 1.1 %pack.1 = bf16[1024,128]{1,0:T(8,128)(2,1)S(1)} custom-call(bf16[512,512]{1,0:T(8,128)(2,1)} %bitcast.21, bf16[512,512]{1,0:T(8,128)(2,1)} %bitcast.27), custom_call_target="tpu_custom_call" | custom-call | bytes 524288 | tf_op jit(solution)/shard_map/pack/pallas_call | solution.py:61
  7.9 0.1 collective-permute-start.3
  8.7 0.1 convert_bitcast_fusion
  8.8 0.5 fusion
  9.3 0.0 copy-done
  9.3 0.0 copy-done.1
  9.3 0.0 copy-start.2
  9.3 0.0 copy-start.3
  9.4 3.3 %prep.1 = (bf16[4096,128]{1,0:T(8,128)(2,1)S(1)}, bf16[4096,128]{1,0:T(8,128)(2,1)S(1)}, bf16[2048,256]{1,0:T(8,128)(2,1)S(1)}, f32[8,128]{1,0:T(8,128)S(1)}, f3...) custom-call(bf16[128,4096]{1,0:T(8,128)(2,1)} %bitcast.45, ...), custom_call_target="tpu_custom_call" | custom-call | flops 2097152 | bytes 6291456 | tf_op jit(solution)/shard_map/prep/pallas_call | solution.py:131
  12.7 2.1 %collective-permute-start = (bf16[1024,128]{1,0:T(8,128)(2,1)S(1)}, bf16[1024,128]{1,0:T(8,128)(2,1)S(1)}, u32[]{:S(2)}, u32[]{:S(2)}) collective-permute-start(bf16[1024,128]{1,0:T(8,128)(2,1)S(1)} %get-tuple-element.49), channel_id=1, source_target_pairs={{0,1},{1,0},{2,3},{3,2},{4,5},{5,4},{6,7},{7,6},{8,9},{9,8},{10,11... | collective-permute-start | bytes 786440 | tf_op jit(solution)/shard_map/ppermute | solution.py:468
  14.7 0.0 collective-permute-done.1.refs_15_
  14.7 0.0 collective-permute-done.2.refs_16_
  14.7 3.3 %collective-permute-done.3.refs_14_ = bf16[1024,128]{1,0:T(8,128)(2,1)S(1)} collective-permute-done((bf16[1024,128]{1,0:T(8,128)(2,1)S(1)}, bf16[1024,128]{1,0:T(8,128)(2,1)S(1)}, u32[]{:S(2)}, u32[]{:S(2)}) %collective-permute-start.3) | collective-permute-done | bytes 262176 | tf_op jit(solution)/shard_map/ppermute | solution.py:468
  18.0 0.0 copy-done.2
  18.0 0.0 copy-done.3
  18.0 5.5 %attend.4 = (bf16[128,4096]{1,0:T(8,128)(2,1)}, bf16[128,4096]{1,0:T(8,128)(2,1)}, f32[40,128]{1,0:T(8,128)S(1)}, f32[2,128,128]{2,1,0:T(8,128)S(1)}, bf16[2,128...) custom-call(s32[1]{0:T(128)} %copy.33.refs_0_, s32[1]{0:T(128)} %bitcast.refs_1_, ...), custom_call_target="tpu_custom_call" | custom-call | flops 1476395008 | bytes 2359296 | tf_op jit(solution)/shard_map/attend/pallas_call | solution.py:386
  23.6 2.5 %collective-permute-start.5 = (bf16[1024,128]{1,0:T(8,128)(2,1)S(1)}, bf16[1024,128]{1,0:T(8,128)(2,1)S(1)}, u32[]{:S(2)}, u32[]{:S(2)}) collective-permute-start(bf16[1024,128]{1,0:T(8,128)(2,1)S(1)} %get-tuple-element.55), channel_id=1, source_target_pairs={{0,1},{1,0},{2,3},{3,2},{4,5},{5,4},{6,7},{7,6},{8,9},{9,8},{10,11... | collective-permute-start | bytes 786440 | tf_op jit(solution)/shard_map/ppermute | solution.py:468
  26.1 0.0 collective-permute-done.refs_14_
  26.1 5.6 %attend.5 = (bf16[128,4096]{1,0:T(8,128)(2,1)}, bf16[128,4096]{1,0:T(8,128)(2,1)}, f32[40,128]{1,0:T(8,128)S(1)}, f32[2,128,128]{2,1,0:T(8,128)S(1)}, bf16[4,128...) custom-call(s32[1]{0:T(128)} %copy.33.refs_0_, ...), custom_call_target="tpu_custom_call", output_to_operand_aliasing={{0}: (19, {}), {1}: (20, {})} | custom-call | flops 1476395008 | bytes 2359296 | tf_op jit(solution)/shard_map/attend/pallas_call | solution.py:386
  31.6 0.0 collective-permute-start.4
  31.6 1.3 %collective-permute-start.6 = (bf16[4,128,128]{2,1,0:T(8,128)(2,1)S(1)}, bf16[4,128,128]{2,1,0:T(8,128)(2,1)S(1)}, u32[]{:S(2)}, u32[]{:S(2)}) collective-permute-start(bf16[4,128,128]{2,1,0:T(8,128)(2,1)S(1)} %get-tuple-element.63), channel_id=1, source_target_pairs={{1,0},{3,2},{5,4},{7,6},{9,8},{11,10},{13,12},{15,14},{17,16},{19,... | collective-permute-start | bytes 393224 | tf_op jit(solution)/shard_map/ppermute | solution.py:474
  32.9 0.0 collective-permute-done.5.refs_14_
  32.9 5.6 %attend.6 = (bf16[128,4096]{1,0:T(8,128)(2,1)}, bf16[128,4096]{1,0:T(8,128)(2,1)}, f32[40,128]{1,0:T(8,128)S(1)}, f32[2,128,128]{2,1,0:T(8,128)S(1)}, bf16[2,128,128]{2,1,0:T(8,128)(2,1)S(1)}) custom-call(s32[1]{0:T(128)} %copy.33.refs_0_, s32[1]{0:T(128)} %bitcast.refs_1_, ...), custom_call_target="tpu_custom_call", output_to_operand_aliasing={{0}: (18, {}), {1}: (19, {})} | custom-call | flops 1476395008 | bytes 2359296 | tf_op jit(solution)/shard_map/attend/pallas_call | solution.py:386
  38.5 1.7 %collective-permute-done.6.refs_21_ = bf16[4,128,128]{2,1,0:T(8,128)(2,1)S(1)} collective-permute-done((bf16[4,128,128]{2,1,0:T(8,128)(2,1)S(1)}, bf16[4,128,128]{2,1,0:T(8,128)(2,1)S(1)}, u32[]{:S(2)}, u32[]{:S(2)}) %collective-permute-start.6) | collective-permute-done | bytes 131104 | tf_op jit(solution)/shard_map/ppermute | solution.py:474
  40.2 0.0 collective-permute-done.4.refs_14_
  40.2 5.5 %attend.7 = (bf16[128,4096]{1,0:T(8,128)(2,1)}, bf16[128,4096]{1,0:T(8,128)(2,1)}, f32[40,128]{1,0:T(8,128)S(1)}, f32[2,128,128]{2,1,0:T(8,128)S(1)}, bf16[4,128...) custom-call(s32[1]{0:T(128)} %copy.33.refs_0_, ...), custom_call_target="tpu_custom_call", output_to_operand_aliasing={{0}: (22, {}), {1}: (23, {})} | custom-call | flops 1476395008 | bytes 2359296 | tf_op jit(solution)/shard_map/attend/pallas_call | solution.py:386
  45.7 1.3 %collective-permute-start.7 = (bf16[4,128,128]{2,1,0:T(8,128)(2,1)S(1)}, bf16[4,128,128]{2,1,0:T(8,128)(2,1)S(1)}, u32[]{:S(2)}, u32[]{:S(2)}) collective-permute-start(bf16[4,128,128]{2,1,0:T(8,128)(2,1)S(1)} %get-tuple-element.70), channel_id=1, source_target_pairs={{1,0},{3,2},{5,4},{7,6},{9,8},{11,10},{13,12},{15,14},{17,16},{19,... | collective-permute-start | bytes 393224 | tf_op jit(solution)/shard_map/ppermute | solution.py:474
  47.0 0.1 collective-permute-start.8
  47.1 1.2 %collective-permute-done.8 = f32[40,128]{1,0:T(8,128)S(1)} collective-permute-done((f32[40,128]{1,0:T(8,128)S(1)}, f32[40,128]{1,0:T(8,128)S(1)}, u32[]{:S(2)}, u32[]{:S(2)}) %collective-permute-start.8) | collective-permute-done | bytes 20512 | tf_op jit(solution)/shard_map/ppermute | solution.py:457
  48.2 1.5 %collective-permute-start.9 = (f32[40,128]{1,0:T(8,128)S(1)}, f32[40,128]{1,0:T(8,128)S(1)}, u32[]{:S(2)}, u32[]{:S(2)}) collective-permute-start(f32[40,128]{1,0:T(8,128)S(1)} %add.66), channel_id=1, source_target_pairs={{0,4},{2,6},{4,0},{6,2},{8,12},{10,14},{12,8},{14,10},{16,20},{18,... | collective-permute-start | bytes 61448 | tf_op jit(solution)/shard_map/ppermute | solution.py:457
  49.7 2.3 %collective-permute-done.9 = f32[40,128]{1,0:T(8,128)S(1)} collective-permute-done((f32[40,128]{1,0:T(8,128)S(1)}, f32[40,128]{1,0:T(8,128)S(1)}, u32[]{:S(2)}, u32[]{:S(2)}) %collective-permute-start.9) | collective-permute-done | bytes 20512 | tf_op jit(solution)/shard_map/ppermute | solution.py:457
  52.0 1.6 %collective-permute-start.10 = (f32[40,128]{1,0:T(8,128)S(1)}, f32[40,128]{1,0:T(8,128)S(1)}, u32[]{:S(2)}, u32[]{:S(2)}) collective-permute-start(f32[40,128]{1,0:T(8,128)S(1)} %add.67), channel_id=1, source_target_pairs={{0,8},{2,10},{4,12},{6,14},{8,0},{10,2},{12,4},{14,6},{16,24},{18,... | collective-permute-start | bytes 61448 | tf_op jit(solution)/shard_map/ppermute | solution.py:457
  53.6 2.2 %collective-permute-done.10 = f32[40,128]{1,0:T(8,128)S(1)} collective-permute-done((f32[40,128]{1,0:T(8,128)S(1)}, f32[40,128]{1,0:T(8,128)S(1)}, u32[]{:S(2)}, u32[]{:S(2)}) %collective-permute-start.10) | collective-permute-done | bytes 20512 | tf_op jit(solution)/shard_map/ppermute | solution.py:457
  55.8 2.6 %collective-permute-start.11 = (f32[40,128]{1,0:T(8,128)S(1)}, f32[40,128]{1,0:T(8,128)S(1)}, u32[]{:S(2)}, u32[]{:S(2)}) collective-permute-start(f32[40,128]{1,0:T(8,128)S(1)} %add.68), channel_id=1, source_target_pairs={{0,16},{2,18},{4,20},{6,22},{8,24},{10,26},{12,28},{14,30},{16,0},... | collective-permute-start | bytes 61448 | tf_op jit(solution)/shard_map/ppermute | solution.py:457
  58.4 2.1 %collective-permute-done.11 = f32[40,128]{1,0:T(8,128)S(1)} collective-permute-done((f32[40,128]{1,0:T(8,128)S(1)}, f32[40,128]{1,0:T(8,128)S(1)}, u32[]{:S(2)}, u32[]{:S(2)}) %collective-permute-start.11) | collective-permute-done | bytes 20512 | tf_op jit(solution)/shard_map/ppermute | solution.py:457
  60.5 2.6 %collective-permute-start.12 = (f32[40,128]{1,0:T(8,128)S(1)}, f32[40,128]{1,0:T(8,128)S(1)}, u32[]{:S(2)}, u32[]{:S(2)}) collective-permute-start(f32[40,128]{1,0:T(8,128)S(1)} %add.69.refs_5_), channel_id=1, source_target_pairs={{0,1},{1,0},{2,3},{3,2},{4,5},{5,4},{6,7},{7,6},{8,9},{9,8},{10,11... | collective-permute-start | bytes 61448 | tf_op jit(solution)/shard_map/ppermute | solution.py:457
  63.2 1.8 %collective-permute-done.12.refs_6_ = f32[40,128]{1,0:T(8,128)S(1)} collective-permute-done((f32[40,128]{1,0:T(8,128)S(1)}, f32[40,128]{1,0:T(8,128)S(1)}, u32[]{:S(2)}, u32[]{:S(2)}) %collective-permute-start.12) | collective-permute-done | bytes 20512 | tf_op jit(solution)/shard_map/ppermute | solution.py:457
  64.9 0.0 collective-permute-done.7.refs_4_
  64.9 0.7 %finish.1 = (bf16[128,512]{1,0:T(8,128)(2,1)}, bf16[128,512]{1,0:T(8,128)(2,1)}, f32[32,128]{1,0:T(8,128)}, f32[4,128]{1,0:T(4,128)}, f32[4,128]{1,0:T(4,128)}) custom-call(f32[256,128]{1,0:T(8,128)S(1)} %get-tuple-element.80.cos_ref.refs_8_.refs_0_, ...), custom_call_target="tpu_custom_call", output_to_operand_aliasing={{0}: (7, {}), {1}: (8, {})} | custom-call | bytes 524288 | tf_op jit(solution)/shard_map/finish/pallas_call | solution.py:430
  (6 shorter events, 0.0 us)
Async XLA Ops:
  0.6 14.1 %collective-permute-start.1 = (bf16[128,512]{1,0:T(8,128)(2,1)}, bf16[128,512]{1,0:T(8,128)(2,1)S(1)}, u32[]{:S(2)}, u32[]{:S(2)}) collective-permute-start(bf16[128,512]{1,0:T(8,128)(2,1)} %bitcast.33), channel_id=1, source_target_pairs={{0,1},{2,3},{4,5},{6,7},{8,9},{10,11},{12,13},{14,15},{16,17},{18,... | collective-permute-start | bytes 393224 | tf_op jit(solution)/shard_map/ppermute | solution.py:471
  5.5 9.2 %collective-permute-start.2 = (bf16[128,512]{1,0:T(8,128)(2,1)}, bf16[128,512]{1,0:T(8,128)(2,1)S(1)}, u32[]{:S(2)}, u32[]{:S(2)}) collective-permute-start(bf16[128,512]{1,0:T(8,128)(2,1)} %bitcast.38), channel_id=1, source_target_pairs={{0,1},{2,3},{4,5},{6,7},{8,9},{10,11},{12,13},{14,15},{16,17},{18,... | collective-permute-start | bytes 393224 | tf_op jit(solution)/shard_map/ppermute | solution.py:471
  6.8 2.5 %copy-start = (bf16[1,512,512]{2,1,0:T(8,128)(2,1)S(1)}, bf16[1,512,512]{2,1,0:T(8,128)(2,1)}, u32[]{:S(2)}) copy-start(bf16[1,512,512]{2,1,0:T(8,128)(2,1)} %param.13) | copy-start | bytes 1572868
  6.8 2.5 %copy-start.1 = (bf16[1,512,512]{2,1,0:T(8,128)(2,1)S(1)}, bf16[1,512,512]{2,1,0:T(8,128)(2,1)}, u32[]{:S(2)}) copy-start(bf16[1,512,512]{2,1,0:T(8,128)(2,1)} %param.14) | copy-start | bytes 1572868
  7.9 10.1 %collective-permute-start.3 = (bf16[1024,128]{1,0:T(8,128)(2,1)S(1)}, bf16[1024,128]{1,0:T(8,128)(2,1)S(1)}, u32[]{:S(2)}, u32[]{:S(2)}) collective-permute-start(bf16[1024,128]{1,0:T(8,128)(2,1)S(1)} %pack.1), channel_id=1, source_target_pairs={{0,1},{1,0},{2,3},{3,2},{4,5},{5,4},{6,7},{7,6},{8,9},{9,8},{10,11... | collective-permute-start | bytes 786440 | tf_op jit(solution)/shard_map/ppermute | solution.py:468
  9.3 8.7 %copy-start.2 = (bf16[1,128,512]{2,1,0:T(8,128)(2,1)S(1)}, bf16[1,128,512]{2,1,0:T(8,128)(2,1)}, u32[]{:S(2)}) copy-start(bf16[1,128,512]{2,1,0:T(8,128)(2,1)} %param.11) | copy-start | bytes 393220
  9.3 8.7 %copy-start.3 = (bf16[1,128,512]{2,1,0:T(8,128)(2,1)S(1)}, bf16[1,128,512]{2,1,0:T(8,128)(2,1)}, u32[]{:S(2)}) copy-start(bf16[1,128,512]{2,1,0:T(8,128)(2,1)} %param.12) | copy-start | bytes 393220
  12.7 13.4 %collective-permute-start = (bf16[1024,128]{1,0:T(8,128)(2,1)S(1)}, bf16[1024,128]{1,0:T(8,128)(2,1)S(1)}, u32[]{:S(2)}, u32[]{:S(2)}) collective-permute-start(bf16[1024,128]{1,0:T(8,128)(2,1)S(1)} %get-tuple-element.49), channel_id=1, source_target_pairs={{0,1},{1,0},{2,3},{3,2},{4,5},{5,4},{6,7},{7,6},{8,9},{9,8},{10,11... | collective-permute-start | bytes 786440 | tf_op jit(solution)/shard_map/ppermute | solution.py:468
  23.6 9.3 %collective-permute-start.5 = (bf16[1024,128]{1,0:T(8,128)(2,1)S(1)}, bf16[1024,128]{1,0:T(8,128)(2,1)S(1)}, u32[]{:S(2)}, u32[]{:S(2)}) collective-permute-start(bf16[1024,128]{1,0:T(8,128)(2,1)S(1)} %get-tuple-element.55), channel_id=1, source_target_pairs={{0,1},{1,0},{2,3},{3,2},{4,5},{5,4},{6,7},{7,6},{8,9},{9,8},{10,11... | collective-permute-start | bytes 786440 | tf_op jit(solution)/shard_map/ppermute | solution.py:468
  31.6 8.6 %collective-permute-start.4 = (bf16[1024,128]{1,0:T(8,128)(2,1)S(1)}, bf16[1024,128]{1,0:T(8,128)(2,1)S(1)}, u32[]{:S(2)}, u32[]{:S(2)}) collective-permute-start(bf16[1024,128]{1,0:T(8,128)(2,1)S(1)} %get-tuple-element.54), channel_id=1, source_target_pairs={{0,1},{1,0},{2,3},{3,2},{4,5},{5,4},{6,7},{7,6},{8,9},{9,8},{10,11... | collective-permute-start | bytes 786440 | tf_op jit(solution)/shard_map/ppermute | solution.py:468
  31.6 8.5 %collective-permute-start.6 = (bf16[4,128,128]{2,1,0:T(8,128)(2,1)S(1)}, bf16[4,128,128]{2,1,0:T(8,128)(2,1)S(1)}, u32[]{:S(2)}, u32[]{:S(2)}) collective-permute-start(bf16[4,128,128]{2,1,0:T(8,128)(2,1)S(1)} %get-tuple-element.63), channel_id=1, source_target_pairs={{1,0},{3,2},{5,4},{7,6},{9,8},{11,10},{13,12},{15,14},{17,16},{19,... | collective-permute-start | bytes 393224 | tf_op jit(solution)/shard_map/ppermute | solution.py:474
  45.7 19.2 %collective-permute-start.7 = (bf16[4,128,128]{2,1,0:T(8,128)(2,1)S(1)}, bf16[4,128,128]{2,1,0:T(8,128)(2,1)S(1)}, u32[]{:S(2)}, u32[]{:S(2)}) collective-permute-start(bf16[4,128,128]{2,1,0:T(8,128)(2,1)S(1)} %get-tuple-element.70), channel_id=1, source_target_pairs={{1,0},{3,2},{5,4},{7,6},{9,8},{11,10},{13,12},{15,14},{17,16},{19,... | collective-permute-start | bytes 393224 | tf_op jit(solution)/shard_map/ppermute | solution.py:474
  47.0 1.3 %collective-permute-start.8 = (f32[40,128]{1,0:T(8,128)S(1)}, f32[40,128]{1,0:T(8,128)S(1)}, u32[]{:S(2)}, u32[]{:S(2)}) collective-permute-start(f32[40,128]{1,0:T(8,128)S(1)} %get-tuple-element.71), channel_id=1, source_target_pairs={{0,2},{2,0},{4,6},{6,4},{8,10},{10,8},{12,14},{14,12},{16,18},{18,... | collective-permute-start | bytes 61448 | tf_op jit(solution)/shard_map/ppermute | solution.py:457
  48.2 3.8 %collective-permute-start.9 = (f32[40,128]{1,0:T(8,128)S(1)}, f32[40,128]{1,0:T(8,128)S(1)}, u32[]{:S(2)}, u32[]{:S(2)}) collective-permute-start(f32[40,128]{1,0:T(8,128)S(1)} %add.66), channel_id=1, source_target_pairs={{0,4},{2,6},{4,0},{6,2},{8,12},{10,14},{12,8},{14,10},{16,20},{18,... | collective-permute-start | bytes 61448 | tf_op jit(solution)/shard_map/ppermute | solution.py:457
  52.0 3.8 %collective-permute-start.10 = (f32[40,128]{1,0:T(8,128)S(1)}, f32[40,128]{1,0:T(8,128)S(1)}, u32[]{:S(2)}, u32[]{:S(2)}) collective-permute-start(f32[40,128]{1,0:T(8,128)S(1)} %add.67), channel_id=1, source_target_pairs={{0,8},{2,10},{4,12},{6,14},{8,0},{10,2},{12,4},{14,6},{16,24},{18,... | collective-permute-start | bytes 61448 | tf_op jit(solution)/shard_map/ppermute | solution.py:457
  55.8 4.7 %collective-permute-start.11 = (f32[40,128]{1,0:T(8,128)S(1)}, f32[40,128]{1,0:T(8,128)S(1)}, u32[]{:S(2)}, u32[]{:S(2)}) collective-permute-start(f32[40,128]{1,0:T(8,128)S(1)} %add.68), channel_id=1, source_target_pairs={{0,16},{2,18},{4,20},{6,22},{8,24},{10,26},{12,28},{14,30},{16,0},... | collective-permute-start | bytes 61448 | tf_op jit(solution)/shard_map/ppermute | solution.py:457
  60.5 4.4 %collective-permute-start.12 = (f32[40,128]{1,0:T(8,128)S(1)}, f32[40,128]{1,0:T(8,128)S(1)}, u32[]{:S(2)}, u32[]{:S(2)}) collective-permute-start(f32[40,128]{1,0:T(8,128)S(1)} %add.69.refs_5_), channel_id=1, source_target_pairs={{0,1},{1,0},{2,3},{3,2},{4,5},{5,4},{6,7},{7,6},{8,9},{9,8},{10,11... | collective-permute-start | bytes 61448 | tf_op jit(solution)/shard_map/ppermute | solution.py:457

commit v6 on v5

--- a/solution.py
+++ b/solution.py
@@ -28,9 +28,7 @@
     return lax.dot_general(a, b, (dims, ((), ())), preferred_element_type=F32)
 
 
-NT = ((1,), (1,))
 NN = ((1,), (0,))
-TN = ((0,), (0,))
 
 
 def whole(shape):
@@ -89,7 +87,7 @@
 
 def prep_kernel(
     tokens, q_ref, do_ref, bq_ref, bk_ref, bv_ref, cos_ref, sin_ref, ck_ref, cv_ref,
-    qs_ref, dos_ref, dot_ref, bias_ref, cos_t_ref, sin_t_ref, pack_ref,
+    qs_ref, qst_ref, dos_ref, dot_ref, bias_ref, cos_t_ref, sin_t_ref, ck_t_ref, cv_t_ref, pack_ref,
 ):
     g = pl.program_id(0)
     cosine, sine = cos_ref[pl.ds(0, tokens), :], sin_ref[pl.ds(0, tokens), :]
@@ -107,25 +105,32 @@
         cols = pl.ds(h * HD, HD)
         rows = pl.ds(pl.multiple_of((g * GROUP + h) * tokens, tokens), tokens)
         x = q_ref[:, cols].astype(F32) + bias_q[h:h + 1]
-        qs_ref[rows, :] = (x * cosine + turn(x) * sine).astype(B16)
+        x = (x * cosine + turn(x) * sine).astype(B16)
+        qs_ref[rows, :] = x
         do = do_ref[:, cols]
         dos_ref[rows, :] = do
         chain, part = h // HEADS, h % HEADS
         place = pl.ds(pl.multiple_of((g * (GROUP // HEADS) + chain) * HD, HD), HD)
+        qst_ref[place, pl.ds(part * tokens, tokens)] = x.T
         dot_ref[place, pl.ds(part * tokens, tokens)] = do.T
+    mine = pl.ds(pl.multiple_of(g * HD, HD), HD)
+    ck_t_ref[mine, :] = ck_ref[:, mine].T
+    cv_t_ref[mine, :] = cv_ref[:, mine].T
 
 
 def prep(q, do, bq, bk, bv, cosine, sine, ck, cv):
     tokens, slots = q.shape[0], ck.shape[0]
     vmem = pl.BlockSpec(memory_space=pltpu.VMEM)
     wide = pl.BlockSpec((tokens, GROUP * HD), lambda i: (0, i))
+    stacked = pltpu.VMEM((HQ * tokens, HD), B16)
+    turned = pltpu.VMEM((HQ // HEADS * HD, HEADS * tokens), B16)
     out_shape = [
-        pltpu.VMEM((HQ * tokens, HD), B16),
-        pltpu.VMEM((HQ * tokens, HD), B16),
-        pltpu.VMEM((HQ // HEADS * HD, HEADS * tokens), B16),
+        stacked, turned, stacked, turned,
         pltpu.VMEM((2 * KV, HD), F32),
         pltpu.VMEM((HD, tokens), F32),
         pltpu.VMEM((HD, tokens), F32),
+        pltpu.VMEM((KV * HD, slots), B16),
+        pltpu.VMEM((KV * HD, slots), B16),
         pltpu.VMEM((2 * slots, HD), B16),
     ]
     return pl.pallas_call(
@@ -165,8 +170,8 @@
         del refs[:count]
         return taken
 
-    (first_ref, rank_ref, qs_ref, dos_ref, dot_ref, bias_ref, cos_t_ref, sin_t_ref,
-     cos_ref, sin_ref, ck_ref, cv_ref, kp_ref, vp_ref) = take(14)
+    (first_ref, rank_ref, qs_ref, qst_ref, dos_ref, dot_ref, bias_ref, cos_t_ref, sin_t_ref,
+     ck_t_ref, cv_t_ref, cos_ref, sin_ref, ck_ref, cv_ref, kp_ref, vp_ref) = take(17)
     far = take(shards - 1)
     far_k = take(shards - 1)
     far_v = take(shards - 1)
@@ -207,8 +212,11 @@
         place = pl.ds(prefix + s * tokens, tokens)
         keys[place] = k.astype(B16)
         values[place] = v.astype(B16)
-    keys_t[...] = keys[...].T
-    values_t[...] = values[...].T
+    keys_t[:, pl.ds(0, slots)] = ck_t_ref[mine, :]
+    values_t[:, pl.ds(0, slots)] = cv_t_ref[mine, :]
+    rest = pl.ds(slots, prefix - slots + slab)
+    keys_t[:, rest] = keys[rest, :].T
+    values_t[:, rest] = values[rest, :].T
     sums_ref[...] = jnp.zeros_like(sums_ref) if old_sums_ref is None else old_sums_ref[...]
     dk_acc[...] = jnp.zeros_like(dk_acc)
     dv_acc[...] = jnp.zeros_like(dv_acc)
@@ -233,12 +241,13 @@
             self.index = index
             self.s, self.pb, self.ds = scratch
             self.rows = pl.ds(pl.multiple_of(index * width, width), width)
+            self.place = pl.ds(pl.multiple_of(index * HD, HD), HD)
             self.top = jnp.full((8, width), NEG, F32)
 
         def scores(self):
-            q = qs_ref[self.rows, :]
+            q = qst_ref[self.place, :]
             for start in tiles:
-                s = dot(keys[pl.ds(start, tile), :], q, NT)
+                s = dot(keys[pl.ds(start, tile), :], q, NN)
                 for i in range(0, tile, tokens):
                     part = s[i:i + tokens]
                     part = jnp.where(allowed(start + i, part), part, NEG)
@@ -272,8 +281,7 @@
 
         def output(self):
             o = dot(values_t[...], self.pb[...], NN).astype(B16)
-            place = pl.ds(pl.multiple_of(self.index * HD, HD), HD)
-            do = dot_ref[place, :].astype(F32)
+            do = dot_ref[self.place, :].astype(F32)
             self.delta = jnp.sum(do * o.astype(F32), axis=0, keepdims=True)
             yield
             for part, cols, _ in self.heads():
@@ -281,10 +289,10 @@
             yield
 
         def dscore(self):
-            do = dos_ref[self.rows, :]
+            do = dot_ref[self.place, :]
             for start in tiles:
                 rows = pl.ds(start, tile)
-                dp = dot(values[rows, :], do, NT)
+                dp = dot(values[rows, :], do, NN)
                 p = self.s[rows, :] * self.inverse
                 self.ds[rows, :] = (p * (dp - self.delta)).astype(B16)
                 yield
@@ -412,20 +420,20 @@
 
 def finish_kernel(shards, *refs):
     owns, backs = refs[2:4], refs[4:4 + shards - 1]
-    sums, other = refs[4 + shards - 1:4 + shards + 1]
+    sums = refs[4 + shards - 1]
     gk_ref, gv_ref, *parts = refs[-5:]
     finish_heads(2, shards, refs[:2], owns, backs, gk_ref, gv_ref)
     start = 0
     for part in parts:
         rows = pl.ds(start, part.shape[0])
-        part[...] = sums[rows, :] + other[rows, :]
+        part[...] = sums[rows, :]
         start += part.shape[0]
 
 
-def finish(shards, cosine, sine, owns, backs, sums, other, gk, gv):
+def finish(shards, cosine, sine, owns, backs, sums, gk, gv):
     tokens = gk.shape[0]
     vmem = pl.BlockSpec(memory_space=pltpu.VMEM)
-    args = [cosine, sine, *owns, *backs, sums, other]
+    args = [cosine, sine, *owns, *backs, sums]
     heads = [(HQ, HD), (KV, HD), (KV, HD)]
     return pl.pallas_call(
         functools.partial(finish_kernel, shards),
@@ -441,21 +449,23 @@
     )(*args, gk, gv)
 
 
-def exchanges(axis):
-    size = lax.axis_size(axis)
-    step = 1
-    while step < size:
-        yield axis, [(i, i ^ step) for i in range(size)]
-        step *= 2
-
-
-def sum_but_last(x, axes):
-    other = None
-    for axis in axes:
-        for name, perm in exchanges(axis):
-            x = x if other is None else x + other
-            other = lax.ppermute(x, name, perm)
-    return x, other
+def sum_everywhere(x, axes):
+    devices = lax.axis_size(axes)
+    if devices & (devices - 1):
+        return lax.psum(x, axes)
+    stride = 1
+    while stride < devices:
+        size = min(devices // stride, 8)
+        groups = [
+            [base + low + i * stride for i in range(size)]
+            for base in range(0, devices, size * stride)
+            for low in range(stride)
+        ]
+        copies = jnp.broadcast_to(x[None], (size,) + x.shape)
+        got = lax.all_to_all(copies, axes, 0, 0, axis_index_groups=groups, tiled=True)
+        x = jnp.sum(got, axis=0)
+        stride *= size
+    return x
 
 
 def body(q_proj, k_proj, v_proj, cache_k, cache_v, bias_q, bias_k, bias_v, start, dout):
@@ -507,8 +517,8 @@
         if g % 2:
             backs = [earlier(x, s) for s, x in zip(shifts, before[3])]
     out, gq, sums, _ = before
-    sums, other = sum_but_last(sums, ("dp", "seq"))
-    gk, gv, *sums = finish(shards, cosine, sine, owns[2:], backs, sums, other, *more)
+    sums = sum_everywhere(sums, ("dp", "seq"))
+    gk, gv, *sums = finish(shards, cosine, sine, owns[2:], backs, sums, *more)
     return (out[None], gq[None], gk[None], gv[None], *[x.reshape(-1) for x in sums])
 
 

time: 65.9 us -> 66.1 us (level)
  blocking collectives: 0 us -> 10.5 us
  waiting for transfers between devices: 14.5 us -> 8.27 us
  starting transfers between devices: 21.8 us -> 16.8 us
  local copies, waits for them, and re-layouts: 0.02 us -> 0.72 us
    all_to_all x0 -> x1, blocking collectives: none -> 10.5 us  [sum_everywhere(): lax.all_to_all(copies, axes, 0, 0, axis_index_groups=groups, tiled=True)]
    ppermute x5 -> x0, waiting for transfers between devices: 9.52 us -> none  [sum_but_last(): other = lax.ppermute(x, name, perm)]
    ppermute x5 -> x0, starting transfers between devices: 8.38 us -> none  [sum_but_last(): other = lax.ppermute(x, name, perm)]
    all_to_all x0 -> x1, waiting for transfers between devices: none -> 3.66 us  [sum_everywhere(): lax.all_to_all(copies, axes, 0, 0, axis_index_groups=groups, tiled=True)]
    all_to_all x0 -> x1, starting transfers between devices: none -> 3.38 us  [sum_everywhere(): lax.all_to_all(copies, axes, 0, 0, axis_index_groups=groups, tiled=True)]
    broadcast_in_dim x0 -> x2, local copies, waits for them, and re-layouts: none -> 0.69 us  [sum_everywhere(): copies = jnp.broadcast_to(x[None], (size,) + x.shape)]
  transfers between devices with their start and end apart: 13 -> 9, of which waited for: 7 -> 3; matrix products, arithmetic and copies ran while one was open for 1% -> 1% of each run, Pallas kernels for 32% -> 32%
where the time goes in v6:
time: 66.1 us; the launch traced here: 65.7 us
  Pallas kernels  27.4 us (41%)
  starting transfers between devices  16.8 us (25%)
  blocking collectives  10.5 us (16%)
  waiting for transfers between devices  8.27 us (13%)
  between operations  1.45 us (2%)
  local copies, waits for them, and re-layouts  0.72 us (1%)
    pallas_call x4, Pallas kernels, attend(): pl.pallas_call(functools.partial(attend_kernel, g, shards), grid=(1,), in...  21.8 us
    all_to_all x1, blocking collectives, sum_everywhere(): lax.all_to_all(copies, axes, 0, 0, axis_index_groups=groups, tiled=True)  10.5 us
    ppermute x2, starting transfers between devices, later(): return lax.ppermute(x, 'seq', [(i, i + s) for i in range(shards - s)])  6.18 us
    ppermute x4, starting transfers between devices, ring(): lax.ppermute(x, 'seq', [(i, (i + s) % shards) for i in range(shards)])  4.66 us
    pallas_call x1, Pallas kernels, prep(): pl.pallas_call(functools.partial(prep_kernel, tokens), grid=(KV,), in_spe...  3.77 us
    all_to_all x1, waiting for transfers between devices, sum_everywhere(): lax.all_to_all(copies, axes, 0, 0, axis_index_groups=groups, tiled=True)  3.66 us
    all_to_all x1, starting transfers between devices, sum_everywhere(): lax.all_to_all(copies, axes, 0, 0, axis_index_groups=groups, tiled=True)  3.38 us
    ppermute x4, waiting for transfers between devices, ring(): lax.ppermute(x, 'seq', [(i, (i + s) % shards) for i in range(shards)])  2.83 us
  transfers between devices with their start and end apart: 9, of which 3 were waited for; matrix products, arithmetic and copies ran while one was open for 1% of the time, Pallas kernels for 32%

profile of v6, /device:TPU:0, one launch (start us, length us, event | category | flops | bytes accessed | tf_op | source)
XLA Modules:
  0.0 65.7 jit_solution(4314201257191683950)
XLA Ops:
  0.6 4.9 %collective-permute-start.1 = (bf16[128,512]{1,0:T(8,128)(2,1)}, bf16[128,512]{1,0:T(8,128)(2,1)S(1)}, u32[]{:S(2)}, u32[]{:S(2)}) collective-permute-start(bf16[128,512]{1,0:T(8,128)(2,1)} %bitcast.33), channel_id=1, source_target_pairs={{0,1},{2,3},{4,5},{6,7},{8,9},{10,11},{12,13},{14,15},{16,17},{18,... | collective-permute-start | bytes 393224 | tf_op jit(solution)/shard_map/ppermute | solution.py:481
  5.5 1.3 %collective-permute-start.2 = (bf16[128,512]{1,0:T(8,128)(2,1)}, bf16[128,512]{1,0:T(8,128)(2,1)S(1)}, u32[]{:S(2)}, u32[]{:S(2)}) collective-permute-start(bf16[128,512]{1,0:T(8,128)(2,1)} %bitcast.38), channel_id=1, source_target_pairs={{0,1},{2,3},{4,5},{6,7},{8,9},{10,11},{12,13},{14,15},{16,17},{18,... | collective-permute-start | bytes 393224 | tf_op jit(solution)/shard_map/ppermute | solution.py:481
  6.8 0.0 copy-start
  6.8 0.0 copy-start.1
  6.8 1.1 %pack.1 = bf16[1024,128]{1,0:T(8,128)(2,1)S(1)} custom-call(bf16[512,512]{1,0:T(8,128)(2,1)} %bitcast.21, bf16[512,512]{1,0:T(8,128)(2,1)} %bitcast.27), custom_call_target="tpu_custom_call" | custom-call | bytes 524288 | tf_op jit(solution)/shard_map/pack/pallas_call | solution.py:59
  7.9 0.1 collective-permute-start.3
  8.7 0.1 convert_bitcast_fusion
  8.8 0.5 fusion
  9.3 0.0 copy-done
  9.3 0.0 copy-done.1
  9.3 0.0 copy-start.2
  9.3 0.0 copy-start.3
  9.4 3.8 %prep.1 = (bf16[4096,128]{1,0:T(8,128)(2,1)S(1)}, bf16[2048,256]{1,0:T(8,128)(2,1)S(1)}, bf16[4096,128]{1,0:T(8,128)(2,1)S(1)}, bf16[2048,256]{1,0:T(8,128)(2,1)...) custom-call(bf16[128,4096]{1,0:T(8,128)(2,1)} %bitcast.45, ...), custom_call_target="tpu_custom_call" | custom-call | flops 2097152 | bytes 6291456 | tf_op jit(solution)/shard_map/prep/pallas_call | solution.py:136
  13.1 2.1 %collective-permute-start = (bf16[1024,128]{1,0:T(8,128)(2,1)S(1)}, bf16[1024,128]{1,0:T(8,128)(2,1)S(1)}, u32[]{:S(2)}, u32[]{:S(2)}) collective-permute-start(bf16[1024,128]{1,0:T(8,128)(2,1)S(1)} %get-tuple-element.55), channel_id=1, source_target_pairs={{0,1},{1,0},{2,3},{3,2},{4,5},{5,4},{6,7},{7,6},{8,9},{9,8},{10,11... | collective-permute-start | bytes 786440 | tf_op jit(solution)/shard_map/ppermute | solution.py:478
  15.2 0.0 collective-permute-done.1.refs_18_
  15.2 0.0 collective-permute-done.2.refs_19_
  15.2 2.8 %collective-permute-done.3.refs_17_ = bf16[1024,128]{1,0:T(8,128)(2,1)S(1)} collective-permute-done((bf16[1024,128]{1,0:T(8,128)(2,1)S(1)}, bf16[1024,128]{1,0:T(8,128)(2,1)S(1)}, u32[]{:S(2)}, u32[]{:S(2)}) %collective-permute-start.3) | collective-permute-done | bytes 262176 | tf_op jit(solution)/shard_map/ppermute | solution.py:478
  18.0 0.0 copy-done.2
  18.0 0.0 copy-done.3
  18.0 5.5 %attend.4 = (bf16[128,4096]{1,0:T(8,128)(2,1)}, bf16[128,4096]{1,0:T(8,128)(2,1)}, f32[40,128]{1,0:T(8,128)S(1)}, f32[2,128,128]{2,1,0:T(8,128)S(1)}, bf16[2,128...) custom-call(s32[1]{0:T(128)} %copy.33.refs_0_, s32[1]{0:T(128)} %bitcast.refs_1_, ...), custom_call_target="tpu_custom_call" | custom-call | flops 1476395008 | bytes 2359296 | tf_op jit(solution)/shard_map/attend/pallas_call | solution.py:394
  23.5 2.5 %collective-permute-start.5 = (bf16[1024,128]{1,0:T(8,128)(2,1)S(1)}, bf16[1024,128]{1,0:T(8,128)(2,1)S(1)}, u32[]{:S(2)}, u32[]{:S(2)}) collective-permute-start(bf16[1024,128]{1,0:T(8,128)(2,1)S(1)} %get-tuple-element.61), channel_id=1, source_target_pairs={{0,1},{1,0},{2,3},{3,2},{4,5},{5,4},{6,7},{7,6},{8,9},{9,8},{10,11... | collective-permute-start | bytes 786440 | tf_op jit(solution)/shard_map/ppermute | solution.py:478
  26.0 0.0 collective-permute-done.refs_17_
  26.0 5.5 %attend.5 = (bf16[128,4096]{1,0:T(8,128)(2,1)}, bf16[128,4096]{1,0:T(8,128)(2,1)}, f32[40,128]{1,0:T(8,128)S(1)}, f32[2,128,128]{2,1,0:T(8,128)S(1)}, bf16[4,128...) custom-call(s32[1]{0:T(128)} %copy.33.refs_0_, ...), custom_call_target="tpu_custom_call", output_to_operand_aliasing={{0}: (22, {}), {1}: (23, {})} | custom-call | flops 1476395008 | bytes 2359296 | tf_op jit(solution)/shard_map/attend/pallas_call | solution.py:394
  31.4 0.0 collective-permute-start.4
  31.5 1.3 %collective-permute-start.6 = (bf16[4,128,128]{2,1,0:T(8,128)(2,1)S(1)}, bf16[4,128,128]{2,1,0:T(8,128)(2,1)S(1)}, u32[]{:S(2)}, u32[]{:S(2)}) collective-permute-start(bf16[4,128,128]{2,1,0:T(8,128)(2,1)S(1)} %get-tuple-element.69), channel_id=1, source_target_pairs={{1,0},{3,2},{5,4},{7,6},{9,8},{11,10},{13,12},{15,14},{17,16},{19,... | collective-permute-start | bytes 393224 | tf_op jit(solution)/shard_map/ppermute | solution.py:484
  32.8 0.0 collective-permute-done.5.refs_17_
  32.8 5.4 %attend.6 = (bf16[128,4096]{1,0:T(8,128)(2,1)}, bf16[128,4096]{1,0:T(8,128)(2,1)}, f32[40,128]{1,0:T(8,128)S(1)}, f32[2,128,128]{2,1,0:T(8,128)S(1)}, bf16[2,128,128]{2,1,0:T(8,128)(2,1)S(1)}) custom-call(s32[1]{0:T(128)} %copy.33.refs_0_, s32[1]{0:T(128)} %bitcast.refs_1_, ...), custom_call_target="tpu_custom_call", output_to_operand_aliasing={{0}: (21, {}), {1}: (22, {})} | custom-call | flops 1476395008 | bytes 2359296 | tf_op jit(solution)/shard_map/attend/pallas_call | solution.py:394
  38.2 1.8 %collective-permute-done.6.refs_24_ = bf16[4,128,128]{2,1,0:T(8,128)(2,1)S(1)} collective-permute-done((bf16[4,128,128]{2,1,0:T(8,128)(2,1)S(1)}, bf16[4,128,128]{2,1,0:T(8,128)(2,1)S(1)}, u32[]{:S(2)}, u32[]{:S(2)}) %collective-permute-start.6) | collective-permute-done | bytes 131104 | tf_op jit(solution)/shard_map/ppermute | solution.py:484
  40.0 0.0 collective-permute-done.4.refs_17_
  40.0 5.4 %attend.7 = (bf16[128,4096]{1,0:T(8,128)(2,1)}, bf16[128,4096]{1,0:T(8,128)(2,1)}, f32[40,128]{1,0:T(8,128)S(1)}, f32[2,128,128]{2,1,0:T(8,128)S(1)}, bf16[4,128...) custom-call(s32[1]{0:T(128)} %copy.33.refs_0_, ...), custom_call_target="tpu_custom_call", output_to_operand_aliasing={{0}: (25, {}), {1}: (26, {})} | custom-call | flops 1476395008 | bytes 2359296 | tf_op jit(solution)/shard_map/attend/pallas_call | solution.py:394
  45.4 0.7 %broadcast_in_dim.41 = f32[8,40,128]{2,1,0:T(8,128)} broadcast(f32[40,128]{1,0:T(8,128)S(1)} %get-tuple-element.77), dimensions={1,2} | broadcast | bytes 184320 | tf_op jit(solution)/shard_map/broadcast_in_dim | solution.py:464
  46.1 3.4 %all-to-all-start = ((f32[8,40,128]{2,1,0:T(8,128)}), f32[8,40,128]{2,1,0:T(8,128)S(1)}, u32[]{:S(2)}, u32[]{:S(2)}) async-start(f32[8,40,128]{2,1,0:T(8,128)} %broadcast_in_dim.41), calls=%async_computation | async-start | bytes 327680 | tf_op jit(solution)/shard_map/all_to_all | solution.py:465
  49.5 1.3 %collective-permute-start.7 = (bf16[4,128,128]{2,1,0:T(8,128)(2,1)S(1)}, bf16[4,128,128]{2,1,0:T(8,128)(2,1)S(1)}, u32[]{:S(2)}, u32[]{:S(2)}) collective-permute-start(bf16[4,128,128]{2,1,0:T(8,128)(2,1)S(1)} %get-tuple-element.76), channel_id=1, source_target_pairs={{1,0},{3,2},{5,4},{7,6},{9,8},{11,10},{13,12},{15,14},{17,16},{19,... | collective-permute-start | bytes 393224 | tf_op jit(solution)/shard_map/ppermute | solution.py:484
  50.8 3.7 %all-to-all-done = f32[8,40,128]{2,1,0:T(8,128)S(1)} async-done(((f32[8,40,128]{2,1,0:T(8,128)}), f32[8,40,128]{2,1,0:T(8,128)S(1)}, u32[]{:S(2)}, u32[]{:S(2)}) %all-to-all-start) | async-done | bytes 163872 | tf_op jit(solution)/shard_map/all_to_all | solution.py:465
  54.5 10.5 %all_to_all.10 = f32[4,40,128]{2,1,0:T(8,128)S(1)} all-to-all(f32[4,40,128]{2,1,0:T(8,128)S(1)} %broadcast_in_dim.42), channel_id=1, replica_groups={{0,8,16,24},{1,9,17,25},{2,10,18,26},{3,11,19,27},{4,12,20,28},{5,13,21..., dimensions={0} | all-to-all | bytes 163840 | tf_op jit(solution)/shard_map/all_to_all | solution.py:465
  65.0 0.0 collective-permute-done.7.refs_4_
  65.0 0.7 %finish.1 = (bf16[128,512]{1,0:T(8,128)(2,1)}, bf16[128,512]{1,0:T(8,128)(2,1)}, f32[32,128]{1,0:T(8,128)}, f32[4,128]{1,0:T(4,128)}, f32[4,128]{1,0:T(4,128)}) custom-call(f32[256,128]{1,0:T(8,128)S(1)} %get-tuple-element.86.cos_ref.refs_11_.refs_0_, ...), custom_call_target="tpu_custom_call", output_to_operand_aliasing={{0}: (6, {}), {1}: (7, {})} | custom-call | bytes 524288 | tf_op jit(solution)/shard_map/finish/pallas_call | solution.py:438
  (5 shorter events, 0.1 us)
Async XLA Ops:
  0.6 14.6 %collective-permute-start.1 = (bf16[128,512]{1,0:T(8,128)(2,1)}, bf16[128,512]{1,0:T(8,128)(2,1)S(1)}, u32[]{:S(2)}, u32[]{:S(2)}) collective-permute-start(bf16[128,512]{1,0:T(8,128)(2,1)} %bitcast.33), channel_id=1, source_target_pairs={{0,1},{2,3},{4,5},{6,7},{8,9},{10,11},{12,13},{14,15},{16,17},{18,... | collective-permute-start | bytes 393224 | tf_op jit(solution)/shard_map/ppermute | solution.py:481
  5.5 9.7 %collective-permute-start.2 = (bf16[128,512]{1,0:T(8,128)(2,1)}, bf16[128,512]{1,0:T(8,128)(2,1)S(1)}, u32[]{:S(2)}, u32[]{:S(2)}) collective-permute-start(bf16[128,512]{1,0:T(8,128)(2,1)} %bitcast.38), channel_id=1, source_target_pairs={{0,1},{2,3},{4,5},{6,7},{8,9},{10,11},{12,13},{14,15},{16,17},{18,... | collective-permute-start | bytes 393224 | tf_op jit(solution)/shard_map/ppermute | solution.py:481
  6.8 2.5 %copy-start = (bf16[1,512,512]{2,1,0:T(8,128)(2,1)S(1)}, bf16[1,512,512]{2,1,0:T(8,128)(2,1)}, u32[]{:S(2)}) copy-start(bf16[1,512,512]{2,1,0:T(8,128)(2,1)} %param.13) | copy-start | bytes 1572868
  6.8 2.5 %copy-start.1 = (bf16[1,512,512]{2,1,0:T(8,128)(2,1)S(1)}, bf16[1,512,512]{2,1,0:T(8,128)(2,1)}, u32[]{:S(2)}) copy-start(bf16[1,512,512]{2,1,0:T(8,128)(2,1)} %param.14) | copy-start | bytes 1572868
  7.9 10.1 %collective-permute-start.3 = (bf16[1024,128]{1,0:T(8,128)(2,1)S(1)}, bf16[1024,128]{1,0:T(8,128)(2,1)S(1)}, u32[]{:S(2)}, u32[]{:S(2)}) collective-permute-start(bf16[1024,128]{1,0:T(8,128)(2,1)S(1)} %pack.1), channel_id=1, source_target_pairs={{0,1},{1,0},{2,3},{3,2},{4,5},{5,4},{6,7},{7,6},{8,9},{9,8},{10,11... | collective-permute-start | bytes 786440 | tf_op jit(solution)/shard_map/ppermute | solution.py:478
  9.3 8.7 %copy-start.2 = (bf16[1,128,512]{2,1,0:T(8,128)(2,1)S(1)}, bf16[1,128,512]{2,1,0:T(8,128)(2,1)}, u32[]{:S(2)}) copy-start(bf16[1,128,512]{2,1,0:T(8,128)(2,1)} %param.11) | copy-start | bytes 393220
  9.3 8.7 %copy-start.3 = (bf16[1,128,512]{2,1,0:T(8,128)(2,1)S(1)}, bf16[1,128,512]{2,1,0:T(8,128)(2,1)}, u32[]{:S(2)}) copy-start(bf16[1,128,512]{2,1,0:T(8,128)(2,1)} %param.12) | copy-start | bytes 393220
  13.1 12.9 %collective-permute-start = (bf16[1024,128]{1,0:T(8,128)(2,1)S(1)}, bf16[1024,128]{1,0:T(8,128)(2,1)S(1)}, u32[]{:S(2)}, u32[]{:S(2)}) collective-permute-start(bf16[1024,128]{1,0:T(8,128)(2,1)S(1)} %get-tuple-element.55), channel_id=1, source_target_pairs={{0,1},{1,0},{2,3},{3,2},{4,5},{5,4},{6,7},{7,6},{8,9},{9,8},{10,11... | collective-permute-start | bytes 786440 | tf_op jit(solution)/shard_map/ppermute | solution.py:478
  23.5 9.3 %collective-permute-start.5 = (bf16[1024,128]{1,0:T(8,128)(2,1)S(1)}, bf16[1024,128]{1,0:T(8,128)(2,1)S(1)}, u32[]{:S(2)}, u32[]{:S(2)}) collective-permute-start(bf16[1024,128]{1,0:T(8,128)(2,1)S(1)} %get-tuple-element.61), channel_id=1, source_target_pairs={{0,1},{1,0},{2,3},{3,2},{4,5},{5,4},{6,7},{7,6},{8,9},{9,8},{10,11... | collective-permute-start | bytes 786440 | tf_op jit(solution)/shard_map/ppermute | solution.py:478
  31.4 8.6 %collective-permute-start.4 = (bf16[1024,128]{1,0:T(8,128)(2,1)S(1)}, bf16[1024,128]{1,0:T(8,128)(2,1)S(1)}, u32[]{:S(2)}, u32[]{:S(2)}) collective-permute-start(bf16[1024,128]{1,0:T(8,128)(2,1)S(1)} %get-tuple-element.60), channel_id=1, source_target_pairs={{0,1},{1,0},{2,3},{3,2},{4,5},{5,4},{6,7},{7,6},{8,9},{9,8},{10,11... | collective-permute-start | bytes 786440 | tf_op jit(solution)/shard_map/ppermute | solution.py:478
  31.5 8.5 %collective-permute-start.6 = (bf16[4,128,128]{2,1,0:T(8,128)(2,1)S(1)}, bf16[4,128,128]{2,1,0:T(8,128)(2,1)S(1)}, u32[]{:S(2)}, u32[]{:S(2)}) collective-permute-start(bf16[4,128,128]{2,1,0:T(8,128)(2,1)S(1)} %get-tuple-element.69), channel_id=1, source_target_pairs={{1,0},{3,2},{5,4},{7,6},{9,8},{11,10},{13,12},{15,14},{17,16},{19,... | collective-permute-start | bytes 393224 | tf_op jit(solution)/shard_map/ppermute | solution.py:484
  46.1 8.3 %all-to-all-start = ((f32[8,40,128]{2,1,0:T(8,128)}), f32[8,40,128]{2,1,0:T(8,128)S(1)}, u32[]{:S(2)}, u32[]{:S(2)}) async-start(f32[8,40,128]{2,1,0:T(8,128)} %broadcast_in_dim.41), calls=%async_computation | async-start | bytes 327680 | tf_op jit(solution)/shard_map/all_to_all | solution.py:465
  49.5 15.5 %collective-permute-start.7 = (bf16[4,128,128]{2,1,0:T(8,128)(2,1)S(1)}, bf16[4,128,128]{2,1,0:T(8,128)(2,1)S(1)}, u32[]{:S(2)}, u32[]{:S(2)}) collective-permute-start(bf16[4,128,128]{2,1,0:T(8,128)(2,1)S(1)} %get-tuple-element.76), channel_id=1, source_target_pairs={{1,0},{3,2},{5,4},{7,6},{9,8},{11,10},{13,12},{15,14},{17,16},{19,... | collective-permute-start | bytes 393224 | tf_op jit(solution)/shard_map/ppermute | solution.py:484

commit v7 on v5

--- a/solution.py
+++ b/solution.py
@@ -28,9 +28,7 @@
     return lax.dot_general(a, b, (dims, ((), ())), preferred_element_type=F32)
 
 
-NT = ((1,), (1,))
 NN = ((1,), (0,))
-TN = ((0,), (0,))
 
 
 def whole(shape):
@@ -87,9 +85,25 @@
         gv_ref[:, cols] = dv.astype(B16)
 
 
+def write_mask(first, rank, shards, slots, mask_ref):
+    tokens = mask_ref.shape[1]
+    row = lax.broadcasted_iota(jnp.int32, (tokens, tokens), 0)
+    col = lax.broadcasted_iota(jnp.int32, (tokens, tokens), 1)
+    prefix = shards * slots
+    for start in range(0, mask_ref.shape[0], tokens):
+        if start < prefix:
+            owner = lax.rem(rank - start // slots + shards, shards)
+            seen = row < first - owner * slots - start % slots
+        elif start == prefix:
+            seen = row <= col
+        else:
+            seen = row < jnp.where(rank >= (start - prefix) // tokens, tokens, 0)
+        mask_ref[pl.ds(start, tokens), :] = jnp.where(seen, 0.0, NEG).astype(B16)
+
+
 def prep_kernel(
-    tokens, q_ref, do_ref, bq_ref, bk_ref, bv_ref, cos_ref, sin_ref, ck_ref, cv_ref,
-    qs_ref, dos_ref, dot_ref, bias_ref, cos_t_ref, sin_t_ref, pack_ref,
+    tokens, shards, first_ref, rank_ref, q_ref, do_ref, bq_ref, bk_ref, bv_ref, cos_ref, sin_ref, ck_ref, cv_ref,
+    qs_ref, qst_ref, dos_ref, dot_ref, bias_ref, cos_t_ref, sin_t_ref, ck_t_ref, cv_t_ref, mask_ref, pack_ref,
 ):
     g = pl.program_id(0)
     cosine, sine = cos_ref[pl.ds(0, tokens), :], sin_ref[pl.ds(0, tokens), :]
@@ -102,36 +116,53 @@
         cos_t_ref[...] = cosine.T
         sin_t_ref[...] = sine.T
         copy_chunk(1, ck_ref, cv_ref, pack_ref)
-
+        write_mask(first_ref[0], rank_ref[0], shards, ck_ref.shape[0], mask_ref)
+
+    row = lax.broadcasted_iota(jnp.int32, (tokens, tokens), 0)
+    col = lax.broadcasted_iota(jnp.int32, (tokens, tokens), 1)
+    one_hot = jnp.where(row == col, 1.0, 0.0).astype(B16)
     for h in range(GROUP):
         cols = pl.ds(h * HD, HD)
         rows = pl.ds(pl.multiple_of((g * GROUP + h) * tokens, tokens), tokens)
         x = q_ref[:, cols].astype(F32) + bias_q[h:h + 1]
-        qs_ref[rows, :] = (x * cosine + turn(x) * sine).astype(B16)
+        x = (x * cosine + turn(x) * sine).astype(B16)
+        qs_ref[rows, :] = x
         do = do_ref[:, cols]
         dos_ref[rows, :] = do
         chain, part = h // HEADS, h % HEADS
         place = pl.ds(pl.multiple_of((g * (GROUP // HEADS) + chain) * HD, HD), HD)
+        depth = HD + tokens
+        upper = pl.multiple_of((g * (GROUP // HEADS) + chain) * depth, depth)
+        lower = pl.multiple_of(upper + HD, HD)
+        qst_ref[pl.ds(upper, HD), pl.ds(part * tokens, tokens)] = x.T
+        qst_ref[pl.ds(lower, tokens), pl.ds(part * tokens, tokens)] = one_hot
         dot_ref[place, pl.ds(part * tokens, tokens)] = do.T
-
-
-def prep(q, do, bq, bk, bv, cosine, sine, ck, cv):
+    mine = pl.ds(pl.multiple_of(g * HD, HD), HD)
+    ck_t_ref[mine, :] = ck_ref[:, mine].T
+    cv_t_ref[mine, :] = cv_ref[:, mine].T
+
+
+def prep(shards, first, rank, q, do, bq, bk, bv, cosine, sine, ck, cv):
     tokens, slots = q.shape[0], ck.shape[0]
     vmem = pl.BlockSpec(memory_space=pltpu.VMEM)
     wide = pl.BlockSpec((tokens, GROUP * HD), lambda i: (0, i))
+    stacked = pltpu.VMEM((HQ * tokens, HD), B16)
+    turned = pltpu.VMEM((HQ // HEADS * HD, HEADS * tokens), B16)
+    deep = pltpu.VMEM((HQ // HEADS * (HD + tokens), HEADS * tokens), B16)
     out_shape = [
-        pltpu.VMEM((HQ * tokens, HD), B16),
-        pltpu.VMEM((HQ * tokens, HD), B16),
-        pltpu.VMEM((HQ // HEADS * HD, HEADS * tokens), B16),
+        stacked, deep, stacked, turned,
         pltpu.VMEM((2 * KV, HD), F32),
         pltpu.VMEM((HD, tokens), F32),
         pltpu.VMEM((HD, tokens), F32),
+        pltpu.VMEM((KV * HD, slots), B16),
+        pltpu.VMEM((KV * HD, slots), B16),
+        pltpu.VMEM((shards * (slots + tokens), tokens), B16),
         pltpu.VMEM((2 * slots, HD), B16),
     ]
     return pl.pallas_call(
-        functools.partial(prep_kernel, tokens),
+        functools.partial(prep_kernel, tokens, shards),
         grid=(KV,),
-        in_specs=[
+        in_specs=[pl.BlockSpec(memory_space=pltpu.SMEM)] * 2 + [
             wide, wide, pl.BlockSpec((GROUP, HD), lambda i: (i, 0)),
             whole((KV, HD)), whole((KV, HD)), vmem, vmem, vmem, vmem,
         ],
@@ -142,7 +173,7 @@
             flops=4 * tokens * HQ * HD, bytes_accessed=12 * tokens * HQ * HD, transcendentals=0
         ),
         name="prep",
-    )(q, do, bq, bk, bv, cosine, sine, ck, cv)
+    )(first, rank, q, do, bq, bk, bv, cosine, sine, ck, cv)
 
 
 def alternate(first, second):
@@ -165,8 +196,8 @@
         del refs[:count]
         return taken
 
-    (first_ref, rank_ref, qs_ref, dos_ref, dot_ref, bias_ref, cos_t_ref, sin_t_ref,
-     cos_ref, sin_ref, ck_ref, cv_ref, kp_ref, vp_ref) = take(14)
+    (qs_ref, qst_ref, dos_ref, dot_ref, bias_ref, cos_t_ref, sin_t_ref,
+     ck_t_ref, cv_t_ref, mask_ref, cos_ref, sin_ref, ck_ref, cv_ref, kp_ref, vp_ref) = take(16)
     far = take(shards - 1)
     far_k = take(shards - 1)
     far_v = take(shards - 1)
@@ -181,23 +212,22 @@
     pack_ref = take(1)[0] if g + 2 < KV else None
     gk_ref, gv_ref = take(2) if g == KV - 1 else (None, None)
     keys, values, keys_t, values_t, dk_acc, dv_acc = take(6)
-    chains = [take(3), take(3)]
+    chains = [take(4), take(4)]
     tokens = kp_ref.shape[0]
     slots = ck_ref.shape[0]
     prefix = shards * slots
     slab = shards * tokens
     total = prefix + slab
-    first = first_ref[0]
-    rank = rank_ref[0]
     mine = pl.ds(g * HD, HD)
 
     if pack_ref is not None:
         copy_chunk(g + 2, ck_ref, cv_ref, pack_ref)
-    keys[pl.ds(0, slots)] = ck_ref[:, mine]
-    values[pl.ds(0, slots)] = cv_ref[:, mine]
+    near, extra = pl.ds(0, HD), pl.ds(HD, tokens)
+    keys[pl.ds(0, slots), near] = ck_ref[:, mine]
+    values[pl.ds(0, slots), near] = cv_ref[:, mine]
     for s in range(1, shards):
-        keys[pl.ds(s * slots, slots)] = far[s - 1][pl.ds(0, slots)]
-        values[pl.ds(s * slots, slots)] = far[s - 1][pl.ds(slots, slots)]
+        keys[pl.ds(s * slots, slots), near] = far[s - 1][pl.ds(0, slots)]
+        values[pl.ds(s * slots, slots), near] = far[s - 1][pl.ds(slots, slots)]
     for s in range(shards):
         rows = pl.ds(s * tokens, tokens)
         kp, vp = (kp_ref, vp_ref) if s == 0 else (far_k[s - 1], far_v[s - 1])
@@ -205,10 +235,17 @@
         k = k * cos_ref[rows, :] + turn(k) * sin_ref[rows, :]
         v = vp[:, mine].astype(F32) + bias_ref[KV + g:KV + g + 1, :]
         place = pl.ds(prefix + s * tokens, tokens)
-        keys[place] = k.astype(B16)
-        values[place] = v.astype(B16)
-    keys_t[...] = keys[...].T
-    values_t[...] = values[...].T
+        keys[place, near] = k.astype(B16)
+        values[place, near] = v.astype(B16)
+    keys[:, extra] = mask_ref[...]
+    values[:, extra] = jnp.ones_like(mask_ref)
+    keys_t[:, pl.ds(0, slots)] = ck_t_ref[mine, :]
+    values_t[:, pl.ds(0, slots)] = cv_t_ref[mine, :]
+    rest = pl.ds(slots, prefix - slots + slab)
+    keys_t[:, rest] = keys[rest, near].T
+    values_t[:, rest] = values[rest, near].T
+    for scratch in chains:
+        scratch[3][...] = jnp.zeros_like(scratch[3])
     sums_ref[...] = jnp.zeros_like(sums_ref) if old_sums_ref is None else old_sums_ref[...]
     dk_acc[...] = jnp.zeros_like(dk_acc)
     dv_acc[...] = jnp.zeros_like(dv_acc)
@@ -216,34 +253,22 @@
     width = HEADS * tokens
     scale = HD ** -0.5
     blocks = range(0, total, tokens)
-    tile = 2 * tokens
-    tiles = range(0, total, tile)
-
-    def allowed(start, s):
-        row = lax.broadcasted_iota(jnp.int32, s.shape, 0)
-        if start < prefix:
-            owner = lax.rem(rank - start // slots + shards, shards)
-            return row < first - owner * slots - start % slots
-        if start < prefix + tokens:
-            return row <= (lax.broadcasted_iota(jnp.int32, s.shape, 1) & (tokens - 1))
-        return row < jnp.where(rank >= (start - prefix) // tokens, tokens, 0)
 
     class Chain:
         def __init__(self, index, scratch):
             self.index = index
-            self.s, self.pb, self.ds = scratch
+            self.s, self.pb, self.ds, self.do = scratch
             self.rows = pl.ds(pl.multiple_of(index * width, width), width)
+            self.place = pl.ds(pl.multiple_of(index * HD, HD), HD)
             self.top = jnp.full((8, width), NEG, F32)
 
         def scores(self):
-            q = qs_ref[self.rows, :]
-            for start in tiles:
-                s = dot(keys[pl.ds(start, tile), :], q, NT)
-                for i in range(0, tile, tokens):
-                    part = s[i:i + tokens]
-                    part = jnp.where(allowed(start + i, part), part, NEG)
-                    self.s[pl.ds(start + i, tokens), :] = part
-                    self.top = jnp.maximum(self.top, fold(part, jnp.max))
+            depth = HD + tokens
+            s = dot(keys[...], qst_ref[pl.ds(pl.multiple_of(self.index * depth, depth), depth), :], NN)
+            for start in blocks:
+                part = s[start:start + tokens]
+                self.s[pl.ds(start, tokens), :] = part
+                self.top = jnp.maximum(self.top, fold(part, jnp.max))
                 yield
 
         def softmax(self):
@@ -255,10 +280,12 @@
                 self.s[rows, :] = e
                 total_e = total_e + fold(e, jnp.sum)
                 yield
-            self.inverse = 1.0 / jnp.sum(total_e, axis=0, keepdims=True)
+            inverse = 1.0 / jnp.sum(total_e, axis=0, keepdims=True)
             for start in blocks:
                 rows = pl.ds(start, tokens)
-                self.pb[rows, :] = (self.s[rows, :] * self.inverse).astype(B16)
+                p = self.s[rows, :] * inverse
+                self.s[rows, :] = p
+                self.pb[rows, :] = p.astype(B16)
                 yield
 
         def heads(self):
@@ -272,21 +299,26 @@
 
         def output(self):
             o = dot(values_t[...], self.pb[...], NN).astype(B16)
-            place = pl.ds(pl.multiple_of(self.index * HD, HD), HD)
-            do = dot_ref[place, :].astype(F32)
-            self.delta = jnp.sum(do * o.astype(F32), axis=0, keepdims=True)
+            do = dot_ref[self.place, :]
+            self.do[pl.ds(0, HD), :] = do
+            left = -jnp.sum(do.astype(F32) * o.astype(F32), axis=0, keepdims=True)
+            row = lax.broadcasted_iota(jnp.int32, (16, width), 0)
+            terms = jnp.zeros((16, width), F32)
+            for i in range(3):
+                term = left.astype(B16).astype(F32)
+                left = left - term
+                terms = jnp.where(row == i, term, terms)
+            self.do[pl.ds(HD, 16), :] = terms.astype(B16)
             yield
             for part, cols, _ in self.heads():
                 out_ref[:, cols] = o[:, part].T
             yield
 
         def dscore(self):
-            do = dos_ref[self.rows, :]
-            for start in tiles:
-                rows = pl.ds(start, tile)
-                dp = dot(values[rows, :], do, NT)
-                p = self.s[rows, :] * self.inverse
-                self.ds[rows, :] = (p * (dp - self.delta)).astype(B16)
+            dp = dot(values[...], self.do[...], NN)
+            for start in blocks:
+                rows = pl.ds(start, tokens)
+                self.ds[rows, :] = (self.s[rows, :] * dp[start:start + tokens]).astype(B16)
                 yield
 
         def grads(self):
@@ -339,20 +371,18 @@
 
 
 def attend(
-    g, shards, first, rank, prepared, cosine, sine, ck, cv, kp, vp, far, far_k, far_v,
+    g, shards, prepared, cosine, sine, ck, cv, kp, vp, far, far_k, far_v,
     before, owns, backs,
 ):
     tokens, slots = kp.shape[0], ck.shape[0]
     slab = shards * tokens
     total = slab + shards * slots
     last = g == KV - 1
-    smem = pl.BlockSpec(memory_space=pltpu.SMEM)
     vmem = pl.BlockSpec(memory_space=pltpu.VMEM)
     anywhere = pl.BlockSpec(memory_space=pl.ANY)
     wide = pl.BlockSpec((tokens, GROUP * HD), lambda i: (0, g))
     half = pl.BlockSpec((tokens, 2 * HD), lambda i: (0, 0))
 
-    args = [first, rank]
     placed = [*prepared, cosine, sine, ck, cv, kp, vp, *far, *far_k, *far_v]
     aliases = {}
     if before is not None:
@@ -362,8 +392,8 @@
             placed += send
         if last:
             placed += [*owns[:2], *backs]
-    args += placed
-    in_specs = [smem] * 2 + [vmem] * len(placed)
+    args = list(placed)
+    in_specs = [vmem] * len(placed)
     if before is not None:
         aliases = {len(args): 0, len(args) + 1: 1}
         args += [out, gq]
@@ -390,11 +420,12 @@
         out_shape=out_shape,
         out_specs=out_specs,
         scratch_shapes=[
-            pltpu.VMEM((total, HD), B16), pltpu.VMEM((total, HD), B16),
+            pltpu.VMEM((total, HD + tokens), B16), pltpu.VMEM((total, HD + tokens), B16),
             pltpu.VMEM((HD, total), B16), pltpu.VMEM((HD, total), B16),
             pltpu.VMEM((slab, HD), F32), pltpu.VMEM((slab, HD), F32),
         ] + [
-            pltpu.VMEM((total, HEADS * tokens), kind) for kind in (F32, B16, B16) * 2
+            pltpu.VMEM((rows, HEADS * tokens), kind)
+            for rows, kind in ((total, F32), (total, B16), (total, B16), (HD + tokens, B16)) * 2
         ],
         input_output_aliases=aliases,
         compiler_params=params(),
@@ -491,14 +522,14 @@
     sine = jnp.sin(angles) * jnp.where(lane < HD // 2, -1.0, 1.0).astype(F32)[None]
 
     *prepared, chunk = prep(
-        hbm(q_proj[0]), hbm(dout[0]), hbm(bias_q.reshape(HQ, HD)),
+        shards, start, rank.reshape(1), hbm(q_proj[0]), hbm(dout[0]), hbm(bias_q.reshape(HQ, HD)),
         hbm(bias_k.reshape(KV, HD)), hbm(bias_v.reshape(KV, HD)), cosine, sine, ck, cv,
     )
     far.append([ring(chunk, s) for s in shifts])
     before, owns, backs = None, [], []
     for g in range(KV):
         before, own, more = attend(
-            g, shards, start, rank.reshape(1), prepared, cosine, sine, ck, cv, kp, vp,
+            g, shards, prepared, cosine, sine, ck, cv, kp, vp,
             far[g], far_k, far_v, before, owns, backs,
         )
         owns.append(own)

time: 65.9 us -> 68.3 us (1.036)
  Pallas kernels: 27.3 us -> 30.7 us
  waiting for transfers between devices: 14.5 us -> 11.3 us
  local copies, waits for them, and re-layouts: 0.02 us -> 2.1 us
    ppermute x4, waiting for transfers between devices: 3.3 us -> 0.01 us  [ring(): lax.ppermute(x, 'seq', [(i, (i + s) % shards) for i in range(shards)])]
    pallas_call x4, Pallas kernels: 22.2 us -> 25.1 us  [attend(): pl.pallas_call(functools.partial(attend_kernel, g, shards), grid=(1,), in...]
    unnamed x8 -> x12, local copies, waits for them, and re-layouts: 0.02 us -> 2.1 us
  transfers between devices with their start and end apart: 13 -> 13, of which waited for: 7 -> 6; matrix products, arithmetic and copies ran while one was open for 1% -> 1% of each run, Pallas kernels for 32% -> 35%
where the time goes in v7:
time: 68.3 us; the launch traced here: 67.9 us
  Pallas kernels  30.7 us (45%)
  starting transfers between devices  21.7 us (32%)
  waiting for transfers between devices  11.3 us (17%)
  local copies, waits for them, and re-layouts  2.1 us (3%)
  between operations  1.46 us (2%)
    pallas_call x4, Pallas kernels, attend(): pl.pallas_call(functools.partial(attend_kernel, g, shards), grid=(1,), in...  25.1 us
    ppermute x5, waiting for transfers between devices, sum_but_last(): other = lax.ppermute(x, name, perm)  9.52 us
    ppermute x5, starting transfers between devices, sum_but_last(): other = lax.ppermute(x, name, perm)  8.37 us
    ppermute x2, starting transfers between devices, later(): return lax.ppermute(x, 'seq', [(i, i + s) for i in range(shards - s)])  6.18 us
    ppermute x4, starting transfers between devices, ring(): lax.ppermute(x, 'seq', [(i, (i + s) % shards) for i in range(shards)])  4.43 us
    pallas_call x1, Pallas kernels, prep(): pl.pallas_call(functools.partial(prep_kernel, tokens, shards), grid=(KV,)...  3.74 us
    ppermute x2, starting transfers between devices, earlier(): return lax.ppermute(x, 'seq', [(i + s, i) for i in range(shards - s)])  2.74 us
    unnamed x12, local copies, waits for them, and re-layouts  2.1 us
  transfers between devices with their start and end apart: 13, of which 6 were waited for; matrix products, arithmetic and copies ran while one was open for 1% of the time, Pallas kernels for 35%

profile of v7, /device:TPU:0, one launch (start us, length us, event | category | flops | bytes accessed | tf_op | source)
XLA Modules:
  0.0 67.9 jit_solution(7346838598256700264)
XLA Ops:
  0.6 4.9 %collective-permute-start.1 = (bf16[128,512]{1,0:T(8,128)(2,1)}, bf16[128,512]{1,0:T(8,128)(2,1)S(1)}, u32[]{:S(2)}, u32[]{:S(2)}) collective-permute-start(bf16[128,512]{1,0:T(8,128)(2,1)} %bitcast.33), channel_id=1, source_target_pairs={{0,1},{2,3},{4,5},{6,7},{8,9},{10,11},{12,13},{14,15},{16,17},{18,... | collective-permute-start | bytes 393224 | tf_op jit(solution)/shard_map/ppermute | solution.py:502
  5.5 1.3 %collective-permute-start.2 = (bf16[128,512]{1,0:T(8,128)(2,1)}, bf16[128,512]{1,0:T(8,128)(2,1)S(1)}, u32[]{:S(2)}, u32[]{:S(2)}) collective-permute-start(bf16[128,512]{1,0:T(8,128)(2,1)} %bitcast.38), channel_id=1, source_target_pairs={{0,1},{2,3},{4,5},{6,7},{8,9},{10,11},{12,13},{14,15},{16,17},{18,... | collective-permute-start | bytes 393224 | tf_op jit(solution)/shard_map/ppermute | solution.py:502
  6.8 0.0 copy-start.1
  6.8 0.0 copy-start.3
  6.9 1.1 %pack.1 = bf16[1024,128]{1,0:T(8,128)(2,1)S(1)} custom-call(bf16[512,512]{1,0:T(8,128)(2,1)} %bitcast.21, bf16[512,512]{1,0:T(8,128)(2,1)} %bitcast.27), custom_call_target="tpu_custom_call" | custom-call | bytes 524288 | tf_op jit(solution)/shard_map/pack/pallas_call | solution.py:59
  7.9 0.0 copy-start.4
  7.9 0.0 copy-start.5
  8.0 0.1 collective-permute-start.3
  8.7 0.1 convert_bitcast_fusion
  8.8 0.5 fusion
  9.3 0.0 copy-start
  9.3 1.0 %copy-done = bf16[1,512,512]{2,1,0:T(8,128)(2,1)S(1)} copy-done((bf16[1,512,512]{2,1,0:T(8,128)(2,1)S(1)}, bf16[1,512,512]{2,1,0:T(8,128)(2,1)}, u32[]{:S(2)}) %copy-start) | copy-done | bytes 524312
  10.4 0.0 copy-start.2
  10.4 1.0 %copy-done.2 = bf16[1,512,512]{2,1,0:T(8,128)(2,1)S(1)} copy-done((bf16[1,512,512]{2,1,0:T(8,128)(2,1)S(1)}, bf16[1,512,512]{2,1,0:T(8,128)(2,1)}, u32[]{:S(2)}) %copy-start.2) | copy-done | bytes 524312
  11.4 3.7 %prep.1 = (bf16[4096,128]{1,0:T(8,128)(2,1)S(1)}, bf16[4096,256]{1,0:T(8,128)(2,1)S(1)}, bf16[4096,128]{1,0:T(8,128)(2,1)S(1)}, bf16[2048,256]{1,0:T(8,128)(2,1)...) custom-call(s32[1]{0:T(128)} %copy.33.first_ref, ...), custom_call_target="tpu_custom_call" | custom-call | flops 2097152 | bytes 6291456 | tf_op jit(solution)/shard_map/prep/pallas_call | solution.py:162
  15.2 2.1 %collective-permute-start = (bf16[1024,128]{1,0:T(8,128)(2,1)S(1)}, bf16[1024,128]{1,0:T(8,128)(2,1)S(1)}, u32[]{:S(2)}, u32[]{:S(2)}) collective-permute-start(bf16[1024,128]{1,0:T(8,128)(2,1)S(1)} %get-tuple-element.57), channel_id=1, source_target_pairs={{0,1},{1,0},{2,3},{3,2},{4,5},{5,4},{6,7},{7,6},{8,9},{9,8},{10,11... | collective-permute-start | bytes 786440 | tf_op jit(solution)/shard_map/ppermute | solution.py:499
  17.2 0.0 collective-permute-done.1.refs_17_
  17.2 0.0 collective-permute-done.2.refs_18_
  17.3 0.0 collective-permute-done.3.refs_16_
  17.3 0.0 copy-done.1
  17.3 0.0 copy-done.3
  17.3 0.0 copy-done.4
  17.3 0.0 copy-done.5
  17.3 6.3 %attend.4 = (bf16[128,4096]{1,0:T(8,128)(2,1)}, bf16[128,4096]{1,0:T(8,128)(2,1)}, f32[40,128]{1,0:T(8,128)S(1)}, f32[2,128,128]{2,1,0:T(8,128)S(1)}, bf16[2,128...) custom-call(bf16[4096,128]{1,0:T(8,128)(2,1)S(1)} %get-tuple-element.47.refs_0_, ...), custom_call_target="tpu_custom_call" | custom-call | flops 1476395008 | bytes 2359296 | tf_op jit(solution)/shard_map/attend/pallas_call | solution.py:416
  23.6 2.3 %collective-permute-start.5 = (bf16[1024,128]{1,0:T(8,128)(2,1)S(1)}, bf16[1024,128]{1,0:T(8,128)(2,1)S(1)}, u32[]{:S(2)}, u32[]{:S(2)}) collective-permute-start(bf16[1024,128]{1,0:T(8,128)(2,1)S(1)} %get-tuple-element.63), channel_id=1, source_target_pairs={{0,1},{1,0},{2,3},{3,2},{4,5},{5,4},{6,7},{7,6},{8,9},{9,8},{10,11... | collective-permute-start | bytes 786440 | tf_op jit(solution)/shard_map/ppermute | solution.py:499
  25.9 0.0 collective-permute-done.refs_16_
  25.9 6.3 %attend.5 = (bf16[128,4096]{1,0:T(8,128)(2,1)}, bf16[128,4096]{1,0:T(8,128)(2,1)}, f32[40,128]{1,0:T(8,128)S(1)}, f32[2,128,128]{2,1,0:T(8,128)S(1)}, bf16[4,128...) custom-call(bf16[4096,128]{1,0:T(8,128)(2,1)S(1)} %get-tuple-element.47.refs, ...), custom_call_target="tpu_custom_call", output_to_operand_aliasing={{0}: (21, {}), {1}: (22, {})} | custom-call | flops 1476395008 | bytes 2359296 | tf_op jit(solution)/shard_map/attend/pallas_call | solution.py:416
  32.2 0.0 collective-permute-start.4
  32.2 1.5 %collective-permute-start.6 = (bf16[4,128,128]{2,1,0:T(8,128)(2,1)S(1)}, bf16[4,128,128]{2,1,0:T(8,128)(2,1)S(1)}, u32[]{:S(2)}, u32[]{:S(2)}) collective-permute-start(bf16[4,128,128]{2,1,0:T(8,128)(2,1)S(1)} %get-tuple-element.71), channel_id=1, source_target_pairs={{1,0},{3,2},{5,4},{7,6},{9,8},{11,10},{13,12},{15,14},{17,16},{19,... | collective-permute-start | bytes 393224 | tf_op jit(solution)/shard_map/ppermute | solution.py:505
  33.7 0.0 collective-permute-done.5.refs_16_
  33.7 6.3 %attend.6 = (bf16[128,4096]{1,0:T(8,128)(2,1)}, bf16[128,4096]{1,0:T(8,128)(2,1)}, f32[40,128]{1,0:T(8,128)S(1)}, f32[2,128,128]{2,1,0:T(8,128)S(1)}, bf16[2,128,128]{2,1,0:T(8,128)(2,1)S(1)}) custom-call(bf16[4096,128]{1,0:T(8,128)(2,1)S(1)} %get-tuple-element.47.refs_0_, ...), custom_call_target="tpu_custom_call", output_to_operand_aliasing={{0}: (20, {}), {1}: (21, {})} | custom-call | flops 1476395008 | bytes 2359296 | tf_op jit(solution)/shard_map/attend/pallas_call | solution.py:416
  39.9 1.8 %collective-permute-done.6.refs_23_ = bf16[4,128,128]{2,1,0:T(8,128)(2,1)S(1)} collective-permute-done((bf16[4,128,128]{2,1,0:T(8,128)(2,1)S(1)}, bf16[4,128,128]{2,1,0:T(8,128)(2,1)S(1)}, u32[]{:S(2)}, u32[]{:S(2)}) %collective-permute-start.6) | collective-permute-done | bytes 131104 | tf_op jit(solution)/shard_map/ppermute | solution.py:505
  41.7 0.0 collective-permute-done.4.refs_16_
  41.7 6.2 %attend.7 = (bf16[128,4096]{1,0:T(8,128)(2,1)}, bf16[128,4096]{1,0:T(8,128)(2,1)}, f32[40,128]{1,0:T(8,128)S(1)}, f32[2,128,128]{2,1,0:T(8,128)S(1)}, bf16[4,128...) custom-call(bf16[4096,128]{1,0:T(8,128)(2,1)S(1)} %get-tuple-element, ...), custom_call_target="tpu_custom_call", output_to_operand_aliasing={{0}: (24, {}), {1}: (25, {})} | custom-call | flops 1476395008 | bytes 2359296 | tf_op jit(solution)/shard_map/attend/pallas_call | solution.py:416
  47.9 1.3 %collective-permute-start.7 = (bf16[4,128,128]{2,1,0:T(8,128)(2,1)S(1)}, bf16[4,128,128]{2,1,0:T(8,128)(2,1)S(1)}, u32[]{:S(2)}, u32[]{:S(2)}) collective-permute-start(bf16[4,128,128]{2,1,0:T(8,128)(2,1)S(1)} %get-tuple-element.78), channel_id=1, source_target_pairs={{1,0},{3,2},{5,4},{7,6},{9,8},{11,10},{13,12},{15,14},{17,16},{19,... | collective-permute-start | bytes 393224 | tf_op jit(solution)/shard_map/ppermute | solution.py:505
  49.2 0.1 collective-permute-start.8
  49.3 1.2 %collective-permute-done.8 = f32[40,128]{1,0:T(8,128)S(1)} collective-permute-done((f32[40,128]{1,0:T(8,128)S(1)}, f32[40,128]{1,0:T(8,128)S(1)}, u32[]{:S(2)}, u32[]{:S(2)}) %collective-permute-start.8) | collective-permute-done | bytes 20512 | tf_op jit(solution)/shard_map/ppermute | solution.py:488
  50.5 1.5 %collective-permute-start.9 = (f32[40,128]{1,0:T(8,128)S(1)}, f32[40,128]{1,0:T(8,128)S(1)}, u32[]{:S(2)}, u32[]{:S(2)}) collective-permute-start(f32[40,128]{1,0:T(8,128)S(1)} %add.66), channel_id=1, source_target_pairs={{0,4},{2,6},{4,0},{6,2},{8,12},{10,14},{12,8},{14,10},{16,20},{18,... | collective-permute-start | bytes 61448 | tf_op jit(solution)/shard_map/ppermute | solution.py:488
  52.0 2.3 %collective-permute-done.9 = f32[40,128]{1,0:T(8,128)S(1)} collective-permute-done((f32[40,128]{1,0:T(8,128)S(1)}, f32[40,128]{1,0:T(8,128)S(1)}, u32[]{:S(2)}, u32[]{:S(2)}) %collective-permute-start.9) | collective-permute-done | bytes 20512 | tf_op jit(solution)/shard_map/ppermute | solution.py:488
  54.3 1.6 %collective-permute-start.10 = (f32[40,128]{1,0:T(8,128)S(1)}, f32[40,128]{1,0:T(8,128)S(1)}, u32[]{:S(2)}, u32[]{:S(2)}) collective-permute-start(f32[40,128]{1,0:T(8,128)S(1)} %add.67), channel_id=1, source_target_pairs={{0,8},{2,10},{4,12},{6,14},{8,0},{10,2},{12,4},{14,6},{16,24},{18,... | collective-permute-start | bytes 61448 | tf_op jit(solution)/shard_map/ppermute | solution.py:488
  55.9 2.2 %collective-permute-done.10 = f32[40,128]{1,0:T(8,128)S(1)} collective-permute-done((f32[40,128]{1,0:T(8,128)S(1)}, f32[40,128]{1,0:T(8,128)S(1)}, u32[]{:S(2)}, u32[]{:S(2)}) %collective-permute-start.10) | collective-permute-done | bytes 20512 | tf_op jit(solution)/shard_map/ppermute | solution.py:488
  58.1 2.6 %collective-permute-start.11 = (f32[40,128]{1,0:T(8,128)S(1)}, f32[40,128]{1,0:T(8,128)S(1)}, u32[]{:S(2)}, u32[]{:S(2)}) collective-permute-start(f32[40,128]{1,0:T(8,128)S(1)} %add.68), channel_id=1, source_target_pairs={{0,16},{2,18},{4,20},{6,22},{8,24},{10,26},{12,28},{14,30},{16,0},... | collective-permute-start | bytes 61448 | tf_op jit(solution)/shard_map/ppermute | solution.py:488
  60.7 2.1 %collective-permute-done.11 = f32[40,128]{1,0:T(8,128)S(1)} collective-permute-done((f32[40,128]{1,0:T(8,128)S(1)}, f32[40,128]{1,0:T(8,128)S(1)}, u32[]{:S(2)}, u32[]{:S(2)}) %collective-permute-start.11) | collective-permute-done | bytes 20512 | tf_op jit(solution)/shard_map/ppermute | solution.py:488
  62.7 2.6 %collective-permute-start.12 = (f32[40,128]{1,0:T(8,128)S(1)}, f32[40,128]{1,0:T(8,128)S(1)}, u32[]{:S(2)}, u32[]{:S(2)}) collective-permute-start(f32[40,128]{1,0:T(8,128)S(1)} %add.69.refs_5_), channel_id=1, source_target_pairs={{0,1},{1,0},{2,3},{3,2},{4,5},{5,4},{6,7},{7,6},{8,9},{9,8},{10,11... | collective-permute-start | bytes 61448 | tf_op jit(solution)/shard_map/ppermute | solution.py:488
  65.4 1.8 %collective-permute-done.12.refs_6_ = f32[40,128]{1,0:T(8,128)S(1)} collective-permute-done((f32[40,128]{1,0:T(8,128)S(1)}, f32[40,128]{1,0:T(8,128)S(1)}, u32[]{:S(2)}, u32[]{:S(2)}) %collective-permute-start.12) | collective-permute-done | bytes 20512 | tf_op jit(solution)/shard_map/ppermute | solution.py:488
  67.2 0.0 collective-permute-done.7.refs_4_
  67.2 0.7 %finish.1 = (bf16[128,512]{1,0:T(8,128)(2,1)}, bf16[128,512]{1,0:T(8,128)(2,1)}, f32[32,128]{1,0:T(8,128)}, f32[4,128]{1,0:T(4,128)}, f32[4,128]{1,0:T(4,128)}) custom-call(f32[256,128]{1,0:T(8,128)S(1)} %get-tuple-element.88.cos_ref.refs_10_.refs_0_, ...), custom_call_target="tpu_custom_call", output_to_operand_aliasing={{0}: (7, {}), {1}: (8, {})} | custom-call | bytes 524288 | tf_op jit(solution)/shard_map/finish/pallas_call | solution.py:461
  (6 shorter events, 0.0 us)
Async XLA Ops:
  0.6 16.6 %collective-permute-start.1 = (bf16[128,512]{1,0:T(8,128)(2,1)}, bf16[128,512]{1,0:T(8,128)(2,1)S(1)}, u32[]{:S(2)}, u32[]{:S(2)}) collective-permute-start(bf16[128,512]{1,0:T(8,128)(2,1)} %bitcast.33), channel_id=1, source_target_pairs={{0,1},{2,3},{4,5},{6,7},{8,9},{10,11},{12,13},{14,15},{16,17},{18,... | collective-permute-start | bytes 393224 | tf_op jit(solution)/shard_map/ppermute | solution.py:502
  5.5 11.7 %collective-permute-start.2 = (bf16[128,512]{1,0:T(8,128)(2,1)}, bf16[128,512]{1,0:T(8,128)(2,1)S(1)}, u32[]{:S(2)}, u32[]{:S(2)}) collective-permute-start(bf16[128,512]{1,0:T(8,128)(2,1)} %bitcast.38), channel_id=1, source_target_pairs={{0,1},{2,3},{4,5},{6,7},{8,9},{10,11},{12,13},{14,15},{16,17},{18,... | collective-permute-start | bytes 393224 | tf_op jit(solution)/shard_map/ppermute | solution.py:502
  6.8 10.4 %copy-start.1 = (bf16[1,512,512]{2,1,0:T(8,128)(2,1)S(1)}, bf16[1,512,512]{2,1,0:T(8,128)(2,1)}, u32[]{:S(2)}) copy-start(bf16[1,512,512]{2,1,0:T(8,128)(2,1)} %param.13) | copy-start | bytes 1572868
  6.8 10.4 %copy-start.3 = (bf16[1,512,512]{2,1,0:T(8,128)(2,1)S(1)}, bf16[1,512,512]{2,1,0:T(8,128)(2,1)}, u32[]{:S(2)}) copy-start(bf16[1,512,512]{2,1,0:T(8,128)(2,1)} %param.14) | copy-start | bytes 1572868
  7.9 9.4 %copy-start.4 = (bf16[1,128,512]{2,1,0:T(8,128)(2,1)S(1)}, bf16[1,128,512]{2,1,0:T(8,128)(2,1)}, u32[]{:S(2)}) copy-start(bf16[1,128,512]{2,1,0:T(8,128)(2,1)} %param.11) | copy-start | bytes 393220
  7.9 9.3 %copy-start.5 = (bf16[1,128,512]{2,1,0:T(8,128)(2,1)S(1)}, bf16[1,128,512]{2,1,0:T(8,128)(2,1)}, u32[]{:S(2)}) copy-start(bf16[1,128,512]{2,1,0:T(8,128)(2,1)} %param.12) | copy-start | bytes 393220
  8.0 9.3 %collective-permute-start.3 = (bf16[1024,128]{1,0:T(8,128)(2,1)S(1)}, bf16[1024,128]{1,0:T(8,128)(2,1)S(1)}, u32[]{:S(2)}, u32[]{:S(2)}) collective-permute-start(bf16[1024,128]{1,0:T(8,128)(2,1)S(1)} %pack.1), channel_id=1, source_target_pairs={{0,1},{1,0},{2,3},{3,2},{4,5},{5,4},{6,7},{7,6},{8,9},{9,8},{10,11... | collective-permute-start | bytes 786440 | tf_op jit(solution)/shard_map/ppermute | solution.py:499
  9.3 1.0 %copy-start = (bf16[1,512,512]{2,1,0:T(8,128)(2,1)S(1)}, bf16[1,512,512]{2,1,0:T(8,128)(2,1)}, u32[]{:S(2)}) copy-start(bf16[1,512,512]{2,1,0:T(8,128)(2,1)} %param.13) | copy-start | bytes 1572868
  10.4 1.0 %copy-start.2 = (bf16[1,512,512]{2,1,0:T(8,128)(2,1)S(1)}, bf16[1,512,512]{2,1,0:T(8,128)(2,1)}, u32[]{:S(2)}) copy-start(bf16[1,512,512]{2,1,0:T(8,128)(2,1)} %param.14) | copy-start | bytes 1572868
  15.2 10.7 %collective-permute-start = (bf16[1024,128]{1,0:T(8,128)(2,1)S(1)}, bf16[1024,128]{1,0:T(8,128)(2,1)S(1)}, u32[]{:S(2)}, u32[]{:S(2)}) collective-permute-start(bf16[1024,128]{1,0:T(8,128)(2,1)S(1)} %get-tuple-element.57), channel_id=1, source_target_pairs={{0,1},{1,0},{2,3},{3,2},{4,5},{5,4},{6,7},{7,6},{8,9},{9,8},{10,11... | collective-permute-start | bytes 786440 | tf_op jit(solution)/shard_map/ppermute | solution.py:499
  23.6 10.1 %collective-permute-start.5 = (bf16[1024,128]{1,0:T(8,128)(2,1)S(1)}, bf16[1024,128]{1,0:T(8,128)(2,1)S(1)}, u32[]{:S(2)}, u32[]{:S(2)}) collective-permute-start(bf16[1024,128]{1,0:T(8,128)(2,1)S(1)} %get-tuple-element.63), channel_id=1, source_target_pairs={{0,1},{1,0},{2,3},{3,2},{4,5},{5,4},{6,7},{7,6},{8,9},{9,8},{10,11... | collective-permute-start | bytes 786440 | tf_op jit(solution)/shard_map/ppermute | solution.py:499
  32.2 9.5 %collective-permute-start.4 = (bf16[1024,128]{1,0:T(8,128)(2,1)S(1)}, bf16[1024,128]{1,0:T(8,128)(2,1)S(1)}, u32[]{:S(2)}, u32[]{:S(2)}) collective-permute-start(bf16[1024,128]{1,0:T(8,128)(2,1)S(1)} %get-tuple-element.62), channel_id=1, source_target_pairs={{0,1},{1,0},{2,3},{3,2},{4,5},{5,4},{6,7},{7,6},{8,9},{9,8},{10,11... | collective-permute-start | bytes 786440 | tf_op jit(solution)/shard_map/ppermute | solution.py:499
  32.2 9.5 %collective-permute-start.6 = (bf16[4,128,128]{2,1,0:T(8,128)(2,1)S(1)}, bf16[4,128,128]{2,1,0:T(8,128)(2,1)S(1)}, u32[]{:S(2)}, u32[]{:S(2)}) collective-permute-start(bf16[4,128,128]{2,1,0:T(8,128)(2,1)S(1)} %get-tuple-element.71), channel_id=1, source_target_pairs={{1,0},{3,2},{5,4},{7,6},{9,8},{11,10},{13,12},{15,14},{17,16},{19,... | collective-permute-start | bytes 393224 | tf_op jit(solution)/shard_map/ppermute | solution.py:505
  47.9 19.2 %collective-permute-start.7 = (bf16[4,128,128]{2,1,0:T(8,128)(2,1)S(1)}, bf16[4,128,128]{2,1,0:T(8,128)(2,1)S(1)}, u32[]{:S(2)}, u32[]{:S(2)}) collective-permute-start(bf16[4,128,128]{2,1,0:T(8,128)(2,1)S(1)} %get-tuple-element.78), channel_id=1, source_target_pairs={{1,0},{3,2},{5,4},{7,6},{9,8},{11,10},{13,12},{15,14},{17,16},{19,... | collective-permute-start | bytes 393224 | tf_op jit(solution)/shard_map/ppermute | solution.py:505
  49.2 1.3 %collective-permute-start.8 = (f32[40,128]{1,0:T(8,128)S(1)}, f32[40,128]{1,0:T(8,128)S(1)}, u32[]{:S(2)}, u32[]{:S(2)}) collective-permute-start(f32[40,128]{1,0:T(8,128)S(1)} %get-tuple-element.79), channel_id=1, source_target_pairs={{0,2},{2,0},{4,6},{6,4},{8,10},{10,8},{12,14},{14,12},{16,18},{18,... | collective-permute-start | bytes 61448 | tf_op jit(solution)/shard_map/ppermute | solution.py:488
  50.5 3.8 %collective-permute-start.9 = (f32[40,128]{1,0:T(8,128)S(1)}, f32[40,128]{1,0:T(8,128)S(1)}, u32[]{:S(2)}, u32[]{:S(2)}) collective-permute-start(f32[40,128]{1,0:T(8,128)S(1)} %add.66), channel_id=1, source_target_pairs={{0,4},{2,6},{4,0},{6,2},{8,12},{10,14},{12,8},{14,10},{16,20},{18,... | collective-permute-start | bytes 61448 | tf_op jit(solution)/shard_map/ppermute | solution.py:488
  54.3 3.8 %collective-permute-start.10 = (f32[40,128]{1,0:T(8,128)S(1)}, f32[40,128]{1,0:T(8,128)S(1)}, u32[]{:S(2)}, u32[]{:S(2)}) collective-permute-start(f32[40,128]{1,0:T(8,128)S(1)} %add.67), channel_id=1, source_target_pairs={{0,8},{2,10},{4,12},{6,14},{8,0},{10,2},{12,4},{14,6},{16,24},{18,... | collective-permute-start | bytes 61448 | tf_op jit(solution)/shard_map/ppermute | solution.py:488
  58.1 4.7 %collective-permute-start.11 = (f32[40,128]{1,0:T(8,128)S(1)}, f32[40,128]{1,0:T(8,128)S(1)}, u32[]{:S(2)}, u32[]{:S(2)}) collective-permute-start(f32[40,128]{1,0:T(8,128)S(1)} %add.68), channel_id=1, source_target_pairs={{0,16},{2,18},{4,20},{6,22},{8,24},{10,26},{12,28},{14,30},{16,0},... | collective-permute-start | bytes 61448 | tf_op jit(solution)/shard_map/ppermute | solution.py:488
  62.7 4.4 %collective-permute-start.12 = (f32[40,128]{1,0:T(8,128)S(1)}, f32[40,128]{1,0:T(8,128)S(1)}, u32[]{:S(2)}, u32[]{:S(2)}) collective-permute-start(f32[40,128]{1,0:T(8,128)S(1)} %add.69.refs_5_), channel_id=1, source_target_pairs={{0,1},{1,0},{2,3},{3,2},{4,5},{5,4},{6,7},{7,6},{8,9},{9,8},{10,11... | collective-permute-start | bytes 61448 | tf_op jit(solution)/shard_map/ppermute | solution.py:488

commit v8 on v6

--- a/solution.py
+++ b/solution.py
@@ -150,14 +150,6 @@
     )(q, do, bq, bk, bv, cosine, sine, ck, cv)
 
 
-def alternate(first, second):
-    pieces = [iter(first), iter(second)]
-    while pieces:
-        for piece in list(pieces):
-            if next(piece, pieces) is pieces:
-                pieces.remove(piece)
-
-
 def fold(x, op):
     return op(x.reshape(x.shape[0] // 8, 8, x.shape[1]), axis=0)
 
@@ -255,20 +247,34 @@
                     self.top = jnp.maximum(self.top, fold(part, jnp.max))
                 yield
 
-        def softmax(self):
+        def exponents(self):
             top = jnp.max(self.top, axis=0, keepdims=True)
-            total_e = jnp.zeros((8, width), F32)
-            for start in blocks:
-                rows = pl.ds(start, tokens)
+            self.weight = jnp.zeros((8, width), F32)
+            for start in tiles:
+                rows = pl.ds(start, tile)
                 e = jnp.exp2((self.s[rows, :] - top) * (scale * math.log2(math.e)))
                 self.s[rows, :] = e
-                total_e = total_e + fold(e, jnp.sum)
+                self.weight = self.weight + fold(e, jnp.sum)
                 yield
-            self.inverse = 1.0 / jnp.sum(total_e, axis=0, keepdims=True)
-            for start in blocks:
-                rows = pl.ds(start, tokens)
-                self.pb[rows, :] = (self.s[rows, :] * self.inverse).astype(B16)
+
+        def probs(self):
+            inverse = 1.0 / jnp.sum(self.weight, axis=0, keepdims=True)
+            for start in tiles:
+                rows = pl.ds(start, tile)
+                p = self.s[rows, :] * inverse
+                self.s[rows, :] = p
+                self.pb[rows, :] = p.astype(B16)
                 yield
+
+        def output(self):
+            o = jnp.zeros((HD, width), F32)
+            for start in tiles:
+                rows = pl.ds(start, tile)
+                o = o + dot(values_t[:, rows], self.pb[rows, :], NN)
+                yield
+            self.o = o.astype(B16)
+            do = dot_ref[self.place, :].astype(F32)
+            self.delta = jnp.sum(do * self.o.astype(F32), axis=0, keepdims=True)
 
         def heads(self):
             for i in range(HEADS):
@@ -279,51 +285,52 @@
                     head,
                 )
 
-        def output(self):
-            o = dot(values_t[...], self.pb[...], NN).astype(B16)
-            do = dot_ref[self.place, :].astype(F32)
-            self.delta = jnp.sum(do * o.astype(F32), axis=0, keepdims=True)
-            yield
-            for part, cols, _ in self.heads():
-                out_ref[:, cols] = o[:, part].T
-            yield
-
-        def dscore(self):
+        def dscores(self):
             do = dot_ref[self.place, :]
             for start in tiles:
                 rows = pl.ds(start, tile)
                 dp = dot(values[rows, :], do, NN)
-                p = self.s[rows, :] * self.inverse
-                self.ds[rows, :] = (p * (dp - self.delta)).astype(B16)
+                self.ds[rows, :] = (self.s[rows, :] * (dp - self.delta)).astype(B16)
                 yield
 
-        def grads(self):
+        def query_grad(self):
+            dq = jnp.zeros((HD, width), F32)
+            for start in tiles:
+                rows = pl.ds(start, tile)
+                dq = dq + dot(keys_t[:, rows], self.ds[rows, :], NN)
+                yield
+            self.dq = (dq * scale).astype(B16).astype(F32)
+
+        def slab_grads(self):
             last = pl.ds(prefix, slab)
+            dv_acc[...] += dot(self.pb[last, :], dos_ref[self.rows, :], NN)
             dk_acc[...] += dot(self.ds[last, :], qs_ref[self.rows, :], NN)
-            dv_acc[...] += dot(self.pb[last, :], dos_ref[self.rows, :], NN)
-            yield
-            dq = (dot(keys_t[...], self.ds[...], NN) * scale).astype(B16).astype(F32)
-            yield
+
+        def store(self):
             for part, cols, head in self.heads():
-                x = dq[:, part]
+                out_ref[:, cols] = self.o[:, part].T
+                x = self.dq[:, part]
                 other = jnp.concatenate([x[HD // 2:], x[:HD // 2]], axis=0)
                 x = (x * cos_t_ref[...] - other * sin_t_ref[...]).T
                 gq_ref[:, cols] = x.astype(B16)
                 sums_ref[pl.ds(head, 1), :] = jnp.sum(x, axis=0, keepdims=True)
-            yield
+
+    def together(*works):
+        for _ in itertools.zip_longest(*works):
+            pass
 
     def pair(i, carry):
         index = g * (GROUP // HEADS) + 2 * i
         a, b = Chain(index, chains[0]), Chain(index + 1, chains[1])
-        for _ in a.scores():
-            pass
-        alternate(b.scores(), a.softmax())
-        alternate(itertools.chain(a.output(), a.dscore()), b.softmax())
-        alternate(b.output(), a.grads())
-        for _ in b.dscore():
-            pass
-        for _ in b.grads():
-            pass
+        together(a.scores())
+        together(b.scores(), a.exponents())
+        together(a.probs(), b.exponents(), a.output())
+        together(a.dscores(), b.probs(), a.query_grad(), b.output())
+        together(b.dscores(), b.query_grad())
+        a.slab_grads()
+        a.store()
+        b.slab_grads()
+        b.store()
         return carry
 
     lax.fori_loop(0, GROUP // (2 * HEADS), pair, 0)
@@ -420,20 +427,20 @@
 
 def finish_kernel(shards, *refs):
     owns, backs = refs[2:4], refs[4:4 + shards - 1]
-    sums = refs[4 + shards - 1]
+    sums = refs[4 + shards - 1:-7]
     gk_ref, gv_ref, *parts = refs[-5:]
     finish_heads(2, shards, refs[:2], owns, backs, gk_ref, gv_ref)
     start = 0
     for part in parts:
         rows = pl.ds(start, part.shape[0])
-        part[...] = sums[rows, :]
+        part[...] = add_up([ref[rows, :] for ref in sums])
         start += part.shape[0]
 
 
 def finish(shards, cosine, sine, owns, backs, sums, gk, gv):
     tokens = gk.shape[0]
     vmem = pl.BlockSpec(memory_space=pltpu.VMEM)
-    args = [cosine, sine, *owns, *backs, sums]
+    args = [cosine, sine, *owns, *backs, *sums]
     heads = [(HQ, HD), (KV, HD), (KV, HD)]
     return pl.pallas_call(
         functools.partial(finish_kernel, shards),
@@ -449,23 +456,23 @@
     )(*args, gk, gv)
 
 
-def sum_everywhere(x, axes):
+def add_up(parts):
+    while len(parts) > 1:
+        parts = [a + b for a, b in zip(parts[::2], parts[1::2])]
+    return parts[0]
+
+
+def sum_but_last(x, axes, near):
     devices = lax.axis_size(axes)
-    if devices & (devices - 1):
-        return lax.psum(x, axes)
-    stride = 1
-    while stride < devices:
-        size = min(devices // stride, 8)
-        groups = [
-            [base + low + i * stride for i in range(size)]
-            for base in range(0, devices, size * stride)
-            for low in range(stride)
-        ]
-        copies = jnp.broadcast_to(x[None], (size,) + x.shape)
-        got = lax.all_to_all(copies, axes, 0, 0, axis_index_groups=groups, tiled=True)
-        x = jnp.sum(got, axis=0)
-        stride *= size
-    return x
+    bits = [1 << i for i in range(devices.bit_length() - 1) if 1 << i != near]
+    stages = [[near]] + [bits[i:i + 2] for i in range(0, len(bits), 2)]
+    parts = [x]
+    for stage in stages:
+        x = add_up(parts)
+        parts = [x]
+        for flip in [sum(c) for n in (1, 2) for c in itertools.combinations(stage, n)]:
+            parts.append(lax.ppermute(x, axes, [(i, i ^ flip) for i in range(devices)]))
+    return parts
 
 
 def body(q_proj, k_proj, v_proj, cache_k, cache_v, bias_q, bias_k, bias_v, start, dout):
@@ -517,8 +524,8 @@
         if g % 2:
             backs = [earlier(x, s) for s, x in zip(shifts, before[3])]
     out, gq, sums, _ = before
-    sums = sum_everywhere(sums, ("dp", "seq"))
-    gk, gv, *sums = finish(shards, cosine, sine, owns[2:], backs, sums, *more)
+    parts = sum_but_last(sums, ("dp", "seq"), shards)
+    gk, gv, *sums = finish(shards, cosine, sine, owns[2:], backs, parts, *more)
     return (out[None], gq[None], gk[None], gv[None], *[x.reshape(-1) for x in sums])
 
 

time: 66.1 us -> 65.4 us (0.989)
  blocking collectives: 10.5 us -> 0 us
  starting transfers between devices: 16.8 us -> 21.5 us
  Pallas kernels: 27.4 us -> 30.5 us
  waiting for transfers between devices: 8.27 us -> 11 us
  local copies, waits for them, and re-layouts: 0.72 us -> 0.02 us
    all_to_all x1 -> x0, blocking collectives: 10.5 us -> none  [sum_everywhere(): lax.all_to_all(copies, axes, 0, 0, axis_index_groups=groups, tiled=True)]
    ppermute x0 -> x7, starting transfers between devices: none -> 7.94 us  [sum_but_last(): parts.append(lax.ppermute(x, axes, [(i, i ^ flip) for i in range(devices)]))]
    ppermute x0 -> x7, waiting for transfers between devices: none -> 7.39 us  [sum_but_last(): parts.append(lax.ppermute(x, axes, [(i, i ^ flip) for i in range(devices)]))]
    all_to_all x1 -> x0, waiting for transfers between devices: 3.66 us -> none  [sum_everywhere(): lax.all_to_all(copies, axes, 0, 0, axis_index_groups=groups, tiled=True)]
    all_to_all x1 -> x0, starting transfers between devices: 3.38 us -> none  [sum_everywhere(): lax.all_to_all(copies, axes, 0, 0, axis_index_groups=groups, tiled=True)]
    pallas_call x4, Pallas kernels: 21.8 us -> 24.9 us  [attend(): pl.pallas_call(functools.partial(attend_kernel, g, shards), grid=(1,), in...]
    ppermute x2, waiting for transfers between devices: 1.77 us -> 0.8 us  [earlier(): return lax.ppermute(x, 'seq', [(i + s, i) for i in range(shards - s)])]
    broadcast_in_dim x2 -> x0, local copies, waits for them, and re-layouts: 0.69 us -> none  [sum_everywhere(): copies = jnp.broadcast_to(x[None], (size,) + x.shape)]
  transfers between devices with their start and end apart: 9 -> 15, of which waited for: 3 -> 7; matrix products, arithmetic and copies ran while one was open for 1% -> 1% of each run, Pallas kernels for 32% -> 36%
where the time goes in v8:
time: 65.4 us; the launch traced here: 65.1 us
  Pallas kernels  30.5 us (47%)
  starting transfers between devices  21.5 us (33%)
  waiting for transfers between devices  11 us (17%)
  between operations  1.44 us (2%)
    pallas_call x4, Pallas kernels, attend(): pl.pallas_call(functools.partial(attend_kernel, g, shards), grid=(1,), in...  24.9 us
    ppermute x7, starting transfers between devices, sum_but_last(): parts.append(lax.ppermute(x, axes, [(i, i ^ flip) for i in range(devices)]))  7.94 us
    ppermute x7, waiting for transfers between devices, sum_but_last(): parts.append(lax.ppermute(x, axes, [(i, i ^ flip) for i in range(devices)]))  7.39 us
    ppermute x2, starting transfers between devices, later(): return lax.ppermute(x, 'seq', [(i, i + s) for i in range(shards - s)])  6.18 us
    ppermute x4, starting transfers between devices, ring(): lax.ppermute(x, 'seq', [(i, (i + s) % shards) for i in range(shards)])  4.67 us
    pallas_call x1, Pallas kernels, prep(): pl.pallas_call(functools.partial(prep_kernel, tokens), grid=(KV,), in_spe...  3.77 us
    ppermute x4, waiting for transfers between devices, ring(): lax.ppermute(x, 'seq', [(i, (i + s) % shards) for i in range(shards)])  2.83 us
    ppermute x2, starting transfers between devices, earlier(): return lax.ppermute(x, 'seq', [(i + s, i) for i in range(shards - s)])  2.74 us
  transfers between devices with their start and end apart: 15, of which 7 were waited for; matrix products, arithmetic and copies ran while one was open for 1% of the time, Pallas kernels for 36%

profile of v8, /device:TPU:0, one launch (start us, length us, event | category | flops | bytes accessed | tf_op | source)
XLA Modules:
  0.0 65.1 jit_solution(1010468917012446725)
XLA Ops:
  0.6 4.9 %collective-permute-start.1 = (bf16[128,512]{1,0:T(8,128)(2,1)}, bf16[128,512]{1,0:T(8,128)(2,1)S(1)}, u32[]{:S(2)}, u32[]{:S(2)}) collective-permute-start(bf16[128,512]{1,0:T(8,128)(2,1)} %bitcast.33), channel_id=1, source_target_pairs={{0,1},{2,3},{4,5},{6,7},{8,9},{10,11},{12,13},{14,15},{16,17},{18,... | collective-permute-start | bytes 393224 | tf_op jit(solution)/shard_map/ppermute | solution.py:488
  5.5 1.3 %collective-permute-start.2 = (bf16[128,512]{1,0:T(8,128)(2,1)}, bf16[128,512]{1,0:T(8,128)(2,1)S(1)}, u32[]{:S(2)}, u32[]{:S(2)}) collective-permute-start(bf16[128,512]{1,0:T(8,128)(2,1)} %bitcast.38), channel_id=1, source_target_pairs={{0,1},{2,3},{4,5},{6,7},{8,9},{10,11},{12,13},{14,15},{16,17},{18,... | collective-permute-start | bytes 393224 | tf_op jit(solution)/shard_map/ppermute | solution.py:488
  6.8 0.0 copy-start
  6.8 0.0 copy-start.1
  6.8 1.1 %pack.1 = bf16[1024,128]{1,0:T(8,128)(2,1)S(1)} custom-call(bf16[512,512]{1,0:T(8,128)(2,1)} %bitcast.21, bf16[512,512]{1,0:T(8,128)(2,1)} %bitcast.27), custom_call_target="tpu_custom_call" | custom-call | bytes 524288 | tf_op jit(solution)/shard_map/pack/pallas_call | solution.py:59
  7.9 0.1 collective-permute-start.3
  8.7 0.1 convert_bitcast_fusion
  8.8 0.5 fusion
  9.3 0.0 copy-done
  9.3 0.0 copy-done.1
  9.3 0.0 copy-start.2
  9.3 0.0 copy-start.3
  9.4 3.8 %prep.1 = (bf16[4096,128]{1,0:T(8,128)(2,1)S(1)}, bf16[2048,256]{1,0:T(8,128)(2,1)S(1)}, bf16[4096,128]{1,0:T(8,128)(2,1)S(1)}, bf16[2048,256]{1,0:T(8,128)(2,1)...) custom-call(bf16[128,4096]{1,0:T(8,128)(2,1)} %bitcast.45, ...), custom_call_target="tpu_custom_call" | custom-call | flops 2097152 | bytes 6291456 | tf_op jit(solution)/shard_map/prep/pallas_call | solution.py:136
  13.1 2.1 %collective-permute-start = (bf16[1024,128]{1,0:T(8,128)(2,1)S(1)}, bf16[1024,128]{1,0:T(8,128)(2,1)S(1)}, u32[]{:S(2)}, u32[]{:S(2)}) collective-permute-start(bf16[1024,128]{1,0:T(8,128)(2,1)S(1)} %get-tuple-element.55), channel_id=1, source_target_pairs={{0,1},{1,0},{2,3},{3,2},{4,5},{5,4},{6,7},{7,6},{8,9},{9,8},{10,11... | collective-permute-start | bytes 786440 | tf_op jit(solution)/shard_map/ppermute | solution.py:485
  15.2 0.0 collective-permute-done.1.refs_18_
  15.2 0.0 collective-permute-done.2.refs_19_
  15.2 2.8 %collective-permute-done.3.refs_17_ = bf16[1024,128]{1,0:T(8,128)(2,1)S(1)} collective-permute-done((bf16[1024,128]{1,0:T(8,128)(2,1)S(1)}, bf16[1024,128]{1,0:T(8,128)(2,1)S(1)}, u32[]{:S(2)}, u32[]{:S(2)}) %collective-permute-start.3) | collective-permute-done | bytes 262176 | tf_op jit(solution)/shard_map/ppermute | solution.py:485
  18.0 0.0 copy-done.2
  18.0 0.0 copy-done.3
  18.0 6.2 %attend.4 = (bf16[128,4096]{1,0:T(8,128)(2,1)}, bf16[128,4096]{1,0:T(8,128)(2,1)}, f32[40,128]{1,0:T(8,128)S(1)}, f32[2,128,128]{2,1,0:T(8,128)S(1)}, bf16[2,128...) custom-call(s32[1]{0:T(128)} %copy.33.refs_0_, s32[1]{0:T(128)} %bitcast.refs_1_, ...), custom_call_target="tpu_custom_call" | custom-call | flops 1476395008 | bytes 2359296 | tf_op jit(solution)/shard_map/attend/pallas_call | solution.py:401
  24.2 2.5 %collective-permute-start.5 = (bf16[1024,128]{1,0:T(8,128)(2,1)S(1)}, bf16[1024,128]{1,0:T(8,128)(2,1)S(1)}, u32[]{:S(2)}, u32[]{:S(2)}) collective-permute-start(bf16[1024,128]{1,0:T(8,128)(2,1)S(1)} %get-tuple-element.61), channel_id=1, source_target_pairs={{0,1},{1,0},{2,3},{3,2},{4,5},{5,4},{6,7},{7,6},{8,9},{9,8},{10,11... | collective-permute-start | bytes 786440 | tf_op jit(solution)/shard_map/ppermute | solution.py:485
  26.7 0.0 collective-permute-done.refs_17_
  26.7 6.2 %attend.5 = (bf16[128,4096]{1,0:T(8,128)(2,1)}, bf16[128,4096]{1,0:T(8,128)(2,1)}, f32[40,128]{1,0:T(8,128)S(1)}, f32[2,128,128]{2,1,0:T(8,128)S(1)}, bf16[4,128...) custom-call(s32[1]{0:T(128)} %copy.33.refs_0_, ...), custom_call_target="tpu_custom_call", output_to_operand_aliasing={{0}: (22, {}), {1}: (23, {})} | custom-call | flops 1476395008 | bytes 2359296 | tf_op jit(solution)/shard_map/attend/pallas_call | solution.py:401
  32.9 0.0 collective-permute-start.4
  33.0 1.5 %collective-permute-start.6 = (bf16[4,128,128]{2,1,0:T(8,128)(2,1)S(1)}, bf16[4,128,128]{2,1,0:T(8,128)(2,1)S(1)}, u32[]{:S(2)}, u32[]{:S(2)}) collective-permute-start(bf16[4,128,128]{2,1,0:T(8,128)(2,1)S(1)} %get-tuple-element.69), channel_id=1, source_target_pairs={{1,0},{3,2},{5,4},{7,6},{9,8},{11,10},{13,12},{15,14},{17,16},{19,... | collective-permute-start | bytes 393224 | tf_op jit(solution)/shard_map/ppermute | solution.py:491
  34.5 0.0 collective-permute-done.5.refs_17_
  34.5 6.3 %attend.6 = (bf16[128,4096]{1,0:T(8,128)(2,1)}, bf16[128,4096]{1,0:T(8,128)(2,1)}, f32[40,128]{1,0:T(8,128)S(1)}, f32[2,128,128]{2,1,0:T(8,128)S(1)}, bf16[2,128,128]{2,1,0:T(8,128)(2,1)S(1)}) custom-call(s32[1]{0:T(128)} %copy.33.refs_0_, s32[1]{0:T(128)} %bitcast.refs_1_, ...), custom_call_target="tpu_custom_call", output_to_operand_aliasing={{0}: (21, {}), {1}: (22, {})} | custom-call | flops 1476395008 | bytes 2359296 | tf_op jit(solution)/shard_map/attend/pallas_call | solution.py:401
  40.7 0.8 %collective-permute-done.6.refs_24_ = bf16[4,128,128]{2,1,0:T(8,128)(2,1)S(1)} collective-permute-done((bf16[4,128,128]{2,1,0:T(8,128)(2,1)S(1)}, bf16[4,128,128]{2,1,0:T(8,128)(2,1)S(1)}, u32[]{:S(2)}, u32[]{:S(2)}) %collective-permute-start.6) | collective-permute-done | bytes 131104 | tf_op jit(solution)/shard_map/ppermute | solution.py:491
  41.5 0.0 collective-permute-done.4.refs_17_
  41.5 6.2 %attend.7 = (bf16[128,4096]{1,0:T(8,128)(2,1)}, bf16[128,4096]{1,0:T(8,128)(2,1)}, f32[40,128]{1,0:T(8,128)S(1)}, f32[2,128,128]{2,1,0:T(8,128)S(1)}, bf16[4,128...) custom-call(s32[1]{0:T(128)} %copy.33.refs_0_, ...), custom_call_target="tpu_custom_call", output_to_operand_aliasing={{0}: (25, {}), {1}: (26, {})} | custom-call | flops 1476395008 | bytes 2359296 | tf_op jit(solution)/shard_map/attend/pallas_call | solution.py:401
  47.8 0.0 collective-permute-start.8
  47.8 1.2 %collective-permute-done.8 = f32[40,128]{1,0:T(8,128)S(1)} collective-permute-done((f32[40,128]{1,0:T(8,128)S(1)}, f32[40,128]{1,0:T(8,128)S(1)}, u32[]{:S(2)}, u32[]{:S(2)}) %collective-permute-start.8) | collective-permute-done | bytes 20512 | tf_op jit(solution)/shard_map/ppermute | solution.py:474
  48.9 2.8 %collective-permute-start.11 = (f32[40,128]{1,0:T(8,128)S(1)}, f32[40,128]{1,0:T(8,128)S(1)}, u32[]{:S(2)}, u32[]{:S(2)}) collective-permute-start(f32[40,128]{1,0:T(8,128)S(1)} %add.66), channel_id=1, source_target_pairs={{0,5},{1,4},{2,7},{3,6},{4,1},{5,0},{6,3},{7,2},{8,13},{9,12},{10,... | collective-permute-start | bytes 61448 | tf_op jit(solution)/shard_map/ppermute | solution.py:474
  51.7 0.5 collective-permute-start.10
  52.3 0.2 collective-permute-start.9
  52.4 1.3 %collective-permute-start.7 = (bf16[4,128,128]{2,1,0:T(8,128)(2,1)S(1)}, bf16[4,128,128]{2,1,0:T(8,128)(2,1)S(1)}, u32[]{:S(2)}, u32[]{:S(2)}) collective-permute-start(bf16[4,128,128]{2,1,0:T(8,128)(2,1)S(1)} %get-tuple-element.76), channel_id=1, source_target_pairs={{1,0},{3,2},{5,4},{7,6},{9,8},{11,10},{13,12},{15,14},{17,16},{19,... | collective-permute-start | bytes 393224 | tf_op jit(solution)/shard_map/ppermute | solution.py:491
  53.7 0.0 collective-permute-done.11
  53.7 1.8 %collective-permute-done.10 = f32[40,128]{1,0:T(8,128)S(1)} collective-permute-done((f32[40,128]{1,0:T(8,128)S(1)}, f32[40,128]{1,0:T(8,128)S(1)}, u32[]{:S(2)}, u32[]{:S(2)}) %collective-permute-start.10) | collective-permute-done | bytes 20512 | tf_op jit(solution)/shard_map/ppermute | solution.py:474
  55.5 0.5 collective-permute-done.9
  56.1 3.7 %collective-permute-start.14 = (f32[40,128]{1,0:T(8,128)S(1)}, f32[40,128]{1,0:T(8,128)S(1)}, u32[]{:S(2)}, u32[]{:S(2)}) collective-permute-start(f32[40,128]{1,0:T(8,128)S(1)} %add_add_fusion.refs_5_), channel_id=1, source_target_pairs={{0,24},{1,25},{2,26},{3,27},{4,28},{5,29},{6,30},{7,31},{8,16},{9,... | collective-permute-start | bytes 61448 | tf_op jit(solution)/shard_map/ppermute | solution.py:474
  59.7 0.0 collective-permute-start.13
  59.7 0.8 %collective-permute-start.12 = (f32[40,128]{1,0:T(8,128)S(1)}, f32[40,128]{1,0:T(8,128)S(1)}, u32[]{:S(2)}, u32[]{:S(2)}) collective-permute-start(f32[40,128]{1,0:T(8,128)S(1)} %add_add_fusion.refs_5_), channel_id=1, source_target_pairs={{0,8},{1,9},{2,10},{3,11},{4,12},{5,13},{6,14},{7,15},{8,0},{9,1},... | collective-permute-start | bytes 61448 | tf_op jit(solution)/shard_map/ppermute | solution.py:474
  60.5 1.3 %collective-permute-done.14.refs_8_ = f32[40,128]{1,0:T(8,128)S(1)} collective-permute-done((f32[40,128]{1,0:T(8,128)S(1)}, f32[40,128]{1,0:T(8,128)S(1)}, u32[]{:S(2)}, u32[]{:S(2)}) %collective-permute-start.14) | collective-permute-done | bytes 20512 | tf_op jit(solution)/shard_map/ppermute | solution.py:474
  61.8 2.6 %collective-permute-done.13.refs_7_ = f32[40,128]{1,0:T(8,128)S(1)} collective-permute-done((f32[40,128]{1,0:T(8,128)S(1)}, f32[40,128]{1,0:T(8,128)S(1)}, u32[]{:S(2)}, u32[]{:S(2)}) %collective-permute-start.13) | collective-permute-done | bytes 20512 | tf_op jit(solution)/shard_map/ppermute | solution.py:474
  64.4 0.0 collective-permute-done.12.refs_6_
  64.4 0.0 collective-permute-done.7.refs_4_
  64.4 0.7 %finish.1 = (bf16[128,512]{1,0:T(8,128)(2,1)}, bf16[128,512]{1,0:T(8,128)(2,1)}, f32[32,128]{1,0:T(8,128)}, f32[4,128]{1,0:T(4,128)}, f32[4,128]{1,0:T(4,128)}) custom-call(f32[256,128]{1,0:T(8,128)S(1)} %get-tuple-element.86.cos_ref.refs_11_.refs_0_, ...), custom_call_target="tpu_custom_call", output_to_operand_aliasing={{0}: (9, {}), {1}: (10, {})} | custom-call | bytes 524288 | tf_op jit(solution)/shard_map/finish/pallas_call | solution.py:445
  (4 shorter events, 0.0 us)
Async XLA Ops:
  0.6 14.6 %collective-permute-start.1 = (bf16[128,512]{1,0:T(8,128)(2,1)}, bf16[128,512]{1,0:T(8,128)(2,1)S(1)}, u32[]{:S(2)}, u32[]{:S(2)}) collective-permute-start(bf16[128,512]{1,0:T(8,128)(2,1)} %bitcast.33), channel_id=1, source_target_pairs={{0,1},{2,3},{4,5},{6,7},{8,9},{10,11},{12,13},{14,15},{16,17},{18,... | collective-permute-start | bytes 393224 | tf_op jit(solution)/shard_map/ppermute | solution.py:488
  5.5 9.7 %collective-permute-start.2 = (bf16[128,512]{1,0:T(8,128)(2,1)}, bf16[128,512]{1,0:T(8,128)(2,1)S(1)}, u32[]{:S(2)}, u32[]{:S(2)}) collective-permute-start(bf16[128,512]{1,0:T(8,128)(2,1)} %bitcast.38), channel_id=1, source_target_pairs={{0,1},{2,3},{4,5},{6,7},{8,9},{10,11},{12,13},{14,15},{16,17},{18,... | collective-permute-start | bytes 393224 | tf_op jit(solution)/shard_map/ppermute | solution.py:488
  6.8 2.5 %copy-start = (bf16[1,512,512]{2,1,0:T(8,128)(2,1)S(1)}, bf16[1,512,512]{2,1,0:T(8,128)(2,1)}, u32[]{:S(2)}) copy-start(bf16[1,512,512]{2,1,0:T(8,128)(2,1)} %param.13) | copy-start | bytes 1572868
  6.8 2.5 %copy-start.1 = (bf16[1,512,512]{2,1,0:T(8,128)(2,1)S(1)}, bf16[1,512,512]{2,1,0:T(8,128)(2,1)}, u32[]{:S(2)}) copy-start(bf16[1,512,512]{2,1,0:T(8,128)(2,1)} %param.14) | copy-start | bytes 1572868
  7.9 10.1 %collective-permute-start.3 = (bf16[1024,128]{1,0:T(8,128)(2,1)S(1)}, bf16[1024,128]{1,0:T(8,128)(2,1)S(1)}, u32[]{:S(2)}, u32[]{:S(2)}) collective-permute-start(bf16[1024,128]{1,0:T(8,128)(2,1)S(1)} %pack.1), channel_id=1, source_target_pairs={{0,1},{1,0},{2,3},{3,2},{4,5},{5,4},{6,7},{7,6},{8,9},{9,8},{10,11... | collective-permute-start | bytes 786440 | tf_op jit(solution)/shard_map/ppermute | solution.py:485
  9.3 8.7 %copy-start.2 = (bf16[1,128,512]{2,1,0:T(8,128)(2,1)S(1)}, bf16[1,128,512]{2,1,0:T(8,128)(2,1)}, u32[]{:S(2)}) copy-start(bf16[1,128,512]{2,1,0:T(8,128)(2,1)} %param.11) | copy-start | bytes 393220
  9.3 8.7 %copy-start.3 = (bf16[1,128,512]{2,1,0:T(8,128)(2,1)S(1)}, bf16[1,128,512]{2,1,0:T(8,128)(2,1)}, u32[]{:S(2)}) copy-start(bf16[1,128,512]{2,1,0:T(8,128)(2,1)} %param.12) | copy-start | bytes 393220
  13.1 13.6 %collective-permute-start = (bf16[1024,128]{1,0:T(8,128)(2,1)S(1)}, bf16[1024,128]{1,0:T(8,128)(2,1)S(1)}, u32[]{:S(2)}, u32[]{:S(2)}) collective-permute-start(bf16[1024,128]{1,0:T(8,128)(2,1)S(1)} %get-tuple-element.55), channel_id=1, source_target_pairs={{0,1},{1,0},{2,3},{3,2},{4,5},{5,4},{6,7},{7,6},{8,9},{9,8},{10,11... | collective-permute-start | bytes 786440 | tf_op jit(solution)/shard_map/ppermute | solution.py:485
  24.2 10.2 %collective-permute-start.5 = (bf16[1024,128]{1,0:T(8,128)(2,1)S(1)}, bf16[1024,128]{1,0:T(8,128)(2,1)S(1)}, u32[]{:S(2)}, u32[]{:S(2)}) collective-permute-start(bf16[1024,128]{1,0:T(8,128)(2,1)S(1)} %get-tuple-element.61), channel_id=1, source_target_pairs={{0,1},{1,0},{2,3},{3,2},{4,5},{5,4},{6,7},{7,6},{8,9},{9,8},{10,11... | collective-permute-start | bytes 786440 | tf_op jit(solution)/shard_map/ppermute | solution.py:485
  32.9 8.6 %collective-permute-start.4 = (bf16[1024,128]{1,0:T(8,128)(2,1)S(1)}, bf16[1024,128]{1,0:T(8,128)(2,1)S(1)}, u32[]{:S(2)}, u32[]{:S(2)}) collective-permute-start(bf16[1024,128]{1,0:T(8,128)(2,1)S(1)} %get-tuple-element.60), channel_id=1, source_target_pairs={{0,1},{1,0},{2,3},{3,2},{4,5},{5,4},{6,7},{7,6},{8,9},{9,8},{10,11... | collective-permute-start | bytes 786440 | tf_op jit(solution)/shard_map/ppermute | solution.py:485
  33.0 8.5 %collective-permute-start.6 = (bf16[4,128,128]{2,1,0:T(8,128)(2,1)S(1)}, bf16[4,128,128]{2,1,0:T(8,128)(2,1)S(1)}, u32[]{:S(2)}, u32[]{:S(2)}) collective-permute-start(bf16[4,128,128]{2,1,0:T(8,128)(2,1)S(1)} %get-tuple-element.69), channel_id=1, source_target_pairs={{1,0},{3,2},{5,4},{7,6},{9,8},{11,10},{13,12},{15,14},{17,16},{19,... | collective-permute-start | bytes 393224 | tf_op jit(solution)/shard_map/ppermute | solution.py:491
  47.8 1.2 %collective-permute-start.8 = (f32[40,128]{1,0:T(8,128)S(1)}, f32[40,128]{1,0:T(8,128)S(1)}, u32[]{:S(2)}, u32[]{:S(2)}) collective-permute-start(f32[40,128]{1,0:T(8,128)S(1)} %get-tuple-element.77), channel_id=1, source_target_pairs={{0,2},{1,3},{2,0},{3,1},{4,6},{5,7},{6,4},{7,5},{8,10},{9,11},{10,... | collective-permute-start | bytes 61448 | tf_op jit(solution)/shard_map/ppermute | solution.py:474
  48.9 4.8 %collective-permute-start.11 = (f32[40,128]{1,0:T(8,128)S(1)}, f32[40,128]{1,0:T(8,128)S(1)}, u32[]{:S(2)}, u32[]{:S(2)}) collective-permute-start(f32[40,128]{1,0:T(8,128)S(1)} %add.66), channel_id=1, source_target_pairs={{0,5},{1,4},{2,7},{3,6},{4,1},{5,0},{6,3},{7,2},{8,13},{9,12},{10,... | collective-permute-start | bytes 61448 | tf_op jit(solution)/shard_map/ppermute | solution.py:474
  51.7 3.8 %collective-permute-start.10 = (f32[40,128]{1,0:T(8,128)S(1)}, f32[40,128]{1,0:T(8,128)S(1)}, u32[]{:S(2)}, u32[]{:S(2)}) collective-permute-start(f32[40,128]{1,0:T(8,128)S(1)} %add.66), channel_id=1, source_target_pairs={{0,4},{1,5},{2,6},{3,7},{4,0},{5,1},{6,2},{7,3},{8,12},{9,13},{10,... | collective-permute-start | bytes 61448 | tf_op jit(solution)/shard_map/ppermute | solution.py:474
  52.3 3.8 %collective-permute-start.9 = (f32[40,128]{1,0:T(8,128)S(1)}, f32[40,128]{1,0:T(8,128)S(1)}, u32[]{:S(2)}, u32[]{:S(2)}) collective-permute-start(f32[40,128]{1,0:T(8,128)S(1)} %add.66), channel_id=1, source_target_pairs={{0,1},{1,0},{2,3},{3,2},{4,5},{5,4},{6,7},{7,6},{8,9},{9,8},{10,11... | collective-permute-start | bytes 61448 | tf_op jit(solution)/shard_map/ppermute | solution.py:474
  52.4 12.0 %collective-permute-start.7 = (bf16[4,128,128]{2,1,0:T(8,128)(2,1)S(1)}, bf16[4,128,128]{2,1,0:T(8,128)(2,1)S(1)}, u32[]{:S(2)}, u32[]{:S(2)}) collective-permute-start(bf16[4,128,128]{2,1,0:T(8,128)(2,1)S(1)} %get-tuple-element.76), channel_id=1, source_target_pairs={{1,0},{3,2},{5,4},{7,6},{9,8},{11,10},{13,12},{15,14},{17,16},{19,... | collective-permute-start | bytes 393224 | tf_op jit(solution)/shard_map/ppermute | solution.py:491
  56.1 5.7 %collective-permute-start.14 = (f32[40,128]{1,0:T(8,128)S(1)}, f32[40,128]{1,0:T(8,128)S(1)}, u32[]{:S(2)}, u32[]{:S(2)}) collective-permute-start(f32[40,128]{1,0:T(8,128)S(1)} %add_add_fusion.refs_5_), channel_id=1, source_target_pairs={{0,24},{1,25},{2,26},{3,27},{4,28},{5,29},{6,30},{7,31},{8,16},{9,... | collective-permute-start | bytes 61448 | tf_op jit(solution)/shard_map/ppermute | solution.py:474
  59.7 4.7 %collective-permute-start.13 = (f32[40,128]{1,0:T(8,128)S(1)}, f32[40,128]{1,0:T(8,128)S(1)}, u32[]{:S(2)}, u32[]{:S(2)}) collective-permute-start(f32[40,128]{1,0:T(8,128)S(1)} %add_add_fusion.refs_5_), channel_id=1, source_target_pairs={{0,16},{1,17},{2,18},{3,19},{4,20},{5,21},{6,22},{7,23},{8,24},{9,... | collective-permute-start | bytes 61448 | tf_op jit(solution)/shard_map/ppermute | solution.py:474
  59.7 4.7 %collective-permute-start.12 = (f32[40,128]{1,0:T(8,128)S(1)}, f32[40,128]{1,0:T(8,128)S(1)}, u32[]{:S(2)}, u32[]{:S(2)}) collective-permute-start(f32[40,128]{1,0:T(8,128)S(1)} %add_add_fusion.refs_5_), channel_id=1, source_target_pairs={{0,8},{1,9},{2,10},{3,11},{4,12},{5,13},{6,14},{7,15},{8,0},{9,1},... | collective-permute-start | bytes 61448 | tf_op jit(solution)/shard_map/ppermute | solution.py:474

commit v9 on v8

--- a/solution.py
+++ b/solution.py
@@ -13,7 +13,7 @@
 KV = 4
 HD = 128
 GROUP = 8
-HEADS = 2
+HEADS = 4
 NEG = -1e30
 SUMS = HQ + 2 * KV
 VMEM = 28 * 1024 * 1024
@@ -178,7 +178,7 @@
     pack_ref = take(1)[0] if g + 2 < KV else None
     gk_ref, gv_ref = take(2) if g == KV - 1 else (None, None)
     keys, values, keys_t, values_t, dk_acc, dv_acc = take(6)
-    chains = [take(3), take(3)]
+    scratch = take(3)
     tokens = kp_ref.shape[0]
     slots = ck_ref.shape[0]
     prefix = shards * slots
@@ -216,9 +216,6 @@
     width = HEADS * tokens
     scale = HD ** -0.5
     blocks = range(0, total, tokens)
-    tile = 2 * tokens
-    tiles = range(0, total, tile)
-
     def allowed(start, s):
         row = lax.broadcasted_iota(jnp.int32, s.shape, 0)
         if start < prefix:
@@ -229,7 +226,7 @@
         return row < jnp.where(rank >= (start - prefix) // tokens, tokens, 0)
 
     class Chain:
-        def __init__(self, index, scratch):
+        def __init__(self, index):
             self.index = index
             self.s, self.pb, self.ds = scratch
             self.rows = pl.ds(pl.multiple_of(index * width, width), width)
@@ -237,42 +234,30 @@
             self.top = jnp.full((8, width), NEG, F32)
 
         def scores(self):
-            q = qst_ref[self.place, :]
-            for start in tiles:
-                s = dot(keys[pl.ds(start, tile), :], q, NN)
-                for i in range(0, tile, tokens):
-                    part = s[i:i + tokens]
-                    part = jnp.where(allowed(start + i, part), part, NEG)
-                    self.s[pl.ds(start + i, tokens), :] = part
-                    self.top = jnp.maximum(self.top, fold(part, jnp.max))
-                yield
-
-        def exponents(self):
+            s = dot(keys[...], qst_ref[self.place, :], NN)
+            for start in blocks:
+                part = s[start:start + tokens]
+                part = jnp.where(allowed(start, part), part, NEG)
+                self.s[pl.ds(start, tokens), :] = part
+                self.top = jnp.maximum(self.top, fold(part, jnp.max))
+
+        def probs(self):
             top = jnp.max(self.top, axis=0, keepdims=True)
-            self.weight = jnp.zeros((8, width), F32)
-            for start in tiles:
-                rows = pl.ds(start, tile)
+            weight = jnp.zeros((8, width), F32)
+            for start in blocks:
+                rows = pl.ds(start, tokens)
                 e = jnp.exp2((self.s[rows, :] - top) * (scale * math.log2(math.e)))
                 self.s[rows, :] = e
-                self.weight = self.weight + fold(e, jnp.sum)
-                yield
-
-        def probs(self):
-            inverse = 1.0 / jnp.sum(self.weight, axis=0, keepdims=True)
-            for start in tiles:
-                rows = pl.ds(start, tile)
+                weight = weight + fold(e, jnp.sum)
+            inverse = 1.0 / jnp.sum(weight, axis=0, keepdims=True)
+            for start in blocks:
+                rows = pl.ds(start, tokens)
                 p = self.s[rows, :] * inverse
                 self.s[rows, :] = p
                 self.pb[rows, :] = p.astype(B16)
-                yield
 
         def output(self):
-            o = jnp.zeros((HD, width), F32)
-            for start in tiles:
-                rows = pl.ds(start, tile)
-                o = o + dot(values_t[:, rows], self.pb[rows, :], NN)
-                yield
-            self.o = o.astype(B16)
+            self.o = dot(values_t[...], self.pb[...], NN).astype(B16)
             do = dot_ref[self.place, :].astype(F32)
             self.delta = jnp.sum(do * self.o.astype(F32), axis=0, keepdims=True)
 
@@ -286,20 +271,14 @@
                 )
 
         def dscores(self):
-            do = dot_ref[self.place, :]
-            for start in tiles:
-                rows = pl.ds(start, tile)
-                dp = dot(values[rows, :], do, NN)
-                self.ds[rows, :] = (self.s[rows, :] * (dp - self.delta)).astype(B16)
-                yield
+            dp = dot(values[...], dot_ref[self.place, :], NN)
+            for start in blocks:
+                rows = pl.ds(start, tokens)
+                part = dp[start:start + tokens]
+                self.ds[rows, :] = (self.s[rows, :] * (part - self.delta)).astype(B16)
 
         def query_grad(self):
-            dq = jnp.zeros((HD, width), F32)
-            for start in tiles:
-                rows = pl.ds(start, tile)
-                dq = dq + dot(keys_t[:, rows], self.ds[rows, :], NN)
-                yield
-            self.dq = (dq * scale).astype(B16).astype(F32)
+            self.dq = (dot(keys_t[...], self.ds[...], NN) * scale).astype(B16).astype(F32)
 
         def slab_grads(self):
             last = pl.ds(prefix, slab)
@@ -315,25 +294,18 @@
                 gq_ref[:, cols] = x.astype(B16)
                 sums_ref[pl.ds(head, 1), :] = jnp.sum(x, axis=0, keepdims=True)
 
-    def together(*works):
-        for _ in itertools.zip_longest(*works):
-            pass
-
-    def pair(i, carry):
-        index = g * (GROUP // HEADS) + 2 * i
-        a, b = Chain(index, chains[0]), Chain(index + 1, chains[1])
-        together(a.scores())
-        together(b.scores(), a.exponents())
-        together(a.probs(), b.exponents(), a.output())
-        together(a.dscores(), b.probs(), a.query_grad(), b.output())
-        together(b.dscores(), b.query_grad())
-        a.slab_grads()
-        a.store()
-        b.slab_grads()
-        b.store()
+    def heads_step(i, carry):
+        chain = Chain(g * (GROUP // HEADS) + i)
+        chain.scores()
+        chain.probs()
+        chain.output()
+        chain.dscores()
+        chain.query_grad()
+        chain.slab_grads()
+        chain.store()
         return carry
 
-    lax.fori_loop(0, GROUP // (2 * HEADS), pair, 0)
+    lax.fori_loop(0, GROUP // HEADS, heads_step, 0)
 
     dk = dk_acc[...] * scale
     dv = dv_acc[...]
@@ -409,7 +381,7 @@
             pltpu.VMEM((HD, total), B16), pltpu.VMEM((HD, total), B16),
             pltpu.VMEM((slab, HD), F32), pltpu.VMEM((slab, HD), F32),
         ] + [
-            pltpu.VMEM((total, HEADS * tokens), kind) for kind in (F32, B16, B16) * 2
+            pltpu.VMEM((total, HEADS * tokens), kind) for kind in (F32, B16, B16)
         ],
         input_output_aliases=aliases,
         compiler_params=params(),

time: 65.4 us -> 60.7 us (0.928)
  Pallas kernels: 30.5 us -> 26 us
    pallas_call x4, Pallas kernels: 24.9 us -> 20.4 us  [attend(): pl.pallas_call(functools.partial(attend_kernel, g, shards), grid=(1,), in...]
    ppermute x2, waiting for transfers between devices: 0.8 us -> 2.13 us  [earlier(): return lax.ppermute(x, 'seq', [(i + s, i) for i in range(shards - s)])]
    ppermute x7, waiting for transfers between devices: 7.39 us -> 6.07 us  [sum_but_last(): parts.append(lax.ppermute(x, axes, [(i, i ^ flip) for i in range(devices)]))]
  transfers between devices with their start and end apart: 15 -> 15, of which waited for: 7 -> 7; matrix products, arithmetic and copies ran while one was open for 1% -> 1% of each run, Pallas kernels for 36% -> 33%
where the time goes in v9:
time: 60.7 us; the launch traced here: 60.5 us
  Pallas kernels  26 us (43%)
  starting transfers between devices  21.3 us (35%)
  waiting for transfers between devices  11 us (18%)
  between operations  1.43 us (2%)
  other arithmetic  0.64 us (1%)
    pallas_call x4, Pallas kernels, attend(): pl.pallas_call(functools.partial(attend_kernel, g, shards), grid=(1,), in...  20.4 us
    ppermute x7, starting transfers between devices, sum_but_last(): parts.append(lax.ppermute(x, axes, [(i, i ^ flip) for i in range(devices)]))  7.94 us
    ppermute x2, starting transfers between devices, later(): return lax.ppermute(x, 'seq', [(i, i + s) for i in range(shards - s)])  6.18 us
    ppermute x7, waiting for transfers between devices, sum_but_last(): parts.append(lax.ppermute(x, axes, [(i, i ^ flip) for i in range(devices)]))  6.07 us
    ppermute x4, starting transfers between devices, ring(): lax.ppermute(x, 'seq', [(i, (i + s) % shards) for i in range(shards)])  4.66 us
    pallas_call x1, Pallas kernels, prep(): pl.pallas_call(functools.partial(prep_kernel, tokens), grid=(KV,), in_spe...  3.78 us
    ppermute x4, waiting for transfers between devices, ring(): lax.ppermute(x, 'seq', [(i, (i + s) % shards) for i in range(shards)])  2.82 us
    ppermute x2, starting transfers between devices, earlier(): return lax.ppermute(x, 'seq', [(i + s, i) for i in range(shards - s)])  2.56 us
  transfers between devices with their start and end apart: 15, of which 7 were waited for; matrix products, arithmetic and copies ran while one was open for 1% of the time, Pallas kernels for 33%

profile of v9, /device:TPU:0, one launch (start us, length us, event | category | flops | bytes accessed | tf_op | source)
XLA Modules:
  0.0 60.5 jit_solution(18076809655479523080)
XLA Ops:
  0.6 4.9 %collective-permute-start.1 = (bf16[128,512]{1,0:T(8,128)(2,1)}, bf16[128,512]{1,0:T(8,128)(2,1)S(1)}, u32[]{:S(2)}, u32[]{:S(2)}) collective-permute-start(bf16[128,512]{1,0:T(8,128)(2,1)} %bitcast.33), channel_id=1, source_target_pairs={{0,1},{2,3},{4,5},{6,7},{8,9},{10,11},{12,13},{14,15},{16,17},{18,... | collective-permute-start | bytes 393224 | tf_op jit(solution)/shard_map/ppermute | solution.py:460
  5.5 1.3 %collective-permute-start.2 = (bf16[128,512]{1,0:T(8,128)(2,1)}, bf16[128,512]{1,0:T(8,128)(2,1)S(1)}, u32[]{:S(2)}, u32[]{:S(2)}) collective-permute-start(bf16[128,512]{1,0:T(8,128)(2,1)} %bitcast.38), channel_id=1, source_target_pairs={{0,1},{2,3},{4,5},{6,7},{8,9},{10,11},{12,13},{14,15},{16,17},{18,... | collective-permute-start | bytes 393224 | tf_op jit(solution)/shard_map/ppermute | solution.py:460
  6.8 0.0 copy-start
  6.8 0.0 copy-start.1
  6.8 1.1 %pack.1 = bf16[1024,128]{1,0:T(8,128)(2,1)S(1)} custom-call(bf16[512,512]{1,0:T(8,128)(2,1)} %bitcast.21, bf16[512,512]{1,0:T(8,128)(2,1)} %bitcast.27), custom_call_target="tpu_custom_call" | custom-call | bytes 524288 | tf_op jit(solution)/shard_map/pack/pallas_call | solution.py:59
  7.9 0.1 collective-permute-start.3
  8.7 0.1 convert_bitcast_fusion
  8.8 0.5 fusion
  9.3 0.0 copy-done
  9.3 0.0 copy-done.1
  9.3 0.0 copy-start.2
  9.3 0.0 copy-start.3
  9.4 3.8 %prep.1 = (bf16[4096,128]{1,0:T(8,128)(2,1)S(1)}, bf16[1024,512]{1,0:T(8,128)(2,1)S(1)}, bf16[4096,128]{1,0:T(8,128)(2,1)S(1)}, bf16[1024,512]{1,0:T(8,128)(2,1)...) custom-call(bf16[128,4096]{1,0:T(8,128)(2,1)} %bitcast.45, ...), custom_call_target="tpu_custom_call" | custom-call | flops 2097152 | bytes 6291456 | tf_op jit(solution)/shard_map/prep/pallas_call | solution.py:136
  13.1 2.1 %collective-permute-start = (bf16[1024,128]{1,0:T(8,128)(2,1)S(1)}, bf16[1024,128]{1,0:T(8,128)(2,1)S(1)}, u32[]{:S(2)}, u32[]{:S(2)}) collective-permute-start(bf16[1024,128]{1,0:T(8,128)(2,1)S(1)} %get-tuple-element.55), channel_id=1, source_target_pairs={{0,1},{1,0},{2,3},{3,2},{4,5},{5,4},{6,7},{7,6},{8,9},{9,8},{10,11... | collective-permute-start | bytes 786440 | tf_op jit(solution)/shard_map/ppermute | solution.py:457
  15.2 0.0 collective-permute-done.1.refs_18_
  15.2 0.0 collective-permute-done.2.refs_19_
  15.2 2.8 %collective-permute-done.3.refs_17_ = bf16[1024,128]{1,0:T(8,128)(2,1)S(1)} collective-permute-done((bf16[1024,128]{1,0:T(8,128)(2,1)S(1)}, bf16[1024,128]{1,0:T(8,128)(2,1)S(1)}, u32[]{:S(2)}, u32[]{:S(2)}) %collective-permute-start.3) | collective-permute-done | bytes 262176 | tf_op jit(solution)/shard_map/ppermute | solution.py:457
  18.0 0.0 copy-done.2
  18.0 0.0 copy-done.3
  18.0 5.1 %attend.4 = (bf16[128,4096]{1,0:T(8,128)(2,1)}, bf16[128,4096]{1,0:T(8,128)(2,1)}, f32[40,128]{1,0:T(8,128)S(1)}, f32[2,128,128]{2,1,0:T(8,128)S(1)}, bf16[2,128...) custom-call(s32[1]{0:T(128)} %copy.33.refs_0_, s32[1]{0:T(128)} %bitcast.refs_1_, ...), custom_call_target="tpu_custom_call" | custom-call | flops 1476395008 | bytes 2359296 | tf_op jit(solution)/shard_map/attend/pallas_call | solution.py:373
  23.1 2.5 %collective-permute-start.5 = (bf16[1024,128]{1,0:T(8,128)(2,1)S(1)}, bf16[1024,128]{1,0:T(8,128)(2,1)S(1)}, u32[]{:S(2)}, u32[]{:S(2)}) collective-permute-start(bf16[1024,128]{1,0:T(8,128)(2,1)S(1)} %get-tuple-element.61), channel_id=1, source_target_pairs={{0,1},{1,0},{2,3},{3,2},{4,5},{5,4},{6,7},{7,6},{8,9},{9,8},{10,11... | collective-permute-start | bytes 786440 | tf_op jit(solution)/shard_map/ppermute | solution.py:457
  25.6 0.0 collective-permute-done.refs_17_
  25.6 5.1 %attend.5 = (bf16[128,4096]{1,0:T(8,128)(2,1)}, bf16[128,4096]{1,0:T(8,128)(2,1)}, f32[40,128]{1,0:T(8,128)S(1)}, f32[2,128,128]{2,1,0:T(8,128)S(1)}, bf16[4,128...) custom-call(s32[1]{0:T(128)} %copy.33.refs_0_, ...), custom_call_target="tpu_custom_call", output_to_operand_aliasing={{0}: (22, {}), {1}: (23, {})} | custom-call | flops 1476395008 | bytes 2359296 | tf_op jit(solution)/shard_map/attend/pallas_call | solution.py:373
  30.7 0.0 collective-permute-start.4
  30.8 1.3 %collective-permute-start.6 = (bf16[4,128,128]{2,1,0:T(8,128)(2,1)S(1)}, bf16[4,128,128]{2,1,0:T(8,128)(2,1)S(1)}, u32[]{:S(2)}, u32[]{:S(2)}) collective-permute-start(bf16[4,128,128]{2,1,0:T(8,128)(2,1)S(1)} %get-tuple-element.69), channel_id=1, source_target_pairs={{1,0},{3,2},{5,4},{7,6},{9,8},{11,10},{13,12},{15,14},{17,16},{19,... | collective-permute-start | bytes 393224 | tf_op jit(solution)/shard_map/ppermute | solution.py:463
  32.0 0.0 collective-permute-done.5.refs_17_
  32.1 5.1 %attend.6 = (bf16[128,4096]{1,0:T(8,128)(2,1)}, bf16[128,4096]{1,0:T(8,128)(2,1)}, f32[40,128]{1,0:T(8,128)S(1)}, f32[2,128,128]{2,1,0:T(8,128)S(1)}, bf16[2,128,128]{2,1,0:T(8,128)(2,1)S(1)}) custom-call(s32[1]{0:T(128)} %copy.33.refs_0_, s32[1]{0:T(128)} %bitcast.refs_1_, ...), custom_call_target="tpu_custom_call", output_to_operand_aliasing={{0}: (21, {}), {1}: (22, {})} | custom-call | flops 1476395008 | bytes 2359296 | tf_op jit(solution)/shard_map/attend/pallas_call | solution.py:373
  37.2 2.1 %collective-permute-done.6.refs_24_ = bf16[4,128,128]{2,1,0:T(8,128)(2,1)S(1)} collective-permute-done((bf16[4,128,128]{2,1,0:T(8,128)(2,1)S(1)}, bf16[4,128,128]{2,1,0:T(8,128)(2,1)S(1)}, u32[]{:S(2)}, u32[]{:S(2)}) %collective-permute-start.6) | collective-permute-done | bytes 131104 | tf_op jit(solution)/shard_map/ppermute | solution.py:463
  39.3 0.0 collective-permute-done.4.refs_17_
  39.3 5.1 %attend.7 = (bf16[128,4096]{1,0:T(8,128)(2,1)}, bf16[128,4096]{1,0:T(8,128)(2,1)}, f32[40,128]{1,0:T(8,128)S(1)}, f32[2,128,128]{2,1,0:T(8,128)S(1)}, bf16[4,128...) custom-call(s32[1]{0:T(128)} %copy.33.refs_0_, ...), custom_call_target="tpu_custom_call", output_to_operand_aliasing={{0}: (25, {}), {1}: (26, {})} | custom-call | flops 1476395008 | bytes 2359296 | tf_op jit(solution)/shard_map/attend/pallas_call | solution.py:373
  44.4 0.0 collective-permute-start.8
  44.4 1.2 %collective-permute-done.8 = f32[40,128]{1,0:T(8,128)S(1)} collective-permute-done((f32[40,128]{1,0:T(8,128)S(1)}, f32[40,128]{1,0:T(8,128)S(1)}, u32[]{:S(2)}, u32[]{:S(2)}) %collective-permute-start.8) | collective-permute-done | bytes 20512 | tf_op jit(solution)/shard_map/ppermute | solution.py:446
  45.6 1.5 %collective-permute-start.11 = (f32[40,128]{1,0:T(8,128)S(1)}, f32[40,128]{1,0:T(8,128)S(1)}, u32[]{:S(2)}, u32[]{:S(2)}) collective-permute-start(f32[40,128]{1,0:T(8,128)S(1)} %add.66), channel_id=1, source_target_pairs={{0,5},{1,4},{2,7},{3,6},{4,1},{5,0},{6,3},{7,2},{8,13},{9,12},{10,... | collective-permute-start | bytes 61448 | tf_op jit(solution)/shard_map/ppermute | solution.py:446
  47.0 0.5 collective-permute-start.10
  47.6 1.5 %collective-permute-start.9 = (f32[40,128]{1,0:T(8,128)S(1)}, f32[40,128]{1,0:T(8,128)S(1)}, u32[]{:S(2)}, u32[]{:S(2)}) collective-permute-start(f32[40,128]{1,0:T(8,128)S(1)} %add.66), channel_id=1, source_target_pairs={{0,1},{1,0},{2,3},{3,2},{4,5},{5,4},{6,7},{7,6},{8,9},{9,8},{10,11... | collective-permute-start | bytes 61448 | tf_op jit(solution)/shard_map/ppermute | solution.py:446
  49.1 1.3 %collective-permute-start.7 = (bf16[4,128,128]{2,1,0:T(8,128)(2,1)S(1)}, bf16[4,128,128]{2,1,0:T(8,128)(2,1)S(1)}, u32[]{:S(2)}, u32[]{:S(2)}) collective-permute-start(bf16[4,128,128]{2,1,0:T(8,128)(2,1)S(1)} %get-tuple-element.76), channel_id=1, source_target_pairs={{1,0},{3,2},{5,4},{7,6},{9,8},{11,10},{13,12},{15,14},{17,16},{19,... | collective-permute-start | bytes 393224 | tf_op jit(solution)/shard_map/ppermute | solution.py:463
  50.4 0.0 collective-permute-done.11
  50.4 0.4 collective-permute-done.10
  50.8 0.5 collective-permute-done.9
  51.4 3.7 %collective-permute-start.14 = (f32[40,128]{1,0:T(8,128)S(1)}, f32[40,128]{1,0:T(8,128)S(1)}, u32[]{:S(2)}, u32[]{:S(2)}) collective-permute-start(f32[40,128]{1,0:T(8,128)S(1)} %add_add_fusion.refs_5_), channel_id=1, source_target_pairs={{0,24},{1,25},{2,26},{3,27},{4,28},{5,29},{6,30},{7,31},{8,16},{9,... | collective-permute-start | bytes 61448 | tf_op jit(solution)/shard_map/ppermute | solution.py:446
  55.0 0.0 collective-permute-start.13
  55.0 0.8 %collective-permute-start.12 = (f32[40,128]{1,0:T(8,128)S(1)}, f32[40,128]{1,0:T(8,128)S(1)}, u32[]{:S(2)}, u32[]{:S(2)}) collective-permute-start(f32[40,128]{1,0:T(8,128)S(1)} %add_add_fusion.refs_5_), channel_id=1, source_target_pairs={{0,8},{1,9},{2,10},{3,11},{4,12},{5,13},{6,14},{7,15},{8,0},{9,1},... | collective-permute-start | bytes 61448 | tf_op jit(solution)/shard_map/ppermute | solution.py:446
  55.8 1.2 %collective-permute-done.14.refs_8_ = f32[40,128]{1,0:T(8,128)S(1)} collective-permute-done((f32[40,128]{1,0:T(8,128)S(1)}, f32[40,128]{1,0:T(8,128)S(1)}, u32[]{:S(2)}, u32[]{:S(2)}) %collective-permute-start.14) | collective-permute-done | bytes 20512 | tf_op jit(solution)/shard_map/ppermute | solution.py:446
  57.0 2.7 %collective-permute-done.13.refs_7_ = f32[40,128]{1,0:T(8,128)S(1)} collective-permute-done((f32[40,128]{1,0:T(8,128)S(1)}, f32[40,128]{1,0:T(8,128)S(1)}, u32[]{:S(2)}, u32[]{:S(2)}) %collective-permute-start.13) | collective-permute-done | bytes 20512 | tf_op jit(solution)/shard_map/ppermute | solution.py:446
  59.7 0.0 collective-permute-done.12.refs_6_
  59.7 0.0 collective-permute-done.7.refs_4_
  59.7 0.7 %finish.1 = (bf16[128,512]{1,0:T(8,128)(2,1)}, bf16[128,512]{1,0:T(8,128)(2,1)}, f32[32,128]{1,0:T(8,128)}, f32[4,128]{1,0:T(4,128)}, f32[4,128]{1,0:T(4,128)}) custom-call(f32[256,128]{1,0:T(8,128)S(1)} %get-tuple-element.86.cos_ref.refs_11_.refs_0_, ...), custom_call_target="tpu_custom_call", output_to_operand_aliasing={{0}: (9, {}), {1}: (10, {})} | custom-call | bytes 524288 | tf_op jit(solution)/shard_map/finish/pallas_call | solution.py:417
  (4 shorter events, 0.0 us)
Async XLA Ops:
  0.6 14.6 %collective-permute-start.1 = (bf16[128,512]{1,0:T(8,128)(2,1)}, bf16[128,512]{1,0:T(8,128)(2,1)S(1)}, u32[]{:S(2)}, u32[]{:S(2)}) collective-permute-start(bf16[128,512]{1,0:T(8,128)(2,1)} %bitcast.33), channel_id=1, source_target_pairs={{0,1},{2,3},{4,5},{6,7},{8,9},{10,11},{12,13},{14,15},{16,17},{18,... | collective-permute-start | bytes 393224 | tf_op jit(solution)/shard_map/ppermute | solution.py:460
  5.5 9.7 %collective-permute-start.2 = (bf16[128,512]{1,0:T(8,128)(2,1)}, bf16[128,512]{1,0:T(8,128)(2,1)S(1)}, u32[]{:S(2)}, u32[]{:S(2)}) collective-permute-start(bf16[128,512]{1,0:T(8,128)(2,1)} %bitcast.38), channel_id=1, source_target_pairs={{0,1},{2,3},{4,5},{6,7},{8,9},{10,11},{12,13},{14,15},{16,17},{18,... | collective-permute-start | bytes 393224 | tf_op jit(solution)/shard_map/ppermute | solution.py:460
  6.8 2.5 %copy-start = (bf16[1,512,512]{2,1,0:T(8,128)(2,1)S(1)}, bf16[1,512,512]{2,1,0:T(8,128)(2,1)}, u32[]{:S(2)}) copy-start(bf16[1,512,512]{2,1,0:T(8,128)(2,1)} %param.13) | copy-start | bytes 1572868
  6.8 2.5 %copy-start.1 = (bf16[1,512,512]{2,1,0:T(8,128)(2,1)S(1)}, bf16[1,512,512]{2,1,0:T(8,128)(2,1)}, u32[]{:S(2)}) copy-start(bf16[1,512,512]{2,1,0:T(8,128)(2,1)} %param.14) | copy-start | bytes 1572868
  7.9 10.1 %collective-permute-start.3 = (bf16[1024,128]{1,0:T(8,128)(2,1)S(1)}, bf16[1024,128]{1,0:T(8,128)(2,1)S(1)}, u32[]{:S(2)}, u32[]{:S(2)}) collective-permute-start(bf16[1024,128]{1,0:T(8,128)(2,1)S(1)} %pack.1), channel_id=1, source_target_pairs={{0,1},{1,0},{2,3},{3,2},{4,5},{5,4},{6,7},{7,6},{8,9},{9,8},{10,11... | collective-permute-start | bytes 786440 | tf_op jit(solution)/shard_map/ppermute | solution.py:457
  9.3 8.7 %copy-start.2 = (bf16[1,128,512]{2,1,0:T(8,128)(2,1)S(1)}, bf16[1,128,512]{2,1,0:T(8,128)(2,1)}, u32[]{:S(2)}) copy-start(bf16[1,128,512]{2,1,0:T(8,128)(2,1)} %param.11) | copy-start | bytes 393220
  9.3 8.7 %copy-start.3 = (bf16[1,128,512]{2,1,0:T(8,128)(2,1)S(1)}, bf16[1,128,512]{2,1,0:T(8,128)(2,1)}, u32[]{:S(2)}) copy-start(bf16[1,128,512]{2,1,0:T(8,128)(2,1)} %param.12) | copy-start | bytes 393220
  13.1 12.5 %collective-permute-start = (bf16[1024,128]{1,0:T(8,128)(2,1)S(1)}, bf16[1024,128]{1,0:T(8,128)(2,1)S(1)}, u32[]{:S(2)}, u32[]{:S(2)}) collective-permute-start(bf16[1024,128]{1,0:T(8,128)(2,1)S(1)} %get-tuple-element.55), channel_id=1, source_target_pairs={{0,1},{1,0},{2,3},{3,2},{4,5},{5,4},{6,7},{7,6},{8,9},{9,8},{10,11... | collective-permute-start | bytes 786440 | tf_op jit(solution)/shard_map/ppermute | solution.py:457
  23.1 8.9 %collective-permute-start.5 = (bf16[1024,128]{1,0:T(8,128)(2,1)S(1)}, bf16[1024,128]{1,0:T(8,128)(2,1)S(1)}, u32[]{:S(2)}, u32[]{:S(2)}) collective-permute-start(bf16[1024,128]{1,0:T(8,128)(2,1)S(1)} %get-tuple-element.61), channel_id=1, source_target_pairs={{0,1},{1,0},{2,3},{3,2},{4,5},{5,4},{6,7},{7,6},{8,9},{9,8},{10,11... | collective-permute-start | bytes 786440 | tf_op jit(solution)/shard_map/ppermute | solution.py:457
  30.7 8.6 %collective-permute-start.4 = (bf16[1024,128]{1,0:T(8,128)(2,1)S(1)}, bf16[1024,128]{1,0:T(8,128)(2,1)S(1)}, u32[]{:S(2)}, u32[]{:S(2)}) collective-permute-start(bf16[1024,128]{1,0:T(8,128)(2,1)S(1)} %get-tuple-element.60), channel_id=1, source_target_pairs={{0,1},{1,0},{2,3},{3,2},{4,5},{5,4},{6,7},{7,6},{8,9},{9,8},{10,11... | collective-permute-start | bytes 786440 | tf_op jit(solution)/shard_map/ppermute | solution.py:457
  30.8 8.5 %collective-permute-start.6 = (bf16[4,128,128]{2,1,0:T(8,128)(2,1)S(1)}, bf16[4,128,128]{2,1,0:T(8,128)(2,1)S(1)}, u32[]{:S(2)}, u32[]{:S(2)}) collective-permute-start(bf16[4,128,128]{2,1,0:T(8,128)(2,1)S(1)} %get-tuple-element.69), channel_id=1, source_target_pairs={{1,0},{3,2},{5,4},{7,6},{9,8},{11,10},{13,12},{15,14},{17,16},{19,... | collective-permute-start | bytes 393224 | tf_op jit(solution)/shard_map/ppermute | solution.py:463
  44.4 1.2 %collective-permute-start.8 = (f32[40,128]{1,0:T(8,128)S(1)}, f32[40,128]{1,0:T(8,128)S(1)}, u32[]{:S(2)}, u32[]{:S(2)}) collective-permute-start(f32[40,128]{1,0:T(8,128)S(1)} %get-tuple-element.77), channel_id=1, source_target_pairs={{0,2},{1,3},{2,0},{3,1},{4,6},{5,7},{6,4},{7,5},{8,10},{9,11},{10,... | collective-permute-start | bytes 61448 | tf_op jit(solution)/shard_map/ppermute | solution.py:446
  45.6 4.8 %collective-permute-start.11 = (f32[40,128]{1,0:T(8,128)S(1)}, f32[40,128]{1,0:T(8,128)S(1)}, u32[]{:S(2)}, u32[]{:S(2)}) collective-permute-start(f32[40,128]{1,0:T(8,128)S(1)} %add.66), channel_id=1, source_target_pairs={{0,5},{1,4},{2,7},{3,6},{4,1},{5,0},{6,3},{7,2},{8,13},{9,12},{10,... | collective-permute-start | bytes 61448 | tf_op jit(solution)/shard_map/ppermute | solution.py:446
  47.0 3.8 %collective-permute-start.10 = (f32[40,128]{1,0:T(8,128)S(1)}, f32[40,128]{1,0:T(8,128)S(1)}, u32[]{:S(2)}, u32[]{:S(2)}) collective-permute-start(f32[40,128]{1,0:T(8,128)S(1)} %add.66), channel_id=1, source_target_pairs={{0,4},{1,5},{2,6},{3,7},{4,0},{5,1},{6,2},{7,3},{8,12},{9,13},{10,... | collective-permute-start | bytes 61448 | tf_op jit(solution)/shard_map/ppermute | solution.py:446
  47.6 3.8 %collective-permute-start.9 = (f32[40,128]{1,0:T(8,128)S(1)}, f32[40,128]{1,0:T(8,128)S(1)}, u32[]{:S(2)}, u32[]{:S(2)}) collective-permute-start(f32[40,128]{1,0:T(8,128)S(1)} %add.66), channel_id=1, source_target_pairs={{0,1},{1,0},{2,3},{3,2},{4,5},{5,4},{6,7},{7,6},{8,9},{9,8},{10,11... | collective-permute-start | bytes 61448 | tf_op jit(solution)/shard_map/ppermute | solution.py:446
  49.1 10.6 %collective-permute-start.7 = (bf16[4,128,128]{2,1,0:T(8,128)(2,1)S(1)}, bf16[4,128,128]{2,1,0:T(8,128)(2,1)S(1)}, u32[]{:S(2)}, u32[]{:S(2)}) collective-permute-start(bf16[4,128,128]{2,1,0:T(8,128)(2,1)S(1)} %get-tuple-element.76), channel_id=1, source_target_pairs={{1,0},{3,2},{5,4},{7,6},{9,8},{11,10},{13,12},{15,14},{17,16},{19,... | collective-permute-start | bytes 393224 | tf_op jit(solution)/shard_map/ppermute | solution.py:463
  51.4 5.6 %collective-permute-start.14 = (f32[40,128]{1,0:T(8,128)S(1)}, f32[40,128]{1,0:T(8,128)S(1)}, u32[]{:S(2)}, u32[]{:S(2)}) collective-permute-start(f32[40,128]{1,0:T(8,128)S(1)} %add_add_fusion.refs_5_), channel_id=1, source_target_pairs={{0,24},{1,25},{2,26},{3,27},{4,28},{5,29},{6,30},{7,31},{8,16},{9,... | collective-permute-start | bytes 61448 | tf_op jit(solution)/shard_map/ppermute | solution.py:446
  55.0 4.7 %collective-permute-start.13 = (f32[40,128]{1,0:T(8,128)S(1)}, f32[40,128]{1,0:T(8,128)S(1)}, u32[]{:S(2)}, u32[]{:S(2)}) collective-permute-start(f32[40,128]{1,0:T(8,128)S(1)} %add_add_fusion.refs_5_), channel_id=1, source_target_pairs={{0,16},{1,17},{2,18},{3,19},{4,20},{5,21},{6,22},{7,23},{8,24},{9,... | collective-permute-start | bytes 61448 | tf_op jit(solution)/shard_map/ppermute | solution.py:446
  55.0 4.7 %collective-permute-start.12 = (f32[40,128]{1,0:T(8,128)S(1)}, f32[40,128]{1,0:T(8,128)S(1)}, u32[]{:S(2)}, u32[]{:S(2)}) collective-permute-start(f32[40,128]{1,0:T(8,128)S(1)} %add_add_fusion.refs_5_), channel_id=1, source_target_pairs={{0,8},{1,9},{2,10},{3,11},{4,12},{5,13},{6,14},{7,15},{8,0},{9,1},... | collective-permute-start | bytes 61448 | tf_op jit(solution)/shard_map/ppermute | solution.py:446

commit v10 on v9

--- a/solution.py
+++ b/solution.py
@@ -50,22 +50,32 @@
     out_ref[pl.ds(rows, rows)] = cv_ref[:, cols]
 
 
-def pack_kernel(ck_ref, cv_ref, *rest):
-    copy_chunk(0, ck_ref, cv_ref, rest[-1])
-
-
-def pack(g, ck, cv, *after):
-    rows = ck.shape[0]
+def pack_kernel(g, with_slab, *refs):
+    out_ref = refs[-1]
+    if with_slab:
+        ck_ref, cv_ref, kp_ref, vp_ref = refs[:4]
+        rows, tokens = ck_ref.shape[0], kp_ref.shape[0]
+        out_ref[pl.ds(2 * rows, tokens)] = kp_ref[...]
+        out_ref[pl.ds(2 * rows + tokens, tokens)] = vp_ref[...]
+        copy_chunk(0, ck_ref, cv_ref, out_ref)
+    else:
+        copy_chunk(g, *refs[:2], out_ref)
+
+
+def pack(g, ck, cv, slab=(), after=()):
+    rows = 2 * ck.shape[0] + sum(x.shape[0] for x in slab)
+    vmem = pl.BlockSpec(memory_space=pltpu.VMEM)
+    in_specs = [column(x.shape[0], g) for x in (ck, cv, *slab)] if slab else [vmem] * 2
     return pl.pallas_call(
-        pack_kernel,
+        functools.partial(pack_kernel, g, bool(slab)),
         grid=(1,),
-        in_specs=[column(rows, g)] * 2 + [pl.BlockSpec(memory_space=pl.ANY)] * len(after),
-        out_specs=pl.BlockSpec(memory_space=pltpu.VMEM),
-        out_shape=pltpu.VMEM((2 * rows, HD), B16),
+        in_specs=in_specs + [pl.BlockSpec(memory_space=pl.ANY)] * len(after),
+        out_specs=vmem,
+        out_shape=pltpu.VMEM((rows, HD), B16),
         compiler_params=params(),
-        cost_estimate=pl.CostEstimate(flops=0, bytes_accessed=8 * rows * HD, transcendentals=0),
+        cost_estimate=pl.CostEstimate(flops=0, bytes_accessed=4 * rows * HD, transcendentals=0),
         name="pack",
-    )(ck, cv, *after)
+    )(ck, cv, *slab, *after)
 
 
 def turn_back(x, cosine, sine):
@@ -87,7 +97,7 @@
 
 def prep_kernel(
     tokens, q_ref, do_ref, bq_ref, bk_ref, bv_ref, cos_ref, sin_ref, ck_ref, cv_ref,
-    qs_ref, qst_ref, dos_ref, dot_ref, bias_ref, cos_t_ref, sin_t_ref, ck_t_ref, cv_t_ref, pack_ref,
+    kp_ref, vp_ref, qs_ref, qst_ref, dos_ref, dot_ref, bias_ref, cos_t_ref, sin_t_ref, ck_t_ref, cv_t_ref, pack_ref, slab_ref,
 ):
     g = pl.program_id(0)
     cosine, sine = cos_ref[pl.ds(0, tokens), :], sin_ref[pl.ds(0, tokens), :]
@@ -100,6 +110,9 @@
         cos_t_ref[...] = cosine.T
         sin_t_ref[...] = sine.T
         copy_chunk(1, ck_ref, cv_ref, pack_ref)
+        others = pl.ds(HD, (KV - 1) * HD)
+        slab_ref[0] = kp_ref[:, others]
+        slab_ref[1] = vp_ref[:, others]
 
     for h in range(GROUP):
         cols = pl.ds(h * HD, HD)
@@ -118,7 +131,7 @@
     cv_t_ref[mine, :] = cv_ref[:, mine].T
 
 
-def prep(q, do, bq, bk, bv, cosine, sine, ck, cv):
+def prep(q, do, bq, bk, bv, cosine, sine, ck, cv, kp, vp):
     tokens, slots = q.shape[0], ck.shape[0]
     vmem = pl.BlockSpec(memory_space=pltpu.VMEM)
     wide = pl.BlockSpec((tokens, GROUP * HD), lambda i: (0, i))
@@ -132,13 +145,14 @@
         pltpu.VMEM((KV * HD, slots), B16),
         pltpu.VMEM((KV * HD, slots), B16),
         pltpu.VMEM((2 * slots, HD), B16),
+        pltpu.VMEM((2, tokens, (KV - 1) * HD), B16),
     ]
     return pl.pallas_call(
         functools.partial(prep_kernel, tokens),
         grid=(KV,),
         in_specs=[
             wide, wide, pl.BlockSpec((GROUP, HD), lambda i: (i, 0)),
-            whole((KV, HD)), whole((KV, HD)), vmem, vmem, vmem, vmem,
+            whole((KV, HD)), whole((KV, HD)), *[vmem] * 6,
         ],
         out_specs=[vmem] * len(out_shape),
         out_shape=out_shape,
@@ -147,7 +161,7 @@
             flops=4 * tokens * HQ * HD, bytes_accessed=12 * tokens * HQ * HD, transcendentals=0
         ),
         name="prep",
-    )(q, do, bq, bk, bv, cosine, sine, ck, cv)
+    )(q, do, bq, bk, bv, cosine, sine, ck, cv, kp, vp)
 
 
 def fold(x, op):
@@ -165,8 +179,7 @@
     (first_ref, rank_ref, qs_ref, qst_ref, dos_ref, dot_ref, bias_ref, cos_t_ref, sin_t_ref,
      ck_t_ref, cv_t_ref, cos_ref, sin_ref, ck_ref, cv_ref, kp_ref, vp_ref) = take(17)
     far = take(shards - 1)
-    far_k = take(shards - 1)
-    far_v = take(shards - 1)
+    far_slab = take(shards - 1) if g else []
     old_sums_ref = take(1)[0] if g else None
     old_send = take(shards - 1) if g % 2 else []
     owns = take(2) if g == KV - 1 else []
@@ -175,7 +188,7 @@
         take(2)
     out_ref, gq_ref, sums_ref, own_ref = take(4)
     send = take(shards - 1)
-    pack_ref = take(1)[0] if g + 2 < KV else None
+    pack_ref = take(1)[0] if g == 0 else None
     gk_ref, gv_ref = take(2) if g == KV - 1 else (None, None)
     keys, values, keys_t, values_t, dk_acc, dv_acc = take(6)
     scratch = take(3)
@@ -197,10 +210,15 @@
         values[pl.ds(s * slots, slots)] = far[s - 1][pl.ds(slots, slots)]
     for s in range(shards):
         rows = pl.ds(s * tokens, tokens)
-        kp, vp = (kp_ref, vp_ref) if s == 0 else (far_k[s - 1], far_v[s - 1])
-        k = kp[:, mine].astype(F32) + bias_ref[g:g + 1, :]
+        if s == 0:
+            kp, vp = kp_ref[:, mine], vp_ref[:, mine]
+        elif g == 0:
+            kp, vp = (far[s - 1][pl.ds(2 * slots + i * tokens, tokens)] for i in range(2))
+        else:
+            kp, vp = (far_slab[s - 1][i, :, pl.ds((g - 1) * HD, HD)] for i in range(2))
+        k = kp.astype(F32) + bias_ref[g:g + 1, :]
         k = k * cos_ref[rows, :] + turn(k) * sin_ref[rows, :]
-        v = vp[:, mine].astype(F32) + bias_ref[KV + g:KV + g + 1, :]
+        v = vp.astype(F32) + bias_ref[KV + g:KV + g + 1, :]
         place = pl.ds(prefix + s * tokens, tokens)
         keys[place] = k.astype(B16)
         values[place] = v.astype(B16)
@@ -241,23 +259,19 @@
                 self.s[pl.ds(start, tokens), :] = part
                 self.top = jnp.maximum(self.top, fold(part, jnp.max))
 
-        def probs(self):
+        def exponents(self):
             top = jnp.max(self.top, axis=0, keepdims=True)
             weight = jnp.zeros((8, width), F32)
             for start in blocks:
                 rows = pl.ds(start, tokens)
                 e = jnp.exp2((self.s[rows, :] - top) * (scale * math.log2(math.e)))
                 self.s[rows, :] = e
+                self.pb[rows, :] = e.astype(B16)
                 weight = weight + fold(e, jnp.sum)
-            inverse = 1.0 / jnp.sum(weight, axis=0, keepdims=True)
-            for start in blocks:
-                rows = pl.ds(start, tokens)
-                p = self.s[rows, :] * inverse
-                self.s[rows, :] = p
-                self.pb[rows, :] = p.astype(B16)
+            self.inverse = 1.0 / jnp.sum(weight, axis=0, keepdims=True)
 
         def output(self):
-            self.o = dot(values_t[...], self.pb[...], NN).astype(B16)
+            self.o = (dot(values_t[...], self.pb[...], NN) * self.inverse).astype(B16)
             do = dot_ref[self.place, :].astype(F32)
             self.delta = jnp.sum(do * self.o.astype(F32), axis=0, keepdims=True)
 
@@ -274,8 +288,10 @@
             dp = dot(values[...], dot_ref[self.place, :], NN)
             for start in blocks:
                 rows = pl.ds(start, tokens)
-                part = dp[start:start + tokens]
-                self.ds[rows, :] = (self.s[rows, :] * (part - self.delta)).astype(B16)
+                p = self.s[rows, :] * self.inverse
+                self.ds[rows, :] = (p * (dp[start:start + tokens] - self.delta)).astype(B16)
+                if start >= prefix:
+                    self.pb[rows, :] = p.astype(B16)
 
         def query_grad(self):
             self.dq = (dot(keys_t[...], self.ds[...], NN) * scale).astype(B16).astype(F32)
@@ -297,7 +313,7 @@
     def heads_step(i, carry):
         chain = Chain(g * (GROUP // HEADS) + i)
         chain.scores()
-        chain.probs()
+        chain.exponents()
         chain.output()
         chain.dscores()
         chain.query_grad()
@@ -326,7 +342,7 @@
 
 
 def attend(
-    g, shards, first, rank, prepared, cosine, sine, ck, cv, kp, vp, far, far_k, far_v,
+    g, shards, first, rank, prepared, cosine, sine, ck, cv, kp, vp, far, far_slab,
     before, owns, backs,
 ):
     tokens, slots = kp.shape[0], ck.shape[0]
@@ -340,7 +356,7 @@
     half = pl.BlockSpec((tokens, 2 * HD), lambda i: (0, 0))
 
     args = [first, rank]
-    placed = [*prepared, cosine, sine, ck, cv, kp, vp, *far, *far_k, *far_v]
+    placed = [*prepared, cosine, sine, ck, cv, kp, vp, *far, *far_slab]
     aliases = {}
     if before is not None:
         out, gq, sums, send = before
@@ -364,7 +380,7 @@
     out_specs = [wide, wide, vmem, vmem]
     out_shape += [pltpu.VMEM((2 + 2 * (g % 2), tokens, HD), B16)] * (shards - 1)
     out_specs += [vmem] * (shards - 1)
-    if g + 2 < KV:
+    if g == 0:
         out_shape.append(pltpu.VMEM((2 * slots, HD), B16))
         out_specs.append(vmem)
     if last:
@@ -451,6 +467,7 @@
     shards = lax.axis_size("seq")
     rank = lax.axis_index("seq").astype(jnp.int32)
     tokens = q_proj.shape[1]
+    shifts = range(1, shards)
     ck, cv, kp, vp = cache_k[0], cache_v[0], k_proj[0], v_proj[0]
 
     def ring(x, s):
@@ -462,11 +479,8 @@
     def earlier(x, s):
         return lax.ppermute(x, "seq", [(i + s, i) for i in range(shards - s)])
 
-    shifts = range(1, shards)
-    far_k = [later(kp, s) for s in shifts]
-    far_v = [later(vp, s) for s in shifts]
     hbm = functools.partial(pltpu.with_memory_space_constraint, memory_space=pltpu.HBM)
-    chunk = pack(0, hbm(ck), hbm(cv))
+    chunk = pack(0, hbm(ck), hbm(cv), (hbm(kp), hbm(vp)))
     far = [[ring(chunk, s) for s in shifts]]
 
     owners = lax.rem(rank - jnp.arange(shards, dtype=jnp.int32) + shards, shards)
@@ -479,19 +493,23 @@
     cosine = jnp.cos(angles)
     sine = jnp.sin(angles) * jnp.where(lane < HD // 2, -1.0, 1.0).astype(F32)[None]
 
-    *prepared, chunk = prep(
+    *prepared, chunk, own = prep(
         hbm(q_proj[0]), hbm(dout[0]), hbm(bias_q.reshape(HQ, HD)),
-        hbm(bias_k.reshape(KV, HD)), hbm(bias_v.reshape(KV, HD)), cosine, sine, ck, cv,
+        hbm(bias_k.reshape(KV, HD)), hbm(bias_v.reshape(KV, HD)), cosine, sine, ck, cv, kp, vp,
     )
     far.append([ring(chunk, s) for s in shifts])
+    far_slab = [later(own, s) for s in shifts]
     before, owns, backs = None, [], []
     for g in range(KV):
+        if g == 1:
+            chunk = pack(KV - 1, ck, cv, after=far[1])
+            far.append([ring(chunk, s) for s in shifts])
         before, own, more = attend(
             g, shards, start, rank.reshape(1), prepared, cosine, sine, ck, cv, kp, vp,
-            far[g], far_k, far_v, before, owns, backs,
+            far[g], far_slab if g else [], before, owns, backs,
         )
         owns.append(own)
-        if g + 2 < KV:
+        if g == 0:
             far.append([ring(more[0], s) for s in shifts])
         if g % 2:
             backs = [earlier(x, s) for s, x in zip(shifts, before[3])]

time: 60.7 us -> 61.9 us (1.020)
  Pallas kernels: 26 us -> 26.9 us
    ppermute x2 -> x1, starting transfers between devices: 6.18 us -> 1.93 us  [later(): return lax.ppermute(x, 'seq', [(i, i + s) for i in range(shards - s)])]
    ppermute x4, starting transfers between devices: 4.66 us -> 7.38 us  [ring(): lax.ppermute(x, 'seq', [(i, (i + s) % shards) for i in range(shards)])]
    ppermute x2, waiting for transfers between devices: 2.13 us -> 0.22 us  [earlier(): return lax.ppermute(x, 'seq', [(i + s, i) for i in range(shards - s)])]
    ppermute x7, starting transfers between devices: 7.94 us -> 9.3 us  [sum_but_last(): parts.append(lax.ppermute(x, axes, [(i, i ^ flip) for i in range(devices)]))]
    ppermute x7, waiting for transfers between devices: 6.07 us -> 7.13 us  [sum_but_last(): parts.append(lax.ppermute(x, axes, [(i, i ^ flip) for i in range(devices)]))]
    pallas_call x4, Pallas kernels: 20.4 us -> 21.4 us  [attend(): pl.pallas_call(functools.partial(attend_kernel, g, shards), grid=(1,), in...]
    ppermute x4, waiting for transfers between devices: 2.82 us -> 3.75 us  [ring(): lax.ppermute(x, 'seq', [(i, (i + s) % shards) for i in range(shards)])]
  transfers between devices with their start and end apart: 15 -> 14, of which waited for: 7 -> 7; matrix products, arithmetic and copies ran while one was open for 1% -> 1% of each run, Pallas kernels for 33% -> 32%
where the time goes in v10:
time: 61.9 us; the launch traced here: 61.7 us
  Pallas kernels  26.9 us (43%)
  starting transfers between devices  21.2 us (34%)
  waiting for transfers between devices  11.1 us (18%)
  between operations  1.41 us (2%)
  other arithmetic  0.64 us (1%)
    pallas_call x4, Pallas kernels, attend(): pl.pallas_call(functools.partial(attend_kernel, g, shards), grid=(1,), in...  21.4 us
    ppermute x7, starting transfers between devices, sum_but_last(): parts.append(lax.ppermute(x, axes, [(i, i ^ flip) for i in range(devices)]))  9.3 us
    ppermute x4, starting transfers between devices, ring(): lax.ppermute(x, 'seq', [(i, (i + s) % shards) for i in range(shards)])  7.38 us
    ppermute x7, waiting for transfers between devices, sum_but_last(): parts.append(lax.ppermute(x, axes, [(i, i ^ flip) for i in range(devices)]))  7.13 us
    ppermute x4, waiting for transfers between devices, ring(): lax.ppermute(x, 'seq', [(i, (i + s) % shards) for i in range(shards)])  3.75 us
    pallas_call x1, Pallas kernels, prep(): pl.pallas_call(functools.partial(prep_kernel, tokens), grid=(KV,), in_spe...  3.67 us
    ppermute x2, starting transfers between devices, earlier(): return lax.ppermute(x, 'seq', [(i + s, i) for i in range(shards - s)])  2.56 us
    ppermute x1, starting transfers between devices, later(): return lax.ppermute(x, 'seq', [(i, i + s) for i in range(shards - s)])  1.93 us
  transfers between devices with their start and end apart: 14, of which 7 were waited for; matrix products, arithmetic and copies ran while one was open for 1% of the time, Pallas kernels for 32%

profile of v10, /device:TPU:0, one launch (start us, length us, event | category | flops | bytes accessed | tf_op | source)
XLA Modules:
  0.0 61.7 jit_solution(16333396853809829712)
XLA Ops:
  0.6 0.0 copy-start
  0.6 0.0 copy-start.1
  0.7 1.1 %pack.3 = bf16[1280,128]{1,0:T(8,128)(2,1)S(1)} custom-call(bf16[512,512]{1,0:T(8,128)(2,1)} %bitcast.21, bf16[512,512]{1,0:T(8,128)(2,1)} %bitcast.28, bf16[128,512]{1,0:T(8,128)(2,1)} %bitcast.35, bf16[128,512]{1,0:T(8,128)(2,1)} %bitcast.41), custom_call_target="tpu_custom_call" | custom-call | bytes 655360 | tf_op jit(solution)/shard_map/pack/pallas_call | solution.py:69
  1.7 3.0 %collective-permute-start.3 = (bf16[1280,128]{1,0:T(8,128)(2,1)S(1)}, bf16[1280,128]{1,0:T(8,128)(2,1)S(1)}, u32[]{:S(2)}, u32[]{:S(2)}) collective-permute-start(bf16[1280,128]{1,0:T(8,128)(2,1)S(1)} %pack.3), channel_id=1, source_target_pairs={{0,1},{1,0},{2,3},{3,2},{4,5},{5,4},{6,7},{7,6},{8,9},{9,8},{10,11... | collective-permute-start | bytes 983048 | tf_op jit(solution)/shard_map/ppermute | solution.py:474
  5.4 0.1 convert_bitcast_fusion
  5.5 0.0 copy-start.2
  5.5 0.0 copy-start.3
  5.5 0.5 fusion
  6.1 0.0 copy-done
  6.1 0.0 copy-done.1
  6.1 0.3 copy-done.2
  6.4 0.1 copy-done.3
  6.5 3.7 %prep.1 = (bf16[4096,128]{1,0:T(8,128)(2,1)S(1)}, bf16[1024,512]{1,0:T(8,128)(2,1)S(1)}, bf16[4096,128]{1,0:T(8,128)(2,1)S(1)}, bf16[1024,512]{1,0:T(8,128)(2,1)...) custom-call(bf16[128,4096]{1,0:T(8,128)(2,1)} %bitcast.49, ...), custom_call_target="tpu_custom_call" | custom-call | flops 2097152 | bytes 6291456 | tf_op jit(solution)/shard_map/prep/pallas_call | solution.py:150
  10.2 1.9 %collective-permute-start.2 = (bf16[2,128,384]{2,1,0:T(8,128)(2,1)S(1)}, bf16[2,128,384]{2,1,0:T(8,128)(2,1)S(1)}, u32[]{:S(2)}, u32[]{:S(2)}) collective-permute-start(bf16[2,128,384]{2,1,0:T(8,128)(2,1)S(1)} %get-tuple-element.56), channel_id=1, source_target_pairs={{0,1},{2,3},{4,5},{6,7},{8,9},{10,11},{12,13},{14,15},{16,17},{18,... | collective-permute-start | bytes 589832 | tf_op jit(solution)/shard_map/ppermute | solution.py:477
  12.1 0.1 collective-permute-start
  12.2 0.3 collective-permute-done.3.refs_17_
  12.5 5.3 %attend.4 = (bf16[128,4096]{1,0:T(8,128)(2,1)}, bf16[128,4096]{1,0:T(8,128)(2,1)}, f32[40,128]{1,0:T(8,128)S(1)}, f32[2,128,128]{2,1,0:T(8,128)S(1)}, bf16[2,128...) custom-call(s32[1]{0:T(128)} %copy.33.refs_0_, s32[1]{0:T(128)} %bitcast.refs_1_, ...), custom_call_target="tpu_custom_call" | custom-call | flops 1476395008 | bytes 2359296 | tf_op jit(solution)/shard_map/attend/pallas_call | solution.py:389
  17.8 1.7 %collective-permute-start.4 = (bf16[1024,128]{1,0:T(8,128)(2,1)S(1)}, bf16[1024,128]{1,0:T(8,128)(2,1)S(1)}, u32[]{:S(2)}, u32[]{:S(2)}) collective-permute-start(bf16[1024,128]{1,0:T(8,128)(2,1)S(1)} %get-tuple-element.57), channel_id=1, source_target_pairs={{0,1},{1,0},{2,3},{3,2},{4,5},{5,4},{6,7},{7,6},{8,9},{9,8},{10,11... | collective-permute-start | bytes 786440 | tf_op jit(solution)/shard_map/ppermute | solution.py:474
  19.6 3.5 %collective-permute-done.refs_2_.refs_17_ = bf16[1024,128]{1,0:T(8,128)(2,1)S(1)} collective-permute-done((bf16[1024,128]{1,0:T(8,128)(2,1)S(1)}, bf16[1024,128]{1,0:T(8,128)(2,1)S(1)}, u32[]{:S(2)}, u32[]{:S(2)}) %collective-permute-start) | collective-permute-done | bytes 262176 | tf_op jit(solution)/shard_map/ppermute | solution.py:474
  23.1 2.5 %collective-permute-start.1 = (bf16[1024,128]{1,0:T(8,128)(2,1)S(1)}, bf16[1024,128]{1,0:T(8,128)(2,1)S(1)}, u32[]{:S(2)}, u32[]{:S(2)}) collective-permute-start(bf16[1024,128]{1,0:T(8,128)(2,1)S(1)} %pack.2), channel_id=1, source_target_pairs={{0,1},{1,0},{2,3},{3,2},{4,5},{5,4},{6,7},{7,6},{8,9},{9,8},{10,11... | collective-permute-start | bytes 786440 | tf_op jit(solution)/shard_map/ppermute | solution.py:474
  25.6 0.0 collective-permute-done.2.refs_18_
  25.6 5.4 %attend.5 = (bf16[128,4096]{1,0:T(8,128)(2,1)}, bf16[128,4096]{1,0:T(8,128)(2,1)}, f32[40,128]{1,0:T(8,128)S(1)}, f32[2,128,128]{2,1,0:T(8,128)S(1)}, bf16[4,128,128]{2,1,0:T(8,128)(2,1)S(1)}) custom-call(s32[1]{0:T(128)} %copy.33.refs_0_, s32[1]{0:T(128)} %bitcast.refs_1_, ...), custom_call_target="tpu_custom_call", output_to_operand_aliasing={{0}: (21, {}), {1}: (22, {})} | custom-call | flops 1476395008 | bytes 2359296 | tf_op jit(solution)/shard_map/attend/pallas_call | solution.py:389
  31.0 1.3 %collective-permute-start.5 = (bf16[4,128,128]{2,1,0:T(8,128)(2,1)S(1)}, bf16[4,128,128]{2,1,0:T(8,128)(2,1)S(1)}, u32[]{:S(2)}, u32[]{:S(2)}) collective-permute-start(bf16[4,128,128]{2,1,0:T(8,128)(2,1)S(1)} %get-tuple-element.69), channel_id=1, source_target_pairs={{1,0},{3,2},{5,4},{7,6},{9,8},{11,10},{13,12},{15,14},{17,16},{19,... | collective-permute-start | bytes 393224 | tf_op jit(solution)/shard_map/ppermute | solution.py:480
  32.3 0.0 collective-permute-done.4.refs_17_
  32.3 5.3 %attend.6 = (bf16[128,4096]{1,0:T(8,128)(2,1)}, bf16[128,4096]{1,0:T(8,128)(2,1)}, f32[40,128]{1,0:T(8,128)S(1)}, f32[2,128,128]{2,1,0:T(8,128)S(1)}, bf16[2,128,128]{2,1,0:T(8,128)(2,1)S(1)}) custom-call(s32[1]{0:T(128)} %copy.33.refs_0_, s32[1]{0:T(128)} %bitcast.refs_1_, ...), custom_call_target="tpu_custom_call", output_to_operand_aliasing={{0}: (20, {}), {1}: (21, {})} | custom-call | flops 1476395008 | bytes 2359296 | tf_op jit(solution)/shard_map/attend/pallas_call | solution.py:389
  37.6 0.2 collective-permute-done.5.refs_23_
  37.8 0.0 collective-permute-done.1.refs_17_
  37.8 5.4 %attend.7 = (bf16[128,4096]{1,0:T(8,128)(2,1)}, bf16[128,4096]{1,0:T(8,128)(2,1)}, f32[40,128]{1,0:T(8,128)S(1)}, f32[2,128,128]{2,1,0:T(8,128)S(1)}, bf16[4,128...) custom-call(s32[1]{0:T(128)} %copy.33.refs_0_, ...), custom_call_target="tpu_custom_call", output_to_operand_aliasing={{0}: (24, {}), {1}: (25, {})} | custom-call | flops 1476395008 | bytes 2359296 | tf_op jit(solution)/shard_map/attend/pallas_call | solution.py:389
  43.2 0.0 collective-permute-start.7
  43.2 1.2 %collective-permute-done.7 = f32[40,128]{1,0:T(8,128)S(1)} collective-permute-done((f32[40,128]{1,0:T(8,128)S(1)}, f32[40,128]{1,0:T(8,128)S(1)}, u32[]{:S(2)}, u32[]{:S(2)}) %collective-permute-start.7) | collective-permute-done | bytes 20512 | tf_op jit(solution)/shard_map/ppermute | solution.py:462
  44.4 3.9 %collective-permute-start.10 = (f32[40,128]{1,0:T(8,128)S(1)}, f32[40,128]{1,0:T(8,128)S(1)}, u32[]{:S(2)}, u32[]{:S(2)}) collective-permute-start(f32[40,128]{1,0:T(8,128)S(1)} %add.66), channel_id=1, source_target_pairs={{0,5},{1,4},{2,7},{3,6},{4,1},{5,0},{6,3},{7,2},{8,13},{9,12},{10,... | collective-permute-start | bytes 61448 | tf_op jit(solution)/shard_map/ppermute | solution.py:462
  48.2 0.0 collective-permute-start.9
  48.3 0.6 collective-permute-start.8
  48.9 1.3 %collective-permute-start.6 = (bf16[4,128,128]{2,1,0:T(8,128)(2,1)S(1)}, bf16[4,128,128]{2,1,0:T(8,128)(2,1)S(1)}, u32[]{:S(2)}, u32[]{:S(2)}) collective-permute-start(bf16[4,128,128]{2,1,0:T(8,128)(2,1)S(1)} %get-tuple-element.76), channel_id=1, source_target_pairs={{1,0},{3,2},{5,4},{7,6},{9,8},{11,10},{13,12},{15,14},{17,16},{19,... | collective-permute-start | bytes 393224 | tf_op jit(solution)/shard_map/ppermute | solution.py:480
  50.2 0.0 collective-permute-done.10
  50.2 1.8 %collective-permute-done.9 = f32[40,128]{1,0:T(8,128)S(1)} collective-permute-done((f32[40,128]{1,0:T(8,128)S(1)}, f32[40,128]{1,0:T(8,128)S(1)}, u32[]{:S(2)}, u32[]{:S(2)}) %collective-permute-start.9) | collective-permute-done | bytes 20512 | tf_op jit(solution)/shard_map/ppermute | solution.py:462
  52.0 0.0 collective-permute-done.8
  52.1 4.2 %collective-permute-start.13 = (f32[40,128]{1,0:T(8,128)S(1)}, f32[40,128]{1,0:T(8,128)S(1)}, u32[]{:S(2)}, u32[]{:S(2)}) collective-permute-start(f32[40,128]{1,0:T(8,128)S(1)} %add_add_fusion.refs_5_), channel_id=1, source_target_pairs={{0,24},{1,25},{2,26},{3,27},{4,28},{5,29},{6,30},{7,31},{8,16},{9,... | collective-permute-start | bytes 61448 | tf_op jit(solution)/shard_map/ppermute | solution.py:462
  56.2 0.0 collective-permute-start.12
  56.2 0.6 %collective-permute-start.11 = (f32[40,128]{1,0:T(8,128)S(1)}, f32[40,128]{1,0:T(8,128)S(1)}, u32[]{:S(2)}, u32[]{:S(2)}) collective-permute-start(f32[40,128]{1,0:T(8,128)S(1)} %add_add_fusion.refs_5_), channel_id=1, source_target_pairs={{0,8},{1,9},{2,10},{3,11},{4,12},{5,13},{6,14},{7,15},{8,0},{9,1},... | collective-permute-start | bytes 61448 | tf_op jit(solution)/shard_map/ppermute | solution.py:462
  56.9 1.1 %collective-permute-done.13.refs_8_ = f32[40,128]{1,0:T(8,128)S(1)} collective-permute-done((f32[40,128]{1,0:T(8,128)S(1)}, f32[40,128]{1,0:T(8,128)S(1)}, u32[]{:S(2)}, u32[]{:S(2)}) %collective-permute-start.13) | collective-permute-done | bytes 20512 | tf_op jit(solution)/shard_map/ppermute | solution.py:462
  58.0 2.9 %collective-permute-done.12.refs_7_ = f32[40,128]{1,0:T(8,128)S(1)} collective-permute-done((f32[40,128]{1,0:T(8,128)S(1)}, f32[40,128]{1,0:T(8,128)S(1)}, u32[]{:S(2)}, u32[]{:S(2)}) %collective-permute-start.12) | collective-permute-done | bytes 20512 | tf_op jit(solution)/shard_map/ppermute | solution.py:462
  60.9 0.0 collective-permute-done.11.refs_6_
  60.9 0.0 collective-permute-done.6.refs_4_
  60.9 0.7 %finish.1 = (bf16[128,512]{1,0:T(8,128)(2,1)}, bf16[128,512]{1,0:T(8,128)(2,1)}, f32[32,128]{1,0:T(8,128)}, f32[4,128]{1,0:T(4,128)}, f32[4,128]{1,0:T(4,128)}) custom-call(f32[256,128]{1,0:T(8,128)S(1)} %get-tuple-element.86.cos_ref.refs_11_.refs_0_, ...), custom_call_target="tpu_custom_call", output_to_operand_aliasing={{0}: (9, {}), {1}: (10, {})} | custom-call | bytes 524288 | tf_op jit(solution)/shard_map/finish/pallas_call | solution.py:433
  (5 shorter events, 0.1 us)
Async XLA Ops:
  0.6 5.4 %copy-start = (bf16[1,512,512]{2,1,0:T(8,128)(2,1)S(1)}, bf16[1,512,512]{2,1,0:T(8,128)(2,1)}, u32[]{:S(2)}) copy-start(bf16[1,512,512]{2,1,0:T(8,128)(2,1)} %param.13) | copy-start | bytes 1572868
  0.6 5.4 %copy-start.1 = (bf16[1,512,512]{2,1,0:T(8,128)(2,1)S(1)}, bf16[1,512,512]{2,1,0:T(8,128)(2,1)}, u32[]{:S(2)}) copy-start(bf16[1,512,512]{2,1,0:T(8,128)(2,1)} %param.14) | copy-start | bytes 1572868
  1.7 10.7 %collective-permute-start.3 = (bf16[1280,128]{1,0:T(8,128)(2,1)S(1)}, bf16[1280,128]{1,0:T(8,128)(2,1)S(1)}, u32[]{:S(2)}, u32[]{:S(2)}) collective-permute-start(bf16[1280,128]{1,0:T(8,128)(2,1)S(1)} %pack.3), channel_id=1, source_target_pairs={{0,1},{1,0},{2,3},{3,2},{4,5},{5,4},{6,7},{7,6},{8,9},{9,8},{10,11... | collective-permute-start | bytes 983048 | tf_op jit(solution)/shard_map/ppermute | solution.py:474
  5.5 0.9 %copy-start.2 = (bf16[1,128,512]{2,1,0:T(8,128)(2,1)S(1)}, bf16[1,128,512]{2,1,0:T(8,128)(2,1)}, u32[]{:S(2)}) copy-start(bf16[1,128,512]{2,1,0:T(8,128)(2,1)} %param.11) | copy-start | bytes 393220
  5.5 1.0 %copy-start.3 = (bf16[1,128,512]{2,1,0:T(8,128)(2,1)S(1)}, bf16[1,128,512]{2,1,0:T(8,128)(2,1)}, u32[]{:S(2)}) copy-start(bf16[1,128,512]{2,1,0:T(8,128)(2,1)} %param.12) | copy-start | bytes 393220
  10.2 15.4 %collective-permute-start.2 = (bf16[2,128,384]{2,1,0:T(8,128)(2,1)S(1)}, bf16[2,128,384]{2,1,0:T(8,128)(2,1)S(1)}, u32[]{:S(2)}, u32[]{:S(2)}) collective-permute-start(bf16[2,128,384]{2,1,0:T(8,128)(2,1)S(1)} %get-tuple-element.56), channel_id=1, source_target_pairs={{0,1},{2,3},{4,5},{6,7},{8,9},{10,11},{12,13},{14,15},{16,17},{18,... | collective-permute-start | bytes 589832 | tf_op jit(solution)/shard_map/ppermute | solution.py:477
  12.1 10.9 %collective-permute-start = (bf16[1024,128]{1,0:T(8,128)(2,1)S(1)}, bf16[1024,128]{1,0:T(8,128)(2,1)S(1)}, u32[]{:S(2)}, u32[]{:S(2)}) collective-permute-start(bf16[1024,128]{1,0:T(8,128)(2,1)S(1)} %get-tuple-element.55), channel_id=1, source_target_pairs={{0,1},{1,0},{2,3},{3,2},{4,5},{5,4},{6,7},{7,6},{8,9},{9,8},{10,11... | collective-permute-start | bytes 786440 | tf_op jit(solution)/shard_map/ppermute | solution.py:474
  17.8 14.4 %collective-permute-start.4 = (bf16[1024,128]{1,0:T(8,128)(2,1)S(1)}, bf16[1024,128]{1,0:T(8,128)(2,1)S(1)}, u32[]{:S(2)}, u32[]{:S(2)}) collective-permute-start(bf16[1024,128]{1,0:T(8,128)(2,1)S(1)} %get-tuple-element.57), channel_id=1, source_target_pairs={{0,1},{1,0},{2,3},{3,2},{4,5},{5,4},{6,7},{7,6},{8,9},{9,8},{10,11... | collective-permute-start | bytes 786440 | tf_op jit(solution)/shard_map/ppermute | solution.py:474
  23.1 14.8 %collective-permute-start.1 = (bf16[1024,128]{1,0:T(8,128)(2,1)S(1)}, bf16[1024,128]{1,0:T(8,128)(2,1)S(1)}, u32[]{:S(2)}, u32[]{:S(2)}) collective-permute-start(bf16[1024,128]{1,0:T(8,128)(2,1)S(1)} %pack.2), channel_id=1, source_target_pairs={{0,1},{1,0},{2,3},{3,2},{4,5},{5,4},{6,7},{7,6},{8,9},{9,8},{10,11... | collective-permute-start | bytes 786440 | tf_op jit(solution)/shard_map/ppermute | solution.py:474
  31.0 6.8 %collective-permute-start.5 = (bf16[4,128,128]{2,1,0:T(8,128)(2,1)S(1)}, bf16[4,128,128]{2,1,0:T(8,128)(2,1)S(1)}, u32[]{:S(2)}, u32[]{:S(2)}) collective-permute-start(bf16[4,128,128]{2,1,0:T(8,128)(2,1)S(1)} %get-tuple-element.69), channel_id=1, source_target_pairs={{1,0},{3,2},{5,4},{7,6},{9,8},{11,10},{13,12},{15,14},{17,16},{19,... | collective-permute-start | bytes 393224 | tf_op jit(solution)/shard_map/ppermute | solution.py:480
  43.2 1.2 %collective-permute-start.7 = (f32[40,128]{1,0:T(8,128)S(1)}, f32[40,128]{1,0:T(8,128)S(1)}, u32[]{:S(2)}, u32[]{:S(2)}) collective-permute-start(f32[40,128]{1,0:T(8,128)S(1)} %get-tuple-element.77), channel_id=1, source_target_pairs={{0,2},{1,3},{2,0},{3,1},{4,6},{5,7},{6,4},{7,5},{8,10},{9,11},{10,... | collective-permute-start | bytes 61448 | tf_op jit(solution)/shard_map/ppermute | solution.py:462
  44.4 5.8 %collective-permute-start.10 = (f32[40,128]{1,0:T(8,128)S(1)}, f32[40,128]{1,0:T(8,128)S(1)}, u32[]{:S(2)}, u32[]{:S(2)}) collective-permute-start(f32[40,128]{1,0:T(8,128)S(1)} %add.66), channel_id=1, source_target_pairs={{0,5},{1,4},{2,7},{3,6},{4,1},{5,0},{6,3},{7,2},{8,13},{9,12},{10,... | collective-permute-start | bytes 61448 | tf_op jit(solution)/shard_map/ppermute | solution.py:462
  48.2 3.8 %collective-permute-start.9 = (f32[40,128]{1,0:T(8,128)S(1)}, f32[40,128]{1,0:T(8,128)S(1)}, u32[]{:S(2)}, u32[]{:S(2)}) collective-permute-start(f32[40,128]{1,0:T(8,128)S(1)} %add.66), channel_id=1, source_target_pairs={{0,4},{1,5},{2,6},{3,7},{4,0},{5,1},{6,2},{7,3},{8,12},{9,13},{10,... | collective-permute-start | bytes 61448 | tf_op jit(solution)/shard_map/ppermute | solution.py:462
  48.3 3.8 %collective-permute-start.8 = (f32[40,128]{1,0:T(8,128)S(1)}, f32[40,128]{1,0:T(8,128)S(1)}, u32[]{:S(2)}, u32[]{:S(2)}) collective-permute-start(f32[40,128]{1,0:T(8,128)S(1)} %add.66), channel_id=1, source_target_pairs={{0,1},{1,0},{2,3},{3,2},{4,5},{5,4},{6,7},{7,6},{8,9},{9,8},{10,11... | collective-permute-start | bytes 61448 | tf_op jit(solution)/shard_map/ppermute | solution.py:462
  48.9 12.0 %collective-permute-start.6 = (bf16[4,128,128]{2,1,0:T(8,128)(2,1)S(1)}, bf16[4,128,128]{2,1,0:T(8,128)(2,1)S(1)}, u32[]{:S(2)}, u32[]{:S(2)}) collective-permute-start(bf16[4,128,128]{2,1,0:T(8,128)(2,1)S(1)} %get-tuple-element.76), channel_id=1, source_target_pairs={{1,0},{3,2},{5,4},{7,6},{9,8},{11,10},{13,12},{15,14},{17,16},{19,... | collective-permute-start | bytes 393224 | tf_op jit(solution)/shard_map/ppermute | solution.py:480
  52.1 5.9 %collective-permute-start.13 = (f32[40,128]{1,0:T(8,128)S(1)}, f32[40,128]{1,0:T(8,128)S(1)}, u32[]{:S(2)}, u32[]{:S(2)}) collective-permute-start(f32[40,128]{1,0:T(8,128)S(1)} %add_add_fusion.refs_5_), channel_id=1, source_target_pairs={{0,24},{1,25},{2,26},{3,27},{4,28},{5,29},{6,30},{7,31},{8,16},{9,... | collective-permute-start | bytes 61448 | tf_op jit(solution)/shard_map/ppermute | solution.py:462
  56.2 4.7 %collective-permute-start.12 = (f32[40,128]{1,0:T(8,128)S(1)}, f32[40,128]{1,0:T(8,128)S(1)}, u32[]{:S(2)}, u32[]{:S(2)}) collective-permute-start(f32[40,128]{1,0:T(8,128)S(1)} %add_add_fusion.refs_5_), channel_id=1, source_target_pairs={{0,16},{1,17},{2,18},{3,19},{4,20},{5,21},{6,22},{7,23},{8,24},{9,... | collective-permute-start | bytes 61448 | tf_op jit(solution)/shard_map/ppermute | solution.py:462
  56.2 4.7 %collective-permute-start.11 = (f32[40,128]{1,0:T(8,128)S(1)}, f32[40,128]{1,0:T(8,128)S(1)}, u32[]{:S(2)}, u32[]{:S(2)}) collective-permute-start(f32[40,128]{1,0:T(8,128)S(1)} %add_add_fusion.refs_5_), channel_id=1, source_target_pairs={{0,8},{1,9},{2,10},{3,11},{4,12},{5,13},{6,14},{7,15},{8,0},{9,1},... | collective-permute-start | bytes 61448 | tf_op jit(solution)/shard_map/ppermute | solution.py:462

commit v11 on v9

--- a/solution.py
+++ b/solution.py
@@ -43,51 +43,39 @@
     return pltpu.CompilerParams(dimension_semantics=("arbitrary",), vmem_limit_bytes=VMEM)
 
 
-def copy_chunk(g, ck_ref, cv_ref, out_ref):
-    rows = ck_ref.shape[0]
-    cols = pl.ds(g * HD, HD)
-    out_ref[pl.ds(0, rows)] = ck_ref[:, cols]
-    out_ref[pl.ds(rows, rows)] = cv_ref[:, cols]
-
-
-def pack_kernel(ck_ref, cv_ref, *rest):
-    copy_chunk(0, ck_ref, cv_ref, rest[-1])
-
-
-def pack(g, ck, cv, *after):
-    rows = ck.shape[0]
+def copy_chunk(cols, sources, out_ref):
+    start = 0
+    for ref in sources:
+        rows = ref.shape[0]
+        out_ref[pl.ds(start, rows)] = ref[:, cols]
+        start += rows
+
+
+def pack_kernel(*refs):
+    copy_chunk(pl.ds(0, HD), refs[:-1], refs[-1])
+
+
+def pack(sources):
+    rows = sum(x.shape[0] for x in sources)
     return pl.pallas_call(
         pack_kernel,
         grid=(1,),
-        in_specs=[column(rows, g)] * 2 + [pl.BlockSpec(memory_space=pl.ANY)] * len(after),
+        in_specs=[column(x.shape[0], 0) for x in sources],
         out_specs=pl.BlockSpec(memory_space=pltpu.VMEM),
-        out_shape=pltpu.VMEM((2 * rows, HD), B16),
+        out_shape=pltpu.VMEM((rows, HD), B16),
         compiler_params=params(),
-        cost_estimate=pl.CostEstimate(flops=0, bytes_accessed=8 * rows * HD, transcendentals=0),
+        cost_estimate=pl.CostEstimate(flops=0, bytes_accessed=4 * rows * HD, transcendentals=0),
         name="pack",
-    )(ck, cv, *after)
+    )(*sources)
 
 
 def turn_back(x, cosine, sine):
     return x * cosine - turn(x) * sine
 
 
-def finish_heads(heads, shards, tables, owns, backs, gk_ref, gv_ref):
-    tokens = gk_ref.shape[0]
-    cosine, sine = (t[pl.ds(0, tokens), :] for t in tables)
-    for i in range(heads):
-        dk, dv = owns[i][0], owns[i][1]
-        for s in range(shards - 1):
-            dk = dk + backs[s][2 * i].astype(F32)
-            dv = dv + backs[s][2 * i + 1].astype(F32)
-        cols = pl.ds(i * HD, HD)
-        gk_ref[:, cols] = turn_back(dk, cosine, sine).astype(B16)
-        gv_ref[:, cols] = dv.astype(B16)
-
-
 def prep_kernel(
     tokens, q_ref, do_ref, bq_ref, bk_ref, bv_ref, cos_ref, sin_ref, ck_ref, cv_ref,
-    qs_ref, qst_ref, dos_ref, dot_ref, bias_ref, cos_t_ref, sin_t_ref, ck_t_ref, cv_t_ref, pack_ref,
+    kp_ref, vp_ref, qs_ref, qst_ref, dos_ref, dot_ref, bias_ref, cos_t_ref, sin_t_ref, ck_t_ref, cv_t_ref, pack_ref,
 ):
     g = pl.program_id(0)
     cosine, sine = cos_ref[pl.ds(0, tokens), :], sin_ref[pl.ds(0, tokens), :]
@@ -99,7 +87,7 @@
         bias_ref[pl.ds(KV, KV), :] = bv_ref[...].astype(F32)
         cos_t_ref[...] = cosine.T
         sin_t_ref[...] = sine.T
-        copy_chunk(1, ck_ref, cv_ref, pack_ref)
+        copy_chunk(pl.ds(HD, HD), (ck_ref, cv_ref, kp_ref, vp_ref), pack_ref)
 
     for h in range(GROUP):
         cols = pl.ds(h * HD, HD)
@@ -118,7 +106,7 @@
     cv_t_ref[mine, :] = cv_ref[:, mine].T
 
 
-def prep(q, do, bq, bk, bv, cosine, sine, ck, cv):
+def prep(q, do, bq, bk, bv, cosine, sine, ck, cv, kp, vp):
     tokens, slots = q.shape[0], ck.shape[0]
     vmem = pl.BlockSpec(memory_space=pltpu.VMEM)
     wide = pl.BlockSpec((tokens, GROUP * HD), lambda i: (0, i))
@@ -131,14 +119,14 @@
         pltpu.VMEM((HD, tokens), F32),
         pltpu.VMEM((KV * HD, slots), B16),
         pltpu.VMEM((KV * HD, slots), B16),
-        pltpu.VMEM((2 * slots, HD), B16),
+        pltpu.VMEM((2 * (slots + tokens), HD), B16),
     ]
     return pl.pallas_call(
         functools.partial(prep_kernel, tokens),
         grid=(KV,),
         in_specs=[
             wide, wide, pl.BlockSpec((GROUP, HD), lambda i: (i, 0)),
-            whole((KV, HD)), whole((KV, HD)), vmem, vmem, vmem, vmem,
+            whole((KV, HD)), whole((KV, HD)), *[vmem] * 6,
         ],
         out_specs=[vmem] * len(out_shape),
         out_shape=out_shape,
@@ -147,7 +135,7 @@
             flops=4 * tokens * HQ * HD, bytes_accessed=12 * tokens * HQ * HD, transcendentals=0
         ),
         name="prep",
-    )(q, do, bq, bk, bv, cosine, sine, ck, cv)
+    )(q, do, bq, bk, bv, cosine, sine, ck, cv, kp, vp)
 
 
 def fold(x, op):
@@ -165,20 +153,15 @@
     (first_ref, rank_ref, qs_ref, qst_ref, dos_ref, dot_ref, bias_ref, cos_t_ref, sin_t_ref,
      ck_t_ref, cv_t_ref, cos_ref, sin_ref, ck_ref, cv_ref, kp_ref, vp_ref) = take(17)
     far = take(shards - 1)
-    far_k = take(shards - 1)
-    far_v = take(shards - 1)
     old_sums_ref = take(1)[0] if g else None
-    old_send = take(shards - 1) if g % 2 else []
-    owns = take(2) if g == KV - 1 else []
-    backs = take(shards - 1) if g == KV - 1 else []
+    old_send = take(shards - 1) if g else []
     if g:
         take(2)
     out_ref, gq_ref, sums_ref, own_ref = take(4)
     send = take(shards - 1)
     pack_ref = take(1)[0] if g + 2 < KV else None
-    gk_ref, gv_ref = take(2) if g == KV - 1 else (None, None)
     keys, values, keys_t, values_t, dk_acc, dv_acc = take(6)
-    scratch = take(3)
+    scratch = [take(3) for _ in range(GROUP // HEADS)]
     tokens = kp_ref.shape[0]
     slots = ck_ref.shape[0]
     prefix = shards * slots
@@ -189,7 +172,7 @@
     mine = pl.ds(g * HD, HD)
 
     if pack_ref is not None:
-        copy_chunk(g + 2, ck_ref, cv_ref, pack_ref)
+        copy_chunk(pl.ds((g + 2) * HD, HD), (ck_ref, cv_ref, kp_ref, vp_ref), pack_ref)
     keys[pl.ds(0, slots)] = ck_ref[:, mine]
     values[pl.ds(0, slots)] = cv_ref[:, mine]
     for s in range(1, shards):
@@ -197,10 +180,13 @@
         values[pl.ds(s * slots, slots)] = far[s - 1][pl.ds(slots, slots)]
     for s in range(shards):
         rows = pl.ds(s * tokens, tokens)
-        kp, vp = (kp_ref, vp_ref) if s == 0 else (far_k[s - 1], far_v[s - 1])
-        k = kp[:, mine].astype(F32) + bias_ref[g:g + 1, :]
+        if s == 0:
+            kp, vp = kp_ref[:, mine], vp_ref[:, mine]
+        else:
+            kp, vp = (far[s - 1][pl.ds(2 * slots + i * tokens, tokens)] for i in range(2))
+        k = kp.astype(F32) + bias_ref[g:g + 1, :]
         k = k * cos_ref[rows, :] + turn(k) * sin_ref[rows, :]
-        v = vp[:, mine].astype(F32) + bias_ref[KV + g:KV + g + 1, :]
+        v = vp.astype(F32) + bias_ref[KV + g:KV + g + 1, :]
         place = pl.ds(prefix + s * tokens, tokens)
         keys[place] = k.astype(B16)
         values[place] = v.astype(B16)
@@ -227,8 +213,9 @@
 
     class Chain:
         def __init__(self, index):
-            self.index = index
-            self.s, self.pb, self.ds = scratch
+            self.index = g * (GROUP // HEADS) + index
+            self.s, self.pb, self.ds = scratch[index]
+            index = self.index
             self.rows = pl.ds(pl.multiple_of(index * width, width), width)
             self.place = pl.ds(pl.multiple_of(index * HD, HD), HD)
             self.top = jnp.full((8, width), NEG, F32)
@@ -241,7 +228,7 @@
                 self.s[pl.ds(start, tokens), :] = part
                 self.top = jnp.maximum(self.top, fold(part, jnp.max))
 
-        def probs(self):
+        def exponents(self):
             top = jnp.max(self.top, axis=0, keepdims=True)
             weight = jnp.zeros((8, width), F32)
             for start in blocks:
@@ -249,10 +236,12 @@
                 e = jnp.exp2((self.s[rows, :] - top) * (scale * math.log2(math.e)))
                 self.s[rows, :] = e
                 weight = weight + fold(e, jnp.sum)
-            inverse = 1.0 / jnp.sum(weight, axis=0, keepdims=True)
+            self.inverse = 1.0 / jnp.sum(weight, axis=0, keepdims=True)
+
+        def probs(self):
             for start in blocks:
                 rows = pl.ds(start, tokens)
-                p = self.s[rows, :] * inverse
+                p = self.s[rows, :] * self.inverse
                 self.s[rows, :] = p
                 self.pb[rows, :] = p.astype(B16)
 
@@ -270,11 +259,13 @@
                     head,
                 )
 
+        def dprobs(self):
+            self.dp = dot(values[...], dot_ref[self.place, :], NN)
+
         def dscores(self):
-            dp = dot(values[...], dot_ref[self.place, :], NN)
             for start in blocks:
                 rows = pl.ds(start, tokens)
-                part = dp[start:start + tokens]
+                part = self.dp[start:start + tokens]
                 self.ds[rows, :] = (self.s[rows, :] * (part - self.delta)).astype(B16)
 
         def query_grad(self):
@@ -294,61 +285,49 @@
                 gq_ref[:, cols] = x.astype(B16)
                 sums_ref[pl.ds(head, 1), :] = jnp.sum(x, axis=0, keepdims=True)
 
-    def heads_step(i, carry):
-        chain = Chain(g * (GROUP // HEADS) + i)
-        chain.scores()
-        chain.probs()
-        chain.output()
-        chain.dscores()
-        chain.query_grad()
-        chain.slab_grads()
-        chain.store()
-        return carry
-
-    lax.fori_loop(0, GROUP // HEADS, heads_step, 0)
+    steps = [
+        Chain.scores, Chain.exponents, Chain.dprobs, Chain.probs, Chain.output,
+        Chain.dscores, Chain.query_grad, Chain.slab_grads, Chain.store,
+    ]
+    group = [Chain(i) for i in range(GROUP // HEADS)]
+    for turn_of in range(len(steps) + len(group) - 1):
+        for i, chain in reversed(list(enumerate(group))):
+            if 0 <= turn_of - i < len(steps):
+                steps[turn_of - i](chain)
 
     dk = dk_acc[...] * scale
     dv = dv_acc[...]
     gk = turn_back(dk, cos_ref[...], sin_ref[...])
     own_ref[0] = dk[:tokens]
     own_ref[1] = dv[:tokens]
-    at = 2 * (g % 2)
+    at = 2 * g
     for j in range(1, shards):
         block = slice(j * tokens, (j + 1) * tokens)
         send[j - 1][at] = dk[block].astype(B16)
         send[j - 1][at + 1] = dv[block].astype(B16)
-        if at:
+        if g:
             send[j - 1][pl.ds(0, at)] = old_send[j - 1][...]
     sums_ref[pl.ds(HQ + g, 1), :] = jnp.sum(gk, axis=0, keepdims=True)
     sums_ref[pl.ds(HQ + KV + g, 1), :] = jnp.sum(dv, axis=0, keepdims=True)
-    if gk_ref is not None:
-        finish_heads(2, shards, (cos_ref, sin_ref), owns, backs, gk_ref, gv_ref)
 
 
 def attend(
-    g, shards, first, rank, prepared, cosine, sine, ck, cv, kp, vp, far, far_k, far_v,
-    before, owns, backs,
+    g, shards, first, rank, prepared, cosine, sine, ck, cv, kp, vp, far, before
 ):
     tokens, slots = kp.shape[0], ck.shape[0]
     slab = shards * tokens
     total = slab + shards * slots
-    last = g == KV - 1
     smem = pl.BlockSpec(memory_space=pltpu.SMEM)
     vmem = pl.BlockSpec(memory_space=pltpu.VMEM)
     anywhere = pl.BlockSpec(memory_space=pl.ANY)
     wide = pl.BlockSpec((tokens, GROUP * HD), lambda i: (0, g))
-    half = pl.BlockSpec((tokens, 2 * HD), lambda i: (0, 0))
 
     args = [first, rank]
-    placed = [*prepared, cosine, sine, ck, cv, kp, vp, *far, *far_k, *far_v]
+    placed = [*prepared, cosine, sine, ck, cv, kp, vp, *far]
     aliases = {}
     if before is not None:
         out, gq, sums, send = before
-        placed.append(sums)
-        if g % 2:
-            placed += send
-        if last:
-            placed += [*owns[:2], *backs]
+        placed += [sums, *send]
     args += placed
     in_specs = [smem] * 2 + [vmem] * len(placed)
     if before is not None:
@@ -362,14 +341,11 @@
         pltpu.VMEM((2, tokens, HD), F32),
     ]
     out_specs = [wide, wide, vmem, vmem]
-    out_shape += [pltpu.VMEM((2 + 2 * (g % 2), tokens, HD), B16)] * (shards - 1)
+    out_shape += [pltpu.VMEM((2 * g + 2, tokens, HD), B16)] * (shards - 1)
     out_specs += [vmem] * (shards - 1)
     if g + 2 < KV:
-        out_shape.append(pltpu.VMEM((2 * slots, HD), B16))
+        out_shape.append(pltpu.VMEM((2 * (slots + tokens), HD), B16))
         out_specs.append(vmem)
-    if last:
-        out_shape += [pltpu.HBM((tokens, KV * HD), B16)] * 2
-        out_specs += [half] * 2
     results = pl.pallas_call(
         functools.partial(attend_kernel, g, shards),
         grid=(1,),
@@ -381,7 +357,7 @@
             pltpu.VMEM((HD, total), B16), pltpu.VMEM((HD, total), B16),
             pltpu.VMEM((slab, HD), F32), pltpu.VMEM((slab, HD), F32),
         ] + [
-            pltpu.VMEM((total, HEADS * tokens), kind) for kind in (F32, B16, B16)
+            pltpu.VMEM((total, HEADS * tokens), kind) for kind in (F32, B16, B16) * (GROUP // HEADS)
         ],
         input_output_aliases=aliases,
         compiler_params=params(),
@@ -398,10 +374,20 @@
 
 
 def finish_kernel(shards, *refs):
-    owns, backs = refs[2:4], refs[4:4 + shards - 1]
-    sums = refs[4 + shards - 1:-7]
-    gk_ref, gv_ref, *parts = refs[-5:]
-    finish_heads(2, shards, refs[:2], owns, backs, gk_ref, gv_ref)
+    cos_ref, sin_ref, *refs = refs
+    owns, refs = refs[:KV], refs[KV:]
+    backs, refs = refs[:shards - 1], refs[shards - 1:]
+    sums, (gk_ref, gv_ref, *parts) = refs[:-5], refs[-5:]
+    tokens = gk_ref.shape[0]
+    cosine, sine = cos_ref[pl.ds(0, tokens), :], sin_ref[pl.ds(0, tokens), :]
+    for g in range(KV):
+        dk, dv = owns[g][0], owns[g][1]
+        for back in backs:
+            dk = dk + back[2 * g].astype(F32)
+            dv = dv + back[2 * g + 1].astype(F32)
+        cols = pl.ds(g * HD, HD)
+        gk_ref[:, cols] = turn_back(dk, cosine, sine).astype(B16)
+        gv_ref[:, cols] = dv.astype(B16)
     start = 0
     for part in parts:
         rows = pl.ds(start, part.shape[0])
@@ -409,23 +395,20 @@
         start += part.shape[0]
 
 
-def finish(shards, cosine, sine, owns, backs, sums, gk, gv):
-    tokens = gk.shape[0]
+def finish(shards, tokens, cosine, sine, owns, backs, sums):
     vmem = pl.BlockSpec(memory_space=pltpu.VMEM)
     args = [cosine, sine, *owns, *backs, *sums]
-    heads = [(HQ, HD), (KV, HD), (KV, HD)]
+    shapes = [((tokens, KV * HD), B16)] * 2 + [((rows, HD), F32) for rows in (HQ, KV, KV)]
     return pl.pallas_call(
         functools.partial(finish_kernel, shards),
         grid=(1,),
-        in_specs=[vmem] * len(args) + [pl.BlockSpec(memory_space=pl.ANY)] * 2,
-        out_specs=[pl.BlockSpec((tokens, 2 * HD), lambda i: (0, 1))] * 2
-        + [whole(shape) for shape in heads],
-        out_shape=[pltpu.HBM(gk.shape, B16)] * 2 + [pltpu.HBM(shape, F32) for shape in heads],
-        input_output_aliases={len(args): 0, len(args) + 1: 1},
+        in_specs=[vmem] * len(args),
+        out_specs=[whole(shape) for shape, _ in shapes],
+        out_shape=[pltpu.HBM(shape, kind) for shape, kind in shapes],
         compiler_params=params(),
         cost_estimate=pl.CostEstimate(flops=0, bytes_accessed=1 << 19, transcendentals=0),
         name="finish",
-    )(*args, gk, gv)
+    )(*args)
 
 
 def add_up(parts):
@@ -436,7 +419,7 @@
 
 def sum_but_last(x, axes, near):
     devices = lax.axis_size(axes)
-    bits = [1 << i for i in range(devices.bit_length() - 1) if 1 << i != near]
+    bits = [1 << i for i in reversed(range(devices.bit_length() - 1)) if 1 << i != near]
     stages = [[near]] + [bits[i:i + 2] for i in range(0, len(bits), 2)]
     parts = [x]
     for stage in stages:
@@ -451,22 +434,17 @@
     shards = lax.axis_size("seq")
     rank = lax.axis_index("seq").astype(jnp.int32)
     tokens = q_proj.shape[1]
+    shifts = range(1, shards)
     ck, cv, kp, vp = cache_k[0], cache_v[0], k_proj[0], v_proj[0]
 
     def ring(x, s):
         return lax.ppermute(x, "seq", [(i, (i + s) % shards) for i in range(shards)])
 
-    def later(x, s):
-        return lax.ppermute(x, "seq", [(i, i + s) for i in range(shards - s)])
-
     def earlier(x, s):
         return lax.ppermute(x, "seq", [(i + s, i) for i in range(shards - s)])
 
-    shifts = range(1, shards)
-    far_k = [later(kp, s) for s in shifts]
-    far_v = [later(vp, s) for s in shifts]
     hbm = functools.partial(pltpu.with_memory_space_constraint, memory_space=pltpu.HBM)
-    chunk = pack(0, hbm(ck), hbm(cv))
+    chunk = pack([hbm(x) for x in (ck, cv, kp, vp)])
     far = [[ring(chunk, s) for s in shifts]]
 
     owners = lax.rem(rank - jnp.arange(shards, dtype=jnp.int32) + shards, shards)
@@ -481,23 +459,21 @@
 
     *prepared, chunk = prep(
         hbm(q_proj[0]), hbm(dout[0]), hbm(bias_q.reshape(HQ, HD)),
-        hbm(bias_k.reshape(KV, HD)), hbm(bias_v.reshape(KV, HD)), cosine, sine, ck, cv,
+        hbm(bias_k.reshape(KV, HD)), hbm(bias_v.reshape(KV, HD)), cosine, sine, ck, cv, kp, vp,
     )
     far.append([ring(chunk, s) for s in shifts])
-    before, owns, backs = None, [], []
+    before, owns = None, []
     for g in range(KV):
         before, own, more = attend(
             g, shards, start, rank.reshape(1), prepared, cosine, sine, ck, cv, kp, vp,
-            far[g], far_k, far_v, before, owns, backs,
+            far[g], before,
         )
         owns.append(own)
-        if g + 2 < KV:
-            far.append([ring(more[0], s) for s in shifts])
-        if g % 2:
-            backs = [earlier(x, s) for s, x in zip(shifts, before[3])]
-    out, gq, sums, _ = before
-    parts = sum_but_last(sums, ("dp", "seq"), shards)
-    gk, gv, *sums = finish(shards, cosine, sine, owns[2:], backs, parts, *more)
+        far += [[ring(chunk, s) for s in shifts] for chunk in more]
+    out, gq, sums, send = before
+    backs = [earlier(x, s) for s, x in zip(shifts, send)]
+    sums = sum_but_last(sums, ("dp", "seq"), shards)
+    gk, gv, *sums = finish(shards, tokens, cosine, sine, owns, backs, sums)
     return (out[None], gq[None], gk[None], gv[None], *[x.reshape(-1) for x in sums])
 
 

time: 60.7 us -> 56.2 us (0.926)
  starting transfers between devices: 21.3 us -> 16.7 us
  Pallas kernels: 26 us -> 24.7 us
  waiting for transfers between devices: 11 us -> 12.2 us
    ppermute x2 -> x0, starting transfers between devices: 6.18 us -> none  [later(): return lax.ppermute(x, 'seq', [(i, i + s) for i in range(shards - s)])]
    ppermute x4, starting transfers between devices: 4.66 us -> 7.38 us  [ring(): lax.ppermute(x, 'seq', [(i, (i + s) % shards) for i in range(shards)])]
    ppermute x2 -> x1, waiting for transfers between devices: 2.13 us -> 0.01 us  [earlier(): return lax.ppermute(x, 'seq', [(i + s, i) for i in range(shards - s)])]
    ppermute x4, waiting for transfers between devices: 2.82 us -> 4.79 us  [ring(): lax.ppermute(x, 'seq', [(i, (i + s) % shards) for i in range(shards)])]
    ppermute x7, waiting for transfers between devices: 6.07 us -> 7.4 us  [sum_but_last(): parts.append(lax.ppermute(x, axes, [(i, i ^ flip) for i in range(devices)]))]
    pallas_call x4, Pallas kernels: 20.4 us -> 19.1 us  [attend(): pl.pallas_call(functools.partial(attend_kernel, g, shards), grid=(1,), in...]
    ppermute x2 -> x1, starting transfers between devices: 2.56 us -> 1.28 us  [earlier(): return lax.ppermute(x, 'seq', [(i + s, i) for i in range(shards - s)])]
  transfers between devices with their start and end apart: 15 -> 12, of which waited for: 7 -> 9; matrix products, arithmetic and copies ran while one was open for 1% -> 1% of each run, Pallas kernels for 33% -> 32%
where the time goes in v11:
time: 56.2 us; the launch traced here: 56 us
  Pallas kernels  24.7 us (44%)
  starting transfers between devices  16.7 us (30%)
  waiting for transfers between devices  12.2 us (22%)
  between operations  1.38 us (2%)
  other arithmetic  0.64 us (1%)
    pallas_call x4, Pallas kernels, attend(): pl.pallas_call(functools.partial(attend_kernel, g, shards), grid=(1,), in...  19.1 us
    ppermute x7, starting transfers between devices, sum_but_last(): parts.append(lax.ppermute(x, axes, [(i, i ^ flip) for i in range(devices)]))  8.01 us
    ppermute x7, waiting for transfers between devices, sum_but_last(): parts.append(lax.ppermute(x, axes, [(i, i ^ flip) for i in range(devices)]))  7.4 us
    ppermute x4, starting transfers between devices, ring(): lax.ppermute(x, 'seq', [(i, (i + s) % shards) for i in range(shards)])  7.38 us
    ppermute x4, waiting for transfers between devices, ring(): lax.ppermute(x, 'seq', [(i, (i + s) % shards) for i in range(shards)])  4.79 us
    pallas_call x1, Pallas kernels, prep(): pl.pallas_call(functools.partial(prep_kernel, tokens), grid=(KV,), in_spe...  3.68 us
    ppermute x1, starting transfers between devices, earlier(): return lax.ppermute(x, 'seq', [(i + s, i) for i in range(shards - s)])  1.28 us
  transfers between devices with their start and end apart: 12, of which 9 were waited for; matrix products, arithmetic and copies ran while one was open for 1% of the time, Pallas kernels for 32%

profile of v11, /device:TPU:0, one launch (start us, length us, event | category | flops | bytes accessed | tf_op | source)
XLA Modules:
  0.0 56.0 jit_solution(13786792972037876588)
XLA Ops:
  0.6 0.0 copy-start
  0.6 0.0 copy-start.1
  0.7 1.1 %pack.1 = bf16[1280,128]{1,0:T(8,128)(2,1)S(1)} custom-call(bf16[512,512]{1,0:T(8,128)(2,1)} %bitcast.21, bf16[512,512]{1,0:T(8,128)(2,1)} %bitcast.27, bf16[128,512]{1,0:T(8,128)(2,1)} %bitcast.33, bf16[128,512]{1,0:T(8,128)(2,1)} %bitcast.39), custom_call_target="tpu_custom_call" | custom-call | bytes 655360 | tf_op jit(solution)/shard_map/pack/pallas_call | solution.py:60
  1.7 3.0 %collective-permute-start.1 = (bf16[1280,128]{1,0:T(8,128)(2,1)S(1)}, bf16[1280,128]{1,0:T(8,128)(2,1)S(1)}, u32[]{:S(2)}, u32[]{:S(2)}) collective-permute-start(bf16[1280,128]{1,0:T(8,128)(2,1)S(1)} %pack.1), channel_id=1, source_target_pairs={{0,1},{1,0},{2,3},{3,2},{4,5},{5,4},{6,7},{7,6},{8,9},{9,8},{10,11... | collective-permute-start | bytes 983048 | tf_op jit(solution)/shard_map/ppermute | solution.py:441
  5.5 0.1 convert_bitcast_fusion
  5.5 0.0 copy-start.2
  5.5 0.0 copy-start.3
  5.5 0.5 fusion
  6.1 0.0 copy-done
  6.1 0.0 copy-done.1
  6.1 0.3 copy-done.2
  6.4 0.1 copy-done.3
  6.5 3.7 %prep.1 = (bf16[4096,128]{1,0:T(8,128)(2,1)S(1)}, bf16[1024,512]{1,0:T(8,128)(2,1)S(1)}, bf16[4096,128]{1,0:T(8,128)(2,1)S(1)}, bf16[1024,512]{1,0:T(8,128)(2,1)...) custom-call(bf16[128,4096]{1,0:T(8,128)(2,1)} %bitcast.47, ...), custom_call_target="tpu_custom_call" | custom-call | flops 2097152 | bytes 6291456 | tf_op jit(solution)/shard_map/prep/pallas_call | solution.py:124
  10.2 0.1 collective-permute-start
  10.3 2.6 %collective-permute-done.1.refs_17_ = bf16[1280,128]{1,0:T(8,128)(2,1)S(1)} collective-permute-done((bf16[1280,128]{1,0:T(8,128)(2,1)S(1)}, bf16[1280,128]{1,0:T(8,128)(2,1)S(1)}, u32[]{:S(2)}, u32[]{:S(2)}) %collective-permute-start.1) | collective-permute-done | bytes 327712 | tf_op jit(solution)/shard_map/ppermute | solution.py:441
  12.9 4.7 %attend.4 = (bf16[128,4096]{1,0:T(8,128)(2,1)}, bf16[128,4096]{1,0:T(8,128)(2,1)}, f32[40,128]{1,0:T(8,128)S(1)}, f32[2,128,128]{2,1,0:T(8,128)S(1)}, bf16[2,128...) custom-call(s32[1]{0:T(128)} %copy.29.refs_0_, s32[1]{0:T(128)} %bitcast.refs_1_, ...), custom_call_target="tpu_custom_call" | custom-call | flops 1476395008 | bytes 2359296 | tf_op jit(solution)/shard_map/attend/pallas_call | solution.py:349
  17.6 2.5 %collective-permute-start.3 = (bf16[1280,128]{1,0:T(8,128)(2,1)S(1)}, bf16[1280,128]{1,0:T(8,128)(2,1)S(1)}, u32[]{:S(2)}, u32[]{:S(2)}) collective-permute-start(bf16[1280,128]{1,0:T(8,128)(2,1)S(1)} %get-tuple-element.59), channel_id=1, source_target_pairs={{0,1},{1,0},{2,3},{3,2},{4,5},{5,4},{6,7},{7,6},{8,9},{9,8},{10,11... | collective-permute-start | bytes 983048 | tf_op jit(solution)/shard_map/ppermute | solution.py:441
  20.1 0.0 collective-permute-done.refs_17_
  20.1 4.8 %attend.5 = (bf16[128,4096]{1,0:T(8,128)(2,1)}, bf16[128,4096]{1,0:T(8,128)(2,1)}, f32[40,128]{1,0:T(8,128)S(1)}, f32[2,128,128]{2,1,0:T(8,128)S(1)}, bf16[4,128...) custom-call(s32[1]{0:T(128)} %copy.29.refs_0_, ...), custom_call_target="tpu_custom_call", output_to_operand_aliasing={{0}: (20, {}), {1}: (21, {})} | custom-call | flops 1476395008 | bytes 2359296 | tf_op jit(solution)/shard_map/attend/pallas_call | solution.py:349
  24.9 1.8 %collective-permute-start.2 = (bf16[1280,128]{1,0:T(8,128)(2,1)S(1)}, bf16[1280,128]{1,0:T(8,128)(2,1)S(1)}, u32[]{:S(2)}, u32[]{:S(2)}) collective-permute-start(bf16[1280,128]{1,0:T(8,128)(2,1)S(1)} %get-tuple-element.58), channel_id=1, source_target_pairs={{0,1},{1,0},{2,3},{3,2},{4,5},{5,4},{6,7},{7,6},{8,9},{9,8},{10,11... | collective-permute-start | bytes 983048 | tf_op jit(solution)/shard_map/ppermute | solution.py:441
  26.7 0.5 collective-permute-done.3.refs_17_
  27.2 4.7 %attend.6 = (bf16[128,4096]{1,0:T(8,128)(2,1)}, bf16[128,4096]{1,0:T(8,128)(2,1)}, f32[40,128]{1,0:T(8,128)S(1)}, f32[2,128,128]{2,1,0:T(8,128)S(1)}, bf16[6,128,128]{2,1,0:T(8,128)(2,1)S(1)}) custom-call(s32[1]{0:T(128)} %copy.29.refs_0_, s32[1]{0:T(128)} %bitcast.refs_1_, ...), custom_call_target="tpu_custom_call", output_to_operand_aliasing={{0}: (20, {}), {1}: (21, {})} | custom-call | flops 1476395008 | bytes 2359296 | tf_op jit(solution)/shard_map/attend/pallas_call | solution.py:349
  31.9 1.7 %collective-permute-done.2.refs_17_ = bf16[1280,128]{1,0:T(8,128)(2,1)S(1)} collective-permute-done((bf16[1280,128]{1,0:T(8,128)(2,1)S(1)}, bf16[1280,128]{1,0:T(8,128)(2,1)S(1)}, u32[]{:S(2)}, u32[]{:S(2)}) %collective-permute-start.2) | collective-permute-done | bytes 327712 | tf_op jit(solution)/shard_map/ppermute | solution.py:441
  33.5 4.9 %attend.7 = (bf16[128,4096]{1,0:T(8,128)(2,1)}, bf16[128,4096]{1,0:T(8,128)(2,1)}, f32[40,128]{1,0:T(8,128)S(1)}, f32[2,128,128]{2,1,0:T(8,128)S(1)}, bf16[8,128,128]{2,1,0:T(8,128)(2,1)S(1)}) custom-call(s32[1]{0:T(128)} %copy.29.refs_0_, s32[1]{0:T(128)} %bitcast.refs_1_, ...), custom_call_target="tpu_custom_call", output_to_operand_aliasing={{0}: (20, {}), {1}: (21, {})} | custom-call | flops 1476395008 | bytes 2359296 | tf_op jit(solution)/shard_map/attend/pallas_call | solution.py:349
  38.4 0.0 collective-permute-start.5
  38.4 1.2 %collective-permute-done.5 = f32[40,128]{1,0:T(8,128)S(1)} collective-permute-done((f32[40,128]{1,0:T(8,128)S(1)}, f32[40,128]{1,0:T(8,128)S(1)}, u32[]{:S(2)}, u32[]{:S(2)}) %collective-permute-start.5) | collective-permute-done | bytes 20512 | tf_op jit(solution)/shard_map/ppermute | solution.py:429
  39.6 3.8 %collective-permute-start.8 = (f32[40,128]{1,0:T(8,128)S(1)}, f32[40,128]{1,0:T(8,128)S(1)}, u32[]{:S(2)}, u32[]{:S(2)}) collective-permute-start(f32[40,128]{1,0:T(8,128)S(1)} %add.66), channel_id=1, source_target_pairs={{0,24},{1,25},{2,26},{3,27},{4,28},{5,29},{6,30},{7,31},{8,16},{9,... | collective-permute-start | bytes 61448 | tf_op jit(solution)/shard_map/ppermute | solution.py:429
  43.4 0.0 collective-permute-start.7
  43.4 0.6 %collective-permute-start.6 = (f32[40,128]{1,0:T(8,128)S(1)}, f32[40,128]{1,0:T(8,128)S(1)}, u32[]{:S(2)}, u32[]{:S(2)}) collective-permute-start(f32[40,128]{1,0:T(8,128)S(1)} %add.66), channel_id=1, source_target_pairs={{0,16},{1,17},{2,18},{3,19},{4,20},{5,21},{6,22},{7,23},{8,24},{9,... | collective-permute-start | bytes 61448 | tf_op jit(solution)/shard_map/ppermute | solution.py:429
  44.1 1.3 %collective-permute-start.4 = (bf16[8,128,128]{2,1,0:T(8,128)(2,1)S(1)}, bf16[8,128,128]{2,1,0:T(8,128)(2,1)S(1)}, u32[]{:S(2)}, u32[]{:S(2)}) collective-permute-start(bf16[8,128,128]{2,1,0:T(8,128)(2,1)S(1)} %get-tuple-element.74), channel_id=1, source_target_pairs={{1,0},{3,2},{5,4},{7,6},{9,8},{11,10},{13,12},{15,14},{17,16},{19,... | collective-permute-start | bytes 786440 | tf_op jit(solution)/shard_map/ppermute | solution.py:444
  45.4 0.0 collective-permute-done.8
  45.4 1.9 %collective-permute-done.7 = f32[40,128]{1,0:T(8,128)S(1)} collective-permute-done((f32[40,128]{1,0:T(8,128)S(1)}, f32[40,128]{1,0:T(8,128)S(1)}, u32[]{:S(2)}, u32[]{:S(2)}) %collective-permute-start.7) | collective-permute-done | bytes 20512 | tf_op jit(solution)/shard_map/ppermute | solution.py:429
  47.3 1.1 %collective-permute-done.6 = f32[40,128]{1,0:T(8,128)S(1)} collective-permute-done((f32[40,128]{1,0:T(8,128)S(1)}, f32[40,128]{1,0:T(8,128)S(1)}, u32[]{:S(2)}, u32[]{:S(2)}) %collective-permute-start.6) | collective-permute-done | bytes 20512 | tf_op jit(solution)/shard_map/ppermute | solution.py:429
  48.4 2.5 %collective-permute-start.11 = (f32[40,128]{1,0:T(8,128)S(1)}, f32[40,128]{1,0:T(8,128)S(1)}, u32[]{:S(2)}, u32[]{:S(2)}) collective-permute-start(f32[40,128]{1,0:T(8,128)S(1)} %add_add_fusion.refs_7_), channel_id=1, source_target_pairs={{0,5},{1,4},{2,7},{3,6},{4,1},{5,0},{6,3},{7,2},{8,13},{9,12},{10,... | collective-permute-start | bytes 61448 | tf_op jit(solution)/shard_map/ppermute | solution.py:429
  50.9 0.5 collective-permute-start.10
  51.4 0.5 collective-permute-start.9
  51.9 1.4 %collective-permute-done.11.refs_10_ = f32[40,128]{1,0:T(8,128)S(1)} collective-permute-done((f32[40,128]{1,0:T(8,128)S(1)}, f32[40,128]{1,0:T(8,128)S(1)}, u32[]{:S(2)}, u32[]{:S(2)}) %collective-permute-start.11) | collective-permute-done | bytes 20512 | tf_op jit(solution)/shard_map/ppermute | solution.py:429
  53.3 1.3 %collective-permute-done.10.refs_9_ = f32[40,128]{1,0:T(8,128)S(1)} collective-permute-done((f32[40,128]{1,0:T(8,128)S(1)}, f32[40,128]{1,0:T(8,128)S(1)}, u32[]{:S(2)}, u32[]{:S(2)}) %collective-permute-start.10) | collective-permute-done | bytes 20512 | tf_op jit(solution)/shard_map/ppermute | solution.py:429
  54.6 0.5 collective-permute-done.9.refs_8_
  55.2 0.0 collective-permute-done.4.refs_6_
  55.2 0.8 %finish.1 = (bf16[128,512]{1,0:T(8,128)(2,1)}, bf16[128,512]{1,0:T(8,128)(2,1)}, f32[32,128]{1,0:T(8,128)}, f32[4,128]{1,0:T(4,128)}, f32[4,128]{1,0:T(4,128)}) custom-call(f32[256,128]{1,0:T(8,128)S(1)} %get-tuple-element.82.cos_ref.refs_11_.refs_0_, f32[256,128]{1,0:T(8,128)S(1)} %get-tuple-element.81.sin_ref.refs_12_.refs_1_, ...), custom_call_target="tpu_custom_call" | custom-call | bytes 524288 | tf_op jit(solution)/shard_map/finish/pallas_call | solution.py:402
  (4 shorter events, 0.0 us)
Async XLA Ops:
  0.6 5.4 %copy-start = (bf16[1,512,512]{2,1,0:T(8,128)(2,1)S(1)}, bf16[1,512,512]{2,1,0:T(8,128)(2,1)}, u32[]{:S(2)}) copy-start(bf16[1,512,512]{2,1,0:T(8,128)(2,1)} %param.13) | copy-start | bytes 1572868
  0.6 5.4 %copy-start.1 = (bf16[1,512,512]{2,1,0:T(8,128)(2,1)S(1)}, bf16[1,512,512]{2,1,0:T(8,128)(2,1)}, u32[]{:S(2)}) copy-start(bf16[1,512,512]{2,1,0:T(8,128)(2,1)} %param.14) | copy-start | bytes 1572868
  1.7 11.1 %collective-permute-start.1 = (bf16[1280,128]{1,0:T(8,128)(2,1)S(1)}, bf16[1280,128]{1,0:T(8,128)(2,1)S(1)}, u32[]{:S(2)}, u32[]{:S(2)}) collective-permute-start(bf16[1280,128]{1,0:T(8,128)(2,1)S(1)} %pack.1), channel_id=1, source_target_pairs={{0,1},{1,0},{2,3},{3,2},{4,5},{5,4},{6,7},{7,6},{8,9},{9,8},{10,11... | collective-permute-start | bytes 983048 | tf_op jit(solution)/shard_map/ppermute | solution.py:441
  5.5 0.9 %copy-start.2 = (bf16[1,128,512]{2,1,0:T(8,128)(2,1)S(1)}, bf16[1,128,512]{2,1,0:T(8,128)(2,1)}, u32[]{:S(2)}) copy-start(bf16[1,128,512]{2,1,0:T(8,128)(2,1)} %param.11) | copy-start | bytes 393220
  5.5 1.0 %copy-start.3 = (bf16[1,128,512]{2,1,0:T(8,128)(2,1)S(1)}, bf16[1,128,512]{2,1,0:T(8,128)(2,1)}, u32[]{:S(2)}) copy-start(bf16[1,128,512]{2,1,0:T(8,128)(2,1)} %param.12) | copy-start | bytes 393220
  10.2 9.9 %collective-permute-start = (bf16[1280,128]{1,0:T(8,128)(2,1)S(1)}, bf16[1280,128]{1,0:T(8,128)(2,1)S(1)}, u32[]{:S(2)}, u32[]{:S(2)}) collective-permute-start(bf16[1280,128]{1,0:T(8,128)(2,1)S(1)} %get-tuple-element.53), channel_id=1, source_target_pairs={{0,1},{1,0},{2,3},{3,2},{4,5},{5,4},{6,7},{7,6},{8,9},{9,8},{10,11... | collective-permute-start | bytes 983048 | tf_op jit(solution)/shard_map/ppermute | solution.py:441
  17.6 9.5 %collective-permute-start.3 = (bf16[1280,128]{1,0:T(8,128)(2,1)S(1)}, bf16[1280,128]{1,0:T(8,128)(2,1)S(1)}, u32[]{:S(2)}, u32[]{:S(2)}) collective-permute-start(bf16[1280,128]{1,0:T(8,128)(2,1)S(1)} %get-tuple-element.59), channel_id=1, source_target_pairs={{0,1},{1,0},{2,3},{3,2},{4,5},{5,4},{6,7},{7,6},{8,9},{9,8},{10,11... | collective-permute-start | bytes 983048 | tf_op jit(solution)/shard_map/ppermute | solution.py:441
  24.9 8.7 %collective-permute-start.2 = (bf16[1280,128]{1,0:T(8,128)(2,1)S(1)}, bf16[1280,128]{1,0:T(8,128)(2,1)S(1)}, u32[]{:S(2)}, u32[]{:S(2)}) collective-permute-start(bf16[1280,128]{1,0:T(8,128)(2,1)S(1)} %get-tuple-element.58), channel_id=1, source_target_pairs={{0,1},{1,0},{2,3},{3,2},{4,5},{5,4},{6,7},{7,6},{8,9},{9,8},{10,11... | collective-permute-start | bytes 983048 | tf_op jit(solution)/shard_map/ppermute | solution.py:441
  38.4 1.2 %collective-permute-start.5 = (f32[40,128]{1,0:T(8,128)S(1)}, f32[40,128]{1,0:T(8,128)S(1)}, u32[]{:S(2)}, u32[]{:S(2)}) collective-permute-start(f32[40,128]{1,0:T(8,128)S(1)} %get-tuple-element.75), channel_id=1, source_target_pairs={{0,2},{1,3},{2,0},{3,1},{4,6},{5,7},{6,4},{7,5},{8,10},{9,11},{10,... | collective-permute-start | bytes 61448 | tf_op jit(solution)/shard_map/ppermute | solution.py:429
  39.6 5.8 %collective-permute-start.8 = (f32[40,128]{1,0:T(8,128)S(1)}, f32[40,128]{1,0:T(8,128)S(1)}, u32[]{:S(2)}, u32[]{:S(2)}) collective-permute-start(f32[40,128]{1,0:T(8,128)S(1)} %add.66), channel_id=1, source_target_pairs={{0,24},{1,25},{2,26},{3,27},{4,28},{5,29},{6,30},{7,31},{8,16},{9,... | collective-permute-start | bytes 61448 | tf_op jit(solution)/shard_map/ppermute | solution.py:429
  43.4 3.8 %collective-permute-start.7 = (f32[40,128]{1,0:T(8,128)S(1)}, f32[40,128]{1,0:T(8,128)S(1)}, u32[]{:S(2)}, u32[]{:S(2)}) collective-permute-start(f32[40,128]{1,0:T(8,128)S(1)} %add.66), channel_id=1, source_target_pairs={{0,8},{1,9},{2,10},{3,11},{4,12},{5,13},{6,14},{7,15},{8,0},{9,1},... | collective-permute-start | bytes 61448 | tf_op jit(solution)/shard_map/ppermute | solution.py:429
  43.4 4.9 %collective-permute-start.6 = (f32[40,128]{1,0:T(8,128)S(1)}, f32[40,128]{1,0:T(8,128)S(1)}, u32[]{:S(2)}, u32[]{:S(2)}) collective-permute-start(f32[40,128]{1,0:T(8,128)S(1)} %add.66), channel_id=1, source_target_pairs={{0,16},{1,17},{2,18},{3,19},{4,20},{5,21},{6,22},{7,23},{8,24},{9,... | collective-permute-start | bytes 61448 | tf_op jit(solution)/shard_map/ppermute | solution.py:429
  44.1 11.1 %collective-permute-start.4 = (bf16[8,128,128]{2,1,0:T(8,128)(2,1)S(1)}, bf16[8,128,128]{2,1,0:T(8,128)(2,1)S(1)}, u32[]{:S(2)}, u32[]{:S(2)}) collective-permute-start(bf16[8,128,128]{2,1,0:T(8,128)(2,1)S(1)} %get-tuple-element.74), channel_id=1, source_target_pairs={{1,0},{3,2},{5,4},{7,6},{9,8},{11,10},{13,12},{15,14},{17,16},{19,... | collective-permute-start | bytes 786440 | tf_op jit(solution)/shard_map/ppermute | solution.py:444
  48.4 5.0 %collective-permute-start.11 = (f32[40,128]{1,0:T(8,128)S(1)}, f32[40,128]{1,0:T(8,128)S(1)}, u32[]{:S(2)}, u32[]{:S(2)}) collective-permute-start(f32[40,128]{1,0:T(8,128)S(1)} %add_add_fusion.refs_7_), channel_id=1, source_target_pairs={{0,5},{1,4},{2,7},{3,6},{4,1},{5,0},{6,3},{7,2},{8,13},{9,12},{10,... | collective-permute-start | bytes 61448 | tf_op jit(solution)/shard_map/ppermute | solution.py:429
  50.9 3.8 %collective-permute-start.10 = (f32[40,128]{1,0:T(8,128)S(1)}, f32[40,128]{1,0:T(8,128)S(1)}, u32[]{:S(2)}, u32[]{:S(2)}) collective-permute-start(f32[40,128]{1,0:T(8,128)S(1)} %add_add_fusion.refs_7_), channel_id=1, source_target_pairs={{0,1},{1,0},{2,3},{3,2},{4,5},{5,4},{6,7},{7,6},{8,9},{9,8},{10,11... | collective-permute-start | bytes 61448 | tf_op jit(solution)/shard_map/ppermute | solution.py:429
  51.4 3.8 %collective-permute-start.9 = (f32[40,128]{1,0:T(8,128)S(1)}, f32[40,128]{1,0:T(8,128)S(1)}, u32[]{:S(2)}, u32[]{:S(2)}) collective-permute-start(f32[40,128]{1,0:T(8,128)S(1)} %add_add_fusion.refs_7_), channel_id=1, source_target_pairs={{0,4},{1,5},{2,6},{3,7},{4,0},{5,1},{6,2},{7,3},{8,12},{9,13},{10,... | collective-permute-start | bytes 61448 | tf_op jit(solution)/shard_map/ppermute | solution.py:429

commit v12 on v11

--- a/solution.py
+++ b/solution.py
@@ -142,6 +142,80 @@
     return op(x.reshape(x.shape[0] // 8, 8, x.shape[1]), axis=0)
 
 
+def allowed(start, s, first, rank, shards, slots, tokens):
+    shift, at = divmod(start, slots + tokens)
+    row = lax.broadcasted_iota(jnp.int32, s.shape, 0)
+    if at < slots:
+        owner = lax.rem(rank - shift + shards, shards)
+        return row < first - owner * slots - at
+    if shift == 0:
+        return row <= (lax.broadcasted_iota(jnp.int32, s.shape, 1) & (tokens - 1))
+    return row < jnp.where(rank >= shift, tokens, 0)
+
+
+def slab_rows(g, sources, bias_ref, cosine, sine):
+    kp, vp = sources
+    k = kp.astype(F32) + bias_ref[g:g + 1, :]
+    v = vp.astype(F32) + bias_ref[KV + g:KV + g + 1, :]
+    return (k * cosine + turn(k) * sine).astype(B16), v.astype(B16)
+
+
+def ahead_kernel(
+    g, shards, first_ref, rank_ref, qst_ref, dot_ref, bias_ref, cos_ref, sin_ref,
+    ck_ref, cv_ref, kp_ref, vp_ref, s_ref, dp_ref, top_ref, keys, values,
+):
+    tokens, slots, width = kp_ref.shape[0], ck_ref.shape[0], qst_ref.shape[1]
+    owned = slots + tokens
+    mine = pl.ds(g * HD, HD)
+    rows = pl.ds(0, tokens)
+    k, v = slab_rows(
+        g, (kp_ref[:, mine], vp_ref[:, mine]), bias_ref, cos_ref[rows, :], sin_ref[rows, :]
+    )
+    keys[pl.ds(0, slots)] = ck_ref[:, mine]
+    keys[pl.ds(slots, tokens)] = k
+    values[pl.ds(0, slots)] = cv_ref[:, mine]
+    values[pl.ds(slots, tokens)] = v
+    for i in range(GROUP // HEADS):
+        place = pl.ds((g * (GROUP // HEADS) + i) * HD, HD)
+        s = dot(keys[...], qst_ref[place, :], NN)
+        top = jnp.full((8, width), NEG, F32)
+        for start in range(0, owned, tokens):
+            part = s[start:start + tokens]
+            seen = allowed(start, part, first_ref[0], rank_ref[0], shards, slots, tokens)
+            part = jnp.where(seen, part, NEG)
+            s_ref[i, pl.ds(start, tokens), :] = part
+            top = jnp.maximum(top, fold(part, jnp.max))
+        top_ref[i] = top
+        dp_ref[i] = dot(values[...], dot_ref[place, :], NN)
+
+
+def look_ahead(g, shards, first, rank, qst, dot_t, bias, cosine, sine, ck, cv, kp, vp):
+    tokens, slots, width = kp.shape[0], ck.shape[0], qst.shape[1]
+    owned = slots + tokens
+    chains = GROUP // HEADS
+    smem = pl.BlockSpec(memory_space=pltpu.SMEM)
+    vmem = pl.BlockSpec(memory_space=pltpu.VMEM)
+    args = [first, rank, qst, dot_t, bias, cosine, sine, ck, cv, kp, vp]
+    return pl.pallas_call(
+        functools.partial(ahead_kernel, g, shards),
+        grid=(1,),
+        in_specs=[smem] * 2 + [vmem] * (len(args) - 2),
+        out_specs=[vmem] * 3,
+        out_shape=[
+            pltpu.VMEM((chains, owned, width), F32),
+            pltpu.VMEM((chains, owned, width), F32),
+            pltpu.VMEM((chains, 8, width), F32),
+        ],
+        scratch_shapes=[pltpu.VMEM((owned, HD), B16)] * 2,
+        compiler_params=params(),
+        cost_estimate=pl.CostEstimate(
+            flops=4 * GROUP * tokens * HD * owned, bytes_accessed=8 * GROUP * tokens * owned,
+            transcendentals=0,
+        ),
+        name="ahead",
+    )(*args)
+
+
 def attend_kernel(g, shards, *refs):
     refs = list(refs)
 
@@ -153,9 +227,12 @@
     (first_ref, rank_ref, qs_ref, qst_ref, dos_ref, dot_ref, bias_ref, cos_t_ref, sin_t_ref,
      ck_t_ref, cv_t_ref, cos_ref, sin_ref, ck_ref, cv_ref, kp_ref, vp_ref) = take(17)
     far = take(shards - 1)
+    ahead = take(3) if g == KV - 1 else []
+    if g == 0:
+        take(1)
     old_sums_ref = take(1)[0] if g else None
     old_send = take(shards - 1) if g else []
-    if g:
+    if 0 < g < KV - 1:
         take(2)
     out_ref, gq_ref, sums_ref, own_ref = take(4)
     send = take(shards - 1)
@@ -164,37 +241,37 @@
     scratch = [take(3) for _ in range(GROUP // HEADS)]
     tokens = kp_ref.shape[0]
     slots = ck_ref.shape[0]
-    prefix = shards * slots
-    slab = shards * tokens
-    total = prefix + slab
+    owned = slots + tokens
+    total = shards * owned
+    known = owned if ahead else 0
     first = first_ref[0]
     rank = rank_ref[0]
     mine = pl.ds(g * HD, HD)
 
     if pack_ref is not None:
         copy_chunk(pl.ds((g + 2) * HD, HD), (ck_ref, cv_ref, kp_ref, vp_ref), pack_ref)
-    keys[pl.ds(0, slots)] = ck_ref[:, mine]
-    values[pl.ds(0, slots)] = cv_ref[:, mine]
-    for s in range(1, shards):
-        keys[pl.ds(s * slots, slots)] = far[s - 1][pl.ds(0, slots)]
-        values[pl.ds(s * slots, slots)] = far[s - 1][pl.ds(slots, slots)]
     for s in range(shards):
+        at = s * owned
         rows = pl.ds(s * tokens, tokens)
         if s == 0:
-            kp, vp = kp_ref[:, mine], vp_ref[:, mine]
+            sources = [ref[:, mine] for ref in (ck_ref, cv_ref, kp_ref, vp_ref)]
         else:
-            kp, vp = (far[s - 1][pl.ds(2 * slots + i * tokens, tokens)] for i in range(2))
-        k = kp.astype(F32) + bias_ref[g:g + 1, :]
-        k = k * cos_ref[rows, :] + turn(k) * sin_ref[rows, :]
-        v = vp.astype(F32) + bias_ref[KV + g:KV + g + 1, :]
-        place = pl.ds(prefix + s * tokens, tokens)
-        keys[place] = k.astype(B16)
-        values[place] = v.astype(B16)
+            sources = [
+                far[s - 1][pl.ds(*part)] for part in
+                ((0, slots), (slots, slots), (2 * slots, tokens), (2 * slots + tokens, tokens))
+            ]
+        k, v = slab_rows(g, sources[2:], bias_ref, cos_ref[rows, :], sin_ref[rows, :])
+        for (natural, transposed), cache, own in zip(
+            ((keys, keys_t), (values, values_t)), sources[:2], (k, v)
+        ):
+            if s or not ahead:
+                natural[pl.ds(at, slots)] = cache
+                natural[pl.ds(at + slots, tokens)] = own
+            transposed[:, pl.ds(at + slots, tokens)] = own.T
+            if s:
+                transposed[:, pl.ds(at, slots)] = cache.T
     keys_t[:, pl.ds(0, slots)] = ck_t_ref[mine, :]
     values_t[:, pl.ds(0, slots)] = cv_t_ref[mine, :]
-    rest = pl.ds(slots, prefix - slots + slab)
-    keys_t[:, rest] = keys[rest, :].T
-    values_t[:, rest] = values[rest, :].T
     sums_ref[...] = jnp.zeros_like(sums_ref) if old_sums_ref is None else old_sums_ref[...]
     dk_acc[...] = jnp.zeros_like(dk_acc)
     dv_acc[...] = jnp.zeros_like(dv_acc)
@@ -202,14 +279,6 @@
     width = HEADS * tokens
     scale = HD ** -0.5
     blocks = range(0, total, tokens)
-    def allowed(start, s):
-        row = lax.broadcasted_iota(jnp.int32, s.shape, 0)
-        if start < prefix:
-            owner = lax.rem(rank - start // slots + shards, shards)
-            return row < first - owner * slots - start % slots
-        if start < prefix + tokens:
-            return row <= (lax.broadcasted_iota(jnp.int32, s.shape, 1) & (tokens - 1))
-        return row < jnp.where(rank >= (start - prefix) // tokens, tokens, 0)
 
     class Chain:
         def __init__(self, index):
@@ -218,13 +287,15 @@
             index = self.index
             self.rows = pl.ds(pl.multiple_of(index * width, width), width)
             self.place = pl.ds(pl.multiple_of(index * HD, HD), HD)
-            self.top = jnp.full((8, width), NEG, F32)
+            self.ahead = [ref.at[self.index % len(scratch)] for ref in ahead]
+            self.top = self.ahead[2][...] if ahead else jnp.full((8, width), NEG, F32)
 
         def scores(self):
-            s = dot(keys[...], qst_ref[self.place, :], NN)
-            for start in blocks:
-                part = s[start:start + tokens]
-                part = jnp.where(allowed(start, part), part, NEG)
+            s = dot(keys[pl.ds(known, total - known), :], qst_ref[self.place, :], NN)
+            for start in blocks[known // tokens:]:
+                part = s[start - known:start - known + tokens]
+                seen = allowed(start, part, first, rank, shards, slots, tokens)
+                part = jnp.where(seen, part, NEG)
                 self.s[pl.ds(start, tokens), :] = part
                 self.top = jnp.maximum(self.top, fold(part, jnp.max))
 
@@ -233,7 +304,8 @@
             weight = jnp.zeros((8, width), F32)
             for start in blocks:
                 rows = pl.ds(start, tokens)
-                e = jnp.exp2((self.s[rows, :] - top) * (scale * math.log2(math.e)))
+                s = (self.ahead[0] if start < known else self.s)[rows, :]
+                e = jnp.exp2((s - top) * (scale * math.log2(math.e)))
                 self.s[rows, :] = e
                 weight = weight + fold(e, jnp.sum)
             self.inverse = 1.0 / jnp.sum(weight, axis=0, keepdims=True)
@@ -260,21 +332,27 @@
                 )
 
         def dprobs(self):
-            self.dp = dot(values[...], dot_ref[self.place, :], NN)
+            rows = pl.ds(known, total - known)
+            self.dp = dot(values[rows, :], dot_ref[self.place, :], NN)
 
         def dscores(self):
             for start in blocks:
                 rows = pl.ds(start, tokens)
-                part = self.dp[start:start + tokens]
+                if start < known:
+                    part = self.ahead[1][rows, :]
+                else:
+                    part = self.dp[start - known:start - known + tokens]
                 self.ds[rows, :] = (self.s[rows, :] * (part - self.delta)).astype(B16)
 
         def query_grad(self):
             self.dq = (dot(keys_t[...], self.ds[...], NN) * scale).astype(B16).astype(F32)
 
         def slab_grads(self):
-            last = pl.ds(prefix, slab)
-            dv_acc[...] += dot(self.pb[last, :], dos_ref[self.rows, :], NN)
-            dk_acc[...] += dot(self.ds[last, :], qs_ref[self.rows, :], NN)
+            for s in range(shards):
+                rows = pl.ds(s * owned + slots, tokens)
+                place = pl.ds(s * tokens, tokens)
+                dv_acc[place, :] += dot(self.pb[rows, :], dos_ref[self.rows, :], NN)
+                dk_acc[place, :] += dot(self.ds[rows, :], qs_ref[self.rows, :], NN)
 
         def store(self):
             for part, cols, head in self.heads():
@@ -312,7 +390,7 @@
 
 
 def attend(
-    g, shards, first, rank, prepared, cosine, sine, ck, cv, kp, vp, far, before
+    g, shards, first, rank, prepared, cosine, sine, ck, cv, kp, vp, far, ahead, before
 ):
     tokens, slots = kp.shape[0], ck.shape[0]
     slab = shards * tokens
@@ -324,23 +402,25 @@
 
     args = [first, rank]
     placed = [*prepared, cosine, sine, ck, cv, kp, vp, *far]
+    placed += ahead if g == KV - 1 else ahead[2:] if g == 0 else []
     aliases = {}
     if before is not None:
         out, gq, sums, send = before
         placed += [sums, *send]
     args += placed
     in_specs = [smem] * 2 + [vmem] * len(placed)
-    if before is not None:
+    last = g == KV - 1
+    if before is not None and not last:
         aliases = {len(args): 0, len(args) + 1: 1}
         args += [out, gq]
         in_specs += [anywhere] * 2
+    kept = pltpu.VMEM((tokens, GROUP * HD), B16) if last else pltpu.HBM((tokens, HQ * HD), B16)
     out_shape = [
-        pltpu.HBM((tokens, HQ * HD), B16),
-        pltpu.HBM((tokens, HQ * HD), B16),
+        kept, kept,
         pltpu.VMEM((SUMS, HD), F32),
         pltpu.VMEM((2, tokens, HD), F32),
     ]
-    out_specs = [wide, wide, vmem, vmem]
+    out_specs = [vmem if last else wide] * 2 + [vmem, vmem]
     out_shape += [pltpu.VMEM((2 * g + 2, tokens, HD), B16)] * (shards - 1)
     out_specs += [vmem] * (shards - 1)
     if g + 2 < KV:
@@ -377,7 +457,9 @@
     cos_ref, sin_ref, *refs = refs
     owns, refs = refs[:KV], refs[KV:]
     backs, refs = refs[:shards - 1], refs[shards - 1:]
-    sums, (gk_ref, gv_ref, *parts) = refs[:-5], refs[-5:]
+    out_part, gq_part, _, _, out_ref, gq_ref, gk_ref, gv_ref = refs
+    out_ref[...] = out_part[...]
+    gq_ref[...] = gq_part[...]
     tokens = gk_ref.shape[0]
     cosine, sine = cos_ref[pl.ds(0, tokens), :], sin_ref[pl.ds(0, tokens), :]
     for g in range(KV):
@@ -388,6 +470,29 @@
         cols = pl.ds(g * HD, HD)
         gk_ref[:, cols] = turn_back(dk, cosine, sine).astype(B16)
         gv_ref[:, cols] = dv.astype(B16)
+
+
+def finish(shards, cosine, sine, owns, backs, parts, out, gq):
+    tokens = out.shape[0]
+    args = [cosine, sine, *owns, *backs, *parts]
+    wide = pl.BlockSpec((tokens, GROUP * HD), lambda i: (0, KV - 1))
+    narrow = (tokens, KV * HD)
+    return pl.pallas_call(
+        functools.partial(finish_kernel, shards),
+        grid=(1,),
+        in_specs=[pl.BlockSpec(memory_space=pltpu.VMEM)] * len(args)
+        + [pl.BlockSpec(memory_space=pl.ANY)] * 2,
+        out_specs=[wide, wide, whole(narrow), whole(narrow)],
+        out_shape=[pltpu.HBM(out.shape, B16)] * 2 + [pltpu.HBM(narrow, B16)] * 2,
+        input_output_aliases={len(args): 0, len(args) + 1: 1},
+        compiler_params=params(),
+        cost_estimate=pl.CostEstimate(flops=0, bytes_accessed=1 << 21, transcendentals=0),
+        name="finish",
+    )(*args, out, gq)
+
+
+def sums_kernel(*refs):
+    sums, parts = refs[:-4], refs[-3:]
     start = 0
     for part in parts:
         rows = pl.ds(start, part.shape[0])
@@ -395,20 +500,19 @@
         start += part.shape[0]
 
 
-def finish(shards, tokens, cosine, sine, owns, backs, sums):
-    vmem = pl.BlockSpec(memory_space=pltpu.VMEM)
-    args = [cosine, sine, *owns, *backs, *sums]
-    shapes = [((tokens, KV * HD), B16)] * 2 + [((rows, HD), F32) for rows in (HQ, KV, KV)]
+def last_sums(sums, after):
+    shapes = [(rows, HD) for rows in (HQ, KV, KV)]
     return pl.pallas_call(
-        functools.partial(finish_kernel, shards),
+        sums_kernel,
         grid=(1,),
-        in_specs=[vmem] * len(args),
-        out_specs=[whole(shape) for shape, _ in shapes],
-        out_shape=[pltpu.HBM(shape, kind) for shape, kind in shapes],
+        in_specs=[pl.BlockSpec(memory_space=pltpu.VMEM)] * len(sums)
+        + [pl.BlockSpec(memory_space=pl.ANY)],
+        out_specs=[whole(shape) for shape in shapes],
+        out_shape=[pltpu.HBM(shape, F32) for shape in shapes],
         compiler_params=params(),
-        cost_estimate=pl.CostEstimate(flops=0, bytes_accessed=1 << 19, transcendentals=0),
-        name="finish",
-    )(*args)
+        cost_estimate=pl.CostEstimate(flops=0, bytes_accessed=1 << 17, transcendentals=0),
+        name="sums",
+    )(*sums, after)
 
 
 def add_up(parts):
@@ -462,18 +566,25 @@
         hbm(bias_k.reshape(KV, HD)), hbm(bias_v.reshape(KV, HD)), cosine, sine, ck, cv, kp, vp,
     )
     far.append([ring(chunk, s) for s in shifts])
+    qst, dot_t, bias = prepared[1], prepared[3], prepared[4]
+    ahead = look_ahead(
+        KV - 1, shards, start, rank.reshape(1), qst, dot_t, bias, cosine, sine, ck, cv, kp, vp
+    )
     before, owns = None, []
     for g in range(KV):
         before, own, more = attend(
             g, shards, start, rank.reshape(1), prepared, cosine, sine, ck, cv, kp, vp,
-            far[g], before,
+            far[g], ahead, before,
         )
+        if g == KV - 2:
+            out, gq = before[:2]
         owns.append(own)
         far += [[ring(chunk, s) for s in shifts] for chunk in more]
-    out, gq, sums, send = before
+    *columns, sums, send = before
     backs = [earlier(x, s) for s, x in zip(shifts, send)]
     sums = sum_but_last(sums, ("dp", "seq"), shards)
-    gk, gv, *sums = finish(shards, tokens, cosine, sine, owns, backs, sums)
+    out, gq, gk, gv = finish(shards, cosine, sine, owns, backs, columns, out, gq)
+    sums = last_sums(sums, gk)
     return (out[None], gq[None], gk[None], gv[None], *[x.reshape(-1) for x in sums])
 
 

time: 56.2 us -> 59 us (1.050)
  local copies, waits for them, and re-layouts: 0.41 us -> 4.79 us
  starting transfers between devices: 16.7 us -> 14.4 us
    unnamed x8 -> x10, local copies, waits for them, and re-layouts: 0.41 us -> 4.79 us
    ppermute x7, waiting for transfers between devices: 7.4 us -> 4.01 us  [sum_but_last(): parts.append(lax.ppermute(x, axes, [(i, i ^ flip) for i in range(devices)]))]
    ppermute x1, waiting for transfers between devices: 0.01 us -> 2.48 us  [earlier(): return lax.ppermute(x, 'seq', [(i + s, i) for i in range(shards - s)])]
    ppermute x4, starting transfers between devices: 7.38 us -> 5.12 us  [ring(): lax.ppermute(x, 'seq', [(i, (i + s) % shards) for i in range(shards)])]
    pallas_call x0 -> x2, Pallas kernels: none -> 1.46 us  [the longest x1 0.85 us: look_ahead(): pl.pallas_call(functools.partial(ahead_kernel, g, shards), grid=(1,), in_...]
    pallas_call x4, Pallas kernels: 19.1 us -> 17.8 us  [attend(): pl.pallas_call(functools.partial(attend_kernel, g, shards), grid=(1,), in...]
    ppermute x4, waiting for transfers between devices: 4.79 us -> 5.94 us  [ring(): lax.ppermute(x, 'seq', [(i, (i + s) % shards) for i in range(shards)])]
  transfers between devices with their start and end apart: 12 -> 12, of which waited for: 9 -> 7; matrix products, arithmetic and copies ran while one was open for 1% -> 1% of each run, Pallas kernels for 32% -> 34%
where the time goes in v12:
time: 59 us; the launch traced here: 58.6 us
  Pallas kernels  25 us (42%)
  starting transfers between devices  14.4 us (24%)
  waiting for transfers between devices  12.4 us (21%)
  local copies, waits for them, and re-layouts  4.79 us (8%)
  between operations  1.4 us (2%)
  other arithmetic  0.64 us (1%)
    pallas_call x4, Pallas kernels, attend(): pl.pallas_call(functools.partial(attend_kernel, g, shards), grid=(1,), in...  17.8 us
    ppermute x7, starting transfers between devices, sum_but_last(): parts.append(lax.ppermute(x, axes, [(i, i ^ flip) for i in range(devices)]))  8.01 us
    ppermute x4, waiting for transfers between devices, ring(): lax.ppermute(x, 'seq', [(i, (i + s) % shards) for i in range(shards)])  5.94 us
    ppermute x4, starting transfers between devices, ring(): lax.ppermute(x, 'seq', [(i, (i + s) % shards) for i in range(shards)])  5.12 us
    unnamed x10, local copies, waits for them, and re-layouts  4.79 us
    ppermute x7, waiting for transfers between devices, sum_but_last(): parts.append(lax.ppermute(x, axes, [(i, i ^ flip) for i in range(devices)]))  4.01 us
    pallas_call x1, Pallas kernels, prep(): pl.pallas_call(functools.partial(prep_kernel, tokens), grid=(KV,), in_spe...  3.68 us
    ppermute x1, waiting for transfers between devices, earlier(): return lax.ppermute(x, 'seq', [(i + s, i) for i in range(shards - s)])  2.48 us
  transfers between devices with their start and end apart: 12, of which 7 were waited for; matrix products, arithmetic and copies ran while one was open for 1% of the time, Pallas kernels for 34%

profile of v12, /device:TPU:0, one launch (start us, length us, event | category | flops | bytes accessed | tf_op | source)
XLA Modules:
  0.0 58.6 jit_solution(7830933557045200611)
XLA Ops:
  0.6 1.0 %pack.1 = bf16[1280,128]{1,0:T(8,128)(2,1)S(1)} custom-call(bf16[512,512]{1,0:T(8,128)(2,1)} %bitcast.21, bf16[512,512]{1,0:T(8,128)(2,1)} %bitcast.28, bf16[128,512]{1,0:T(8,128)(2,1)} %bitcast.35, bf16[128,512]{1,0:T(8,128)(2,1)} %bitcast.42), custom_call_target="tpu_custom_call" | custom-call | bytes 655360 | tf_op jit(solution)/shard_map/pack/pallas_call | solution.py:60
  1.6 3.0 %collective-permute-start = (bf16[1280,128]{1,0:T(8,128)(2,1)S(1)}, bf16[1280,128]{1,0:T(8,128)(2,1)S(1)}, u32[]{:S(2)}, u32[]{:S(2)}) collective-permute-start(bf16[1280,128]{1,0:T(8,128)(2,1)S(1)} %pack.1), channel_id=1, source_target_pairs={{0,1},{1,0},{2,3},{3,2},{4,5},{5,4},{6,7},{7,6},{8,9},{9,8},{10,11... | collective-permute-start | bytes 983048 | tf_op jit(solution)/shard_map/ppermute | solution.py:545
  5.3 0.1 convert_bitcast_fusion
  5.4 0.5 fusion
  6.0 0.0 copy-start
  6.0 1.0 %copy-done = bf16[1,512,512]{2,1,0:T(8,128)(2,1)S(1)} copy-done((bf16[1,512,512]{2,1,0:T(8,128)(2,1)S(1)}, bf16[1,512,512]{2,1,0:T(8,128)(2,1)}, u32[]{:S(2)}) %copy-start) | copy-done | bytes 524312
  7.0 0.0 copy-start.1
  7.0 1.0 %copy-done.1 = bf16[1,512,512]{2,1,0:T(8,128)(2,1)S(1)} copy-done((bf16[1,512,512]{2,1,0:T(8,128)(2,1)S(1)}, bf16[1,512,512]{2,1,0:T(8,128)(2,1)}, u32[]{:S(2)}) %copy-start.1) | copy-done | bytes 524312
  8.1 0.0 copy-start.2
  8.1 0.9 %copy-done.2 = bf16[1,128,512]{2,1,0:T(8,128)(2,1)S(1)} copy-done((bf16[1,128,512]{2,1,0:T(8,128)(2,1)S(1)}, bf16[1,128,512]{2,1,0:T(8,128)(2,1)}, u32[]{:S(2)}) %copy-start.2) | copy-done | bytes 131096
  9.0 0.0 copy-start.3
  9.0 0.9 %copy-done.3 = bf16[1,128,512]{2,1,0:T(8,128)(2,1)S(1)} copy-done((bf16[1,128,512]{2,1,0:T(8,128)(2,1)S(1)}, bf16[1,128,512]{2,1,0:T(8,128)(2,1)}, u32[]{:S(2)}) %copy-start.3) | copy-done | bytes 131096
  9.9 3.7 %prep.1 = (bf16[4096,128]{1,0:T(8,128)(2,1)S(1)}, bf16[1024,512]{1,0:T(8,128)(2,1)S(1)}, bf16[4096,128]{1,0:T(8,128)(2,1)S(1)}, bf16[1024,512]{1,0:T(8,128)(2,1)...) custom-call(bf16[128,4096]{1,0:T(8,128)(2,1)} %bitcast.52, ...), custom_call_target="tpu_custom_call" | custom-call | flops 2097152 | bytes 6291456 | tf_op jit(solution)/shard_map/prep/pallas_call | solution.py:124
  13.5 0.1 collective-permute-start.1
  13.6 0.8 %ahead.1 = (f32[2,640,512]{2,1,0:T(8,128)S(1)}, f32[2,640,512]{2,1,0:T(8,128)S(1)}, f32[2,8,512]{2,1,0:T(8,128)S(1)}) custom-call(s32[1]{0:T(128)} %copy.29.first_ref.refs_0_, s32[1]{0:T(128)} %bitcast.2.rank_ref.refs_1_, bf16[1024,512]{1,0:T(8,128)(2,1)S(1)} %get-tuple-element.50.qst_ref.refs_3_, bf16[1024,512]{1,0:T(8,128)(2,1)S(1)} %get-tuple-element.52.dot_ref.refs_5_, ...), custom_call_target="tpu_custom_call" | custom-call | flops 335544320 | bytes 5242880 | tf_op jit(solution)/shard_map/ahead/pallas_call | solution.py:199
  14.5 0.0 collective-permute-done.refs_17_
  14.5 4.7 %attend.4 = (bf16[128,4096]{1,0:T(8,128)(2,1)}, bf16[128,4096]{1,0:T(8,128)(2,1)}, f32[40,128]{1,0:T(8,128)S(1)}, f32[2,128,128]{2,1,0:T(8,128)S(1)}, bf16[2,128...) custom-call(s32[1]{0:T(128)} %copy.29.first_ref.refs_0_, s32[1]{0:T(128)} %bitcast.2.rank_ref.refs_1_, ...), custom_call_target="tpu_custom_call" | custom-call | flops 1476395008 | bytes 2359296 | tf_op jit(solution)/shard_map/attend/pallas_call | solution.py:429
  19.2 2.0 %collective-permute-start.2 = (bf16[1280,128]{1,0:T(8,128)(2,1)S(1)}, bf16[1280,128]{1,0:T(8,128)(2,1)S(1)}, u32[]{:S(2)}, u32[]{:S(2)}) collective-permute-start(bf16[1280,128]{1,0:T(8,128)(2,1)S(1)} %get-tuple-element.66), channel_id=1, source_target_pairs={{0,1},{1,0},{2,3},{3,2},{4,5},{5,4},{6,7},{7,6},{8,9},{9,8},{10,11... | collective-permute-start | bytes 983048 | tf_op jit(solution)/shard_map/ppermute | solution.py:545
  21.2 2.9 %collective-permute-done.1.refs_17_ = bf16[1280,128]{1,0:T(8,128)(2,1)S(1)} collective-permute-done((bf16[1280,128]{1,0:T(8,128)(2,1)S(1)}, bf16[1280,128]{1,0:T(8,128)(2,1)S(1)}, u32[]{:S(2)}, u32[]{:S(2)}) %collective-permute-start.1) | collective-permute-done | bytes 327712 | tf_op jit(solution)/shard_map/ppermute | solution.py:545
  24.1 4.7 %attend.5 = (bf16[128,4096]{1,0:T(8,128)(2,1)}, bf16[128,4096]{1,0:T(8,128)(2,1)}, f32[40,128]{1,0:T(8,128)S(1)}, f32[2,128,128]{2,1,0:T(8,128)S(1)}, bf16[4,128...) custom-call(s32[1]{0:T(128)} %copy.29.first_ref.refs_0_, ...), custom_call_target="tpu_custom_call", output_to_operand_aliasing={{0}: (20, {}), {1}: (21, {})} | custom-call | flops 1476395008 | bytes 2359296 | tf_op jit(solution)/shard_map/attend/pallas_call | solution.py:429
  28.8 0.0 collective-permute-start.3
  28.8 1.9 %collective-permute-done.2.refs_17_ = bf16[1280,128]{1,0:T(8,128)(2,1)S(1)} collective-permute-done((bf16[1280,128]{1,0:T(8,128)(2,1)S(1)}, bf16[1280,128]{1,0:T(8,128)(2,1)S(1)}, u32[]{:S(2)}, u32[]{:S(2)}) %collective-permute-start.2) | collective-permute-done | bytes 327712 | tf_op jit(solution)/shard_map/ppermute | solution.py:545
  30.8 4.9 %attend.6 = (bf16[128,4096]{1,0:T(8,128)(2,1)}, bf16[128,4096]{1,0:T(8,128)(2,1)}, f32[40,128]{1,0:T(8,128)S(1)}, f32[2,128,128]{2,1,0:T(8,128)S(1)}, bf16[6,128,128]{2,1,0:T(8,128)(2,1)S(1)}) custom-call(s32[1]{0:T(128)} %copy.29.first_ref.refs_0_, s32[1]{0:T(128)} %bitcast.2.rank_ref.refs_1_, ...), custom_call_target="tpu_custom_call", output_to_operand_aliasing={{0}: (20, {}), {1}: (21, {})} | custom-call | flops 1476395008 | bytes 2359296 | tf_op jit(solution)/shard_map/attend/pallas_call | solution.py:429
  35.7 1.1 %collective-permute-done.3.refs_17_ = bf16[1280,128]{1,0:T(8,128)(2,1)S(1)} collective-permute-done((bf16[1280,128]{1,0:T(8,128)(2,1)S(1)}, bf16[1280,128]{1,0:T(8,128)(2,1)S(1)}, u32[]{:S(2)}, u32[]{:S(2)}) %collective-permute-start.3) | collective-permute-done | bytes 327712 | tf_op jit(solution)/shard_map/ppermute | solution.py:545
  36.8 3.5 %attend.7 = (bf16[128,1024]{1,0:T(8,128)(2,1)S(1)}, bf16[128,1024]{1,0:T(8,128)(2,1)S(1)}, f32[40,128]{1,0:T(8,128)S(1)}, f32[2,128,128]{2,1,0:T(8,128)S(1)}, bf16[8,128,128]{2,1,0:T(8,128)(2,1)S(1)}) custom-call(s32[1]{0:T(128)} %copy.29.first_ref.refs_0_, s32[1]{0:T(128)} %bitcast.2.rank_ref.refs_1_, bf16[4096,128]{1,0:T(8,128)(2,1)S(1)} %get-tuple-element.49.refs_2_, ...), custom_call_target="tpu_custom_call" | custom-call | flops 1476395008 | bytes 2359296 | tf_op jit(solution)/shard_map/attend/pallas_call | solution.py:429
  40.3 0.1 collective-permute-start.5
  40.4 1.2 %collective-permute-done.5 = f32[40,128]{1,0:T(8,128)S(1)} collective-permute-done((f32[40,128]{1,0:T(8,128)S(1)}, f32[40,128]{1,0:T(8,128)S(1)}, u32[]{:S(2)}, u32[]{:S(2)}) %collective-permute-start.5) | collective-permute-done | bytes 20512 | tf_op jit(solution)/shard_map/ppermute | solution.py:533
  41.6 3.6 %collective-permute-start.8 = (f32[40,128]{1,0:T(8,128)S(1)}, f32[40,128]{1,0:T(8,128)S(1)}, u32[]{:S(2)}, u32[]{:S(2)}) collective-permute-start(f32[40,128]{1,0:T(8,128)S(1)} %add.66), channel_id=1, source_target_pairs={{0,24},{1,25},{2,26},{3,27},{4,28},{5,29},{6,30},{7,31},{8,16},{9,... | collective-permute-start | bytes 61448 | tf_op jit(solution)/shard_map/ppermute | solution.py:533
  45.2 0.0 collective-permute-start.7
  45.2 0.8 %collective-permute-start.6 = (f32[40,128]{1,0:T(8,128)S(1)}, f32[40,128]{1,0:T(8,128)S(1)}, u32[]{:S(2)}, u32[]{:S(2)}) collective-permute-start(f32[40,128]{1,0:T(8,128)S(1)} %add.66), channel_id=1, source_target_pairs={{0,16},{1,17},{2,18},{3,19},{4,20},{5,21},{6,22},{7,23},{8,24},{9,... | collective-permute-start | bytes 61448 | tf_op jit(solution)/shard_map/ppermute | solution.py:533
  45.9 1.3 %collective-permute-start.4 = (bf16[8,128,128]{2,1,0:T(8,128)(2,1)S(1)}, bf16[8,128,128]{2,1,0:T(8,128)(2,1)S(1)}, u32[]{:S(2)}, u32[]{:S(2)}) collective-permute-start(bf16[8,128,128]{2,1,0:T(8,128)(2,1)S(1)} %get-tuple-element.78), channel_id=1, source_target_pairs={{1,0},{3,2},{5,4},{7,6},{9,8},{11,10},{13,12},{15,14},{17,16},{19,... | collective-permute-start | bytes 786440 | tf_op jit(solution)/shard_map/ppermute | solution.py:548
  47.2 0.0 collective-permute-done.8
  47.2 1.7 %collective-permute-done.7 = f32[40,128]{1,0:T(8,128)S(1)} collective-permute-done((f32[40,128]{1,0:T(8,128)S(1)}, f32[40,128]{1,0:T(8,128)S(1)}, u32[]{:S(2)}, u32[]{:S(2)}) %collective-permute-start.7) | collective-permute-done | bytes 20512 | tf_op jit(solution)/shard_map/ppermute | solution.py:533
  49.0 1.1 %collective-permute-done.6 = f32[40,128]{1,0:T(8,128)S(1)} collective-permute-done((f32[40,128]{1,0:T(8,128)S(1)}, f32[40,128]{1,0:T(8,128)S(1)}, u32[]{:S(2)}, u32[]{:S(2)}) %collective-permute-start.6) | collective-permute-done | bytes 20512 | tf_op jit(solution)/shard_map/ppermute | solution.py:533
  50.1 1.5 %collective-permute-start.11 = (f32[40,128]{1,0:T(8,128)S(1)}, f32[40,128]{1,0:T(8,128)S(1)}, u32[]{:S(2)}, u32[]{:S(2)}) collective-permute-start(f32[40,128]{1,0:T(8,128)S(1)} %add_add_fusion.refs_0_), channel_id=1, source_target_pairs={{0,5},{1,4},{2,7},{3,6},{4,1},{5,0},{6,3},{7,2},{8,13},{9,12},{10,... | collective-permute-start | bytes 61448 | tf_op jit(solution)/shard_map/ppermute | solution.py:533
  51.6 1.5 %collective-permute-start.10 = (f32[40,128]{1,0:T(8,128)S(1)}, f32[40,128]{1,0:T(8,128)S(1)}, u32[]{:S(2)}, u32[]{:S(2)}) collective-permute-start(f32[40,128]{1,0:T(8,128)S(1)} %add_add_fusion.refs_0_), channel_id=1, source_target_pairs={{0,1},{1,0},{2,3},{3,2},{4,5},{5,4},{6,7},{7,6},{8,9},{9,8},{10,11... | collective-permute-start | bytes 61448 | tf_op jit(solution)/shard_map/ppermute | solution.py:533
  53.1 0.5 collective-permute-start.9
  53.6 2.5 %collective-permute-done.4.refs_6_ = bf16[8,128,128]{2,1,0:T(8,128)(2,1)S(1)} collective-permute-done((bf16[8,128,128]{2,1,0:T(8,128)(2,1)S(1)}, bf16[8,128,128]{2,1,0:T(8,128)(2,1)S(1)}, u32[]{:S(2)}, u32[]{:S(2)}) %collective-permute-start.4) | collective-permute-done | bytes 262176 | tf_op jit(solution)/shard_map/ppermute | solution.py:548
  56.1 1.0 %finish.1 = (bf16[128,4096]{1,0:T(8,128)(2,1)}, bf16[128,4096]{1,0:T(8,128)(2,1)}, bf16[128,512]{1,0:T(8,128)(2,1)}, bf16[128,512]{1,0:T(8,128)(2,1)}) custom-call(f32[256,128]{1,0:T(8,128)S(1)} %get-tuple-element.92.cos_ref.refs_11_.refs_0_, ...), custom_call_target="tpu_custom_call", output_to_operand_aliasing={{0}: (9, {}), {1}: (10, {})} | custom-call | bytes 2097152 | tf_op jit(solution)/shard_map/finish/pallas_call | solution.py:480
  57.1 0.0 collective-permute-done.11.refs_3_
  57.1 0.0 collective-permute-done.10.refs_2_
  57.1 0.0 collective-permute-done.9.refs_1_
  57.1 0.0 copy-start.4
  57.1 0.9 %copy-done.4 = bf16[128,512]{1,0:T(8,128)(2,1)S(1)} copy-done((bf16[128,512]{1,0:T(8,128)(2,1)S(1)}, bf16[128,512]{1,0:T(8,128)(2,1)}, u32[]{:S(2)}) %copy-start.4) | copy-done | bytes 131096
  58.0 0.6 %sums.1 = (f32[32,128]{1,0:T(8,128)}, f32[4,128]{1,0:T(4,128)}, f32[4,128]{1,0:T(4,128)}) custom-call(f32[40,128]{1,0:T(8,128)S(1)} %add_add_fusion.refs_0_, f32[40,128]{1,0:T(8,128)S(1)} %collective-permute-done.9.refs_1_, f32[40,128]{1,0:T(8,128)S(1)} %collective-permute-done.10.refs_2_, f32[40,128]{1,0:T(8,128)S(1)} %collective-permute-done.11.refs_3_, ...), custom_call_target="tpu_custom_call" | custom-call | bytes 131072 | tf_op jit(solution)/shard_map/sums/pallas_call | solution.py:505
  (4 shorter events, 0.0 us)
Async XLA Ops:
  1.6 12.9 %collective-permute-start = (bf16[1280,128]{1,0:T(8,128)(2,1)S(1)}, bf16[1280,128]{1,0:T(8,128)(2,1)S(1)}, u32[]{:S(2)}, u32[]{:S(2)}) collective-permute-start(bf16[1280,128]{1,0:T(8,128)(2,1)S(1)} %pack.1), channel_id=1, source_target_pairs={{0,1},{1,0},{2,3},{3,2},{4,5},{5,4},{6,7},{7,6},{8,9},{9,8},{10,11... | collective-permute-start | bytes 983048 | tf_op jit(solution)/shard_map/ppermute | solution.py:545
  6.0 1.0 %copy-start = (bf16[1,512,512]{2,1,0:T(8,128)(2,1)S(1)}, bf16[1,512,512]{2,1,0:T(8,128)(2,1)}, u32[]{:S(2)}) copy-start(bf16[1,512,512]{2,1,0:T(8,128)(2,1)} %param.13) | copy-start | bytes 1572868
  7.0 1.0 %copy-start.1 = (bf16[1,512,512]{2,1,0:T(8,128)(2,1)S(1)}, bf16[1,512,512]{2,1,0:T(8,128)(2,1)}, u32[]{:S(2)}) copy-start(bf16[1,512,512]{2,1,0:T(8,128)(2,1)} %param.14) | copy-start | bytes 1572868
  8.1 0.9 %copy-start.2 = (bf16[1,128,512]{2,1,0:T(8,128)(2,1)S(1)}, bf16[1,128,512]{2,1,0:T(8,128)(2,1)}, u32[]{:S(2)}) copy-start(bf16[1,128,512]{2,1,0:T(8,128)(2,1)} %param.11) | copy-start | bytes 393220
  9.0 0.9 %copy-start.3 = (bf16[1,128,512]{2,1,0:T(8,128)(2,1)S(1)}, bf16[1,128,512]{2,1,0:T(8,128)(2,1)}, u32[]{:S(2)}) copy-start(bf16[1,128,512]{2,1,0:T(8,128)(2,1)} %param.12) | copy-start | bytes 393220
  13.5 10.6 %collective-permute-start.1 = (bf16[1280,128]{1,0:T(8,128)(2,1)S(1)}, bf16[1280,128]{1,0:T(8,128)(2,1)S(1)}, u32[]{:S(2)}, u32[]{:S(2)}) collective-permute-start(bf16[1280,128]{1,0:T(8,128)(2,1)S(1)} %get-tuple-element.60), channel_id=1, source_target_pairs={{0,1},{1,0},{2,3},{3,2},{4,5},{5,4},{6,7},{7,6},{8,9},{9,8},{10,11... | collective-permute-start | bytes 983048 | tf_op jit(solution)/shard_map/ppermute | solution.py:545
  19.2 11.6 %collective-permute-start.2 = (bf16[1280,128]{1,0:T(8,128)(2,1)S(1)}, bf16[1280,128]{1,0:T(8,128)(2,1)S(1)}, u32[]{:S(2)}, u32[]{:S(2)}) collective-permute-start(bf16[1280,128]{1,0:T(8,128)(2,1)S(1)} %get-tuple-element.66), channel_id=1, source_target_pairs={{0,1},{1,0},{2,3},{3,2},{4,5},{5,4},{6,7},{7,6},{8,9},{9,8},{10,11... | collective-permute-start | bytes 983048 | tf_op jit(solution)/shard_map/ppermute | solution.py:545
  28.8 8.0 %collective-permute-start.3 = (bf16[1280,128]{1,0:T(8,128)(2,1)S(1)}, bf16[1280,128]{1,0:T(8,128)(2,1)S(1)}, u32[]{:S(2)}, u32[]{:S(2)}) collective-permute-start(bf16[1280,128]{1,0:T(8,128)(2,1)S(1)} %get-tuple-element.72), channel_id=1, source_target_pairs={{0,1},{1,0},{2,3},{3,2},{4,5},{5,4},{6,7},{7,6},{8,9},{9,8},{10,11... | collective-permute-start | bytes 983048 | tf_op jit(solution)/shard_map/ppermute | solution.py:545
  40.3 1.3 %collective-permute-start.5 = (f32[40,128]{1,0:T(8,128)S(1)}, f32[40,128]{1,0:T(8,128)S(1)}, u32[]{:S(2)}, u32[]{:S(2)}) collective-permute-start(f32[40,128]{1,0:T(8,128)S(1)} %get-tuple-element.87), channel_id=1, source_target_pairs={{0,2},{1,3},{2,0},{3,1},{4,6},{5,7},{6,4},{7,5},{8,10},{9,11},{10,... | collective-permute-start | bytes 61448 | tf_op jit(solution)/shard_map/ppermute | solution.py:533
  41.6 5.7 %collective-permute-start.8 = (f32[40,128]{1,0:T(8,128)S(1)}, f32[40,128]{1,0:T(8,128)S(1)}, u32[]{:S(2)}, u32[]{:S(2)}) collective-permute-start(f32[40,128]{1,0:T(8,128)S(1)} %add.66), channel_id=1, source_target_pairs={{0,24},{1,25},{2,26},{3,27},{4,28},{5,29},{6,30},{7,31},{8,16},{9,... | collective-permute-start | bytes 61448 | tf_op jit(solution)/shard_map/ppermute | solution.py:533
  45.2 3.8 %collective-permute-start.7 = (f32[40,128]{1,0:T(8,128)S(1)}, f32[40,128]{1,0:T(8,128)S(1)}, u32[]{:S(2)}, u32[]{:S(2)}) collective-permute-start(f32[40,128]{1,0:T(8,128)S(1)} %add.66), channel_id=1, source_target_pairs={{0,8},{1,9},{2,10},{3,11},{4,12},{5,13},{6,14},{7,15},{8,0},{9,1},... | collective-permute-start | bytes 61448 | tf_op jit(solution)/shard_map/ppermute | solution.py:533
  45.2 4.9 %collective-permute-start.6 = (f32[40,128]{1,0:T(8,128)S(1)}, f32[40,128]{1,0:T(8,128)S(1)}, u32[]{:S(2)}, u32[]{:S(2)}) collective-permute-start(f32[40,128]{1,0:T(8,128)S(1)} %add.66), channel_id=1, source_target_pairs={{0,16},{1,17},{2,18},{3,19},{4,20},{5,21},{6,22},{7,23},{8,24},{9,... | collective-permute-start | bytes 61448 | tf_op jit(solution)/shard_map/ppermute | solution.py:533
  45.9 10.2 %collective-permute-start.4 = (bf16[8,128,128]{2,1,0:T(8,128)(2,1)S(1)}, bf16[8,128,128]{2,1,0:T(8,128)(2,1)S(1)}, u32[]{:S(2)}, u32[]{:S(2)}) collective-permute-start(bf16[8,128,128]{2,1,0:T(8,128)(2,1)S(1)} %get-tuple-element.78), channel_id=1, source_target_pairs={{1,0},{3,2},{5,4},{7,6},{9,8},{11,10},{13,12},{15,14},{17,16},{19,... | collective-permute-start | bytes 786440 | tf_op jit(solution)/shard_map/ppermute | solution.py:548
  50.1 7.0 %collective-permute-start.11 = (f32[40,128]{1,0:T(8,128)S(1)}, f32[40,128]{1,0:T(8,128)S(1)}, u32[]{:S(2)}, u32[]{:S(2)}) collective-permute-start(f32[40,128]{1,0:T(8,128)S(1)} %add_add_fusion.refs_0_), channel_id=1, source_target_pairs={{0,5},{1,4},{2,7},{3,6},{4,1},{5,0},{6,3},{7,2},{8,13},{9,12},{10,... | collective-permute-start | bytes 61448 | tf_op jit(solution)/shard_map/ppermute | solution.py:533
  51.6 5.5 %collective-permute-start.10 = (f32[40,128]{1,0:T(8,128)S(1)}, f32[40,128]{1,0:T(8,128)S(1)}, u32[]{:S(2)}, u32[]{:S(2)}) collective-permute-start(f32[40,128]{1,0:T(8,128)S(1)} %add_add_fusion.refs_0_), channel_id=1, source_target_pairs={{0,1},{1,0},{2,3},{3,2},{4,5},{5,4},{6,7},{7,6},{8,9},{9,8},{10,11... | collective-permute-start | bytes 61448 | tf_op jit(solution)/shard_map/ppermute | solution.py:533
  53.1 4.0 %collective-permute-start.9 = (f32[40,128]{1,0:T(8,128)S(1)}, f32[40,128]{1,0:T(8,128)S(1)}, u32[]{:S(2)}, u32[]{:S(2)}) collective-permute-start(f32[40,128]{1,0:T(8,128)S(1)} %add_add_fusion.refs_0_), channel_id=1, source_target_pairs={{0,4},{1,5},{2,6},{3,7},{4,0},{5,1},{6,2},{7,3},{8,12},{9,13},{10,... | collective-permute-start | bytes 61448 | tf_op jit(solution)/shard_map/ppermute | solution.py:533
  57.1 0.9 %copy-start.4 = (bf16[128,512]{1,0:T(8,128)(2,1)S(1)}, bf16[128,512]{1,0:T(8,128)(2,1)}, u32[]{:S(2)}) copy-start(bf16[128,512]{1,0:T(8,128)(2,1)} %get-tuple-element.85.refs_4_) | copy-start | bytes 393220

commit v13 on v12

--- a/solution.py
+++ b/solution.py
@@ -74,12 +74,15 @@
 
 
 def prep_kernel(
-    tokens, q_ref, do_ref, bq_ref, bk_ref, bv_ref, cos_ref, sin_ref, ck_ref, cv_ref,
-    kp_ref, vp_ref, qs_ref, qst_ref, dos_ref, dot_ref, bias_ref, cos_t_ref, sin_t_ref, ck_t_ref, cv_t_ref, pack_ref,
+    q_ref, do_ref, bq_ref, bk_ref, bv_ref, cos_ref, sin_ref, ck_ref, cv_ref, kp_ref, vp_ref,
+    qs_ref, qst_ref, dos_ref, dot_ref, bias_ref, cos_t_ref, sin_t_ref, ck_t_ref, cv_t_ref,
+    ck_out, cv_out, kp_out, vp_out, pack_ref,
 ):
     g = pl.program_id(0)
+    tokens = q_ref.shape[0]
     cosine, sine = cos_ref[pl.ds(0, tokens), :], sin_ref[pl.ds(0, tokens), :]
     bias_q = bq_ref[...].astype(F32)
+    own = (ck_ref, cv_ref, kp_ref, vp_ref)
 
     @pl.when(g == 0)
     def _():
@@ -87,7 +90,10 @@
         bias_ref[pl.ds(KV, KV), :] = bv_ref[...].astype(F32)
         cos_t_ref[...] = cosine.T
         sin_t_ref[...] = sine.T
-        copy_chunk(pl.ds(HD, HD), (ck_ref, cv_ref, kp_ref, vp_ref), pack_ref)
+
+    @pl.when(g == 1)
+    def _():
+        copy_chunk(pl.ds(0, HD), own, pack_ref)
 
     for h in range(GROUP):
         cols = pl.ds(h * HD, HD)
@@ -102,12 +108,14 @@
         qst_ref[place, pl.ds(part * tokens, tokens)] = x.T
         dot_ref[place, pl.ds(part * tokens, tokens)] = do.T
     mine = pl.ds(pl.multiple_of(g * HD, HD), HD)
-    ck_t_ref[mine, :] = ck_ref[:, mine].T
-    cv_t_ref[mine, :] = cv_ref[:, mine].T
-
-
-def prep(q, do, bq, bk, bv, cosine, sine, ck, cv, kp, vp):
-    tokens, slots = q.shape[0], ck.shape[0]
+    ck_t_ref[mine, :] = ck_ref[...].T
+    cv_t_ref[mine, :] = cv_ref[...].T
+    for ref, out in zip(own, (ck_out, cv_out, kp_out, vp_out)):
+        out[:, mine] = ref[...]
+
+
+def prep(q, do, bq, bk, bv, cosine, sine, own):
+    tokens, slots = q.shape[0], own[0].shape[0]
     vmem = pl.BlockSpec(memory_space=pltpu.VMEM)
     wide = pl.BlockSpec((tokens, GROUP * HD), lambda i: (0, i))
     stacked = pltpu.VMEM((HQ * tokens, HD), B16)
@@ -119,14 +127,16 @@
         pltpu.VMEM((HD, tokens), F32),
         pltpu.VMEM((KV * HD, slots), B16),
         pltpu.VMEM((KV * HD, slots), B16),
+        *[pltpu.VMEM(x.shape, B16) for x in own],
         pltpu.VMEM((2 * (slots + tokens), HD), B16),
     ]
     return pl.pallas_call(
-        functools.partial(prep_kernel, tokens),
+        prep_kernel,
         grid=(KV,),
         in_specs=[
             wide, wide, pl.BlockSpec((GROUP, HD), lambda i: (i, 0)),
-            whole((KV, HD)), whole((KV, HD)), *[vmem] * 6,
+            whole((KV, HD)), whole((KV, HD)), vmem, vmem,
+            *[pl.BlockSpec((x.shape[0], HD), lambda i: (0, i)) for x in own],
         ],
         out_specs=[vmem] * len(out_shape),
         out_shape=out_shape,
@@ -135,7 +145,7 @@
             flops=4 * tokens * HQ * HD, bytes_accessed=12 * tokens * HQ * HD, transcendentals=0
         ),
         name="prep",
-    )(q, do, bq, bk, bv, cosine, sine, ck, cv, kp, vp)
+    )(q, do, bq, bk, bv, cosine, sine, *own)
 
 
 def fold(x, op):
@@ -227,8 +237,8 @@
     (first_ref, rank_ref, qs_ref, qst_ref, dos_ref, dot_ref, bias_ref, cos_t_ref, sin_t_ref,
      ck_t_ref, cv_t_ref, cos_ref, sin_ref, ck_ref, cv_ref, kp_ref, vp_ref) = take(17)
     far = take(shards - 1)
-    ahead = take(3) if g == KV - 1 else []
-    if g == 0:
+    ahead = take(3)
+    if g + 1 < KV:
         take(1)
     old_sums_ref = take(1)[0] if g else None
     old_send = take(shards - 1) if g else []
@@ -243,7 +253,7 @@
     slots = ck_ref.shape[0]
     owned = slots + tokens
     total = shards * owned
-    known = owned if ahead else 0
+    known = owned
     first = first_ref[0]
     rank = rank_ref[0]
     mine = pl.ds(g * HD, HD)
@@ -264,7 +274,7 @@
         for (natural, transposed), cache, own in zip(
             ((keys, keys_t), (values, values_t)), sources[:2], (k, v)
         ):
-            if s or not ahead:
+            if s:
                 natural[pl.ds(at, slots)] = cache
                 natural[pl.ds(at + slots, tokens)] = own
             transposed[:, pl.ds(at + slots, tokens)] = own.T
@@ -288,7 +298,7 @@
             self.rows = pl.ds(pl.multiple_of(index * width, width), width)
             self.place = pl.ds(pl.multiple_of(index * HD, HD), HD)
             self.ahead = [ref.at[self.index % len(scratch)] for ref in ahead]
-            self.top = self.ahead[2][...] if ahead else jnp.full((8, width), NEG, F32)
+            self.top = self.ahead[2][...]
 
         def scores(self):
             s = dot(keys[pl.ds(known, total - known), :], qst_ref[self.place, :], NN)
@@ -402,7 +412,7 @@
 
     args = [first, rank]
     placed = [*prepared, cosine, sine, ck, cv, kp, vp, *far]
-    placed += ahead if g == KV - 1 else ahead[2:] if g == 0 else []
+    placed += [*ahead[g], *[x[2] for x in ahead[g + 1:g + 2]]]
     aliases = {}
     if before is not None:
         out, gq, sums, send = before
@@ -539,7 +549,6 @@
     rank = lax.axis_index("seq").astype(jnp.int32)
     tokens = q_proj.shape[1]
     shifts = range(1, shards)
-    ck, cv, kp, vp = cache_k[0], cache_v[0], k_proj[0], v_proj[0]
 
     def ring(x, s):
         return lax.ppermute(x, "seq", [(i, (i + s) % shards) for i in range(shards)])
@@ -548,7 +557,8 @@
         return lax.ppermute(x, "seq", [(i + s, i) for i in range(shards - s)])
 
     hbm = functools.partial(pltpu.with_memory_space_constraint, memory_space=pltpu.HBM)
-    chunk = pack([hbm(x) for x in (ck, cv, kp, vp)])
+    own = [hbm(x[0]) for x in (cache_k, cache_v, k_proj, v_proj)]
+    chunk = pack(own)
     far = [[ring(chunk, s) for s in shifts]]
 
     owners = lax.rem(rank - jnp.arange(shards, dtype=jnp.int32) + shards, shards)
@@ -561,15 +571,18 @@
     cosine = jnp.cos(angles)
     sine = jnp.sin(angles) * jnp.where(lane < HD // 2, -1.0, 1.0).astype(F32)[None]
 
-    *prepared, chunk = prep(
+    *prepared, ck, cv, kp, vp, chunk = prep(
         hbm(q_proj[0]), hbm(dout[0]), hbm(bias_q.reshape(HQ, HD)),
-        hbm(bias_k.reshape(KV, HD)), hbm(bias_v.reshape(KV, HD)), cosine, sine, ck, cv, kp, vp,
+        hbm(bias_k.reshape(KV, HD)), hbm(bias_v.reshape(KV, HD)), cosine, sine, own,
     )
     far.append([ring(chunk, s) for s in shifts])
     qst, dot_t, bias = prepared[1], prepared[3], prepared[4]
-    ahead = look_ahead(
-        KV - 1, shards, start, rank.reshape(1), qst, dot_t, bias, cosine, sine, ck, cv, kp, vp
-    )
+    ahead = [
+        look_ahead(
+            g, shards, start, rank.reshape(1), qst, dot_t, bias, cosine, sine, ck, cv, kp, vp
+        )
+        for g in range(KV)
+    ]
     before, owns = None, []
     for g in range(KV):
         before, own, more = attend(
@@ -584,7 +597,7 @@
     backs = [earlier(x, s) for s, x in zip(shifts, send)]
     sums = sum_but_last(sums, ("dp", "seq"), shards)
     out, gq, gk, gv = finish(shards, cosine, sine, owns, backs, columns, out, gq)
-    sums = last_sums(sums, gk)
+    sums = last_sums(sums, hbm(gk))
     return (out[None], gq[None], gk[None], gv[None], *[x.reshape(-1) for x in sums])
 
 

time: 59 us -> 55.7 us (0.944)
  local copies, waits for them, and re-layouts: 4.79 us -> 0 us
  starting transfers between devices: 14.4 us -> 16.5 us
  waiting for transfers between devices: 12.4 us -> 10.9 us
  Pallas kernels: 25 us -> 26.1 us
    unnamed x10 -> x0, local copies, waits for them, and re-layouts: 4.79 us -> none
    ppermute x4, waiting for transfers between devices: 5.94 us -> 3.22 us  [ring(): lax.ppermute(x, 'seq', [(i, (i + s) % shards) for i in range(shards)])]
    pallas_call x1 -> x4, Pallas kernels: 0.85 us -> 3.4 us  [look_ahead(): pl.pallas_call(functools.partial(ahead_kernel, g, shards), grid=(1,), in_...]
    ppermute x4, starting transfers between devices: 5.12 us -> 7.25 us  [ring(): lax.ppermute(x, 'seq', [(i, (i + s) % shards) for i in range(shards)])]
    pallas_call x4, Pallas kernels: 17.8 us -> 15.9 us  [attend(): pl.pallas_call(functools.partial(attend_kernel, g, shards), grid=(1,), in...]
    ppermute x7, waiting for transfers between devices: 4.01 us -> 5.67 us  [sum_but_last(): parts.append(lax.ppermute(x, axes, [(i, i ^ flip) for i in range(devices)]))]
  transfers between devices with their start and end apart: 12 -> 12, of which waited for: 7 -> 8; matrix products, arithmetic and copies ran while one was open for 1% -> 1% of each run, Pallas kernels for 34% -> 38%
where the time goes in v13:
time: 55.7 us; the launch traced here: 55.5 us
  Pallas kernels  26.1 us (47%)
  starting transfers between devices  16.5 us (30%)
  waiting for transfers between devices  10.9 us (20%)
  between operations  1.38 us (2%)
  other arithmetic  0.64 us (1%)
    pallas_call x4, Pallas kernels, attend(): pl.pallas_call(functools.partial(attend_kernel, g, shards), grid=(1,), in...  15.9 us
    ppermute x7, starting transfers between devices, sum_but_last(): parts.append(lax.ppermute(x, axes, [(i, i ^ flip) for i in range(devices)]))  8 us
    ppermute x4, starting transfers between devices, ring(): lax.ppermute(x, 'seq', [(i, (i + s) % shards) for i in range(shards)])  7.25 us
    ppermute x7, waiting for transfers between devices, sum_but_last(): parts.append(lax.ppermute(x, axes, [(i, i ^ flip) for i in range(devices)]))  5.67 us
    pallas_call x1, Pallas kernels, prep(): pl.pallas_call(prep_kernel, grid=(KV,), in_specs=[wide, wide, pl.BlockSpe...  4.2 us
    pallas_call x4, Pallas kernels, look_ahead(): pl.pallas_call(functools.partial(ahead_kernel, g, shards), grid=(1,), in_...  3.4 us
    ppermute x4, waiting for transfers between devices, ring(): lax.ppermute(x, 'seq', [(i, (i + s) % shards) for i in range(shards)])  3.22 us
    ppermute x1, waiting for transfers between devices, earlier(): return lax.ppermute(x, 'seq', [(i + s, i) for i in range(shards - s)])  2 us
  transfers between devices with their start and end apart: 12, of which 8 were waited for; matrix products, arithmetic and copies ran while one was open for 1% of the time, Pallas kernels for 38%

profile of v13, /device:TPU:0, one launch (start us, length us, event | category | flops | bytes accessed | tf_op | source)
XLA Modules:
  0.0 55.5 jit_solution(15819249677577666576)
XLA Ops:
  0.6 1.0 %pack.1 = bf16[1280,128]{1,0:T(8,128)(2,1)S(1)} custom-call(bf16[512,512]{1,0:T(8,128)(2,1)} %bitcast.23, bf16[512,512]{1,0:T(8,128)(2,1)} %bitcast.25, bf16[128,512]{1,0:T(8,128)(2,1)} %bitcast.29, bf16[128,512]{1,0:T(8,128)(2,1)} %bitcast.31), custom_call_target="tpu_custom_call" | custom-call | bytes 655360 | tf_op jit(solution)/shard_map/pack/pallas_call | solution.py:60
  1.6 3.0 %collective-permute-start = (bf16[1280,128]{1,0:T(8,128)(2,1)S(1)}, bf16[1280,128]{1,0:T(8,128)(2,1)S(1)}, u32[]{:S(2)}, u32[]{:S(2)}) collective-permute-start(bf16[1280,128]{1,0:T(8,128)(2,1)S(1)} %pack.1), channel_id=1, source_target_pairs={{0,1},{1,0},{2,3},{3,2},{4,5},{5,4},{6,7},{7,6},{8,9},{9,8},{10,11... | collective-permute-start | bytes 983048 | tf_op jit(solution)/shard_map/ppermute | solution.py:554
  5.3 0.1 convert_bitcast_fusion
  5.4 0.5 fusion
  6.0 4.2 %prep.1 = (bf16[4096,128]{1,0:T(8,128)(2,1)S(1)}, bf16[1024,512]{1,0:T(8,128)(2,1)S(1)}, bf16[4096,128]{1,0:T(8,128)(2,1)S(1)}, bf16[1024,512]{1,0:T(8,128)(2,1)...) custom-call(bf16[128,4096]{1,0:T(8,128)(2,1)} %bitcast.27, ...), custom_call_target="tpu_custom_call" | custom-call | flops 2097152 | bytes 6291456 | tf_op jit(solution)/shard_map/prep/pallas_call | solution.py:133
  10.2 0.1 collective-permute-start.1
  10.3 0.9 %ahead.4 = (f32[2,640,512]{2,1,0:T(8,128)S(1)}, f32[2,640,512]{2,1,0:T(8,128)S(1)}, f32[2,8,512]{2,1,0:T(8,128)S(1)}) custom-call(s32[1]{0:T(128)} %copy.29.first_ref.refs_0_, s32[1]{0:T(128)} %bitcast.2.rank_ref.refs_1_, bf16[1024,512]{1,0:T(8,128)(2,1)S(1)} %get-tuple-element.63.qst_ref.refs_3_, bf16[1024,512]{1,0:T(8,128)(2,1)S(1)} %get-tuple-element.65.dot_ref.refs_5_, ...), custom_call_target="tpu_custom_call" | custom-call | flops 335544320 | bytes 5242880 | tf_op jit(solution)/shard_map/ahead/pallas_call | solution.py:209
  11.1 0.9 %ahead.5 = (f32[2,640,512]{2,1,0:T(8,128)S(1)}, f32[2,640,512]{2,1,0:T(8,128)S(1)}, f32[2,8,512]{2,1,0:T(8,128)S(1)}) custom-call(s32[1]{0:T(128)} %copy.29.first_ref.refs_0_, s32[1]{0:T(128)} %bitcast.2.rank_ref.refs_1_, bf16[1024,512]{1,0:T(8,128)(2,1)S(1)} %get-tuple-element.63.qst_ref.refs_3_, bf16[1024,512]{1,0:T(8,128)(2,1)S(1)} %get-tuple-element.65.dot_ref.refs_5_, ...), custom_call_target="tpu_custom_call" | custom-call | flops 335544320 | bytes 5242880 | tf_op jit(solution)/shard_map/ahead/pallas_call | solution.py:209
  12.0 0.9 %ahead.6 = (f32[2,640,512]{2,1,0:T(8,128)S(1)}, f32[2,640,512]{2,1,0:T(8,128)S(1)}, f32[2,8,512]{2,1,0:T(8,128)S(1)}) custom-call(s32[1]{0:T(128)} %copy.29.first_ref.refs_0_, s32[1]{0:T(128)} %bitcast.2.rank_ref.refs_1_, bf16[1024,512]{1,0:T(8,128)(2,1)S(1)} %get-tuple-element.63.qst_ref.refs_3_, bf16[1024,512]{1,0:T(8,128)(2,1)S(1)} %get-tuple-element.65.dot_ref.refs_5_, ...), custom_call_target="tpu_custom_call" | custom-call | flops 335544320 | bytes 5242880 | tf_op jit(solution)/shard_map/ahead/pallas_call | solution.py:209
  12.8 0.0 collective-permute-done.refs_17_
  12.8 4.2 %attend.4 = (bf16[128,4096]{1,0:T(8,128)(2,1)}, bf16[128,4096]{1,0:T(8,128)(2,1)}, f32[40,128]{1,0:T(8,128)S(1)}, f32[2,128,128]{2,1,0:T(8,128)S(1)}, bf16[2,128...) custom-call(s32[1]{0:T(128)} %copy.29.first_ref.refs_0_, s32[1]{0:T(128)} %bitcast.2.rank_ref.refs_1_, ...), custom_call_target="tpu_custom_call" | custom-call | flops 1476395008 | bytes 2359296 | tf_op jit(solution)/shard_map/attend/pallas_call | solution.py:439
  17.0 2.4 %collective-permute-start.2 = (bf16[1280,128]{1,0:T(8,128)(2,1)S(1)}, bf16[1280,128]{1,0:T(8,128)(2,1)S(1)}, u32[]{:S(2)}, u32[]{:S(2)}) collective-permute-start(bf16[1280,128]{1,0:T(8,128)(2,1)S(1)} %get-tuple-element.89), channel_id=1, source_target_pairs={{0,1},{1,0},{2,3},{3,2},{4,5},{5,4},{6,7},{7,6},{8,9},{9,8},{10,11... | collective-permute-start | bytes 983048 | tf_op jit(solution)/shard_map/ppermute | solution.py:554
  19.4 0.2 collective-permute-done.1.refs_17_
  19.6 4.1 %attend.5 = (bf16[128,4096]{1,0:T(8,128)(2,1)}, bf16[128,4096]{1,0:T(8,128)(2,1)}, f32[40,128]{1,0:T(8,128)S(1)}, f32[2,128,128]{2,1,0:T(8,128)S(1)}, bf16[4,128...) custom-call(s32[1]{0:T(128)} %copy.29.first_ref.refs_0_, ...), custom_call_target="tpu_custom_call", output_to_operand_aliasing={{0}: (24, {}), {1}: (25, {})} | custom-call | flops 1476395008 | bytes 2359296 | tf_op jit(solution)/shard_map/attend/pallas_call | solution.py:439
  23.7 1.7 %collective-permute-start.3 = (bf16[1280,128]{1,0:T(8,128)(2,1)S(1)}, bf16[1280,128]{1,0:T(8,128)(2,1)S(1)}, u32[]{:S(2)}, u32[]{:S(2)}) collective-permute-start(bf16[1280,128]{1,0:T(8,128)(2,1)S(1)} %get-tuple-element.98), channel_id=1, source_target_pairs={{0,1},{1,0},{2,3},{3,2},{4,5},{5,4},{6,7},{7,6},{8,9},{9,8},{10,11... | collective-permute-start | bytes 983048 | tf_op jit(solution)/shard_map/ppermute | solution.py:554
  25.4 0.8 %ahead.7 = (f32[2,640,512]{2,1,0:T(8,128)S(1)}, f32[2,640,512]{2,1,0:T(8,128)S(1)}, f32[2,8,512]{2,1,0:T(8,128)S(1)}) custom-call(s32[1]{0:T(128)} %copy.29.first_ref.refs_0_, s32[1]{0:T(128)} %bitcast.2.rank_ref.refs_1_, bf16[1024,512]{1,0:T(8,128)(2,1)S(1)} %get-tuple-element.63.qst_ref.refs_3_, bf16[1024,512]{1,0:T(8,128)(2,1)S(1)} %get-tuple-element.65.dot_ref.refs_5_, ...), custom_call_target="tpu_custom_call" | custom-call | flops 335544320 | bytes 5242880 | tf_op jit(solution)/shard_map/ahead/pallas_call | solution.py:209
  26.2 1.5 %collective-permute-done.2.refs_17_ = bf16[1280,128]{1,0:T(8,128)(2,1)S(1)} collective-permute-done((bf16[1280,128]{1,0:T(8,128)(2,1)S(1)}, bf16[1280,128]{1,0:T(8,128)(2,1)S(1)}, u32[]{:S(2)}, u32[]{:S(2)}) %collective-permute-start.2) | collective-permute-done | bytes 327712 | tf_op jit(solution)/shard_map/ppermute | solution.py:554
  27.8 4.2 %attend.6 = (bf16[128,4096]{1,0:T(8,128)(2,1)}, bf16[128,4096]{1,0:T(8,128)(2,1)}, f32[40,128]{1,0:T(8,128)S(1)}, f32[2,128,128]{2,1,0:T(8,128)S(1)}, bf16[6,128,128]{2,1,0:T(8,128)(2,1)S(1)}) custom-call(s32[1]{0:T(128)} %copy.29.first_ref.refs_0_, s32[1]{0:T(128)} %bitcast.2.rank_ref.refs_1_, ...), custom_call_target="tpu_custom_call", output_to_operand_aliasing={{0}: (24, {}), {1}: (25, {})} | custom-call | flops 1476395008 | bytes 2359296 | tf_op jit(solution)/shard_map/attend/pallas_call | solution.py:439
  32.0 1.5 %collective-permute-done.3.refs_17_ = bf16[1280,128]{1,0:T(8,128)(2,1)S(1)} collective-permute-done((bf16[1280,128]{1,0:T(8,128)(2,1)S(1)}, bf16[1280,128]{1,0:T(8,128)(2,1)S(1)}, u32[]{:S(2)}, u32[]{:S(2)}) %collective-permute-start.3) | collective-permute-done | bytes 327712 | tf_op jit(solution)/shard_map/ppermute | solution.py:554
  33.5 3.5 %attend.7 = (bf16[128,1024]{1,0:T(8,128)(2,1)S(1)}, bf16[128,1024]{1,0:T(8,128)(2,1)S(1)}, f32[40,128]{1,0:T(8,128)S(1)}, f32[2,128,128]{2,1,0:T(8,128)S(1)}, bf16[8,128,128]{2,1,0:T(8,128)(2,1)S(1)}) custom-call(s32[1]{0:T(128)} %copy.29.first_ref.refs_0_, s32[1]{0:T(128)} %bitcast.2.rank_ref.refs_1_, bf16[4096,128]{1,0:T(8,128)(2,1)S(1)} %get-tuple-element.62.refs_2_, ...), custom_call_target="tpu_custom_call" | custom-call | flops 1476395008 | bytes 2359296 | tf_op jit(solution)/shard_map/attend/pallas_call | solution.py:439
  36.9 0.1 collective-permute-start.5
  37.0 1.2 %collective-permute-done.5 = f32[40,128]{1,0:T(8,128)S(1)} collective-permute-done((f32[40,128]{1,0:T(8,128)S(1)}, f32[40,128]{1,0:T(8,128)S(1)}, u32[]{:S(2)}, u32[]{:S(2)}) %collective-permute-start.5) | collective-permute-done | bytes 20512 | tf_op jit(solution)/shard_map/ppermute | solution.py:543
  38.2 1.8 %collective-permute-start.7 = (f32[40,128]{1,0:T(8,128)S(1)}, f32[40,128]{1,0:T(8,128)S(1)}, u32[]{:S(2)}, u32[]{:S(2)}) collective-permute-start(f32[40,128]{1,0:T(8,128)S(1)} %add.66), channel_id=1, source_target_pairs={{0,8},{1,9},{2,10},{3,11},{4,12},{5,13},{6,14},{7,15},{8,0},{9,1},... | collective-permute-start | bytes 61448 | tf_op jit(solution)/shard_map/ppermute | solution.py:543
  40.0 2.5 %collective-permute-start.8 = (f32[40,128]{1,0:T(8,128)S(1)}, f32[40,128]{1,0:T(8,128)S(1)}, u32[]{:S(2)}, u32[]{:S(2)}) collective-permute-start(f32[40,128]{1,0:T(8,128)S(1)} %add.66), channel_id=1, source_target_pairs={{0,24},{1,25},{2,26},{3,27},{4,28},{5,29},{6,30},{7,31},{8,16},{9,... | collective-permute-start | bytes 61448 | tf_op jit(solution)/shard_map/ppermute | solution.py:543
  42.5 0.1 collective-permute-start.6
  42.6 1.3 %collective-permute-start.4 = (bf16[8,128,128]{2,1,0:T(8,128)(2,1)S(1)}, bf16[8,128,128]{2,1,0:T(8,128)(2,1)S(1)}, u32[]{:S(2)}, u32[]{:S(2)}) collective-permute-start(bf16[8,128,128]{2,1,0:T(8,128)(2,1)S(1)} %get-tuple-element.104), channel_id=1, source_target_pairs={{1,0},{3,2},{5,4},{7,6},{9,8},{11,10},{13,12},{15,14},{17,16},{19,... | collective-permute-start | bytes 786440 | tf_op jit(solution)/shard_map/ppermute | solution.py:557
  43.9 0.0 collective-permute-done.7
  43.9 1.7 %collective-permute-done.8 = f32[40,128]{1,0:T(8,128)S(1)} collective-permute-done((f32[40,128]{1,0:T(8,128)S(1)}, f32[40,128]{1,0:T(8,128)S(1)}, u32[]{:S(2)}, u32[]{:S(2)}) %collective-permute-start.8) | collective-permute-done | bytes 20512 | tf_op jit(solution)/shard_map/ppermute | solution.py:543
  45.6 1.6 %collective-permute-done.6 = f32[40,128]{1,0:T(8,128)S(1)} collective-permute-done((f32[40,128]{1,0:T(8,128)S(1)}, f32[40,128]{1,0:T(8,128)S(1)}, u32[]{:S(2)}, u32[]{:S(2)}) %collective-permute-start.6) | collective-permute-done | bytes 20512 | tf_op jit(solution)/shard_map/ppermute | solution.py:543
  47.2 1.5 %collective-permute-start.9 = (f32[40,128]{1,0:T(8,128)S(1)}, f32[40,128]{1,0:T(8,128)S(1)}, u32[]{:S(2)}, u32[]{:S(2)}) collective-permute-start(f32[40,128]{1,0:T(8,128)S(1)} %add_add_fusion.refs_0_), channel_id=1, source_target_pairs={{0,4},{1,5},{2,6},{3,7},{4,0},{5,1},{6,2},{7,3},{8,12},{9,13},{10,... | collective-permute-start | bytes 61448 | tf_op jit(solution)/shard_map/ppermute | solution.py:543
  48.7 1.5 %collective-permute-start.10 = (f32[40,128]{1,0:T(8,128)S(1)}, f32[40,128]{1,0:T(8,128)S(1)}, u32[]{:S(2)}, u32[]{:S(2)}) collective-permute-start(f32[40,128]{1,0:T(8,128)S(1)} %add_add_fusion.refs_0_), channel_id=1, source_target_pairs={{0,1},{1,0},{2,3},{3,2},{4,5},{5,4},{6,7},{7,6},{8,9},{9,8},{10,11... | collective-permute-start | bytes 61448 | tf_op jit(solution)/shard_map/ppermute | solution.py:543
  50.2 0.5 collective-permute-start.11
  50.7 2.0 %collective-permute-done.4.refs_6_ = bf16[8,128,128]{2,1,0:T(8,128)(2,1)S(1)} collective-permute-done((bf16[8,128,128]{2,1,0:T(8,128)(2,1)S(1)}, bf16[8,128,128]{2,1,0:T(8,128)(2,1)S(1)}, u32[]{:S(2)}, u32[]{:S(2)}) %collective-permute-start.4) | collective-permute-done | bytes 262176 | tf_op jit(solution)/shard_map/ppermute | solution.py:557
  52.7 1.0 %finish.1 = (bf16[128,4096]{1,0:T(8,128)(2,1)}, bf16[128,4096]{1,0:T(8,128)(2,1)}, bf16[128,512]{1,0:T(8,128)(2,1)}, bf16[128,512]{1,0:T(8,128)(2,1)}) custom-call(f32[256,128]{1,0:T(8,128)S(1)} %get-tuple-element.118.cos_ref.refs_11_.refs_0_, ...), custom_call_target="tpu_custom_call", output_to_operand_aliasing={{0}: (9, {}), {1}: (10, {})} | custom-call | bytes 2097152 | tf_op jit(solution)/shard_map/finish/pallas_call | solution.py:490
  53.7 0.0 collective-permute-done.9.refs_1_
  53.7 0.0 collective-permute-done.10.refs_2_
  53.7 1.2 %collective-permute-done.11.refs_3_ = f32[40,128]{1,0:T(8,128)S(1)} collective-permute-done((f32[40,128]{1,0:T(8,128)S(1)}, f32[40,128]{1,0:T(8,128)S(1)}, u32[]{:S(2)}, u32[]{:S(2)}) %collective-permute-start.11) | collective-permute-done | bytes 20512 | tf_op jit(solution)/shard_map/ppermute | solution.py:543
  54.9 0.6 %sums.1 = (f32[32,128]{1,0:T(8,128)}, f32[4,128]{1,0:T(4,128)}, f32[4,128]{1,0:T(4,128)}) custom-call(f32[40,128]{1,0:T(8,128)S(1)} %add_add_fusion.refs_0_, f32[40,128]{1,0:T(8,128)S(1)} %collective-permute-done.9.refs_1_, f32[40,128]{1,0:T(8,128)S(1)} %collective-permute-done.10.refs_2_, f32[40,128]{1,0:T(8,128)S(1)} %collective-permute-done.11.refs_3_, ...), custom_call_target="tpu_custom_call" | custom-call | bytes 131072 | tf_op jit(solution)/shard_map/sums/pallas_call | solution.py:515
  (4 shorter events, 0.0 us)
Async XLA Ops:
  1.6 11.2 %collective-permute-start = (bf16[1280,128]{1,0:T(8,128)(2,1)S(1)}, bf16[1280,128]{1,0:T(8,128)(2,1)S(1)}, u32[]{:S(2)}, u32[]{:S(2)}) collective-permute-start(bf16[1280,128]{1,0:T(8,128)(2,1)S(1)} %pack.1), channel_id=1, source_target_pairs={{0,1},{1,0},{2,3},{3,2},{4,5},{5,4},{6,7},{7,6},{8,9},{9,8},{10,11... | collective-permute-start | bytes 983048 | tf_op jit(solution)/shard_map/ppermute | solution.py:554
  10.2 9.4 %collective-permute-start.1 = (bf16[1280,128]{1,0:T(8,128)(2,1)S(1)}, bf16[1280,128]{1,0:T(8,128)(2,1)S(1)}, u32[]{:S(2)}, u32[]{:S(2)}) collective-permute-start(bf16[1280,128]{1,0:T(8,128)(2,1)S(1)} %get-tuple-element.80), channel_id=1, source_target_pairs={{0,1},{1,0},{2,3},{3,2},{4,5},{5,4},{6,7},{7,6},{8,9},{9,8},{10,11... | collective-permute-start | bytes 983048 | tf_op jit(solution)/shard_map/ppermute | solution.py:554
  17.0 10.8 %collective-permute-start.2 = (bf16[1280,128]{1,0:T(8,128)(2,1)S(1)}, bf16[1280,128]{1,0:T(8,128)(2,1)S(1)}, u32[]{:S(2)}, u32[]{:S(2)}) collective-permute-start(bf16[1280,128]{1,0:T(8,128)(2,1)S(1)} %get-tuple-element.89), channel_id=1, source_target_pairs={{0,1},{1,0},{2,3},{3,2},{4,5},{5,4},{6,7},{7,6},{8,9},{9,8},{10,11... | collective-permute-start | bytes 983048 | tf_op jit(solution)/shard_map/ppermute | solution.py:554
  23.7 9.8 %collective-permute-start.3 = (bf16[1280,128]{1,0:T(8,128)(2,1)S(1)}, bf16[1280,128]{1,0:T(8,128)(2,1)S(1)}, u32[]{:S(2)}, u32[]{:S(2)}) collective-permute-start(bf16[1280,128]{1,0:T(8,128)(2,1)S(1)} %get-tuple-element.98), channel_id=1, source_target_pairs={{0,1},{1,0},{2,3},{3,2},{4,5},{5,4},{6,7},{7,6},{8,9},{9,8},{10,11... | collective-permute-start | bytes 983048 | tf_op jit(solution)/shard_map/ppermute | solution.py:554
  36.9 1.3 %collective-permute-start.5 = (f32[40,128]{1,0:T(8,128)S(1)}, f32[40,128]{1,0:T(8,128)S(1)}, u32[]{:S(2)}, u32[]{:S(2)}) collective-permute-start(f32[40,128]{1,0:T(8,128)S(1)} %get-tuple-element.113), channel_id=1, source_target_pairs={{0,2},{1,3},{2,0},{3,1},{4,6},{5,7},{6,4},{7,5},{8,10},{9,11},{10,... | collective-permute-start | bytes 61448 | tf_op jit(solution)/shard_map/ppermute | solution.py:543
  38.2 5.7 %collective-permute-start.7 = (f32[40,128]{1,0:T(8,128)S(1)}, f32[40,128]{1,0:T(8,128)S(1)}, u32[]{:S(2)}, u32[]{:S(2)}) collective-permute-start(f32[40,128]{1,0:T(8,128)S(1)} %add.66), channel_id=1, source_target_pairs={{0,8},{1,9},{2,10},{3,11},{4,12},{5,13},{6,14},{7,15},{8,0},{9,1},... | collective-permute-start | bytes 61448 | tf_op jit(solution)/shard_map/ppermute | solution.py:543
  40.0 5.6 %collective-permute-start.8 = (f32[40,128]{1,0:T(8,128)S(1)}, f32[40,128]{1,0:T(8,128)S(1)}, u32[]{:S(2)}, u32[]{:S(2)}) collective-permute-start(f32[40,128]{1,0:T(8,128)S(1)} %add.66), channel_id=1, source_target_pairs={{0,24},{1,25},{2,26},{3,27},{4,28},{5,29},{6,30},{7,31},{8,16},{9,... | collective-permute-start | bytes 61448 | tf_op jit(solution)/shard_map/ppermute | solution.py:543
  42.5 4.7 %collective-permute-start.6 = (f32[40,128]{1,0:T(8,128)S(1)}, f32[40,128]{1,0:T(8,128)S(1)}, u32[]{:S(2)}, u32[]{:S(2)}) collective-permute-start(f32[40,128]{1,0:T(8,128)S(1)} %add.66), channel_id=1, source_target_pairs={{0,16},{1,17},{2,18},{3,19},{4,20},{5,21},{6,22},{7,23},{8,24},{9,... | collective-permute-start | bytes 61448 | tf_op jit(solution)/shard_map/ppermute | solution.py:543
  42.6 10.1 %collective-permute-start.4 = (bf16[8,128,128]{2,1,0:T(8,128)(2,1)S(1)}, bf16[8,128,128]{2,1,0:T(8,128)(2,1)S(1)}, u32[]{:S(2)}, u32[]{:S(2)}) collective-permute-start(bf16[8,128,128]{2,1,0:T(8,128)(2,1)S(1)} %get-tuple-element.104), channel_id=1, source_target_pairs={{1,0},{3,2},{5,4},{7,6},{9,8},{11,10},{13,12},{15,14},{17,16},{19,... | collective-permute-start | bytes 786440 | tf_op jit(solution)/shard_map/ppermute | solution.py:557
  47.2 6.5 %collective-permute-start.9 = (f32[40,128]{1,0:T(8,128)S(1)}, f32[40,128]{1,0:T(8,128)S(1)}, u32[]{:S(2)}, u32[]{:S(2)}) collective-permute-start(f32[40,128]{1,0:T(8,128)S(1)} %add_add_fusion.refs_0_), channel_id=1, source_target_pairs={{0,4},{1,5},{2,6},{3,7},{4,0},{5,1},{6,2},{7,3},{8,12},{9,13},{10,... | collective-permute-start | bytes 61448 | tf_op jit(solution)/shard_map/ppermute | solution.py:543
  48.7 5.0 %collective-permute-start.10 = (f32[40,128]{1,0:T(8,128)S(1)}, f32[40,128]{1,0:T(8,128)S(1)}, u32[]{:S(2)}, u32[]{:S(2)}) collective-permute-start(f32[40,128]{1,0:T(8,128)S(1)} %add_add_fusion.refs_0_), channel_id=1, source_target_pairs={{0,1},{1,0},{2,3},{3,2},{4,5},{5,4},{6,7},{7,6},{8,9},{9,8},{10,11... | collective-permute-start | bytes 61448 | tf_op jit(solution)/shard_map/ppermute | solution.py:543
  50.2 4.7 %collective-permute-start.11 = (f32[40,128]{1,0:T(8,128)S(1)}, f32[40,128]{1,0:T(8,128)S(1)}, u32[]{:S(2)}, u32[]{:S(2)}) collective-permute-start(f32[40,128]{1,0:T(8,128)S(1)} %add_add_fusion.refs_0_), channel_id=1, source_target_pairs={{0,5},{1,4},{2,7},{3,6},{4,1},{5,0},{6,3},{7,2},{8,13},{9,12},{10,... | collective-permute-start | bytes 61448 | tf_op jit(solution)/shard_map/ppermute | solution.py:543

commit v14 on v13

--- a/solution.py
+++ b/solution.py
@@ -241,7 +241,7 @@
     if g + 1 < KV:
         take(1)
     old_sums_ref = take(1)[0] if g else None
-    old_send = take(shards - 1) if g else []
+    old_send = take(shards - 1) if 0 < g < KV - 1 else []
     if 0 < g < KV - 1:
         take(2)
     out_ref, gq_ref, sums_ref, own_ref = take(4)
@@ -388,12 +388,12 @@
     gk = turn_back(dk, cos_ref[...], sin_ref[...])
     own_ref[0] = dk[:tokens]
     own_ref[1] = dv[:tokens]
-    at = 2 * g
+    at = 2 * g if g < KV - 1 else 0
     for j in range(1, shards):
         block = slice(j * tokens, (j + 1) * tokens)
         send[j - 1][at] = dk[block].astype(B16)
         send[j - 1][at + 1] = dv[block].astype(B16)
-        if g:
+        if at:
             send[j - 1][pl.ds(0, at)] = old_send[j - 1][...]
     sums_ref[pl.ds(HQ + g, 1), :] = jnp.sum(gk, axis=0, keepdims=True)
     sums_ref[pl.ds(HQ + KV + g, 1), :] = jnp.sum(dv, axis=0, keepdims=True)
@@ -410,16 +410,16 @@
     anywhere = pl.BlockSpec(memory_space=pl.ANY)
     wide = pl.BlockSpec((tokens, GROUP * HD), lambda i: (0, g))
 
+    last = g == KV - 1
     args = [first, rank]
     placed = [*prepared, cosine, sine, ck, cv, kp, vp, *far]
     placed += [*ahead[g], *[x[2] for x in ahead[g + 1:g + 2]]]
     aliases = {}
     if before is not None:
         out, gq, sums, send = before
-        placed += [sums, *send]
+        placed += [sums, *([] if last else send)]
     args += placed
     in_specs = [smem] * 2 + [vmem] * len(placed)
-    last = g == KV - 1
     if before is not None and not last:
         aliases = {len(args): 0, len(args) + 1: 1}
         args += [out, gq]
@@ -431,7 +431,7 @@
         pltpu.VMEM((2, tokens, HD), F32),
     ]
     out_specs = [vmem if last else wide] * 2 + [vmem, vmem]
-    out_shape += [pltpu.VMEM((2 * g + 2, tokens, HD), B16)] * (shards - 1)
+    out_shape += [pltpu.VMEM((2 if last else 2 * g + 2, tokens, HD), B16)] * (shards - 1)
     out_specs += [vmem] * (shards - 1)
     if g + 2 < KV:
         out_shape.append(pltpu.VMEM((2 * (slots + tokens), HD), B16))
@@ -463,46 +463,44 @@
     return (out, gq, sums, send), own, results[4 + shards - 1:]
 
 
+def place_kernel(out_part, gq_part, _, __, out_ref, gq_ref):
+    out_ref[...] = out_part[...]
+    gq_ref[...] = gq_part[...]
+
+
+def place(parts, out, gq):
+    wide = pl.BlockSpec((out.shape[0], GROUP * HD), lambda i: (0, KV - 1))
+    return pl.pallas_call(
+        place_kernel,
+        grid=(1,),
+        in_specs=[pl.BlockSpec(memory_space=pltpu.VMEM)] * 2
+        + [pl.BlockSpec(memory_space=pl.ANY)] * 2,
+        out_specs=[wide, wide],
+        out_shape=[pltpu.HBM(out.shape, B16)] * 2,
+        input_output_aliases={2: 0, 3: 1},
+        compiler_params=params(),
+        cost_estimate=pl.CostEstimate(flops=0, bytes_accessed=1 << 21, transcendentals=0),
+        name="place",
+    )(*parts, out, gq)
+
+
 def finish_kernel(shards, *refs):
     cos_ref, sin_ref, *refs = refs
     owns, refs = refs[:KV], refs[KV:]
-    backs, refs = refs[:shards - 1], refs[shards - 1:]
-    out_part, gq_part, _, _, out_ref, gq_ref, gk_ref, gv_ref = refs
-    out_ref[...] = out_part[...]
-    gq_ref[...] = gq_part[...]
+    early, late = refs[:shards - 1], refs[shards - 1:2 * (shards - 1)]
+    sums = refs[2 * (shards - 1):-6]
+    gk_ref, gv_ref, *parts = refs[-5:]
     tokens = gk_ref.shape[0]
     cosine, sine = cos_ref[pl.ds(0, tokens), :], sin_ref[pl.ds(0, tokens), :]
     for g in range(KV):
         dk, dv = owns[g][0], owns[g][1]
-        for back in backs:
-            dk = dk + back[2 * g].astype(F32)
-            dv = dv + back[2 * g + 1].astype(F32)
+        last = g == KV - 1
+        for back in late if last else early:
+            dk = dk + back[0 if last else 2 * g].astype(F32)
+            dv = dv + back[1 if last else 2 * g + 1].astype(F32)
         cols = pl.ds(g * HD, HD)
         gk_ref[:, cols] = turn_back(dk, cosine, sine).astype(B16)
         gv_ref[:, cols] = dv.astype(B16)
-
-
-def finish(shards, cosine, sine, owns, backs, parts, out, gq):
-    tokens = out.shape[0]
-    args = [cosine, sine, *owns, *backs, *parts]
-    wide = pl.BlockSpec((tokens, GROUP * HD), lambda i: (0, KV - 1))
-    narrow = (tokens, KV * HD)
-    return pl.pallas_call(
-        functools.partial(finish_kernel, shards),
-        grid=(1,),
-        in_specs=[pl.BlockSpec(memory_space=pltpu.VMEM)] * len(args)
-        + [pl.BlockSpec(memory_space=pl.ANY)] * 2,
-        out_specs=[wide, wide, whole(narrow), whole(narrow)],
-        out_shape=[pltpu.HBM(out.shape, B16)] * 2 + [pltpu.HBM(narrow, B16)] * 2,
-        input_output_aliases={len(args): 0, len(args) + 1: 1},
-        compiler_params=params(),
-        cost_estimate=pl.CostEstimate(flops=0, bytes_accessed=1 << 21, transcendentals=0),
-        name="finish",
-    )(*args, out, gq)
-
-
-def sums_kernel(*refs):
-    sums, parts = refs[:-4], refs[-3:]
     start = 0
     for part in parts:
         rows = pl.ds(start, part.shape[0])
@@ -510,19 +508,39 @@
         start += part.shape[0]
 
 
-def last_sums(sums, after):
-    shapes = [(rows, HD) for rows in (HQ, KV, KV)]
+def finish(shards, cosine, sine, owns, early, late, sums, after):
+    tokens = owns[0].shape[1]
+    args = [cosine, sine, *owns, *early, *late, *sums]
+    shapes = [((tokens, KV * HD), B16)] * 2 + [((rows, HD), F32) for rows in (HQ, KV, KV)]
     return pl.pallas_call(
-        sums_kernel,
+        functools.partial(finish_kernel, shards),
         grid=(1,),
-        in_specs=[pl.BlockSpec(memory_space=pltpu.VMEM)] * len(sums)
+        in_specs=[pl.BlockSpec(memory_space=pltpu.VMEM)] * len(args)
         + [pl.BlockSpec(memory_space=pl.ANY)],
-        out_specs=[whole(shape) for shape in shapes],
-        out_shape=[pltpu.HBM(shape, F32) for shape in shapes],
+        out_specs=[whole(shape) for shape, _ in shapes],
+        out_shape=[pltpu.HBM(shape, kind) for shape, kind in shapes],
         compiler_params=params(),
-        cost_estimate=pl.CostEstimate(flops=0, bytes_accessed=1 << 17, transcendentals=0),
-        name="sums",
-    )(*sums, after)
+        cost_estimate=pl.CostEstimate(flops=0, bytes_accessed=1 << 19, transcendentals=0),
+        name="finish",
+    )(*args, after)
+
+
+def join_kernel(a_ref, b_ref, *refs):
+    refs[-1][...] = a_ref[...] + b_ref[...]
+
+
+def join(parts, held):
+    args = [*parts, *held]
+    return pl.pallas_call(
+        join_kernel,
+        grid=(1,),
+        in_specs=[pl.BlockSpec(memory_space=pltpu.VMEM)] * len(args),
+        out_specs=pl.BlockSpec(memory_space=pltpu.VMEM),
+        out_shape=pltpu.VMEM(parts[0].shape, parts[0].dtype),
+        compiler_params=params(),
+        cost_estimate=pl.CostEstimate(flops=0, bytes_accessed=1 << 16, transcendentals=0),
+        name="join",
+    )(*args)
 
 
 def add_up(parts):
@@ -531,13 +549,13 @@
     return parts[0]
 
 
-def sum_but_last(x, axes, near):
+def sum_but_last(x, axes, near, held):
     devices = lax.axis_size(axes)
     bits = [1 << i for i in reversed(range(devices.bit_length() - 1)) if 1 << i != near]
     stages = [[near]] + [bits[i:i + 2] for i in range(0, len(bits), 2)]
     parts = [x]
-    for stage in stages:
-        x = add_up(parts)
+    for i, stage in enumerate(stages):
+        x = join(parts, held) if i == 1 else add_up(parts)
         parts = [x]
         for flip in [sum(c) for n in (1, 2) for c in itertools.combinations(stage, n)]:
             parts.append(lax.ppermute(x, axes, [(i, i ^ flip) for i in range(devices)]))
@@ -591,13 +609,14 @@
         )
         if g == KV - 2:
             out, gq = before[:2]
+            early = [earlier(x, s) for s, x in zip(shifts, before[3])]
         owns.append(own)
         far += [[ring(chunk, s) for s in shifts] for chunk in more]
     *columns, sums, send = before
-    backs = [earlier(x, s) for s, x in zip(shifts, send)]
-    sums = sum_but_last(sums, ("dp", "seq"), shards)
-    out, gq, gk, gv = finish(shards, cosine, sine, owns, backs, columns, out, gq)
-    sums = last_sums(sums, hbm(gk))
+    late = [earlier(x, s) for s, x in zip(shifts, send)]
+    sums = sum_but_last(sums, ("dp", "seq"), shards, early)
+    out, gq = place(columns, out, gq)
+    gk, gv, *sums = finish(shards, cosine, sine, owns, early, late, sums, hbm(out))
     return (out[None], gq[None], gk[None], gv[None], *[x.reshape(-1) for x in sums])
 
 

time: 55.7 us -> 57.3 us (1.029)
  starting transfers between devices: 16.5 us -> 18 us
    ppermute x7, waiting for transfers between devices: 5.67 us -> 7.62 us  [sum_but_last(): parts.append(lax.ppermute(x, axes, [(i, i ^ flip) for i in range(devices)]))]
    ppermute x4, waiting for transfers between devices: 3.22 us -> 1.68 us  [ring(): lax.ppermute(x, 'seq', [(i, (i + s) % shards) for i in range(shards)])]
    ppermute x1 -> x2, starting transfers between devices: 1.28 us -> 2.56 us  [earlier(): return lax.ppermute(x, 'seq', [(i + s, i) for i in range(shards - s)])]
    ppermute x1 -> x2, waiting for transfers between devices: 2 us -> 1.58 us  [earlier(): return lax.ppermute(x, 'seq', [(i + s, i) for i in range(shards - s)])]
  transfers between devices with their start and end apart: 12 -> 13, of which waited for: 8 -> 10; matrix products, arithmetic and copies ran while one was open for 1% -> 1% of each run, Pallas kernels for 38% -> 43%
where the time goes in v14:
time: 57.3 us; the launch traced here: 57 us
  Pallas kernels  26.1 us (46%)
  starting transfers between devices  18 us (31%)
  waiting for transfers between devices  10.9 us (19%)
  between operations  1.38 us (2%)
  other arithmetic  0.64 us (1%)
    pallas_call x4, Pallas kernels, attend(): pl.pallas_call(functools.partial(attend_kernel, g, shards), grid=(1,), in...  15.9 us
    ppermute x7, starting transfers between devices, sum_but_last(): parts.append(lax.ppermute(x, axes, [(i, i ^ flip) for i in range(devices)]))  8.04 us
    ppermute x7, waiting for transfers between devices, sum_but_last(): parts.append(lax.ppermute(x, axes, [(i, i ^ flip) for i in range(devices)]))  7.62 us
    ppermute x4, starting transfers between devices, ring(): lax.ppermute(x, 'seq', [(i, (i + s) % shards) for i in range(shards)])  7.42 us
    pallas_call x1, Pallas kernels, prep(): pl.pallas_call(prep_kernel, grid=(KV,), in_specs=[wide, wide, pl.BlockSpe...  4.2 us
    pallas_call x4, Pallas kernels, look_ahead(): pl.pallas_call(functools.partial(ahead_kernel, g, shards), grid=(1,), in_...  3.4 us
    ppermute x2, starting transfers between devices, earlier(): return lax.ppermute(x, 'seq', [(i + s, i) for i in range(shards - s)])  2.56 us
    ppermute x4, waiting for transfers between devices, ring(): lax.ppermute(x, 'seq', [(i, (i + s) % shards) for i in range(shards)])  1.68 us
  transfers between devices with their start and end apart: 13, of which 10 were waited for; matrix products, arithmetic and copies ran while one was open for 1% of the time, Pallas kernels for 43%

profile of v14, /device:TPU:0, one launch (start us, length us, event | category | flops | bytes accessed | tf_op | source)
XLA Modules:
  0.0 57.0 jit_solution(10629644153265288846)
XLA Ops:
  0.6 1.0 %pack.1 = bf16[1280,128]{1,0:T(8,128)(2,1)S(1)} custom-call(bf16[512,512]{1,0:T(8,128)(2,1)} %bitcast.23, bf16[512,512]{1,0:T(8,128)(2,1)} %bitcast.25, bf16[128,512]{1,0:T(8,128)(2,1)} %bitcast.29, bf16[128,512]{1,0:T(8,128)(2,1)} %bitcast.31), custom_call_target="tpu_custom_call" | custom-call | bytes 655360 | tf_op jit(solution)/shard_map/pack/pallas_call | solution.py:60
  1.6 3.0 %collective-permute-start.1 = (bf16[1280,128]{1,0:T(8,128)(2,1)S(1)}, bf16[1280,128]{1,0:T(8,128)(2,1)S(1)}, u32[]{:S(2)}, u32[]{:S(2)}) collective-permute-start(bf16[1280,128]{1,0:T(8,128)(2,1)S(1)} %pack.1), channel_id=1, source_target_pairs={{0,1},{1,0},{2,3},{3,2},{4,5},{5,4},{6,7},{7,6},{8,9},{9,8},{10,11... | collective-permute-start | bytes 983048 | tf_op jit(solution)/shard_map/ppermute | solution.py:572
  5.4 0.1 convert_bitcast_fusion
  5.4 0.5 fusion
  6.0 4.2 %prep.1 = (bf16[4096,128]{1,0:T(8,128)(2,1)S(1)}, bf16[1024,512]{1,0:T(8,128)(2,1)S(1)}, bf16[4096,128]{1,0:T(8,128)(2,1)S(1)}, bf16[1024,512]{1,0:T(8,128)(2,1)...) custom-call(bf16[128,4096]{1,0:T(8,128)(2,1)} %bitcast.27, ...), custom_call_target="tpu_custom_call" | custom-call | flops 2097152 | bytes 6291456 | tf_op jit(solution)/shard_map/prep/pallas_call | solution.py:133
  10.2 0.1 collective-permute-start
  10.3 0.8 %ahead.4 = (f32[2,640,512]{2,1,0:T(8,128)S(1)}, f32[2,640,512]{2,1,0:T(8,128)S(1)}, f32[2,8,512]{2,1,0:T(8,128)S(1)}) custom-call(s32[1]{0:T(128)} %copy.29.first_ref.refs_0_, s32[1]{0:T(128)} %bitcast.rank_ref.refs_1_, bf16[1024,512]{1,0:T(8,128)(2,1)S(1)} %get-tuple-element.63.qst_ref.refs_3_, bf16[1024,512]{1,0:T(8,128)(2,1)S(1)} %get-tuple-element.65.dot_ref.refs_5_, ...), custom_call_target="tpu_custom_call" | custom-call | flops 335544320 | bytes 5242880 | tf_op jit(solution)/shard_map/ahead/pallas_call | solution.py:209
  11.1 0.9 %ahead.6 = (f32[2,640,512]{2,1,0:T(8,128)S(1)}, f32[2,640,512]{2,1,0:T(8,128)S(1)}, f32[2,8,512]{2,1,0:T(8,128)S(1)}) custom-call(s32[1]{0:T(128)} %copy.29.first_ref.refs_0_, s32[1]{0:T(128)} %bitcast.rank_ref.refs_1_, bf16[1024,512]{1,0:T(8,128)(2,1)S(1)} %get-tuple-element.63.qst_ref.refs_3_, bf16[1024,512]{1,0:T(8,128)(2,1)S(1)} %get-tuple-element.65.dot_ref.refs_5_, ...), custom_call_target="tpu_custom_call" | custom-call | flops 335544320 | bytes 5242880 | tf_op jit(solution)/shard_map/ahead/pallas_call | solution.py:209
  12.0 0.8 %collective-permute-done.1.refs_17_ = bf16[1280,128]{1,0:T(8,128)(2,1)S(1)} collective-permute-done((bf16[1280,128]{1,0:T(8,128)(2,1)S(1)}, bf16[1280,128]{1,0:T(8,128)(2,1)S(1)}, u32[]{:S(2)}, u32[]{:S(2)}) %collective-permute-start.1) | collective-permute-done | bytes 327712 | tf_op jit(solution)/shard_map/ppermute | solution.py:572
  12.8 4.2 %attend.4 = (bf16[128,4096]{1,0:T(8,128)(2,1)}, bf16[128,4096]{1,0:T(8,128)(2,1)}, f32[40,128]{1,0:T(8,128)S(1)}, f32[2,128,128]{2,1,0:T(8,128)S(1)}, bf16[2,128...) custom-call(s32[1]{0:T(128)} %copy.29.first_ref.refs_0_, s32[1]{0:T(128)} %bitcast.rank_ref.refs_1_, ...), custom_call_target="tpu_custom_call" | custom-call | flops 1476395008 | bytes 2359296 | tf_op jit(solution)/shard_map/attend/pallas_call | solution.py:439
  16.9 2.5 %collective-permute-start.3 = (bf16[1280,128]{1,0:T(8,128)(2,1)S(1)}, bf16[1280,128]{1,0:T(8,128)(2,1)S(1)}, u32[]{:S(2)}, u32[]{:S(2)}) collective-permute-start(bf16[1280,128]{1,0:T(8,128)(2,1)S(1)} %get-tuple-element.91), channel_id=1, source_target_pairs={{0,1},{1,0},{2,3},{3,2},{4,5},{5,4},{6,7},{7,6},{8,9},{9,8},{10,11... | collective-permute-start | bytes 983048 | tf_op jit(solution)/shard_map/ppermute | solution.py:572
  19.4 0.8 %ahead.5 = (f32[2,640,512]{2,1,0:T(8,128)S(1)}, f32[2,640,512]{2,1,0:T(8,128)S(1)}, f32[2,8,512]{2,1,0:T(8,128)S(1)}) custom-call(s32[1]{0:T(128)} %copy.29.first_ref.refs_0_, s32[1]{0:T(128)} %bitcast.rank_ref.refs_1_, bf16[1024,512]{1,0:T(8,128)(2,1)S(1)} %get-tuple-element.63.qst_ref.refs_3_, bf16[1024,512]{1,0:T(8,128)(2,1)S(1)} %get-tuple-element.65.dot_ref.refs_5_, ...), custom_call_target="tpu_custom_call" | custom-call | flops 335544320 | bytes 5242880 | tf_op jit(solution)/shard_map/ahead/pallas_call | solution.py:209
  20.3 0.1 collective-permute-done.refs_17_
  20.3 4.1 %attend.5 = (bf16[128,4096]{1,0:T(8,128)(2,1)}, bf16[128,4096]{1,0:T(8,128)(2,1)}, f32[40,128]{1,0:T(8,128)S(1)}, f32[2,128,128]{2,1,0:T(8,128)S(1)}, bf16[4,128...) custom-call(s32[1]{0:T(128)} %copy.29.first_ref.refs_0_, ...), custom_call_target="tpu_custom_call", output_to_operand_aliasing={{0}: (24, {}), {1}: (25, {})} | custom-call | flops 1476395008 | bytes 2359296 | tf_op jit(solution)/shard_map/attend/pallas_call | solution.py:439
  24.4 1.8 %collective-permute-start.2 = (bf16[1280,128]{1,0:T(8,128)(2,1)S(1)}, bf16[1280,128]{1,0:T(8,128)(2,1)S(1)}, u32[]{:S(2)}, u32[]{:S(2)}) collective-permute-start(bf16[1280,128]{1,0:T(8,128)(2,1)S(1)} %get-tuple-element.87), channel_id=1, source_target_pairs={{0,1},{1,0},{2,3},{3,2},{4,5},{5,4},{6,7},{7,6},{8,9},{9,8},{10,11... | collective-permute-start | bytes 983048 | tf_op jit(solution)/shard_map/ppermute | solution.py:572
  26.2 0.8 %ahead.7 = (f32[2,640,512]{2,1,0:T(8,128)S(1)}, f32[2,640,512]{2,1,0:T(8,128)S(1)}, f32[2,8,512]{2,1,0:T(8,128)S(1)}) custom-call(s32[1]{0:T(128)} %copy.29.first_ref.refs_0_, s32[1]{0:T(128)} %bitcast.rank_ref.refs_1_, bf16[1024,512]{1,0:T(8,128)(2,1)S(1)} %get-tuple-element.63.qst_ref.refs_3_, bf16[1024,512]{1,0:T(8,128)(2,1)S(1)} %get-tuple-element.65.dot_ref.refs_5_, ...), custom_call_target="tpu_custom_call" | custom-call | flops 335544320 | bytes 5242880 | tf_op jit(solution)/shard_map/ahead/pallas_call | solution.py:209
  27.1 0.7 %collective-permute-done.3.refs_17_ = bf16[1280,128]{1,0:T(8,128)(2,1)S(1)} collective-permute-done((bf16[1280,128]{1,0:T(8,128)(2,1)S(1)}, bf16[1280,128]{1,0:T(8,128)(2,1)S(1)}, u32[]{:S(2)}, u32[]{:S(2)}) %collective-permute-start.3) | collective-permute-done | bytes 327712 | tf_op jit(solution)/shard_map/ppermute | solution.py:572
  27.8 4.3 %attend.6 = (bf16[128,4096]{1,0:T(8,128)(2,1)}, bf16[128,4096]{1,0:T(8,128)(2,1)}, f32[40,128]{1,0:T(8,128)S(1)}, f32[2,128,128]{2,1,0:T(8,128)S(1)}, bf16[6,128,128]{2,1,0:T(8,128)(2,1)S(1)}) custom-call(s32[1]{0:T(128)} %copy.29.first_ref.refs_0_, s32[1]{0:T(128)} %bitcast.rank_ref.refs_1_, ...), custom_call_target="tpu_custom_call", output_to_operand_aliasing={{0}: (24, {}), {1}: (25, {})} | custom-call | flops 1476395008 | bytes 2359296 | tf_op jit(solution)/shard_map/attend/pallas_call | solution.py:439
  32.1 1.3 %collective-permute-start.4 = (bf16[6,128,128]{2,1,0:T(8,128)(2,1)S(1)}, bf16[6,128,128]{2,1,0:T(8,128)(2,1)S(1)}, u32[]{:S(2)}, u32[]{:S(2)}) collective-permute-start(bf16[6,128,128]{2,1,0:T(8,128)(2,1)S(1)} %get-tuple-element.109), channel_id=1, source_target_pairs={{1,0},{3,2},{5,4},{7,6},{9,8},{11,10},{13,12},{15,14},{17,16},{19,... | collective-permute-start | bytes 589832 | tf_op jit(solution)/shard_map/ppermute | solution.py:575
  33.4 0.1 collective-permute-done.2.refs_17_
  33.5 3.4 %attend.7 = (bf16[128,1024]{1,0:T(8,128)(2,1)S(1)}, bf16[128,1024]{1,0:T(8,128)(2,1)S(1)}, f32[40,128]{1,0:T(8,128)S(1)}, f32[2,128,128]{2,1,0:T(8,128)S(1)}, bf16[2,128,128]{2,1,0:T(8,128)(2,1)S(1)}) custom-call(s32[1]{0:T(128)} %copy.29.first_ref.refs_0_, s32[1]{0:T(128)} %bitcast.rank_ref.refs_1_, bf16[4096,128]{1,0:T(8,128)(2,1)S(1)} %get-tuple-element.62.refs_2_, ...), custom_call_target="tpu_custom_call" | custom-call | flops 1476395008 | bytes 2359296 | tf_op jit(solution)/shard_map/attend/pallas_call | solution.py:439
  36.8 0.1 collective-permute-start.6
  36.9 1.2 %collective-permute-done.6.b_ref = f32[40,128]{1,0:T(8,128)S(1)} collective-permute-done((f32[40,128]{1,0:T(8,128)S(1)}, f32[40,128]{1,0:T(8,128)S(1)}, u32[]{:S(2)}, u32[]{:S(2)}) %collective-permute-start.6) | collective-permute-done | bytes 20512 | tf_op jit(solution)/shard_map/ppermute | solution.py:561
  38.1 1.6 %collective-permute-done.4.refs_0_.refs_6_ = bf16[6,128,128]{2,1,0:T(8,128)(2,1)S(1)} collective-permute-done((bf16[6,128,128]{2,1,0:T(8,128)(2,1)S(1)}, bf16[6,128,128]{2,1,0:T(8,128)(2,1)S(1)}, u32[]{:S(2)}, u32[]{:S(2)}) %collective-permute-start.4) | collective-permute-done | bytes 196640 | tf_op jit(solution)/shard_map/ppermute | solution.py:575
  39.7 1.8 %collective-permute-start.8 = (f32[40,128]{1,0:T(8,128)S(1)}, f32[40,128]{1,0:T(8,128)S(1)}, u32[]{:S(2)}, u32[]{:S(2)}) collective-permute-start(f32[40,128]{1,0:T(8,128)S(1)} %join.1), channel_id=1, source_target_pairs={{0,8},{1,9},{2,10},{3,11},{4,12},{5,13},{6,14},{7,15},{8,0},{9,1},... | collective-permute-start | bytes 61448 | tf_op jit(solution)/shard_map/ppermute | solution.py:561
  41.5 2.5 %collective-permute-start.9 = (f32[40,128]{1,0:T(8,128)S(1)}, f32[40,128]{1,0:T(8,128)S(1)}, u32[]{:S(2)}, u32[]{:S(2)}) collective-permute-start(f32[40,128]{1,0:T(8,128)S(1)} %join.1), channel_id=1, source_target_pairs={{0,24},{1,25},{2,26},{3,27},{4,28},{5,29},{6,30},{7,31},{8,16},{9,... | collective-permute-start | bytes 61448 | tf_op jit(solution)/shard_map/ppermute | solution.py:561
  44.0 0.1 collective-permute-start.7
  44.1 1.3 %collective-permute-start.5 = (bf16[2,128,128]{2,1,0:T(8,128)(2,1)S(1)}, bf16[2,128,128]{2,1,0:T(8,128)(2,1)S(1)}, u32[]{:S(2)}, u32[]{:S(2)}) collective-permute-start(bf16[2,128,128]{2,1,0:T(8,128)(2,1)S(1)} %get-tuple-element.110), channel_id=1, source_target_pairs={{1,0},{3,2},{5,4},{7,6},{9,8},{11,10},{13,12},{15,14},{17,16},{19,... | collective-permute-start | bytes 196616 | tf_op jit(solution)/shard_map/ppermute | solution.py:575
  45.4 0.0 collective-permute-done.8
  45.4 1.7 %collective-permute-done.9 = f32[40,128]{1,0:T(8,128)S(1)} collective-permute-done((f32[40,128]{1,0:T(8,128)S(1)}, f32[40,128]{1,0:T(8,128)S(1)}, u32[]{:S(2)}, u32[]{:S(2)}) %collective-permute-start.9) | collective-permute-done | bytes 20512 | tf_op jit(solution)/shard_map/ppermute | solution.py:561
  47.1 1.8 %collective-permute-done.7 = f32[40,128]{1,0:T(8,128)S(1)} collective-permute-done((f32[40,128]{1,0:T(8,128)S(1)}, f32[40,128]{1,0:T(8,128)S(1)}, u32[]{:S(2)}, u32[]{:S(2)}) %collective-permute-start.7) | collective-permute-done | bytes 20512 | tf_op jit(solution)/shard_map/ppermute | solution.py:561
  48.9 1.5 %collective-permute-start.10 = (f32[40,128]{1,0:T(8,128)S(1)}, f32[40,128]{1,0:T(8,128)S(1)}, u32[]{:S(2)}, u32[]{:S(2)}) collective-permute-start(f32[40,128]{1,0:T(8,128)S(1)} %add_add_fusion.refs_8_), channel_id=1, source_target_pairs={{0,4},{1,5},{2,6},{3,7},{4,0},{5,1},{6,2},{7,3},{8,12},{9,13},{10,... | collective-permute-start | bytes 61448 | tf_op jit(solution)/shard_map/ppermute | solution.py:561
  50.4 1.1 %collective-permute-start.11 = (f32[40,128]{1,0:T(8,128)S(1)}, f32[40,128]{1,0:T(8,128)S(1)}, u32[]{:S(2)}, u32[]{:S(2)}) collective-permute-start(f32[40,128]{1,0:T(8,128)S(1)} %add_add_fusion.refs_8_), channel_id=1, source_target_pairs={{0,1},{1,0},{2,3},{3,2},{4,5},{5,4},{6,7},{7,6},{8,9},{9,8},{10,11... | collective-permute-start | bytes 61448 | tf_op jit(solution)/shard_map/ppermute | solution.py:561
  51.5 0.9 %collective-permute-start.12 = (f32[40,128]{1,0:T(8,128)S(1)}, f32[40,128]{1,0:T(8,128)S(1)}, u32[]{:S(2)}, u32[]{:S(2)}) collective-permute-start(f32[40,128]{1,0:T(8,128)S(1)} %add_add_fusion.refs_8_), channel_id=1, source_target_pairs={{0,5},{1,4},{2,7},{3,6},{4,1},{5,0},{6,3},{7,2},{8,13},{9,12},{10,... | collective-permute-start | bytes 61448 | tf_op jit(solution)/shard_map/ppermute | solution.py:561
  52.4 0.8 %place.1 = (bf16[128,4096]{1,0:T(8,128)(2,1)}, bf16[128,4096]{1,0:T(8,128)(2,1)}) custom-call(bf16[128,1024]{1,0:T(8,128)(2,1)S(1)} %get-tuple-element.99.out_part, bf16[128,1024]{1,0:T(8,128)(2,1)S(1)} %get-tuple-element.100.gq_part, bf16[128,4096]{1,0:T(8,128)(2,1)} %get-tuple-element.101._, ...), custom_call_target="tpu_custom_call", output_to_operand_aliasing={{0}: (2, {}), {1}: (3, {})} | custom-call | bytes 2097152 | tf_op jit(solution)/shard_map/place/pallas_call | solution.py:473
  53.2 0.0 collective-permute-done.5.refs_7_
  53.3 0.0 collective-permute-done.10.refs_9_
  53.3 1.0 %collective-permute-done.11.refs_10_ = f32[40,128]{1,0:T(8,128)S(1)} collective-permute-done((f32[40,128]{1,0:T(8,128)S(1)}, f32[40,128]{1,0:T(8,128)S(1)}, u32[]{:S(2)}, u32[]{:S(2)}) %collective-permute-start.11) | collective-permute-done | bytes 20512 | tf_op jit(solution)/shard_map/ppermute | solution.py:561
  54.2 2.0 %collective-permute-done.12.refs_11_ = f32[40,128]{1,0:T(8,128)S(1)} collective-permute-done((f32[40,128]{1,0:T(8,128)S(1)}, f32[40,128]{1,0:T(8,128)S(1)}, u32[]{:S(2)}, u32[]{:S(2)}) %collective-permute-start.12) | collective-permute-done | bytes 20512 | tf_op jit(solution)/shard_map/ppermute | solution.py:561
  56.2 0.8 %finish.1 = (bf16[128,512]{1,0:T(8,128)(2,1)}, bf16[128,512]{1,0:T(8,128)(2,1)}, f32[32,128]{1,0:T(8,128)}, f32[4,128]{1,0:T(4,128)}, f32[4,128]{1,0:T(4,128)}) custom-call(f32[256,128]{1,0:T(8,128)S(1)} %get-tuple-element.118.cos_ref.refs_11_.refs_0_, f32[256,128]{1,0:T(8,128)S(1)} %get-tuple-element.117.sin_ref.refs_12_.refs_1_, ...), custom_call_target="tpu_custom_call" | custom-call | bytes 524288 | tf_op jit(solution)/shard_map/finish/pallas_call | solution.py:515
  (4 shorter events, 0.0 us)
Async XLA Ops:
  1.6 11.1 %collective-permute-start.1 = (bf16[1280,128]{1,0:T(8,128)(2,1)S(1)}, bf16[1280,128]{1,0:T(8,128)(2,1)S(1)}, u32[]{:S(2)}, u32[]{:S(2)}) collective-permute-start(bf16[1280,128]{1,0:T(8,128)(2,1)S(1)} %pack.1), channel_id=1, source_target_pairs={{0,1},{1,0},{2,3},{3,2},{4,5},{5,4},{6,7},{7,6},{8,9},{9,8},{10,11... | collective-permute-start | bytes 983048 | tf_op jit(solution)/shard_map/ppermute | solution.py:572
  10.2 10.2 %collective-permute-start = (bf16[1280,128]{1,0:T(8,128)(2,1)S(1)}, bf16[1280,128]{1,0:T(8,128)(2,1)S(1)}, u32[]{:S(2)}, u32[]{:S(2)}) collective-permute-start(bf16[1280,128]{1,0:T(8,128)(2,1)S(1)} %get-tuple-element.75), channel_id=1, source_target_pairs={{0,1},{1,0},{2,3},{3,2},{4,5},{5,4},{6,7},{7,6},{8,9},{9,8},{10,11... | collective-permute-start | bytes 983048 | tf_op jit(solution)/shard_map/ppermute | solution.py:572
  16.9 10.9 %collective-permute-start.3 = (bf16[1280,128]{1,0:T(8,128)(2,1)S(1)}, bf16[1280,128]{1,0:T(8,128)(2,1)S(1)}, u32[]{:S(2)}, u32[]{:S(2)}) collective-permute-start(bf16[1280,128]{1,0:T(8,128)(2,1)S(1)} %get-tuple-element.91), channel_id=1, source_target_pairs={{0,1},{1,0},{2,3},{3,2},{4,5},{5,4},{6,7},{7,6},{8,9},{9,8},{10,11... | collective-permute-start | bytes 983048 | tf_op jit(solution)/shard_map/ppermute | solution.py:572
  24.4 9.1 %collective-permute-start.2 = (bf16[1280,128]{1,0:T(8,128)(2,1)S(1)}, bf16[1280,128]{1,0:T(8,128)(2,1)S(1)}, u32[]{:S(2)}, u32[]{:S(2)}) collective-permute-start(bf16[1280,128]{1,0:T(8,128)(2,1)S(1)} %get-tuple-element.87), channel_id=1, source_target_pairs={{0,1},{1,0},{2,3},{3,2},{4,5},{5,4},{6,7},{7,6},{8,9},{9,8},{10,11... | collective-permute-start | bytes 983048 | tf_op jit(solution)/shard_map/ppermute | solution.py:572
  32.1 7.6 %collective-permute-start.4 = (bf16[6,128,128]{2,1,0:T(8,128)(2,1)S(1)}, bf16[6,128,128]{2,1,0:T(8,128)(2,1)S(1)}, u32[]{:S(2)}, u32[]{:S(2)}) collective-permute-start(bf16[6,128,128]{2,1,0:T(8,128)(2,1)S(1)} %get-tuple-element.109), channel_id=1, source_target_pairs={{1,0},{3,2},{5,4},{7,6},{9,8},{11,10},{13,12},{15,14},{17,16},{19,... | collective-permute-start | bytes 589832 | tf_op jit(solution)/shard_map/ppermute | solution.py:575
  36.8 1.3 %collective-permute-start.6 = (f32[40,128]{1,0:T(8,128)S(1)}, f32[40,128]{1,0:T(8,128)S(1)}, u32[]{:S(2)}, u32[]{:S(2)}) collective-permute-start(f32[40,128]{1,0:T(8,128)S(1)} %get-tuple-element.111.a_ref), channel_id=1, source_target_pairs={{0,2},{1,3},{2,0},{3,1},{4,6},{5,7},{6,4},{7,5},{8,10},{9,11},{10,... | collective-permute-start | bytes 61448 | tf_op jit(solution)/shard_map/ppermute | solution.py:561
  39.7 5.7 %collective-permute-start.8 = (f32[40,128]{1,0:T(8,128)S(1)}, f32[40,128]{1,0:T(8,128)S(1)}, u32[]{:S(2)}, u32[]{:S(2)}) collective-permute-start(f32[40,128]{1,0:T(8,128)S(1)} %join.1), channel_id=1, source_target_pairs={{0,8},{1,9},{2,10},{3,11},{4,12},{5,13},{6,14},{7,15},{8,0},{9,1},... | collective-permute-start | bytes 61448 | tf_op jit(solution)/shard_map/ppermute | solution.py:561
  41.5 5.6 %collective-permute-start.9 = (f32[40,128]{1,0:T(8,128)S(1)}, f32[40,128]{1,0:T(8,128)S(1)}, u32[]{:S(2)}, u32[]{:S(2)}) collective-permute-start(f32[40,128]{1,0:T(8,128)S(1)} %join.1), channel_id=1, source_target_pairs={{0,24},{1,25},{2,26},{3,27},{4,28},{5,29},{6,30},{7,31},{8,16},{9,... | collective-permute-start | bytes 61448 | tf_op jit(solution)/shard_map/ppermute | solution.py:561
  44.0 4.9 %collective-permute-start.7 = (f32[40,128]{1,0:T(8,128)S(1)}, f32[40,128]{1,0:T(8,128)S(1)}, u32[]{:S(2)}, u32[]{:S(2)}) collective-permute-start(f32[40,128]{1,0:T(8,128)S(1)} %join.1), channel_id=1, source_target_pairs={{0,16},{1,17},{2,18},{3,19},{4,20},{5,21},{6,22},{7,23},{8,24},{9,... | collective-permute-start | bytes 61448 | tf_op jit(solution)/shard_map/ppermute | solution.py:561
  44.1 9.2 %collective-permute-start.5 = (bf16[2,128,128]{2,1,0:T(8,128)(2,1)S(1)}, bf16[2,128,128]{2,1,0:T(8,128)(2,1)S(1)}, u32[]{:S(2)}, u32[]{:S(2)}) collective-permute-start(bf16[2,128,128]{2,1,0:T(8,128)(2,1)S(1)} %get-tuple-element.110), channel_id=1, source_target_pairs={{1,0},{3,2},{5,4},{7,6},{9,8},{11,10},{13,12},{15,14},{17,16},{19,... | collective-permute-start | bytes 196616 | tf_op jit(solution)/shard_map/ppermute | solution.py:575
  48.9 4.4 %collective-permute-start.10 = (f32[40,128]{1,0:T(8,128)S(1)}, f32[40,128]{1,0:T(8,128)S(1)}, u32[]{:S(2)}, u32[]{:S(2)}) collective-permute-start(f32[40,128]{1,0:T(8,128)S(1)} %add_add_fusion.refs_8_), channel_id=1, source_target_pairs={{0,4},{1,5},{2,6},{3,7},{4,0},{5,1},{6,2},{7,3},{8,12},{9,13},{10,... | collective-permute-start | bytes 61448 | tf_op jit(solution)/shard_map/ppermute | solution.py:561
  50.4 3.8 %collective-permute-start.11 = (f32[40,128]{1,0:T(8,128)S(1)}, f32[40,128]{1,0:T(8,128)S(1)}, u32[]{:S(2)}, u32[]{:S(2)}) collective-permute-start(f32[40,128]{1,0:T(8,128)S(1)} %add_add_fusion.refs_8_), channel_id=1, source_target_pairs={{0,1},{1,0},{2,3},{3,2},{4,5},{5,4},{6,7},{7,6},{8,9},{9,8},{10,11... | collective-permute-start | bytes 61448 | tf_op jit(solution)/shard_map/ppermute | solution.py:561
  51.5 4.7 %collective-permute-start.12 = (f32[40,128]{1,0:T(8,128)S(1)}, f32[40,128]{1,0:T(8,128)S(1)}, u32[]{:S(2)}, u32[]{:S(2)}) collective-permute-start(f32[40,128]{1,0:T(8,128)S(1)} %add_add_fusion.refs_8_), channel_id=1, source_target_pairs={{0,5},{1,4},{2,7},{3,6},{4,1},{5,0},{6,3},{7,2},{8,13},{9,12},{10,... | collective-permute-start | bytes 61448 | tf_op jit(solution)/shard_map/ppermute | solution.py:561

commit v15 on v14

--- a/solution.py
+++ b/solution.py
@@ -241,7 +241,7 @@
     if g + 1 < KV:
         take(1)
     old_sums_ref = take(1)[0] if g else None
-    old_send = take(shards - 1) if 0 < g < KV - 1 else []
+    old_send = take(shards - 1) if g else []
     if 0 < g < KV - 1:
         take(2)
     out_ref, gq_ref, sums_ref, own_ref = take(4)
@@ -388,7 +388,7 @@
     gk = turn_back(dk, cos_ref[...], sin_ref[...])
     own_ref[0] = dk[:tokens]
     own_ref[1] = dv[:tokens]
-    at = 2 * g if g < KV - 1 else 0
+    at = 2 * g
     for j in range(1, shards):
         block = slice(j * tokens, (j + 1) * tokens)
         send[j - 1][at] = dk[block].astype(B16)
@@ -417,7 +417,7 @@
     aliases = {}
     if before is not None:
         out, gq, sums, send = before
-        placed += [sums, *([] if last else send)]
+        placed += [sums, *send]
     args += placed
     in_specs = [smem] * 2 + [vmem] * len(placed)
     if before is not None and not last:
@@ -431,7 +431,7 @@
         pltpu.VMEM((2, tokens, HD), F32),
     ]
     out_specs = [vmem if last else wide] * 2 + [vmem, vmem]
-    out_shape += [pltpu.VMEM((2 if last else 2 * g + 2, tokens, HD), B16)] * (shards - 1)
+    out_shape += [pltpu.VMEM((2 * g + 2, tokens, HD), B16)] * (shards - 1)
     out_specs += [vmem] * (shards - 1)
     if g + 2 < KV:
         out_shape.append(pltpu.VMEM((2 * (slots + tokens), HD), B16))
@@ -487,17 +487,15 @@
 def finish_kernel(shards, *refs):
     cos_ref, sin_ref, *refs = refs
     owns, refs = refs[:KV], refs[KV:]
-    early, late = refs[:shards - 1], refs[shards - 1:2 * (shards - 1)]
-    sums = refs[2 * (shards - 1):-6]
+    backs, sums = refs[:shards - 1], refs[shards - 1:-6]
     gk_ref, gv_ref, *parts = refs[-5:]
     tokens = gk_ref.shape[0]
     cosine, sine = cos_ref[pl.ds(0, tokens), :], sin_ref[pl.ds(0, tokens), :]
     for g in range(KV):
         dk, dv = owns[g][0], owns[g][1]
-        last = g == KV - 1
-        for back in late if last else early:
-            dk = dk + back[0 if last else 2 * g].astype(F32)
-            dv = dv + back[1 if last else 2 * g + 1].astype(F32)
+        for back in backs:
+            dk = dk + back[2 * g].astype(F32)
+            dv = dv + back[2 * g + 1].astype(F32)
         cols = pl.ds(g * HD, HD)
         gk_ref[:, cols] = turn_back(dk, cosine, sine).astype(B16)
         gv_ref[:, cols] = dv.astype(B16)
@@ -508,9 +506,9 @@
         start += part.shape[0]
 
 
-def finish(shards, cosine, sine, owns, early, late, sums, after):
+def finish(shards, cosine, sine, owns, backs, sums, after):
     tokens = owns[0].shape[1]
-    args = [cosine, sine, *owns, *early, *late, *sums]
+    args = [cosine, sine, *owns, *backs, *sums]
     shapes = [((tokens, KV * HD), B16)] * 2 + [((rows, HD), F32) for rows in (HQ, KV, KV)]
     return pl.pallas_call(
         functools.partial(finish_kernel, shards),
@@ -525,37 +523,19 @@
     )(*args, after)
 
 
-def join_kernel(a_ref, b_ref, *refs):
-    refs[-1][...] = a_ref[...] + b_ref[...]
-
-
-def join(parts, held):
-    args = [*parts, *held]
-    return pl.pallas_call(
-        join_kernel,
-        grid=(1,),
-        in_specs=[pl.BlockSpec(memory_space=pltpu.VMEM)] * len(args),
-        out_specs=pl.BlockSpec(memory_space=pltpu.VMEM),
-        out_shape=pltpu.VMEM(parts[0].shape, parts[0].dtype),
-        compiler_params=params(),
-        cost_estimate=pl.CostEstimate(flops=0, bytes_accessed=1 << 16, transcendentals=0),
-        name="join",
-    )(*args)
-
-
 def add_up(parts):
     while len(parts) > 1:
         parts = [a + b for a, b in zip(parts[::2], parts[1::2])]
     return parts[0]
 
 
-def sum_but_last(x, axes, near, held):
+def sum_but_last(x, axes, near):
     devices = lax.axis_size(axes)
     bits = [1 << i for i in reversed(range(devices.bit_length() - 1)) if 1 << i != near]
     stages = [[near]] + [bits[i:i + 2] for i in range(0, len(bits), 2)]
     parts = [x]
-    for i, stage in enumerate(stages):
-        x = join(parts, held) if i == 1 else add_up(parts)
+    for stage in stages:
+        x = add_up(parts)
         parts = [x]
         for flip in [sum(c) for n in (1, 2) for c in itertools.combinations(stage, n)]:
             parts.append(lax.ppermute(x, axes, [(i, i ^ flip) for i in range(devices)]))
@@ -609,14 +589,13 @@
         )
         if g == KV - 2:
             out, gq = before[:2]
-            early = [earlier(x, s) for s, x in zip(shifts, before[3])]
         owns.append(own)
         far += [[ring(chunk, s) for s in shifts] for chunk in more]
     *columns, sums, send = before
-    late = [earlier(x, s) for s, x in zip(shifts, send)]
-    sums = sum_but_last(sums, ("dp", "seq"), shards, early)
+    backs = [earlier(x, s) for s, x in zip(shifts, send)]
+    sums = sum_but_last(sums, ("dp", "seq"), shards)
     out, gq = place(columns, out, gq)
-    gk, gv, *sums = finish(shards, cosine, sine, owns, early, late, sums, hbm(out))
+    gk, gv, *sums = finish(shards, cosine, sine, owns, backs, sums, hbm(out))
     return (out[None], gq[None], gk[None], gv[None], *[x.reshape(-1) for x in sums])
 
 

time: 57.3 us -> 56 us (0.977)
  starting transfers between devices: 18 us -> 16.5 us
    ppermute x2 -> x1, waiting for transfers between devices: 1.58 us -> 0.01 us  [earlier(): return lax.ppermute(x, 'seq', [(i + s, i) for i in range(shards - s)])]
    ppermute x4, waiting for transfers between devices: 1.68 us -> 3.21 us  [ring(): lax.ppermute(x, 'seq', [(i, (i + s) % shards) for i in range(shards)])]
    ppermute x2 -> x1, starting transfers between devices: 2.56 us -> 1.28 us  [earlier(): return lax.ppermute(x, 'seq', [(i + s, i) for i in range(shards - s)])]
  transfers between devices with their start and end apart: 13 -> 12, of which waited for: 10 -> 8; matrix products, arithmetic and copies ran while one was open for 1% -> 1% of each run, Pallas kernels for 43% -> 37%
where the time goes in v15:
time: 56 us; the launch traced here: 55.8 us
  Pallas kernels  26.2 us (47%)
  starting transfers between devices  16.5 us (29%)
  waiting for transfers between devices  11.1 us (20%)
  between operations  1.38 us (2%)
  other arithmetic  0.64 us (1%)
    pallas_call x4, Pallas kernels, attend(): pl.pallas_call(functools.partial(attend_kernel, g, shards), grid=(1,), in...  15.9 us
    ppermute x7, starting transfers between devices, sum_but_last(): parts.append(lax.ppermute(x, axes, [(i, i ^ flip) for i in range(devices)]))  7.99 us
    ppermute x7, waiting for transfers between devices, sum_but_last(): parts.append(lax.ppermute(x, axes, [(i, i ^ flip) for i in range(devices)]))  7.84 us
    ppermute x4, starting transfers between devices, ring(): lax.ppermute(x, 'seq', [(i, (i + s) % shards) for i in range(shards)])  7.25 us
    pallas_call x1, Pallas kernels, prep(): pl.pallas_call(prep_kernel, grid=(KV,), in_specs=[wide, wide, pl.BlockSpe...  4.2 us
    pallas_call x4, Pallas kernels, look_ahead(): pl.pallas_call(functools.partial(ahead_kernel, g, shards), grid=(1,), in_...  3.41 us
    ppermute x4, waiting for transfers between devices, ring(): lax.ppermute(x, 'seq', [(i, (i + s) % shards) for i in range(shards)])  3.21 us
    ppermute x1, starting transfers between devices, earlier(): return lax.ppermute(x, 'seq', [(i + s, i) for i in range(shards - s)])  1.28 us
  transfers between devices with their start and end apart: 12, of which 8 were waited for; matrix products, arithmetic and copies ran while one was open for 1% of the time, Pallas kernels for 37%

profile of v15, /device:TPU:0, one launch (start us, length us, event | category | flops | bytes accessed | tf_op | source)
XLA Modules:
  0.0 55.8 jit_solution(2155961758841999680)
XLA Ops:
  0.6 1.0 %pack.1 = bf16[1280,128]{1,0:T(8,128)(2,1)S(1)} custom-call(bf16[512,512]{1,0:T(8,128)(2,1)} %bitcast.23, bf16[512,512]{1,0:T(8,128)(2,1)} %bitcast.25, bf16[128,512]{1,0:T(8,128)(2,1)} %bitcast.29, bf16[128,512]{1,0:T(8,128)(2,1)} %bitcast.31), custom_call_target="tpu_custom_call" | custom-call | bytes 655360 | tf_op jit(solution)/shard_map/pack/pallas_call | solution.py:60
  1.6 3.0 %collective-permute-start.1 = (bf16[1280,128]{1,0:T(8,128)(2,1)S(1)}, bf16[1280,128]{1,0:T(8,128)(2,1)S(1)}, u32[]{:S(2)}, u32[]{:S(2)}) collective-permute-start(bf16[1280,128]{1,0:T(8,128)(2,1)S(1)} %pack.1), channel_id=1, source_target_pairs={{0,1},{1,0},{2,3},{3,2},{4,5},{5,4},{6,7},{7,6},{8,9},{9,8},{10,11... | collective-permute-start | bytes 983048 | tf_op jit(solution)/shard_map/ppermute | solution.py:552
  5.4 0.1 convert_bitcast_fusion
  5.4 0.5 fusion
  6.0 4.2 %prep.1 = (bf16[4096,128]{1,0:T(8,128)(2,1)S(1)}, bf16[1024,512]{1,0:T(8,128)(2,1)S(1)}, bf16[4096,128]{1,0:T(8,128)(2,1)S(1)}, bf16[1024,512]{1,0:T(8,128)(2,1)...) custom-call(bf16[128,4096]{1,0:T(8,128)(2,1)} %bitcast.27, ...), custom_call_target="tpu_custom_call" | custom-call | flops 2097152 | bytes 6291456 | tf_op jit(solution)/shard_map/prep/pallas_call | solution.py:133
  10.2 0.1 collective-permute-start
  10.3 0.8 %ahead.4 = (f32[2,640,512]{2,1,0:T(8,128)S(1)}, f32[2,640,512]{2,1,0:T(8,128)S(1)}, f32[2,8,512]{2,1,0:T(8,128)S(1)}) custom-call(s32[1]{0:T(128)} %copy.29.first_ref.refs_0_, s32[1]{0:T(128)} %bitcast.rank_ref.refs_1_, bf16[1024,512]{1,0:T(8,128)(2,1)S(1)} %get-tuple-element.63.qst_ref.refs_3_, bf16[1024,512]{1,0:T(8,128)(2,1)S(1)} %get-tuple-element.65.dot_ref.refs_5_, ...), custom_call_target="tpu_custom_call" | custom-call | flops 335544320 | bytes 5242880 | tf_op jit(solution)/shard_map/ahead/pallas_call | solution.py:209
  11.1 0.9 %ahead.5 = (f32[2,640,512]{2,1,0:T(8,128)S(1)}, f32[2,640,512]{2,1,0:T(8,128)S(1)}, f32[2,8,512]{2,1,0:T(8,128)S(1)}) custom-call(s32[1]{0:T(128)} %copy.29.first_ref.refs_0_, s32[1]{0:T(128)} %bitcast.rank_ref.refs_1_, bf16[1024,512]{1,0:T(8,128)(2,1)S(1)} %get-tuple-element.63.qst_ref.refs_3_, bf16[1024,512]{1,0:T(8,128)(2,1)S(1)} %get-tuple-element.65.dot_ref.refs_5_, ...), custom_call_target="tpu_custom_call" | custom-call | flops 335544320 | bytes 5242880 | tf_op jit(solution)/shard_map/ahead/pallas_call | solution.py:209
  12.0 0.9 %ahead.6 = (f32[2,640,512]{2,1,0:T(8,128)S(1)}, f32[2,640,512]{2,1,0:T(8,128)S(1)}, f32[2,8,512]{2,1,0:T(8,128)S(1)}) custom-call(s32[1]{0:T(128)} %copy.29.first_ref.refs_0_, s32[1]{0:T(128)} %bitcast.rank_ref.refs_1_, bf16[1024,512]{1,0:T(8,128)(2,1)S(1)} %get-tuple-element.63.qst_ref.refs_3_, bf16[1024,512]{1,0:T(8,128)(2,1)S(1)} %get-tuple-element.65.dot_ref.refs_5_, ...), custom_call_target="tpu_custom_call" | custom-call | flops 335544320 | bytes 5242880 | tf_op jit(solution)/shard_map/ahead/pallas_call | solution.py:209
  12.8 0.0 collective-permute-done.1.refs_17_
  12.8 4.2 %attend.4 = (bf16[128,4096]{1,0:T(8,128)(2,1)}, bf16[128,4096]{1,0:T(8,128)(2,1)}, f32[40,128]{1,0:T(8,128)S(1)}, f32[2,128,128]{2,1,0:T(8,128)S(1)}, bf16[2,128...) custom-call(s32[1]{0:T(128)} %copy.29.first_ref.refs_0_, s32[1]{0:T(128)} %bitcast.rank_ref.refs_1_, ...), custom_call_target="tpu_custom_call" | custom-call | flops 1476395008 | bytes 2359296 | tf_op jit(solution)/shard_map/attend/pallas_call | solution.py:439
  17.0 2.4 %collective-permute-start.3 = (bf16[1280,128]{1,0:T(8,128)(2,1)S(1)}, bf16[1280,128]{1,0:T(8,128)(2,1)S(1)}, u32[]{:S(2)}, u32[]{:S(2)}) collective-permute-start(bf16[1280,128]{1,0:T(8,128)(2,1)S(1)} %get-tuple-element.91), channel_id=1, source_target_pairs={{0,1},{1,0},{2,3},{3,2},{4,5},{5,4},{6,7},{7,6},{8,9},{9,8},{10,11... | collective-permute-start | bytes 983048 | tf_op jit(solution)/shard_map/ppermute | solution.py:552
  19.4 0.2 collective-permute-done.refs_17_
  19.6 4.1 %attend.5 = (bf16[128,4096]{1,0:T(8,128)(2,1)}, bf16[128,4096]{1,0:T(8,128)(2,1)}, f32[40,128]{1,0:T(8,128)S(1)}, f32[2,128,128]{2,1,0:T(8,128)S(1)}, bf16[4,128...) custom-call(s32[1]{0:T(128)} %copy.29.first_ref.refs_0_, ...), custom_call_target="tpu_custom_call", output_to_operand_aliasing={{0}: (24, {}), {1}: (25, {})} | custom-call | flops 1476395008 | bytes 2359296 | tf_op jit(solution)/shard_map/attend/pallas_call | solution.py:439
  23.7 1.7 %collective-permute-start.2 = (bf16[1280,128]{1,0:T(8,128)(2,1)S(1)}, bf16[1280,128]{1,0:T(8,128)(2,1)S(1)}, u32[]{:S(2)}, u32[]{:S(2)}) collective-permute-start(bf16[1280,128]{1,0:T(8,128)(2,1)S(1)} %get-tuple-element.87), channel_id=1, source_target_pairs={{0,1},{1,0},{2,3},{3,2},{4,5},{5,4},{6,7},{7,6},{8,9},{9,8},{10,11... | collective-permute-start | bytes 983048 | tf_op jit(solution)/shard_map/ppermute | solution.py:552
  25.4 0.8 %ahead.7 = (f32[2,640,512]{2,1,0:T(8,128)S(1)}, f32[2,640,512]{2,1,0:T(8,128)S(1)}, f32[2,8,512]{2,1,0:T(8,128)S(1)}) custom-call(s32[1]{0:T(128)} %copy.29.first_ref.refs_0_, s32[1]{0:T(128)} %bitcast.rank_ref.refs_1_, bf16[1024,512]{1,0:T(8,128)(2,1)S(1)} %get-tuple-element.63.qst_ref.refs_3_, bf16[1024,512]{1,0:T(8,128)(2,1)S(1)} %get-tuple-element.65.dot_ref.refs_5_, ...), custom_call_target="tpu_custom_call" | custom-call | flops 335544320 | bytes 5242880 | tf_op jit(solution)/shard_map/ahead/pallas_call | solution.py:209
  26.2 1.5 %collective-permute-done.3.refs_17_ = bf16[1280,128]{1,0:T(8,128)(2,1)S(1)} collective-permute-done((bf16[1280,128]{1,0:T(8,128)(2,1)S(1)}, bf16[1280,128]{1,0:T(8,128)(2,1)S(1)}, u32[]{:S(2)}, u32[]{:S(2)}) %collective-permute-start.3) | collective-permute-done | bytes 327712 | tf_op jit(solution)/shard_map/ppermute | solution.py:552
  27.8 4.2 %attend.6 = (bf16[128,4096]{1,0:T(8,128)(2,1)}, bf16[128,4096]{1,0:T(8,128)(2,1)}, f32[40,128]{1,0:T(8,128)S(1)}, f32[2,128,128]{2,1,0:T(8,128)S(1)}, bf16[6,128,128]{2,1,0:T(8,128)(2,1)S(1)}) custom-call(s32[1]{0:T(128)} %copy.29.first_ref.refs_0_, s32[1]{0:T(128)} %bitcast.rank_ref.refs_1_, ...), custom_call_target="tpu_custom_call", output_to_operand_aliasing={{0}: (24, {}), {1}: (25, {})} | custom-call | flops 1476395008 | bytes 2359296 | tf_op jit(solution)/shard_map/attend/pallas_call | solution.py:439
  32.0 1.5 %collective-permute-done.2.refs_17_ = bf16[1280,128]{1,0:T(8,128)(2,1)S(1)} collective-permute-done((bf16[1280,128]{1,0:T(8,128)(2,1)S(1)}, bf16[1280,128]{1,0:T(8,128)(2,1)S(1)}, u32[]{:S(2)}, u32[]{:S(2)}) %collective-permute-start.2) | collective-permute-done | bytes 327712 | tf_op jit(solution)/shard_map/ppermute | solution.py:552
  33.5 3.5 %attend.7 = (bf16[128,1024]{1,0:T(8,128)(2,1)S(1)}, bf16[128,1024]{1,0:T(8,128)(2,1)S(1)}, f32[40,128]{1,0:T(8,128)S(1)}, f32[2,128,128]{2,1,0:T(8,128)S(1)}, bf16[8,128,128]{2,1,0:T(8,128)(2,1)S(1)}) custom-call(s32[1]{0:T(128)} %copy.29.first_ref.refs_0_, s32[1]{0:T(128)} %bitcast.rank_ref.refs_1_, bf16[4096,128]{1,0:T(8,128)(2,1)S(1)} %get-tuple-element.62.refs_2_, ...), custom_call_target="tpu_custom_call" | custom-call | flops 1476395008 | bytes 2359296 | tf_op jit(solution)/shard_map/attend/pallas_call | solution.py:439
  37.0 0.1 collective-permute-start.5
  37.0 1.2 %collective-permute-done.5 = f32[40,128]{1,0:T(8,128)S(1)} collective-permute-done((f32[40,128]{1,0:T(8,128)S(1)}, f32[40,128]{1,0:T(8,128)S(1)}, u32[]{:S(2)}, u32[]{:S(2)}) %collective-permute-start.5) | collective-permute-done | bytes 20512 | tf_op jit(solution)/shard_map/ppermute | solution.py:541
  38.2 1.8 %collective-permute-start.7 = (f32[40,128]{1,0:T(8,128)S(1)}, f32[40,128]{1,0:T(8,128)S(1)}, u32[]{:S(2)}, u32[]{:S(2)}) collective-permute-start(f32[40,128]{1,0:T(8,128)S(1)} %add.66), channel_id=1, source_target_pairs={{0,8},{1,9},{2,10},{3,11},{4,12},{5,13},{6,14},{7,15},{8,0},{9,1},... | collective-permute-start | bytes 61448 | tf_op jit(solution)/shard_map/ppermute | solution.py:541
  40.0 2.5 %collective-permute-start.8 = (f32[40,128]{1,0:T(8,128)S(1)}, f32[40,128]{1,0:T(8,128)S(1)}, u32[]{:S(2)}, u32[]{:S(2)}) collective-permute-start(f32[40,128]{1,0:T(8,128)S(1)} %add.66), channel_id=1, source_target_pairs={{0,24},{1,25},{2,26},{3,27},{4,28},{5,29},{6,30},{7,31},{8,16},{9,... | collective-permute-start | bytes 61448 | tf_op jit(solution)/shard_map/ppermute | solution.py:541
  42.5 0.1 collective-permute-start.6
  42.6 1.3 %collective-permute-start.4 = (bf16[8,128,128]{2,1,0:T(8,128)(2,1)S(1)}, bf16[8,128,128]{2,1,0:T(8,128)(2,1)S(1)}, u32[]{:S(2)}, u32[]{:S(2)}) collective-permute-start(bf16[8,128,128]{2,1,0:T(8,128)(2,1)S(1)} %get-tuple-element.110), channel_id=1, source_target_pairs={{1,0},{3,2},{5,4},{7,6},{9,8},{11,10},{13,12},{15,14},{17,16},{19,... | collective-permute-start | bytes 786440 | tf_op jit(solution)/shard_map/ppermute | solution.py:555
  43.9 0.0 collective-permute-done.7
  43.9 1.7 %collective-permute-done.8 = f32[40,128]{1,0:T(8,128)S(1)} collective-permute-done((f32[40,128]{1,0:T(8,128)S(1)}, f32[40,128]{1,0:T(8,128)S(1)}, u32[]{:S(2)}, u32[]{:S(2)}) %collective-permute-start.8) | collective-permute-done | bytes 20512 | tf_op jit(solution)/shard_map/ppermute | solution.py:541
  45.6 1.6 %collective-permute-done.6 = f32[40,128]{1,0:T(8,128)S(1)} collective-permute-done((f32[40,128]{1,0:T(8,128)S(1)}, f32[40,128]{1,0:T(8,128)S(1)}, u32[]{:S(2)}, u32[]{:S(2)}) %collective-permute-start.6) | collective-permute-done | bytes 20512 | tf_op jit(solution)/shard_map/ppermute | solution.py:541
  47.2 1.8 %collective-permute-start.9 = (f32[40,128]{1,0:T(8,128)S(1)}, f32[40,128]{1,0:T(8,128)S(1)}, u32[]{:S(2)}, u32[]{:S(2)}) collective-permute-start(f32[40,128]{1,0:T(8,128)S(1)} %add_add_fusion.refs_7_), channel_id=1, source_target_pairs={{0,4},{1,5},{2,6},{3,7},{4,0},{5,1},{6,2},{7,3},{8,12},{9,13},{10,... | collective-permute-start | bytes 61448 | tf_op jit(solution)/shard_map/ppermute | solution.py:541
  48.9 1.3 %collective-permute-start.10 = (f32[40,128]{1,0:T(8,128)S(1)}, f32[40,128]{1,0:T(8,128)S(1)}, u32[]{:S(2)}, u32[]{:S(2)}) collective-permute-start(f32[40,128]{1,0:T(8,128)S(1)} %add_add_fusion.refs_7_), channel_id=1, source_target_pairs={{0,1},{1,0},{2,3},{3,2},{4,5},{5,4},{6,7},{7,6},{8,9},{9,8},{10,11... | collective-permute-start | bytes 61448 | tf_op jit(solution)/shard_map/ppermute | solution.py:541
  50.2 0.5 collective-permute-start.11
  50.7 0.8 %place.1 = (bf16[128,4096]{1,0:T(8,128)(2,1)}, bf16[128,4096]{1,0:T(8,128)(2,1)}) custom-call(bf16[128,1024]{1,0:T(8,128)(2,1)S(1)} %get-tuple-element.100.out_part, bf16[128,1024]{1,0:T(8,128)(2,1)S(1)} %get-tuple-element.101.gq_part, bf16[128,4096]{1,0:T(8,128)(2,1)} %get-tuple-element.102._, ...), custom_call_target="tpu_custom_call", output_to_operand_aliasing={{0}: (2, {}), {1}: (3, {})} | custom-call | bytes 2097152 | tf_op jit(solution)/shard_map/place/pallas_call | solution.py:473
  51.5 0.0 collective-permute-done.9.refs_8_
  51.5 1.4 %collective-permute-done.10.refs_9_ = f32[40,128]{1,0:T(8,128)S(1)} collective-permute-done((f32[40,128]{1,0:T(8,128)S(1)}, f32[40,128]{1,0:T(8,128)S(1)}, u32[]{:S(2)}, u32[]{:S(2)}) %collective-permute-start.10) | collective-permute-done | bytes 20512 | tf_op jit(solution)/shard_map/ppermute | solution.py:541
  52.9 2.0 %collective-permute-done.11.refs_10_ = f32[40,128]{1,0:T(8,128)S(1)} collective-permute-done((f32[40,128]{1,0:T(8,128)S(1)}, f32[40,128]{1,0:T(8,128)S(1)}, u32[]{:S(2)}, u32[]{:S(2)}) %collective-permute-start.11) | collective-permute-done | bytes 20512 | tf_op jit(solution)/shard_map/ppermute | solution.py:541
  54.9 0.0 collective-permute-done.4.refs_6_
  54.9 0.8 %finish.1 = (bf16[128,512]{1,0:T(8,128)(2,1)}, bf16[128,512]{1,0:T(8,128)(2,1)}, f32[32,128]{1,0:T(8,128)}, f32[4,128]{1,0:T(4,128)}, f32[4,128]{1,0:T(4,128)}) custom-call(f32[256,128]{1,0:T(8,128)S(1)} %get-tuple-element.118.cos_ref.refs_11_.refs_0_, f32[256,128]{1,0:T(8,128)S(1)} %get-tuple-element.117.sin_ref.refs_12_.refs_1_, ...), custom_call_target="tpu_custom_call" | custom-call | bytes 524288 | tf_op jit(solution)/shard_map/finish/pallas_call | solution.py:513
  (4 shorter events, 0.0 us)
Async XLA Ops:
  1.6 11.2 %collective-permute-start.1 = (bf16[1280,128]{1,0:T(8,128)(2,1)S(1)}, bf16[1280,128]{1,0:T(8,128)(2,1)S(1)}, u32[]{:S(2)}, u32[]{:S(2)}) collective-permute-start(bf16[1280,128]{1,0:T(8,128)(2,1)S(1)} %pack.1), channel_id=1, source_target_pairs={{0,1},{1,0},{2,3},{3,2},{4,5},{5,4},{6,7},{7,6},{8,9},{9,8},{10,11... | collective-permute-start | bytes 983048 | tf_op jit(solution)/shard_map/ppermute | solution.py:552
  10.2 9.4 %collective-permute-start = (bf16[1280,128]{1,0:T(8,128)(2,1)S(1)}, bf16[1280,128]{1,0:T(8,128)(2,1)S(1)}, u32[]{:S(2)}, u32[]{:S(2)}) collective-permute-start(bf16[1280,128]{1,0:T(8,128)(2,1)S(1)} %get-tuple-element.75), channel_id=1, source_target_pairs={{0,1},{1,0},{2,3},{3,2},{4,5},{5,4},{6,7},{7,6},{8,9},{9,8},{10,11... | collective-permute-start | bytes 983048 | tf_op jit(solution)/shard_map/ppermute | solution.py:552
  17.0 10.8 %collective-permute-start.3 = (bf16[1280,128]{1,0:T(8,128)(2,1)S(1)}, bf16[1280,128]{1,0:T(8,128)(2,1)S(1)}, u32[]{:S(2)}, u32[]{:S(2)}) collective-permute-start(bf16[1280,128]{1,0:T(8,128)(2,1)S(1)} %get-tuple-element.91), channel_id=1, source_target_pairs={{0,1},{1,0},{2,3},{3,2},{4,5},{5,4},{6,7},{7,6},{8,9},{9,8},{10,11... | collective-permute-start | bytes 983048 | tf_op jit(solution)/shard_map/ppermute | solution.py:552
  23.7 9.8 %collective-permute-start.2 = (bf16[1280,128]{1,0:T(8,128)(2,1)S(1)}, bf16[1280,128]{1,0:T(8,128)(2,1)S(1)}, u32[]{:S(2)}, u32[]{:S(2)}) collective-permute-start(bf16[1280,128]{1,0:T(8,128)(2,1)S(1)} %get-tuple-element.87), channel_id=1, source_target_pairs={{0,1},{1,0},{2,3},{3,2},{4,5},{5,4},{6,7},{7,6},{8,9},{9,8},{10,11... | collective-permute-start | bytes 983048 | tf_op jit(solution)/shard_map/ppermute | solution.py:552
  37.0 1.3 %collective-permute-start.5 = (f32[40,128]{1,0:T(8,128)S(1)}, f32[40,128]{1,0:T(8,128)S(1)}, u32[]{:S(2)}, u32[]{:S(2)}) collective-permute-start(f32[40,128]{1,0:T(8,128)S(1)} %get-tuple-element.111), channel_id=1, source_target_pairs={{0,2},{1,3},{2,0},{3,1},{4,6},{5,7},{6,4},{7,5},{8,10},{9,11},{10,... | collective-permute-start | bytes 61448 | tf_op jit(solution)/shard_map/ppermute | solution.py:541
  38.2 5.7 %collective-permute-start.7 = (f32[40,128]{1,0:T(8,128)S(1)}, f32[40,128]{1,0:T(8,128)S(1)}, u32[]{:S(2)}, u32[]{:S(2)}) collective-permute-start(f32[40,128]{1,0:T(8,128)S(1)} %add.66), channel_id=1, source_target_pairs={{0,8},{1,9},{2,10},{3,11},{4,12},{5,13},{6,14},{7,15},{8,0},{9,1},... | collective-permute-start | bytes 61448 | tf_op jit(solution)/shard_map/ppermute | solution.py:541
  40.0 5.6 %collective-permute-start.8 = (f32[40,128]{1,0:T(8,128)S(1)}, f32[40,128]{1,0:T(8,128)S(1)}, u32[]{:S(2)}, u32[]{:S(2)}) collective-permute-start(f32[40,128]{1,0:T(8,128)S(1)} %add.66), channel_id=1, source_target_pairs={{0,24},{1,25},{2,26},{3,27},{4,28},{5,29},{6,30},{7,31},{8,16},{9,... | collective-permute-start | bytes 61448 | tf_op jit(solution)/shard_map/ppermute | solution.py:541
  42.5 4.7 %collective-permute-start.6 = (f32[40,128]{1,0:T(8,128)S(1)}, f32[40,128]{1,0:T(8,128)S(1)}, u32[]{:S(2)}, u32[]{:S(2)}) collective-permute-start(f32[40,128]{1,0:T(8,128)S(1)} %add.66), channel_id=1, source_target_pairs={{0,16},{1,17},{2,18},{3,19},{4,20},{5,21},{6,22},{7,23},{8,24},{9,... | collective-permute-start | bytes 61448 | tf_op jit(solution)/shard_map/ppermute | solution.py:541
  42.6 12.3 %collective-permute-start.4 = (bf16[8,128,128]{2,1,0:T(8,128)(2,1)S(1)}, bf16[8,128,128]{2,1,0:T(8,128)(2,1)S(1)}, u32[]{:S(2)}, u32[]{:S(2)}) collective-permute-start(bf16[8,128,128]{2,1,0:T(8,128)(2,1)S(1)} %get-tuple-element.110), channel_id=1, source_target_pairs={{1,0},{3,2},{5,4},{7,6},{9,8},{11,10},{13,12},{15,14},{17,16},{19,... | collective-permute-start | bytes 786440 | tf_op jit(solution)/shard_map/ppermute | solution.py:555
  47.2 4.4 %collective-permute-start.9 = (f32[40,128]{1,0:T(8,128)S(1)}, f32[40,128]{1,0:T(8,128)S(1)}, u32[]{:S(2)}, u32[]{:S(2)}) collective-permute-start(f32[40,128]{1,0:T(8,128)S(1)} %add_add_fusion.refs_7_), channel_id=1, source_target_pairs={{0,4},{1,5},{2,6},{3,7},{4,0},{5,1},{6,2},{7,3},{8,12},{9,13},{10,... | collective-permute-start | bytes 61448 | tf_op jit(solution)/shard_map/ppermute | solution.py:541
  48.9 4.0 %collective-permute-start.10 = (f32[40,128]{1,0:T(8,128)S(1)}, f32[40,128]{1,0:T(8,128)S(1)}, u32[]{:S(2)}, u32[]{:S(2)}) collective-permute-start(f32[40,128]{1,0:T(8,128)S(1)} %add_add_fusion.refs_7_), channel_id=1, source_target_pairs={{0,1},{1,0},{2,3},{3,2},{4,5},{5,4},{6,7},{7,6},{8,9},{9,8},{10,11... | collective-permute-start | bytes 61448 | tf_op jit(solution)/shard_map/ppermute | solution.py:541
  50.2 4.7 %collective-permute-start.11 = (f32[40,128]{1,0:T(8,128)S(1)}, f32[40,128]{1,0:T(8,128)S(1)}, u32[]{:S(2)}, u32[]{:S(2)}) collective-permute-start(f32[40,128]{1,0:T(8,128)S(1)} %add_add_fusion.refs_7_), channel_id=1, source_target_pairs={{0,5},{1,4},{2,7},{3,6},{4,1},{5,0},{6,3},{7,2},{8,13},{9,12},{10,... | collective-permute-start | bytes 61448 | tf_op jit(solution)/shard_map/ppermute | solution.py:541

commit v16 on v13

--- a/solution.py
+++ b/solution.py
@@ -531,13 +531,31 @@
     return parts[0]
 
 
-def sum_but_last(x, axes, near):
+def join_kernel(count, *refs):
+    refs[-1][...] = add_up([ref[...] for ref in refs[:count]])
+
+
+def join(parts, held):
+    args = [*parts, *held]
+    return pl.pallas_call(
+        functools.partial(join_kernel, len(parts)),
+        grid=(1,),
+        in_specs=[pl.BlockSpec(memory_space=pltpu.VMEM)] * len(args),
+        out_specs=pl.BlockSpec(memory_space=pltpu.VMEM),
+        out_shape=pltpu.VMEM(parts[0].shape, parts[0].dtype),
+        compiler_params=params(),
+        cost_estimate=pl.CostEstimate(flops=0, bytes_accessed=1 << 16, transcendentals=0),
+        name="join",
+    )(*args)
+
+
+def sum_but_last(x, axes, near, held):
     devices = lax.axis_size(axes)
     bits = [1 << i for i in reversed(range(devices.bit_length() - 1)) if 1 << i != near]
     stages = [[near]] + [bits[i:i + 2] for i in range(0, len(bits), 2)]
     parts = [x]
-    for stage in stages:
-        x = add_up(parts)
+    for i, stage in enumerate(stages):
+        x = join(parts, held) if i == 2 else add_up(parts)
         parts = [x]
         for flip in [sum(c) for n in (1, 2) for c in itertools.combinations(stage, n)]:
             parts.append(lax.ppermute(x, axes, [(i, i ^ flip) for i in range(devices)]))
@@ -595,7 +613,7 @@
         far += [[ring(chunk, s) for s in shifts] for chunk in more]
     *columns, sums, send = before
     backs = [earlier(x, s) for s, x in zip(shifts, send)]
-    sums = sum_but_last(sums, ("dp", "seq"), shards)
+    sums = sum_but_last(sums, ("dp", "seq"), shards, backs)
     out, gq, gk, gv = finish(shards, cosine, sine, owns, backs, columns, out, gq)
     sums = last_sums(sums, hbm(gk))
     return (out[None], gq[None], gk[None], gv[None], *[x.reshape(-1) for x in sums])

time: 55.7 us -> 59.2 us (1.063)
  waiting for transfers between devices: 10.9 us -> 13.7 us
  starting transfers between devices: 16.5 us -> 17.2 us
    ppermute x7, waiting for transfers between devices: 5.67 us -> 10.5 us  [sum_but_last(): parts.append(lax.ppermute(x, axes, [(i, i ^ flip) for i in range(devices)]))]
    ppermute x1, waiting for transfers between devices: 2 us -> 0.01 us  [earlier(): return lax.ppermute(x, 'seq', [(i + s, i) for i in range(shards - s)])]
    ppermute x7, starting transfers between devices: 8 us -> 8.67 us  [sum_but_last(): parts.append(lax.ppermute(x, axes, [(i, i ^ flip) for i in range(devices)]))]
  transfers between devices with their start and end apart: 12 -> 12, of which waited for: 8 -> 9; matrix products, arithmetic and copies ran while one was open for 1% -> 1% of each run, Pallas kernels for 38% -> 36%
where the time goes in v16:
time: 59.2 us; the launch traced here: 59 us
  Pallas kernels  26.1 us (44%)
  starting transfers between devices  17.2 us (29%)
  waiting for transfers between devices  13.7 us (23%)
  between operations  1.38 us (2%)
  other arithmetic  0.63 us (1%)
    pallas_call x4, Pallas kernels, attend(): pl.pallas_call(functools.partial(attend_kernel, g, shards), grid=(1,), in...  15.9 us
    ppermute x7, waiting for transfers between devices, sum_but_last(): parts.append(lax.ppermute(x, axes, [(i, i ^ flip) for i in range(devices)]))  10.5 us
    ppermute x7, starting transfers between devices, sum_but_last(): parts.append(lax.ppermute(x, axes, [(i, i ^ flip) for i in range(devices)]))  8.67 us
    ppermute x4, starting transfers between devices, ring(): lax.ppermute(x, 'seq', [(i, (i + s) % shards) for i in range(shards)])  7.26 us
    pallas_call x1, Pallas kernels, prep(): pl.pallas_call(prep_kernel, grid=(KV,), in_specs=[wide, wide, pl.BlockSpe...  4.2 us
    pallas_call x4, Pallas kernels, look_ahead(): pl.pallas_call(functools.partial(ahead_kernel, g, shards), grid=(1,), in_...  3.4 us
    ppermute x4, waiting for transfers between devices, ring(): lax.ppermute(x, 'seq', [(i, (i + s) % shards) for i in range(shards)])  3.2 us
    ppermute x1, starting transfers between devices, earlier(): return lax.ppermute(x, 'seq', [(i + s, i) for i in range(shards - s)])  1.29 us
  transfers between devices with their start and end apart: 12, of which 9 were waited for; matrix products, arithmetic and copies ran while one was open for 1% of the time, Pallas kernels for 36%

profile of v16, /device:TPU:0, one launch (start us, length us, event | category | flops | bytes accessed | tf_op | source)
XLA Modules:
  0.0 59.0 jit_solution(7693067247610804729)
XLA Ops:
  0.6 1.0 %pack.1 = bf16[1280,128]{1,0:T(8,128)(2,1)S(1)} custom-call(bf16[512,512]{1,0:T(8,128)(2,1)} %bitcast.23, bf16[512,512]{1,0:T(8,128)(2,1)} %bitcast.25, bf16[128,512]{1,0:T(8,128)(2,1)} %bitcast.29, bf16[128,512]{1,0:T(8,128)(2,1)} %bitcast.31), custom_call_target="tpu_custom_call" | custom-call | bytes 655360 | tf_op jit(solution)/shard_map/pack/pallas_call | solution.py:60
  1.6 3.0 %collective-permute-start = (bf16[1280,128]{1,0:T(8,128)(2,1)S(1)}, bf16[1280,128]{1,0:T(8,128)(2,1)S(1)}, u32[]{:S(2)}, u32[]{:S(2)}) collective-permute-start(bf16[1280,128]{1,0:T(8,128)(2,1)S(1)} %pack.1), channel_id=1, source_target_pairs={{0,1},{1,0},{2,3},{3,2},{4,5},{5,4},{6,7},{7,6},{8,9},{9,8},{10,11... | collective-permute-start | bytes 983048 | tf_op jit(solution)/shard_map/ppermute | solution.py:572
  5.3 0.1 convert_bitcast_fusion
  5.4 0.5 fusion
  6.0 4.2 %prep.1 = (bf16[4096,128]{1,0:T(8,128)(2,1)S(1)}, bf16[1024,512]{1,0:T(8,128)(2,1)S(1)}, bf16[4096,128]{1,0:T(8,128)(2,1)S(1)}, bf16[1024,512]{1,0:T(8,128)(2,1)...) custom-call(bf16[128,4096]{1,0:T(8,128)(2,1)} %bitcast.27, ...), custom_call_target="tpu_custom_call" | custom-call | flops 2097152 | bytes 6291456 | tf_op jit(solution)/shard_map/prep/pallas_call | solution.py:133
  10.2 0.1 collective-permute-start.1
  10.3 0.9 %ahead.4 = (f32[2,640,512]{2,1,0:T(8,128)S(1)}, f32[2,640,512]{2,1,0:T(8,128)S(1)}, f32[2,8,512]{2,1,0:T(8,128)S(1)}) custom-call(s32[1]{0:T(128)} %copy.29.first_ref.refs_0_, s32[1]{0:T(128)} %bitcast.2.rank_ref.refs_1_, bf16[1024,512]{1,0:T(8,128)(2,1)S(1)} %get-tuple-element.63.qst_ref.refs_3_, bf16[1024,512]{1,0:T(8,128)(2,1)S(1)} %get-tuple-element.65.dot_ref.refs_5_, ...), custom_call_target="tpu_custom_call" | custom-call | flops 335544320 | bytes 5242880 | tf_op jit(solution)/shard_map/ahead/pallas_call | solution.py:209
  11.1 0.9 %ahead.5 = (f32[2,640,512]{2,1,0:T(8,128)S(1)}, f32[2,640,512]{2,1,0:T(8,128)S(1)}, f32[2,8,512]{2,1,0:T(8,128)S(1)}) custom-call(s32[1]{0:T(128)} %copy.29.first_ref.refs_0_, s32[1]{0:T(128)} %bitcast.2.rank_ref.refs_1_, bf16[1024,512]{1,0:T(8,128)(2,1)S(1)} %get-tuple-element.63.qst_ref.refs_3_, bf16[1024,512]{1,0:T(8,128)(2,1)S(1)} %get-tuple-element.65.dot_ref.refs_5_, ...), custom_call_target="tpu_custom_call" | custom-call | flops 335544320 | bytes 5242880 | tf_op jit(solution)/shard_map/ahead/pallas_call | solution.py:209
  12.0 0.9 %ahead.6 = (f32[2,640,512]{2,1,0:T(8,128)S(1)}, f32[2,640,512]{2,1,0:T(8,128)S(1)}, f32[2,8,512]{2,1,0:T(8,128)S(1)}) custom-call(s32[1]{0:T(128)} %copy.29.first_ref.refs_0_, s32[1]{0:T(128)} %bitcast.2.rank_ref.refs_1_, bf16[1024,512]{1,0:T(8,128)(2,1)S(1)} %get-tuple-element.63.qst_ref.refs_3_, bf16[1024,512]{1,0:T(8,128)(2,1)S(1)} %get-tuple-element.65.dot_ref.refs_5_, ...), custom_call_target="tpu_custom_call" | custom-call | flops 335544320 | bytes 5242880 | tf_op jit(solution)/shard_map/ahead/pallas_call | solution.py:209
  12.8 0.0 collective-permute-done.refs_17_
  12.8 4.2 %attend.4 = (bf16[128,4096]{1,0:T(8,128)(2,1)}, bf16[128,4096]{1,0:T(8,128)(2,1)}, f32[40,128]{1,0:T(8,128)S(1)}, f32[2,128,128]{2,1,0:T(8,128)S(1)}, bf16[2,128...) custom-call(s32[1]{0:T(128)} %copy.29.first_ref.refs_0_, s32[1]{0:T(128)} %bitcast.2.rank_ref.refs_1_, ...), custom_call_target="tpu_custom_call" | custom-call | flops 1476395008 | bytes 2359296 | tf_op jit(solution)/shard_map/attend/pallas_call | solution.py:439
  17.0 2.4 %collective-permute-start.2 = (bf16[1280,128]{1,0:T(8,128)(2,1)S(1)}, bf16[1280,128]{1,0:T(8,128)(2,1)S(1)}, u32[]{:S(2)}, u32[]{:S(2)}) collective-permute-start(bf16[1280,128]{1,0:T(8,128)(2,1)S(1)} %get-tuple-element.89), channel_id=1, source_target_pairs={{0,1},{1,0},{2,3},{3,2},{4,5},{5,4},{6,7},{7,6},{8,9},{9,8},{10,11... | collective-permute-start | bytes 983048 | tf_op jit(solution)/shard_map/ppermute | solution.py:572
  19.4 0.2 collective-permute-done.1.refs_17_
  19.6 4.1 %attend.5 = (bf16[128,4096]{1,0:T(8,128)(2,1)}, bf16[128,4096]{1,0:T(8,128)(2,1)}, f32[40,128]{1,0:T(8,128)S(1)}, f32[2,128,128]{2,1,0:T(8,128)S(1)}, bf16[4,128...) custom-call(s32[1]{0:T(128)} %copy.29.first_ref.refs_0_, ...), custom_call_target="tpu_custom_call", output_to_operand_aliasing={{0}: (24, {}), {1}: (25, {})} | custom-call | flops 1476395008 | bytes 2359296 | tf_op jit(solution)/shard_map/attend/pallas_call | solution.py:439
  23.7 1.7 %collective-permute-start.3 = (bf16[1280,128]{1,0:T(8,128)(2,1)S(1)}, bf16[1280,128]{1,0:T(8,128)(2,1)S(1)}, u32[]{:S(2)}, u32[]{:S(2)}) collective-permute-start(bf16[1280,128]{1,0:T(8,128)(2,1)S(1)} %get-tuple-element.98), channel_id=1, source_target_pairs={{0,1},{1,0},{2,3},{3,2},{4,5},{5,4},{6,7},{7,6},{8,9},{9,8},{10,11... | collective-permute-start | bytes 983048 | tf_op jit(solution)/shard_map/ppermute | solution.py:572
  25.4 0.8 %ahead.7 = (f32[2,640,512]{2,1,0:T(8,128)S(1)}, f32[2,640,512]{2,1,0:T(8,128)S(1)}, f32[2,8,512]{2,1,0:T(8,128)S(1)}) custom-call(s32[1]{0:T(128)} %copy.29.first_ref.refs_0_, s32[1]{0:T(128)} %bitcast.2.rank_ref.refs_1_, bf16[1024,512]{1,0:T(8,128)(2,1)S(1)} %get-tuple-element.63.qst_ref.refs_3_, bf16[1024,512]{1,0:T(8,128)(2,1)S(1)} %get-tuple-element.65.dot_ref.refs_5_, ...), custom_call_target="tpu_custom_call" | custom-call | flops 335544320 | bytes 5242880 | tf_op jit(solution)/shard_map/ahead/pallas_call | solution.py:209
  26.2 1.5 %collective-permute-done.2.refs_17_ = bf16[1280,128]{1,0:T(8,128)(2,1)S(1)} collective-permute-done((bf16[1280,128]{1,0:T(8,128)(2,1)S(1)}, bf16[1280,128]{1,0:T(8,128)(2,1)S(1)}, u32[]{:S(2)}, u32[]{:S(2)}) %collective-permute-start.2) | collective-permute-done | bytes 327712 | tf_op jit(solution)/shard_map/ppermute | solution.py:572
  27.8 4.2 %attend.6 = (bf16[128,4096]{1,0:T(8,128)(2,1)}, bf16[128,4096]{1,0:T(8,128)(2,1)}, f32[40,128]{1,0:T(8,128)S(1)}, f32[2,128,128]{2,1,0:T(8,128)S(1)}, bf16[6,128,128]{2,1,0:T(8,128)(2,1)S(1)}) custom-call(s32[1]{0:T(128)} %copy.29.first_ref.refs_0_, s32[1]{0:T(128)} %bitcast.2.rank_ref.refs_1_, ...), custom_call_target="tpu_custom_call", output_to_operand_aliasing={{0}: (24, {}), {1}: (25, {})} | custom-call | flops 1476395008 | bytes 2359296 | tf_op jit(solution)/shard_map/attend/pallas_call | solution.py:439
  32.0 1.5 %collective-permute-done.3.refs_17_ = bf16[1280,128]{1,0:T(8,128)(2,1)S(1)} collective-permute-done((bf16[1280,128]{1,0:T(8,128)(2,1)S(1)}, bf16[1280,128]{1,0:T(8,128)(2,1)S(1)}, u32[]{:S(2)}, u32[]{:S(2)}) %collective-permute-start.3) | collective-permute-done | bytes 327712 | tf_op jit(solution)/shard_map/ppermute | solution.py:572
  33.5 3.5 %attend.7 = (bf16[128,1024]{1,0:T(8,128)(2,1)S(1)}, bf16[128,1024]{1,0:T(8,128)(2,1)S(1)}, f32[40,128]{1,0:T(8,128)S(1)}, f32[2,128,128]{2,1,0:T(8,128)S(1)}, bf16[8,128,128]{2,1,0:T(8,128)(2,1)S(1)}) custom-call(s32[1]{0:T(128)} %copy.29.first_ref.refs_0_, s32[1]{0:T(128)} %bitcast.2.rank_ref.refs_1_, bf16[4096,128]{1,0:T(8,128)(2,1)S(1)} %get-tuple-element.62.refs_2_, ...), custom_call_target="tpu_custom_call" | custom-call | flops 1476395008 | bytes 2359296 | tf_op jit(solution)/shard_map/attend/pallas_call | solution.py:439
  36.9 1.3 %collective-permute-start.4 = (bf16[8,128,128]{2,1,0:T(8,128)(2,1)S(1)}, bf16[8,128,128]{2,1,0:T(8,128)(2,1)S(1)}, u32[]{:S(2)}, u32[]{:S(2)}) collective-permute-start(bf16[8,128,128]{2,1,0:T(8,128)(2,1)S(1)} %get-tuple-element.104), channel_id=1, source_target_pairs={{1,0},{3,2},{5,4},{7,6},{9,8},{11,10},{13,12},{15,14},{17,16},{19,... | collective-permute-start | bytes 786440 | tf_op jit(solution)/shard_map/ppermute | solution.py:575
  38.2 0.1 collective-permute-start.5
  38.3 1.2 %collective-permute-done.5 = f32[40,128]{1,0:T(8,128)S(1)} collective-permute-done((f32[40,128]{1,0:T(8,128)S(1)}, f32[40,128]{1,0:T(8,128)S(1)}, u32[]{:S(2)}, u32[]{:S(2)}) %collective-permute-start.5) | collective-permute-done | bytes 20512 | tf_op jit(solution)/shard_map/ppermute | solution.py:561
  39.5 2.8 %collective-permute-start.6 = (f32[40,128]{1,0:T(8,128)S(1)}, f32[40,128]{1,0:T(8,128)S(1)}, u32[]{:S(2)}, u32[]{:S(2)}) collective-permute-start(f32[40,128]{1,0:T(8,128)S(1)} %add.57.refs_0_), channel_id=1, source_target_pairs={{0,16},{1,17},{2,18},{3,19},{4,20},{5,21},{6,22},{7,23},{8,24},{9,... | collective-permute-start | bytes 61448 | tf_op jit(solution)/shard_map/ppermute | solution.py:561
  42.3 1.6 %collective-permute-start.7 = (f32[40,128]{1,0:T(8,128)S(1)}, f32[40,128]{1,0:T(8,128)S(1)}, u32[]{:S(2)}, u32[]{:S(2)}) collective-permute-start(f32[40,128]{1,0:T(8,128)S(1)} %add.57.refs_0_), channel_id=1, source_target_pairs={{0,8},{1,9},{2,10},{3,11},{4,12},{5,13},{6,14},{7,15},{8,0},{9,1},... | collective-permute-start | bytes 61448 | tf_op jit(solution)/shard_map/ppermute | solution.py:561
  43.9 0.0 collective-permute-start.8
  43.9 0.3 collective-permute-done.6.refs_1_
  44.2 1.9 %collective-permute-done.7.refs_2_ = f32[40,128]{1,0:T(8,128)S(1)} collective-permute-done((f32[40,128]{1,0:T(8,128)S(1)}, f32[40,128]{1,0:T(8,128)S(1)}, u32[]{:S(2)}, u32[]{:S(2)}) %collective-permute-start.7) | collective-permute-done | bytes 20512 | tf_op jit(solution)/shard_map/ppermute | solution.py:561
  46.1 3.4 %collective-permute-done.8.refs_3_ = f32[40,128]{1,0:T(8,128)S(1)} collective-permute-done((f32[40,128]{1,0:T(8,128)S(1)}, f32[40,128]{1,0:T(8,128)S(1)}, u32[]{:S(2)}, u32[]{:S(2)}) %collective-permute-start.8) | collective-permute-done | bytes 20512 | tf_op jit(solution)/shard_map/ppermute | solution.py:561
  49.5 0.0 collective-permute-done.4.refs_6_.refs_4_
  49.5 1.6 %collective-permute-start.9 = (f32[40,128]{1,0:T(8,128)S(1)}, f32[40,128]{1,0:T(8,128)S(1)}, u32[]{:S(2)}, u32[]{:S(2)}) collective-permute-start(f32[40,128]{1,0:T(8,128)S(1)} %join.1.refs_0_), channel_id=1, source_target_pairs={{0,4},{1,5},{2,6},{3,7},{4,0},{5,1},{6,2},{7,3},{8,12},{9,13},{10,... | collective-permute-start | bytes 61448 | tf_op jit(solution)/shard_map/ppermute | solution.py:561
  51.0 2.7 %collective-permute-start.10 = (f32[40,128]{1,0:T(8,128)S(1)}, f32[40,128]{1,0:T(8,128)S(1)}, u32[]{:S(2)}, u32[]{:S(2)}) collective-permute-start(f32[40,128]{1,0:T(8,128)S(1)} %join.1.refs_0_), channel_id=1, source_target_pairs={{0,1},{1,0},{2,3},{3,2},{4,5},{5,4},{6,7},{7,6},{8,9},{9,8},{10,11... | collective-permute-start | bytes 61448 | tf_op jit(solution)/shard_map/ppermute | solution.py:561
  53.7 0.0 collective-permute-start.11
  53.7 1.0 %finish.1 = (bf16[128,4096]{1,0:T(8,128)(2,1)}, bf16[128,4096]{1,0:T(8,128)(2,1)}, bf16[128,512]{1,0:T(8,128)(2,1)}, bf16[128,512]{1,0:T(8,128)(2,1)}) custom-call(f32[256,128]{1,0:T(8,128)S(1)} %get-tuple-element.118.cos_ref.refs_11_.refs_0_, ...), custom_call_target="tpu_custom_call", output_to_operand_aliasing={{0}: (9, {}), {1}: (10, {})} | custom-call | bytes 2097152 | tf_op jit(solution)/shard_map/finish/pallas_call | solution.py:490
  54.7 0.0 collective-permute-done.9.refs_1_
  54.7 0.9 %collective-permute-done.10.refs_2_ = f32[40,128]{1,0:T(8,128)S(1)} collective-permute-done((f32[40,128]{1,0:T(8,128)S(1)}, f32[40,128]{1,0:T(8,128)S(1)}, u32[]{:S(2)}, u32[]{:S(2)}) %collective-permute-start.10) | collective-permute-done | bytes 20512 | tf_op jit(solution)/shard_map/ppermute | solution.py:561
  55.5 2.8 %collective-permute-done.11.refs_3_ = f32[40,128]{1,0:T(8,128)S(1)} collective-permute-done((f32[40,128]{1,0:T(8,128)S(1)}, f32[40,128]{1,0:T(8,128)S(1)}, u32[]{:S(2)}, u32[]{:S(2)}) %collective-permute-start.11) | collective-permute-done | bytes 20512 | tf_op jit(solution)/shard_map/ppermute | solution.py:561
  58.4 0.6 %sums.1 = (f32[32,128]{1,0:T(8,128)}, f32[4,128]{1,0:T(4,128)}, f32[4,128]{1,0:T(4,128)}) custom-call(f32[40,128]{1,0:T(8,128)S(1)} %join.1.refs_0_, f32[40,128]{1,0:T(8,128)S(1)} %collective-permute-done.9.refs_1_, f32[40,128]{1,0:T(8,128)S(1)} %collective-permute-done.10.refs_2_, f32[40,128]{1,0:T(8,128)S(1)} %collective-permute-done.11.refs_3_, ...), custom_call_target="tpu_custom_call" | custom-call | bytes 131072 | tf_op jit(solution)/shard_map/sums/pallas_call | solution.py:515
  (4 shorter events, 0.0 us)
Async XLA Ops:
  1.6 11.2 %collective-permute-start = (bf16[1280,128]{1,0:T(8,128)(2,1)S(1)}, bf16[1280,128]{1,0:T(8,128)(2,1)S(1)}, u32[]{:S(2)}, u32[]{:S(2)}) collective-permute-start(bf16[1280,128]{1,0:T(8,128)(2,1)S(1)} %pack.1), channel_id=1, source_target_pairs={{0,1},{1,0},{2,3},{3,2},{4,5},{5,4},{6,7},{7,6},{8,9},{9,8},{10,11... | collective-permute-start | bytes 983048 | tf_op jit(solution)/shard_map/ppermute | solution.py:572
  10.2 9.4 %collective-permute-start.1 = (bf16[1280,128]{1,0:T(8,128)(2,1)S(1)}, bf16[1280,128]{1,0:T(8,128)(2,1)S(1)}, u32[]{:S(2)}, u32[]{:S(2)}) collective-permute-start(bf16[1280,128]{1,0:T(8,128)(2,1)S(1)} %get-tuple-element.80), channel_id=1, source_target_pairs={{0,1},{1,0},{2,3},{3,2},{4,5},{5,4},{6,7},{7,6},{8,9},{9,8},{10,11... | collective-permute-start | bytes 983048 | tf_op jit(solution)/shard_map/ppermute | solution.py:572
  17.0 10.8 %collective-permute-start.2 = (bf16[1280,128]{1,0:T(8,128)(2,1)S(1)}, bf16[1280,128]{1,0:T(8,128)(2,1)S(1)}, u32[]{:S(2)}, u32[]{:S(2)}) collective-permute-start(bf16[1280,128]{1,0:T(8,128)(2,1)S(1)} %get-tuple-element.89), channel_id=1, source_target_pairs={{0,1},{1,0},{2,3},{3,2},{4,5},{5,4},{6,7},{7,6},{8,9},{9,8},{10,11... | collective-permute-start | bytes 983048 | tf_op jit(solution)/shard_map/ppermute | solution.py:572
  23.7 9.8 %collective-permute-start.3 = (bf16[1280,128]{1,0:T(8,128)(2,1)S(1)}, bf16[1280,128]{1,0:T(8,128)(2,1)S(1)}, u32[]{:S(2)}, u32[]{:S(2)}) collective-permute-start(bf16[1280,128]{1,0:T(8,128)(2,1)S(1)} %get-tuple-element.98), channel_id=1, source_target_pairs={{0,1},{1,0},{2,3},{3,2},{4,5},{5,4},{6,7},{7,6},{8,9},{9,8},{10,11... | collective-permute-start | bytes 983048 | tf_op jit(solution)/shard_map/ppermute | solution.py:572
  36.9 12.5 %collective-permute-start.4 = (bf16[8,128,128]{2,1,0:T(8,128)(2,1)S(1)}, bf16[8,128,128]{2,1,0:T(8,128)(2,1)S(1)}, u32[]{:S(2)}, u32[]{:S(2)}) collective-permute-start(bf16[8,128,128]{2,1,0:T(8,128)(2,1)S(1)} %get-tuple-element.104), channel_id=1, source_target_pairs={{1,0},{3,2},{5,4},{7,6},{9,8},{11,10},{13,12},{15,14},{17,16},{19,... | collective-permute-start | bytes 786440 | tf_op jit(solution)/shard_map/ppermute | solution.py:575
  38.2 1.3 %collective-permute-start.5 = (f32[40,128]{1,0:T(8,128)S(1)}, f32[40,128]{1,0:T(8,128)S(1)}, u32[]{:S(2)}, u32[]{:S(2)}) collective-permute-start(f32[40,128]{1,0:T(8,128)S(1)} %get-tuple-element.113), channel_id=1, source_target_pairs={{0,2},{1,3},{2,0},{3,1},{4,6},{5,7},{6,4},{7,5},{8,10},{9,11},{10,... | collective-permute-start | bytes 61448 | tf_op jit(solution)/shard_map/ppermute | solution.py:561
  39.5 4.7 %collective-permute-start.6 = (f32[40,128]{1,0:T(8,128)S(1)}, f32[40,128]{1,0:T(8,128)S(1)}, u32[]{:S(2)}, u32[]{:S(2)}) collective-permute-start(f32[40,128]{1,0:T(8,128)S(1)} %add.57.refs_0_), channel_id=1, source_target_pairs={{0,16},{1,17},{2,18},{3,19},{4,20},{5,21},{6,22},{7,23},{8,24},{9,... | collective-permute-start | bytes 61448 | tf_op jit(solution)/shard_map/ppermute | solution.py:561
  42.3 3.8 %collective-permute-start.7 = (f32[40,128]{1,0:T(8,128)S(1)}, f32[40,128]{1,0:T(8,128)S(1)}, u32[]{:S(2)}, u32[]{:S(2)}) collective-permute-start(f32[40,128]{1,0:T(8,128)S(1)} %add.57.refs_0_), channel_id=1, source_target_pairs={{0,8},{1,9},{2,10},{3,11},{4,12},{5,13},{6,14},{7,15},{8,0},{9,1},... | collective-permute-start | bytes 61448 | tf_op jit(solution)/shard_map/ppermute | solution.py:561
  43.9 5.6 %collective-permute-start.8 = (f32[40,128]{1,0:T(8,128)S(1)}, f32[40,128]{1,0:T(8,128)S(1)}, u32[]{:S(2)}, u32[]{:S(2)}) collective-permute-start(f32[40,128]{1,0:T(8,128)S(1)} %add.57.refs_0_), channel_id=1, source_target_pairs={{0,24},{1,25},{2,26},{3,27},{4,28},{5,29},{6,30},{7,31},{8,16},{9,... | collective-permute-start | bytes 61448 | tf_op jit(solution)/shard_map/ppermute | solution.py:561
  49.5 5.2 %collective-permute-start.9 = (f32[40,128]{1,0:T(8,128)S(1)}, f32[40,128]{1,0:T(8,128)S(1)}, u32[]{:S(2)}, u32[]{:S(2)}) collective-permute-start(f32[40,128]{1,0:T(8,128)S(1)} %join.1.refs_0_), channel_id=1, source_target_pairs={{0,4},{1,5},{2,6},{3,7},{4,0},{5,1},{6,2},{7,3},{8,12},{9,13},{10,... | collective-permute-start | bytes 61448 | tf_op jit(solution)/shard_map/ppermute | solution.py:561
  51.0 4.5 %collective-permute-start.10 = (f32[40,128]{1,0:T(8,128)S(1)}, f32[40,128]{1,0:T(8,128)S(1)}, u32[]{:S(2)}, u32[]{:S(2)}) collective-permute-start(f32[40,128]{1,0:T(8,128)S(1)} %join.1.refs_0_), channel_id=1, source_target_pairs={{0,1},{1,0},{2,3},{3,2},{4,5},{5,4},{6,7},{7,6},{8,9},{9,8},{10,11... | collective-permute-start | bytes 61448 | tf_op jit(solution)/shard_map/ppermute | solution.py:561
  53.7 4.7 %collective-permute-start.11 = (f32[40,128]{1,0:T(8,128)S(1)}, f32[40,128]{1,0:T(8,128)S(1)}, u32[]{:S(2)}, u32[]{:S(2)}) collective-permute-start(f32[40,128]{1,0:T(8,128)S(1)} %join.1.refs_0_), channel_id=1, source_target_pairs={{0,5},{1,4},{2,7},{3,6},{4,1},{5,0},{6,3},{7,2},{8,13},{9,12},{10,... | collective-permute-start | bytes 61448 | tf_op jit(solution)/shard_map/ppermute | solution.py:561

commit v17 on v13

--- a/solution.py
+++ b/solution.py
@@ -533,7 +533,7 @@
 
 def sum_but_last(x, axes, near):
     devices = lax.axis_size(axes)
-    bits = [1 << i for i in reversed(range(devices.bit_length() - 1)) if 1 << i != near]
+    bits = [1 << i for i in range(devices.bit_length() - 1) if 1 << i != near]
     stages = [[near]] + [bits[i:i + 2] for i in range(0, len(bits), 2)]
     parts = [x]
     for stage in stages:

time: 55.7 us -> 55.8 us (level)
    ppermute x7, waiting for transfers between devices: 5.67 us -> 6.25 us  [sum_but_last(): parts.append(lax.ppermute(x, axes, [(i, i ^ flip) for i in range(devices)]))]
where the time goes in v17:
time: 55.8 us; the launch traced here: 55.6 us
  Pallas kernels  26.1 us (47%)
  starting transfers between devices  16.5 us (30%)
  waiting for transfers between devices  11 us (20%)
  between operations  1.38 us (2%)
  other arithmetic  0.64 us (1%)
    pallas_call x4, Pallas kernels, attend(): pl.pallas_call(functools.partial(attend_kernel, g, shards), grid=(1,), in...  15.9 us
    ppermute x7, starting transfers between devices, sum_but_last(): parts.append(lax.ppermute(x, axes, [(i, i ^ flip) for i in range(devices)]))  8.01 us
    ppermute x4, starting transfers between devices, ring(): lax.ppermute(x, 'seq', [(i, (i + s) % shards) for i in range(shards)])  7.25 us
    ppermute x7, waiting for transfers between devices, sum_but_last(): parts.append(lax.ppermute(x, axes, [(i, i ^ flip) for i in range(devices)]))  6.25 us
    pallas_call x1, Pallas kernels, prep(): pl.pallas_call(prep_kernel, grid=(KV,), in_specs=[wide, wide, pl.BlockSpe...  4.2 us
    pallas_call x4, Pallas kernels, look_ahead(): pl.pallas_call(functools.partial(ahead_kernel, g, shards), grid=(1,), in_...  3.4 us
    ppermute x4, waiting for transfers between devices, ring(): lax.ppermute(x, 'seq', [(i, (i + s) % shards) for i in range(shards)])  3.22 us
    ppermute x1, waiting for transfers between devices, earlier(): return lax.ppermute(x, 'seq', [(i + s, i) for i in range(shards - s)])  1.5 us
  transfers between devices with their start and end apart: 12, of which 8 were waited for; matrix products, arithmetic and copies ran while one was open for 1% of the time, Pallas kernels for 38%

profile of v17, /device:TPU:0, one launch (start us, length us, event | category | flops | bytes accessed | tf_op | source)
XLA Modules:
  0.0 55.6 jit_solution(4737244211309499695)
XLA Ops:
  0.6 1.0 %pack.1 = bf16[1280,128]{1,0:T(8,128)(2,1)S(1)} custom-call(bf16[512,512]{1,0:T(8,128)(2,1)} %bitcast.23, bf16[512,512]{1,0:T(8,128)(2,1)} %bitcast.25, bf16[128,512]{1,0:T(8,128)(2,1)} %bitcast.29, bf16[128,512]{1,0:T(8,128)(2,1)} %bitcast.31), custom_call_target="tpu_custom_call" | custom-call | bytes 655360 | tf_op jit(solution)/shard_map/pack/pallas_call | solution.py:60
  1.6 3.0 %collective-permute-start = (bf16[1280,128]{1,0:T(8,128)(2,1)S(1)}, bf16[1280,128]{1,0:T(8,128)(2,1)S(1)}, u32[]{:S(2)}, u32[]{:S(2)}) collective-permute-start(bf16[1280,128]{1,0:T(8,128)(2,1)S(1)} %pack.1), channel_id=1, source_target_pairs={{0,1},{1,0},{2,3},{3,2},{4,5},{5,4},{6,7},{7,6},{8,9},{9,8},{10,11... | collective-permute-start | bytes 983048 | tf_op jit(solution)/shard_map/ppermute | solution.py:554
  5.3 0.1 convert_bitcast_fusion
  5.4 0.5 fusion
  6.0 4.2 %prep.1 = (bf16[4096,128]{1,0:T(8,128)(2,1)S(1)}, bf16[1024,512]{1,0:T(8,128)(2,1)S(1)}, bf16[4096,128]{1,0:T(8,128)(2,1)S(1)}, bf16[1024,512]{1,0:T(8,128)(2,1)...) custom-call(bf16[128,4096]{1,0:T(8,128)(2,1)} %bitcast.27, ...), custom_call_target="tpu_custom_call" | custom-call | flops 2097152 | bytes 6291456 | tf_op jit(solution)/shard_map/prep/pallas_call | solution.py:133
  10.2 0.1 collective-permute-start.1
  10.3 0.9 %ahead.4 = (f32[2,640,512]{2,1,0:T(8,128)S(1)}, f32[2,640,512]{2,1,0:T(8,128)S(1)}, f32[2,8,512]{2,1,0:T(8,128)S(1)}) custom-call(s32[1]{0:T(128)} %copy.29.first_ref.refs_0_, s32[1]{0:T(128)} %bitcast.2.rank_ref.refs_1_, bf16[1024,512]{1,0:T(8,128)(2,1)S(1)} %get-tuple-element.63.qst_ref.refs_3_, bf16[1024,512]{1,0:T(8,128)(2,1)S(1)} %get-tuple-element.65.dot_ref.refs_5_, ...), custom_call_target="tpu_custom_call" | custom-call | flops 335544320 | bytes 5242880 | tf_op jit(solution)/shard_map/ahead/pallas_call | solution.py:209
  11.1 0.9 %ahead.5 = (f32[2,640,512]{2,1,0:T(8,128)S(1)}, f32[2,640,512]{2,1,0:T(8,128)S(1)}, f32[2,8,512]{2,1,0:T(8,128)S(1)}) custom-call(s32[1]{0:T(128)} %copy.29.first_ref.refs_0_, s32[1]{0:T(128)} %bitcast.2.rank_ref.refs_1_, bf16[1024,512]{1,0:T(8,128)(2,1)S(1)} %get-tuple-element.63.qst_ref.refs_3_, bf16[1024,512]{1,0:T(8,128)(2,1)S(1)} %get-tuple-element.65.dot_ref.refs_5_, ...), custom_call_target="tpu_custom_call" | custom-call | flops 335544320 | bytes 5242880 | tf_op jit(solution)/shard_map/ahead/pallas_call | solution.py:209
  12.0 0.9 %ahead.6 = (f32[2,640,512]{2,1,0:T(8,128)S(1)}, f32[2,640,512]{2,1,0:T(8,128)S(1)}, f32[2,8,512]{2,1,0:T(8,128)S(1)}) custom-call(s32[1]{0:T(128)} %copy.29.first_ref.refs_0_, s32[1]{0:T(128)} %bitcast.2.rank_ref.refs_1_, bf16[1024,512]{1,0:T(8,128)(2,1)S(1)} %get-tuple-element.63.qst_ref.refs_3_, bf16[1024,512]{1,0:T(8,128)(2,1)S(1)} %get-tuple-element.65.dot_ref.refs_5_, ...), custom_call_target="tpu_custom_call" | custom-call | flops 335544320 | bytes 5242880 | tf_op jit(solution)/shard_map/ahead/pallas_call | solution.py:209
  12.8 0.0 collective-permute-done.refs_17_
  12.8 4.2 %attend.4 = (bf16[128,4096]{1,0:T(8,128)(2,1)}, bf16[128,4096]{1,0:T(8,128)(2,1)}, f32[40,128]{1,0:T(8,128)S(1)}, f32[2,128,128]{2,1,0:T(8,128)S(1)}, bf16[2,128...) custom-call(s32[1]{0:T(128)} %copy.29.first_ref.refs_0_, s32[1]{0:T(128)} %bitcast.2.rank_ref.refs_1_, ...), custom_call_target="tpu_custom_call" | custom-call | flops 1476395008 | bytes 2359296 | tf_op jit(solution)/shard_map/attend/pallas_call | solution.py:439
  17.0 2.4 %collective-permute-start.2 = (bf16[1280,128]{1,0:T(8,128)(2,1)S(1)}, bf16[1280,128]{1,0:T(8,128)(2,1)S(1)}, u32[]{:S(2)}, u32[]{:S(2)}) collective-permute-start(bf16[1280,128]{1,0:T(8,128)(2,1)S(1)} %get-tuple-element.89), channel_id=1, source_target_pairs={{0,1},{1,0},{2,3},{3,2},{4,5},{5,4},{6,7},{7,6},{8,9},{9,8},{10,11... | collective-permute-start | bytes 983048 | tf_op jit(solution)/shard_map/ppermute | solution.py:554
  19.4 0.2 collective-permute-done.1.refs_17_
  19.6 4.1 %attend.5 = (bf16[128,4096]{1,0:T(8,128)(2,1)}, bf16[128,4096]{1,0:T(8,128)(2,1)}, f32[40,128]{1,0:T(8,128)S(1)}, f32[2,128,128]{2,1,0:T(8,128)S(1)}, bf16[4,128...) custom-call(s32[1]{0:T(128)} %copy.29.first_ref.refs_0_, ...), custom_call_target="tpu_custom_call", output_to_operand_aliasing={{0}: (24, {}), {1}: (25, {})} | custom-call | flops 1476395008 | bytes 2359296 | tf_op jit(solution)/shard_map/attend/pallas_call | solution.py:439
  23.7 1.7 %collective-permute-start.3 = (bf16[1280,128]{1,0:T(8,128)(2,1)S(1)}, bf16[1280,128]{1,0:T(8,128)(2,1)S(1)}, u32[]{:S(2)}, u32[]{:S(2)}) collective-permute-start(bf16[1280,128]{1,0:T(8,128)(2,1)S(1)} %get-tuple-element.98), channel_id=1, source_target_pairs={{0,1},{1,0},{2,3},{3,2},{4,5},{5,4},{6,7},{7,6},{8,9},{9,8},{10,11... | collective-permute-start | bytes 983048 | tf_op jit(solution)/shard_map/ppermute | solution.py:554
  25.4 0.8 %ahead.7 = (f32[2,640,512]{2,1,0:T(8,128)S(1)}, f32[2,640,512]{2,1,0:T(8,128)S(1)}, f32[2,8,512]{2,1,0:T(8,128)S(1)}) custom-call(s32[1]{0:T(128)} %copy.29.first_ref.refs_0_, s32[1]{0:T(128)} %bitcast.2.rank_ref.refs_1_, bf16[1024,512]{1,0:T(8,128)(2,1)S(1)} %get-tuple-element.63.qst_ref.refs_3_, bf16[1024,512]{1,0:T(8,128)(2,1)S(1)} %get-tuple-element.65.dot_ref.refs_5_, ...), custom_call_target="tpu_custom_call" | custom-call | flops 335544320 | bytes 5242880 | tf_op jit(solution)/shard_map/ahead/pallas_call | solution.py:209
  26.2 1.5 %collective-permute-done.2.refs_17_ = bf16[1280,128]{1,0:T(8,128)(2,1)S(1)} collective-permute-done((bf16[1280,128]{1,0:T(8,128)(2,1)S(1)}, bf16[1280,128]{1,0:T(8,128)(2,1)S(1)}, u32[]{:S(2)}, u32[]{:S(2)}) %collective-permute-start.2) | collective-permute-done | bytes 327712 | tf_op jit(solution)/shard_map/ppermute | solution.py:554
  27.8 4.2 %attend.6 = (bf16[128,4096]{1,0:T(8,128)(2,1)}, bf16[128,4096]{1,0:T(8,128)(2,1)}, f32[40,128]{1,0:T(8,128)S(1)}, f32[2,128,128]{2,1,0:T(8,128)S(1)}, bf16[6,128,128]{2,1,0:T(8,128)(2,1)S(1)}) custom-call(s32[1]{0:T(128)} %copy.29.first_ref.refs_0_, s32[1]{0:T(128)} %bitcast.2.rank_ref.refs_1_, ...), custom_call_target="tpu_custom_call", output_to_operand_aliasing={{0}: (24, {}), {1}: (25, {})} | custom-call | flops 1476395008 | bytes 2359296 | tf_op jit(solution)/shard_map/attend/pallas_call | solution.py:439
  32.0 1.5 %collective-permute-done.3.refs_17_ = bf16[1280,128]{1,0:T(8,128)(2,1)S(1)} collective-permute-done((bf16[1280,128]{1,0:T(8,128)(2,1)S(1)}, bf16[1280,128]{1,0:T(8,128)(2,1)S(1)}, u32[]{:S(2)}, u32[]{:S(2)}) %collective-permute-start.3) | collective-permute-done | bytes 327712 | tf_op jit(solution)/shard_map/ppermute | solution.py:554
  33.5 3.5 %attend.7 = (bf16[128,1024]{1,0:T(8,128)(2,1)S(1)}, bf16[128,1024]{1,0:T(8,128)(2,1)S(1)}, f32[40,128]{1,0:T(8,128)S(1)}, f32[2,128,128]{2,1,0:T(8,128)S(1)}, bf16[8,128,128]{2,1,0:T(8,128)(2,1)S(1)}) custom-call(s32[1]{0:T(128)} %copy.29.first_ref.refs_0_, s32[1]{0:T(128)} %bitcast.2.rank_ref.refs_1_, bf16[4096,128]{1,0:T(8,128)(2,1)S(1)} %get-tuple-element.62.refs_2_, ...), custom_call_target="tpu_custom_call" | custom-call | flops 1476395008 | bytes 2359296 | tf_op jit(solution)/shard_map/attend/pallas_call | solution.py:439
  36.9 0.1 collective-permute-start.5
  37.0 1.2 %collective-permute-done.5 = f32[40,128]{1,0:T(8,128)S(1)} collective-permute-done((f32[40,128]{1,0:T(8,128)S(1)}, f32[40,128]{1,0:T(8,128)S(1)}, u32[]{:S(2)}, u32[]{:S(2)}) %collective-permute-start.5) | collective-permute-done | bytes 20512 | tf_op jit(solution)/shard_map/ppermute | solution.py:543
  38.2 1.7 %collective-permute-start.7 = (f32[40,128]{1,0:T(8,128)S(1)}, f32[40,128]{1,0:T(8,128)S(1)}, u32[]{:S(2)}, u32[]{:S(2)}) collective-permute-start(f32[40,128]{1,0:T(8,128)S(1)} %add.66), channel_id=1, source_target_pairs={{0,4},{1,5},{2,6},{3,7},{4,0},{5,1},{6,2},{7,3},{8,12},{9,13},{10,... | collective-permute-start | bytes 61448 | tf_op jit(solution)/shard_map/ppermute | solution.py:543
  39.9 1.5 %collective-permute-start.8 = (f32[40,128]{1,0:T(8,128)S(1)}, f32[40,128]{1,0:T(8,128)S(1)}, u32[]{:S(2)}, u32[]{:S(2)}) collective-permute-start(f32[40,128]{1,0:T(8,128)S(1)} %add.66), channel_id=1, source_target_pairs={{0,5},{1,4},{2,7},{3,6},{4,1},{5,0},{6,3},{7,2},{8,13},{9,12},{10,... | collective-permute-start | bytes 61448 | tf_op jit(solution)/shard_map/ppermute | solution.py:543
  41.4 0.3 collective-permute-start.6
  41.7 1.3 %collective-permute-start.4 = (bf16[8,128,128]{2,1,0:T(8,128)(2,1)S(1)}, bf16[8,128,128]{2,1,0:T(8,128)(2,1)S(1)}, u32[]{:S(2)}, u32[]{:S(2)}) collective-permute-start(bf16[8,128,128]{2,1,0:T(8,128)(2,1)S(1)} %get-tuple-element.104), channel_id=1, source_target_pairs={{1,0},{3,2},{5,4},{7,6},{9,8},{11,10},{13,12},{15,14},{17,16},{19,... | collective-permute-start | bytes 786440 | tf_op jit(solution)/shard_map/ppermute | solution.py:557
  43.0 0.0 collective-permute-done.7
  43.0 1.6 %collective-permute-done.8 = f32[40,128]{1,0:T(8,128)S(1)} collective-permute-done((f32[40,128]{1,0:T(8,128)S(1)}, f32[40,128]{1,0:T(8,128)S(1)}, u32[]{:S(2)}, u32[]{:S(2)}) %collective-permute-start.8) | collective-permute-done | bytes 20512 | tf_op jit(solution)/shard_map/ppermute | solution.py:543
  44.6 0.6 %collective-permute-done.6 = f32[40,128]{1,0:T(8,128)S(1)} collective-permute-done((f32[40,128]{1,0:T(8,128)S(1)}, f32[40,128]{1,0:T(8,128)S(1)}, u32[]{:S(2)}, u32[]{:S(2)}) %collective-permute-start.6) | collective-permute-done | bytes 20512 | tf_op jit(solution)/shard_map/ppermute | solution.py:543
  45.2 1.6 %collective-permute-start.9 = (f32[40,128]{1,0:T(8,128)S(1)}, f32[40,128]{1,0:T(8,128)S(1)}, u32[]{:S(2)}, u32[]{:S(2)}) collective-permute-start(f32[40,128]{1,0:T(8,128)S(1)} %add_add_fusion.refs_0_), channel_id=1, source_target_pairs={{0,8},{1,9},{2,10},{3,11},{4,12},{5,13},{6,14},{7,15},{8,0},{9,1},... | collective-permute-start | bytes 61448 | tf_op jit(solution)/shard_map/ppermute | solution.py:543
  46.8 2.6 %collective-permute-start.10 = (f32[40,128]{1,0:T(8,128)S(1)}, f32[40,128]{1,0:T(8,128)S(1)}, u32[]{:S(2)}, u32[]{:S(2)}) collective-permute-start(f32[40,128]{1,0:T(8,128)S(1)} %add_add_fusion.refs_0_), channel_id=1, source_target_pairs={{0,16},{1,17},{2,18},{3,19},{4,20},{5,21},{6,22},{7,23},{8,24},{9,... | collective-permute-start | bytes 61448 | tf_op jit(solution)/shard_map/ppermute | solution.py:543
  49.4 0.2 collective-permute-start.11
  49.6 1.5 %collective-permute-done.4.refs_6_ = bf16[8,128,128]{2,1,0:T(8,128)(2,1)S(1)} collective-permute-done((bf16[8,128,128]{2,1,0:T(8,128)(2,1)S(1)}, bf16[8,128,128]{2,1,0:T(8,128)(2,1)S(1)}, u32[]{:S(2)}, u32[]{:S(2)}) %collective-permute-start.4) | collective-permute-done | bytes 262176 | tf_op jit(solution)/shard_map/ppermute | solution.py:557
  51.1 1.0 %finish.1 = (bf16[128,4096]{1,0:T(8,128)(2,1)}, bf16[128,4096]{1,0:T(8,128)(2,1)}, bf16[128,512]{1,0:T(8,128)(2,1)}, bf16[128,512]{1,0:T(8,128)(2,1)}) custom-call(f32[256,128]{1,0:T(8,128)S(1)} %get-tuple-element.118.cos_ref.refs_11_.refs_0_, ...), custom_call_target="tpu_custom_call", output_to_operand_aliasing={{0}: (9, {}), {1}: (10, {})} | custom-call | bytes 2097152 | tf_op jit(solution)/shard_map/finish/pallas_call | solution.py:490
  52.1 0.0 collective-permute-done.9.refs_1_
  52.1 0.0 collective-permute-done.10.refs_2_
  52.1 2.9 %collective-permute-done.11.refs_3_ = f32[40,128]{1,0:T(8,128)S(1)} collective-permute-done((f32[40,128]{1,0:T(8,128)S(1)}, f32[40,128]{1,0:T(8,128)S(1)}, u32[]{:S(2)}, u32[]{:S(2)}) %collective-permute-start.11) | collective-permute-done | bytes 20512 | tf_op jit(solution)/shard_map/ppermute | solution.py:543
  55.0 0.6 %sums.1 = (f32[32,128]{1,0:T(8,128)}, f32[4,128]{1,0:T(4,128)}, f32[4,128]{1,0:T(4,128)}) custom-call(f32[40,128]{1,0:T(8,128)S(1)} %add_add_fusion.refs_0_, f32[40,128]{1,0:T(8,128)S(1)} %collective-permute-done.9.refs_1_, f32[40,128]{1,0:T(8,128)S(1)} %collective-permute-done.10.refs_2_, f32[40,128]{1,0:T(8,128)S(1)} %collective-permute-done.11.refs_3_, ...), custom_call_target="tpu_custom_call" | custom-call | bytes 131072 | tf_op jit(solution)/shard_map/sums/pallas_call | solution.py:515
  (4 shorter events, 0.0 us)
Async XLA Ops:
  1.6 11.2 %collective-permute-start = (bf16[1280,128]{1,0:T(8,128)(2,1)S(1)}, bf16[1280,128]{1,0:T(8,128)(2,1)S(1)}, u32[]{:S(2)}, u32[]{:S(2)}) collective-permute-start(bf16[1280,128]{1,0:T(8,128)(2,1)S(1)} %pack.1), channel_id=1, source_target_pairs={{0,1},{1,0},{2,3},{3,2},{4,5},{5,4},{6,7},{7,6},{8,9},{9,8},{10,11... | collective-permute-start | bytes 983048 | tf_op jit(solution)/shard_map/ppermute | solution.py:554
  10.2 9.4 %collective-permute-start.1 = (bf16[1280,128]{1,0:T(8,128)(2,1)S(1)}, bf16[1280,128]{1,0:T(8,128)(2,1)S(1)}, u32[]{:S(2)}, u32[]{:S(2)}) collective-permute-start(bf16[1280,128]{1,0:T(8,128)(2,1)S(1)} %get-tuple-element.80), channel_id=1, source_target_pairs={{0,1},{1,0},{2,3},{3,2},{4,5},{5,4},{6,7},{7,6},{8,9},{9,8},{10,11... | collective-permute-start | bytes 983048 | tf_op jit(solution)/shard_map/ppermute | solution.py:554
  17.0 10.8 %collective-permute-start.2 = (bf16[1280,128]{1,0:T(8,128)(2,1)S(1)}, bf16[1280,128]{1,0:T(8,128)(2,1)S(1)}, u32[]{:S(2)}, u32[]{:S(2)}) collective-permute-start(bf16[1280,128]{1,0:T(8,128)(2,1)S(1)} %get-tuple-element.89), channel_id=1, source_target_pairs={{0,1},{1,0},{2,3},{3,2},{4,5},{5,4},{6,7},{7,6},{8,9},{9,8},{10,11... | collective-permute-start | bytes 983048 | tf_op jit(solution)/shard_map/ppermute | solution.py:554
  23.7 9.8 %collective-permute-start.3 = (bf16[1280,128]{1,0:T(8,128)(2,1)S(1)}, bf16[1280,128]{1,0:T(8,128)(2,1)S(1)}, u32[]{:S(2)}, u32[]{:S(2)}) collective-permute-start(bf16[1280,128]{1,0:T(8,128)(2,1)S(1)} %get-tuple-element.98), channel_id=1, source_target_pairs={{0,1},{1,0},{2,3},{3,2},{4,5},{5,4},{6,7},{7,6},{8,9},{9,8},{10,11... | collective-permute-start | bytes 983048 | tf_op jit(solution)/shard_map/ppermute | solution.py:554
  36.9 1.3 %collective-permute-start.5 = (f32[40,128]{1,0:T(8,128)S(1)}, f32[40,128]{1,0:T(8,128)S(1)}, u32[]{:S(2)}, u32[]{:S(2)}) collective-permute-start(f32[40,128]{1,0:T(8,128)S(1)} %get-tuple-element.113), channel_id=1, source_target_pairs={{0,2},{1,3},{2,0},{3,1},{4,6},{5,7},{6,4},{7,5},{8,10},{9,11},{10,... | collective-permute-start | bytes 61448 | tf_op jit(solution)/shard_map/ppermute | solution.py:543
  38.2 4.8 %collective-permute-start.7 = (f32[40,128]{1,0:T(8,128)S(1)}, f32[40,128]{1,0:T(8,128)S(1)}, u32[]{:S(2)}, u32[]{:S(2)}) collective-permute-start(f32[40,128]{1,0:T(8,128)S(1)} %add.66), channel_id=1, source_target_pairs={{0,4},{1,5},{2,6},{3,7},{4,0},{5,1},{6,2},{7,3},{8,12},{9,13},{10,... | collective-permute-start | bytes 61448 | tf_op jit(solution)/shard_map/ppermute | solution.py:543
  39.9 4.7 %collective-permute-start.8 = (f32[40,128]{1,0:T(8,128)S(1)}, f32[40,128]{1,0:T(8,128)S(1)}, u32[]{:S(2)}, u32[]{:S(2)}) collective-permute-start(f32[40,128]{1,0:T(8,128)S(1)} %add.66), channel_id=1, source_target_pairs={{0,5},{1,4},{2,7},{3,6},{4,1},{5,0},{6,3},{7,2},{8,13},{9,12},{10,... | collective-permute-start | bytes 61448 | tf_op jit(solution)/shard_map/ppermute | solution.py:543
  41.4 3.8 %collective-permute-start.6 = (f32[40,128]{1,0:T(8,128)S(1)}, f32[40,128]{1,0:T(8,128)S(1)}, u32[]{:S(2)}, u32[]{:S(2)}) collective-permute-start(f32[40,128]{1,0:T(8,128)S(1)} %add.66), channel_id=1, source_target_pairs={{0,1},{1,0},{2,3},{3,2},{4,5},{5,4},{6,7},{7,6},{8,9},{9,8},{10,11... | collective-permute-start | bytes 61448 | tf_op jit(solution)/shard_map/ppermute | solution.py:543
  41.7 9.4 %collective-permute-start.4 = (bf16[8,128,128]{2,1,0:T(8,128)(2,1)S(1)}, bf16[8,128,128]{2,1,0:T(8,128)(2,1)S(1)}, u32[]{:S(2)}, u32[]{:S(2)}) collective-permute-start(bf16[8,128,128]{2,1,0:T(8,128)(2,1)S(1)} %get-tuple-element.104), channel_id=1, source_target_pairs={{1,0},{3,2},{5,4},{7,6},{9,8},{11,10},{13,12},{15,14},{17,16},{19,... | collective-permute-start | bytes 786440 | tf_op jit(solution)/shard_map/ppermute | solution.py:557
  45.2 6.9 %collective-permute-start.9 = (f32[40,128]{1,0:T(8,128)S(1)}, f32[40,128]{1,0:T(8,128)S(1)}, u32[]{:S(2)}, u32[]{:S(2)}) collective-permute-start(f32[40,128]{1,0:T(8,128)S(1)} %add_add_fusion.refs_0_), channel_id=1, source_target_pairs={{0,8},{1,9},{2,10},{3,11},{4,12},{5,13},{6,14},{7,15},{8,0},{9,1},... | collective-permute-start | bytes 61448 | tf_op jit(solution)/shard_map/ppermute | solution.py:543
  46.8 5.3 %collective-permute-start.10 = (f32[40,128]{1,0:T(8,128)S(1)}, f32[40,128]{1,0:T(8,128)S(1)}, u32[]{:S(2)}, u32[]{:S(2)}) collective-permute-start(f32[40,128]{1,0:T(8,128)S(1)} %add_add_fusion.refs_0_), channel_id=1, source_target_pairs={{0,16},{1,17},{2,18},{3,19},{4,20},{5,21},{6,22},{7,23},{8,24},{9,... | collective-permute-start | bytes 61448 | tf_op jit(solution)/shard_map/ppermute | solution.py:543
  49.4 5.6 %collective-permute-start.11 = (f32[40,128]{1,0:T(8,128)S(1)}, f32[40,128]{1,0:T(8,128)S(1)}, u32[]{:S(2)}, u32[]{:S(2)}) collective-permute-start(f32[40,128]{1,0:T(8,128)S(1)} %add_add_fusion.refs_0_), channel_id=1, source_target_pairs={{0,24},{1,25},{2,26},{3,27},{4,28},{5,29},{6,30},{7,31},{8,16},{9,... | collective-permute-start | bytes 61448 | tf_op jit(solution)/shard_map/ppermute | solution.py:543

commit v18 on v17

--- a/solution.py
+++ b/solution.py
@@ -534,7 +534,7 @@
 def sum_but_last(x, axes, near):
     devices = lax.axis_size(axes)
     bits = [1 << i for i in range(devices.bit_length() - 1) if 1 << i != near]
-    stages = [[near]] + [bits[i:i + 2] for i in range(0, len(bits), 2)]
+    stages = [[near], bits[:2]] + [[bit] for bit in bits[2:]]
     parts = [x]
     for stage in stages:
         x = add_up(parts)

time: 55.8 us -> 54.5 us (0.977)
  waiting for transfers between devices: 11 us -> 9.7 us
    ppermute x1, waiting for transfers between devices: 1.5 us -> 0.01 us  [earlier(): return lax.ppermute(x, 'seq', [(i + s, i) for i in range(shards - s)])]
    ppermute x7 -> x6, waiting for transfers between devices: 6.25 us -> 6.47 us  [sum_but_last(): parts.append(lax.ppermute(x, axes, [(i, i ^ flip) for i in range(devices)]))]
    ppermute x7 -> x6, starting transfers between devices: 8.01 us -> 8 us  [sum_but_last(): parts.append(lax.ppermute(x, axes, [(i, i ^ flip) for i in range(devices)]))]
  transfers between devices with their start and end apart: 12 -> 11, of which waited for: 8 -> 8; matrix products, arithmetic and copies ran while one was open for 1% -> 1% of each run, Pallas kernels for 38% -> 39%
where the time goes in v18:
time: 54.5 us; the launch traced here: 54.3 us
  Pallas kernels  26.1 us (48%)
  starting transfers between devices  16.5 us (30%)
  waiting for transfers between devices  9.7 us (18%)
  between operations  1.38 us (3%)
  other arithmetic  0.64 us (1%)
    pallas_call x4, Pallas kernels, attend(): pl.pallas_call(functools.partial(attend_kernel, g, shards), grid=(1,), in...  15.9 us
    ppermute x6, starting transfers between devices, sum_but_last(): parts.append(lax.ppermute(x, axes, [(i, i ^ flip) for i in range(devices)]))  8 us
    ppermute x4, starting transfers between devices, ring(): lax.ppermute(x, 'seq', [(i, (i + s) % shards) for i in range(shards)])  7.25 us
    ppermute x6, waiting for transfers between devices, sum_but_last(): parts.append(lax.ppermute(x, axes, [(i, i ^ flip) for i in range(devices)]))  6.47 us
    pallas_call x1, Pallas kernels, prep(): pl.pallas_call(prep_kernel, grid=(KV,), in_specs=[wide, wide, pl.BlockSpe...  4.2 us
    pallas_call x4, Pallas kernels, look_ahead(): pl.pallas_call(functools.partial(ahead_kernel, g, shards), grid=(1,), in_...  3.4 us
    ppermute x4, waiting for transfers between devices, ring(): lax.ppermute(x, 'seq', [(i, (i + s) % shards) for i in range(shards)])  3.22 us
    ppermute x1, starting transfers between devices, earlier(): return lax.ppermute(x, 'seq', [(i + s, i) for i in range(shards - s)])  1.28 us
  transfers between devices with their start and end apart: 11, of which 8 were waited for; matrix products, arithmetic and copies ran while one was open for 1% of the time, Pallas kernels for 39%

profile of v18, /device:TPU:0, one launch (start us, length us, event | category | flops | bytes accessed | tf_op | source)
XLA Modules:
  0.0 54.3 jit_solution(9860154641461612584)
XLA Ops:
  0.6 1.0 %pack.1 = bf16[1280,128]{1,0:T(8,128)(2,1)S(1)} custom-call(bf16[512,512]{1,0:T(8,128)(2,1)} %bitcast.23, bf16[512,512]{1,0:T(8,128)(2,1)} %bitcast.25, bf16[128,512]{1,0:T(8,128)(2,1)} %bitcast.29, bf16[128,512]{1,0:T(8,128)(2,1)} %bitcast.31), custom_call_target="tpu_custom_call" | custom-call | bytes 655360 | tf_op jit(solution)/shard_map/pack/pallas_call | solution.py:60
  1.6 3.0 %collective-permute-start = (bf16[1280,128]{1,0:T(8,128)(2,1)S(1)}, bf16[1280,128]{1,0:T(8,128)(2,1)S(1)}, u32[]{:S(2)}, u32[]{:S(2)}) collective-permute-start(bf16[1280,128]{1,0:T(8,128)(2,1)S(1)} %pack.1), channel_id=1, source_target_pairs={{0,1},{1,0},{2,3},{3,2},{4,5},{5,4},{6,7},{7,6},{8,9},{9,8},{10,11... | collective-permute-start | bytes 983048 | tf_op jit(solution)/shard_map/ppermute | solution.py:554
  5.3 0.1 convert_bitcast_fusion
  5.4 0.5 fusion
  6.0 4.2 %prep.1 = (bf16[4096,128]{1,0:T(8,128)(2,1)S(1)}, bf16[1024,512]{1,0:T(8,128)(2,1)S(1)}, bf16[4096,128]{1,0:T(8,128)(2,1)S(1)}, bf16[1024,512]{1,0:T(8,128)(2,1)...) custom-call(bf16[128,4096]{1,0:T(8,128)(2,1)} %bitcast.27, ...), custom_call_target="tpu_custom_call" | custom-call | flops 2097152 | bytes 6291456 | tf_op jit(solution)/shard_map/prep/pallas_call | solution.py:133
  10.2 0.1 collective-permute-start.1
  10.3 0.9 %ahead.4 = (f32[2,640,512]{2,1,0:T(8,128)S(1)}, f32[2,640,512]{2,1,0:T(8,128)S(1)}, f32[2,8,512]{2,1,0:T(8,128)S(1)}) custom-call(s32[1]{0:T(128)} %copy.29.first_ref.refs_0_, s32[1]{0:T(128)} %bitcast.2.rank_ref.refs_1_, bf16[1024,512]{1,0:T(8,128)(2,1)S(1)} %get-tuple-element.63.qst_ref.refs_3_, bf16[1024,512]{1,0:T(8,128)(2,1)S(1)} %get-tuple-element.65.dot_ref.refs_5_, ...), custom_call_target="tpu_custom_call" | custom-call | flops 335544320 | bytes 5242880 | tf_op jit(solution)/shard_map/ahead/pallas_call | solution.py:209
  11.1 0.9 %ahead.5 = (f32[2,640,512]{2,1,0:T(8,128)S(1)}, f32[2,640,512]{2,1,0:T(8,128)S(1)}, f32[2,8,512]{2,1,0:T(8,128)S(1)}) custom-call(s32[1]{0:T(128)} %copy.29.first_ref.refs_0_, s32[1]{0:T(128)} %bitcast.2.rank_ref.refs_1_, bf16[1024,512]{1,0:T(8,128)(2,1)S(1)} %get-tuple-element.63.qst_ref.refs_3_, bf16[1024,512]{1,0:T(8,128)(2,1)S(1)} %get-tuple-element.65.dot_ref.refs_5_, ...), custom_call_target="tpu_custom_call" | custom-call | flops 335544320 | bytes 5242880 | tf_op jit(solution)/shard_map/ahead/pallas_call | solution.py:209
  12.0 0.9 %ahead.6 = (f32[2,640,512]{2,1,0:T(8,128)S(1)}, f32[2,640,512]{2,1,0:T(8,128)S(1)}, f32[2,8,512]{2,1,0:T(8,128)S(1)}) custom-call(s32[1]{0:T(128)} %copy.29.first_ref.refs_0_, s32[1]{0:T(128)} %bitcast.2.rank_ref.refs_1_, bf16[1024,512]{1,0:T(8,128)(2,1)S(1)} %get-tuple-element.63.qst_ref.refs_3_, bf16[1024,512]{1,0:T(8,128)(2,1)S(1)} %get-tuple-element.65.dot_ref.refs_5_, ...), custom_call_target="tpu_custom_call" | custom-call | flops 335544320 | bytes 5242880 | tf_op jit(solution)/shard_map/ahead/pallas_call | solution.py:209
  12.8 0.0 collective-permute-done.refs_17_
  12.8 4.2 %attend.4 = (bf16[128,4096]{1,0:T(8,128)(2,1)}, bf16[128,4096]{1,0:T(8,128)(2,1)}, f32[40,128]{1,0:T(8,128)S(1)}, f32[2,128,128]{2,1,0:T(8,128)S(1)}, bf16[2,128...) custom-call(s32[1]{0:T(128)} %copy.29.first_ref.refs_0_, s32[1]{0:T(128)} %bitcast.2.rank_ref.refs_1_, ...), custom_call_target="tpu_custom_call" | custom-call | flops 1476395008 | bytes 2359296 | tf_op jit(solution)/shard_map/attend/pallas_call | solution.py:439
  17.0 2.4 %collective-permute-start.2 = (bf16[1280,128]{1,0:T(8,128)(2,1)S(1)}, bf16[1280,128]{1,0:T(8,128)(2,1)S(1)}, u32[]{:S(2)}, u32[]{:S(2)}) collective-permute-start(bf16[1280,128]{1,0:T(8,128)(2,1)S(1)} %get-tuple-element.89), channel_id=1, source_target_pairs={{0,1},{1,0},{2,3},{3,2},{4,5},{5,4},{6,7},{7,6},{8,9},{9,8},{10,11... | collective-permute-start | bytes 983048 | tf_op jit(solution)/shard_map/ppermute | solution.py:554
  19.4 0.2 collective-permute-done.1.refs_17_
  19.6 4.1 %attend.5 = (bf16[128,4096]{1,0:T(8,128)(2,1)}, bf16[128,4096]{1,0:T(8,128)(2,1)}, f32[40,128]{1,0:T(8,128)S(1)}, f32[2,128,128]{2,1,0:T(8,128)S(1)}, bf16[4,128...) custom-call(s32[1]{0:T(128)} %copy.29.first_ref.refs_0_, ...), custom_call_target="tpu_custom_call", output_to_operand_aliasing={{0}: (24, {}), {1}: (25, {})} | custom-call | flops 1476395008 | bytes 2359296 | tf_op jit(solution)/shard_map/attend/pallas_call | solution.py:439
  23.7 1.7 %collective-permute-start.3 = (bf16[1280,128]{1,0:T(8,128)(2,1)S(1)}, bf16[1280,128]{1,0:T(8,128)(2,1)S(1)}, u32[]{:S(2)}, u32[]{:S(2)}) collective-permute-start(bf16[1280,128]{1,0:T(8,128)(2,1)S(1)} %get-tuple-element.98), channel_id=1, source_target_pairs={{0,1},{1,0},{2,3},{3,2},{4,5},{5,4},{6,7},{7,6},{8,9},{9,8},{10,11... | collective-permute-start | bytes 983048 | tf_op jit(solution)/shard_map/ppermute | solution.py:554
  25.4 0.8 %ahead.7 = (f32[2,640,512]{2,1,0:T(8,128)S(1)}, f32[2,640,512]{2,1,0:T(8,128)S(1)}, f32[2,8,512]{2,1,0:T(8,128)S(1)}) custom-call(s32[1]{0:T(128)} %copy.29.first_ref.refs_0_, s32[1]{0:T(128)} %bitcast.2.rank_ref.refs_1_, bf16[1024,512]{1,0:T(8,128)(2,1)S(1)} %get-tuple-element.63.qst_ref.refs_3_, bf16[1024,512]{1,0:T(8,128)(2,1)S(1)} %get-tuple-element.65.dot_ref.refs_5_, ...), custom_call_target="tpu_custom_call" | custom-call | flops 335544320 | bytes 5242880 | tf_op jit(solution)/shard_map/ahead/pallas_call | solution.py:209
  26.2 1.5 %collective-permute-done.2.refs_17_ = bf16[1280,128]{1,0:T(8,128)(2,1)S(1)} collective-permute-done((bf16[1280,128]{1,0:T(8,128)(2,1)S(1)}, bf16[1280,128]{1,0:T(8,128)(2,1)S(1)}, u32[]{:S(2)}, u32[]{:S(2)}) %collective-permute-start.2) | collective-permute-done | bytes 327712 | tf_op jit(solution)/shard_map/ppermute | solution.py:554
  27.8 4.2 %attend.6 = (bf16[128,4096]{1,0:T(8,128)(2,1)}, bf16[128,4096]{1,0:T(8,128)(2,1)}, f32[40,128]{1,0:T(8,128)S(1)}, f32[2,128,128]{2,1,0:T(8,128)S(1)}, bf16[6,128,128]{2,1,0:T(8,128)(2,1)S(1)}) custom-call(s32[1]{0:T(128)} %copy.29.first_ref.refs_0_, s32[1]{0:T(128)} %bitcast.2.rank_ref.refs_1_, ...), custom_call_target="tpu_custom_call", output_to_operand_aliasing={{0}: (24, {}), {1}: (25, {})} | custom-call | flops 1476395008 | bytes 2359296 | tf_op jit(solution)/shard_map/attend/pallas_call | solution.py:439
  32.0 1.5 %collective-permute-done.3.refs_17_ = bf16[1280,128]{1,0:T(8,128)(2,1)S(1)} collective-permute-done((bf16[1280,128]{1,0:T(8,128)(2,1)S(1)}, bf16[1280,128]{1,0:T(8,128)(2,1)S(1)}, u32[]{:S(2)}, u32[]{:S(2)}) %collective-permute-start.3) | collective-permute-done | bytes 327712 | tf_op jit(solution)/shard_map/ppermute | solution.py:554
  33.5 3.5 %attend.7 = (bf16[128,1024]{1,0:T(8,128)(2,1)S(1)}, bf16[128,1024]{1,0:T(8,128)(2,1)S(1)}, f32[40,128]{1,0:T(8,128)S(1)}, f32[2,128,128]{2,1,0:T(8,128)S(1)}, bf16[8,128,128]{2,1,0:T(8,128)(2,1)S(1)}) custom-call(s32[1]{0:T(128)} %copy.29.first_ref.refs_0_, s32[1]{0:T(128)} %bitcast.2.rank_ref.refs_1_, bf16[4096,128]{1,0:T(8,128)(2,1)S(1)} %get-tuple-element.62.refs_2_, ...), custom_call_target="tpu_custom_call" | custom-call | flops 1476395008 | bytes 2359296 | tf_op jit(solution)/shard_map/attend/pallas_call | solution.py:439
  36.9 0.1 collective-permute-start.5
  37.0 1.2 %collective-permute-done.5 = f32[40,128]{1,0:T(8,128)S(1)} collective-permute-done((f32[40,128]{1,0:T(8,128)S(1)}, f32[40,128]{1,0:T(8,128)S(1)}, u32[]{:S(2)}, u32[]{:S(2)}) %collective-permute-start.5) | collective-permute-done | bytes 20512 | tf_op jit(solution)/shard_map/ppermute | solution.py:543
  38.2 1.7 %collective-permute-start.7 = (f32[40,128]{1,0:T(8,128)S(1)}, f32[40,128]{1,0:T(8,128)S(1)}, u32[]{:S(2)}, u32[]{:S(2)}) collective-permute-start(f32[40,128]{1,0:T(8,128)S(1)} %add.69), channel_id=1, source_target_pairs={{0,4},{1,5},{2,6},{3,7},{4,0},{5,1},{6,2},{7,3},{8,12},{9,13},{10,... | collective-permute-start | bytes 61448 | tf_op jit(solution)/shard_map/ppermute | solution.py:543
  39.9 1.5 %collective-permute-start.8 = (f32[40,128]{1,0:T(8,128)S(1)}, f32[40,128]{1,0:T(8,128)S(1)}, u32[]{:S(2)}, u32[]{:S(2)}) collective-permute-start(f32[40,128]{1,0:T(8,128)S(1)} %add.69), channel_id=1, source_target_pairs={{0,5},{1,4},{2,7},{3,6},{4,1},{5,0},{6,3},{7,2},{8,13},{9,12},{10,... | collective-permute-start | bytes 61448 | tf_op jit(solution)/shard_map/ppermute | solution.py:543
  41.4 0.3 collective-permute-start.6
  41.7 1.3 %collective-permute-start.4 = (bf16[8,128,128]{2,1,0:T(8,128)(2,1)S(1)}, bf16[8,128,128]{2,1,0:T(8,128)(2,1)S(1)}, u32[]{:S(2)}, u32[]{:S(2)}) collective-permute-start(bf16[8,128,128]{2,1,0:T(8,128)(2,1)S(1)} %get-tuple-element.104), channel_id=1, source_target_pairs={{1,0},{3,2},{5,4},{7,6},{9,8},{11,10},{13,12},{15,14},{17,16},{19,... | collective-permute-start | bytes 786440 | tf_op jit(solution)/shard_map/ppermute | solution.py:557
  43.0 0.0 collective-permute-done.7
  43.0 1.6 %collective-permute-done.8 = f32[40,128]{1,0:T(8,128)S(1)} collective-permute-done((f32[40,128]{1,0:T(8,128)S(1)}, f32[40,128]{1,0:T(8,128)S(1)}, u32[]{:S(2)}, u32[]{:S(2)}) %collective-permute-start.8) | collective-permute-done | bytes 20512 | tf_op jit(solution)/shard_map/ppermute | solution.py:543
  44.6 0.6 %collective-permute-done.6 = f32[40,128]{1,0:T(8,128)S(1)} collective-permute-done((f32[40,128]{1,0:T(8,128)S(1)}, f32[40,128]{1,0:T(8,128)S(1)}, u32[]{:S(2)}, u32[]{:S(2)}) %collective-permute-start.6) | collective-permute-done | bytes 20512 | tf_op jit(solution)/shard_map/ppermute | solution.py:543
  45.2 1.6 %collective-permute-start.9 = (f32[40,128]{1,0:T(8,128)S(1)}, f32[40,128]{1,0:T(8,128)S(1)}, u32[]{:S(2)}, u32[]{:S(2)}) collective-permute-start(f32[40,128]{1,0:T(8,128)S(1)} %add_add_fusion), channel_id=1, source_target_pairs={{0,8},{1,9},{2,10},{3,11},{4,12},{5,13},{6,14},{7,15},{8,0},{9,1},... | collective-permute-start | bytes 61448 | tf_op jit(solution)/shard_map/ppermute | solution.py:543
  46.8 2.2 %collective-permute-done.9 = f32[40,128]{1,0:T(8,128)S(1)} collective-permute-done((f32[40,128]{1,0:T(8,128)S(1)}, f32[40,128]{1,0:T(8,128)S(1)}, u32[]{:S(2)}, u32[]{:S(2)}) %collective-permute-start.9) | collective-permute-done | bytes 20512 | tf_op jit(solution)/shard_map/ppermute | solution.py:543
  49.0 2.8 %collective-permute-start.10 = (f32[40,128]{1,0:T(8,128)S(1)}, f32[40,128]{1,0:T(8,128)S(1)}, u32[]{:S(2)}, u32[]{:S(2)}) collective-permute-start(f32[40,128]{1,0:T(8,128)S(1)} %add.73.refs_0_), channel_id=1, source_target_pairs={{0,16},{1,17},{2,18},{3,19},{4,20},{5,21},{6,22},{7,23},{8,24},{9,... | collective-permute-start | bytes 61448 | tf_op jit(solution)/shard_map/ppermute | solution.py:543
  51.8 0.0 collective-permute-done.4.refs_6_
  51.8 1.0 %finish.1 = (bf16[128,4096]{1,0:T(8,128)(2,1)}, bf16[128,4096]{1,0:T(8,128)(2,1)}, bf16[128,512]{1,0:T(8,128)(2,1)}, bf16[128,512]{1,0:T(8,128)(2,1)}) custom-call(f32[256,128]{1,0:T(8,128)S(1)} %get-tuple-element.118.cos_ref.refs_11_.refs_0_, ...), custom_call_target="tpu_custom_call", output_to_operand_aliasing={{0}: (9, {}), {1}: (10, {})} | custom-call | bytes 2097152 | tf_op jit(solution)/shard_map/finish/pallas_call | solution.py:490
  52.8 0.9 %collective-permute-done.10.refs_1_ = f32[40,128]{1,0:T(8,128)S(1)} collective-permute-done((f32[40,128]{1,0:T(8,128)S(1)}, f32[40,128]{1,0:T(8,128)S(1)}, u32[]{:S(2)}, u32[]{:S(2)}) %collective-permute-start.10) | collective-permute-done | bytes 20512 | tf_op jit(solution)/shard_map/ppermute | solution.py:543
  53.7 0.6 %sums.1 = (f32[32,128]{1,0:T(8,128)}, f32[4,128]{1,0:T(4,128)}, f32[4,128]{1,0:T(4,128)}) custom-call(f32[40,128]{1,0:T(8,128)S(1)} %add.73.refs_0_, f32[40,128]{1,0:T(8,128)S(1)} %collective-permute-done.10.refs_1_, bf16[128,512]{1,0:T(8,128)(2,1)} %get-tuple-element.111.refs_2_), custom_call_target="tpu_custom_call" | custom-call | bytes 131072 | tf_op jit(solution)/shard_map/sums/pallas_call | solution.py:515
  (5 shorter events, 0.0 us)
Async XLA Ops:
  1.6 11.2 %collective-permute-start = (bf16[1280,128]{1,0:T(8,128)(2,1)S(1)}, bf16[1280,128]{1,0:T(8,128)(2,1)S(1)}, u32[]{:S(2)}, u32[]{:S(2)}) collective-permute-start(bf16[1280,128]{1,0:T(8,128)(2,1)S(1)} %pack.1), channel_id=1, source_target_pairs={{0,1},{1,0},{2,3},{3,2},{4,5},{5,4},{6,7},{7,6},{8,9},{9,8},{10,11... | collective-permute-start | bytes 983048 | tf_op jit(solution)/shard_map/ppermute | solution.py:554
  10.2 9.4 %collective-permute-start.1 = (bf16[1280,128]{1,0:T(8,128)(2,1)S(1)}, bf16[1280,128]{1,0:T(8,128)(2,1)S(1)}, u32[]{:S(2)}, u32[]{:S(2)}) collective-permute-start(bf16[1280,128]{1,0:T(8,128)(2,1)S(1)} %get-tuple-element.80), channel_id=1, source_target_pairs={{0,1},{1,0},{2,3},{3,2},{4,5},{5,4},{6,7},{7,6},{8,9},{9,8},{10,11... | collective-permute-start | bytes 983048 | tf_op jit(solution)/shard_map/ppermute | solution.py:554
  17.0 10.8 %collective-permute-start.2 = (bf16[1280,128]{1,0:T(8,128)(2,1)S(1)}, bf16[1280,128]{1,0:T(8,128)(2,1)S(1)}, u32[]{:S(2)}, u32[]{:S(2)}) collective-permute-start(bf16[1280,128]{1,0:T(8,128)(2,1)S(1)} %get-tuple-element.89), channel_id=1, source_target_pairs={{0,1},{1,0},{2,3},{3,2},{4,5},{5,4},{6,7},{7,6},{8,9},{9,8},{10,11... | collective-permute-start | bytes 983048 | tf_op jit(solution)/shard_map/ppermute | solution.py:554
  23.7 9.8 %collective-permute-start.3 = (bf16[1280,128]{1,0:T(8,128)(2,1)S(1)}, bf16[1280,128]{1,0:T(8,128)(2,1)S(1)}, u32[]{:S(2)}, u32[]{:S(2)}) collective-permute-start(bf16[1280,128]{1,0:T(8,128)(2,1)S(1)} %get-tuple-element.98), channel_id=1, source_target_pairs={{0,1},{1,0},{2,3},{3,2},{4,5},{5,4},{6,7},{7,6},{8,9},{9,8},{10,11... | collective-permute-start | bytes 983048 | tf_op jit(solution)/shard_map/ppermute | solution.py:554
  36.9 1.3 %collective-permute-start.5 = (f32[40,128]{1,0:T(8,128)S(1)}, f32[40,128]{1,0:T(8,128)S(1)}, u32[]{:S(2)}, u32[]{:S(2)}) collective-permute-start(f32[40,128]{1,0:T(8,128)S(1)} %get-tuple-element.113), channel_id=1, source_target_pairs={{0,2},{1,3},{2,0},{3,1},{4,6},{5,7},{6,4},{7,5},{8,10},{9,11},{10,... | collective-permute-start | bytes 61448 | tf_op jit(solution)/shard_map/ppermute | solution.py:543
  38.2 4.8 %collective-permute-start.7 = (f32[40,128]{1,0:T(8,128)S(1)}, f32[40,128]{1,0:T(8,128)S(1)}, u32[]{:S(2)}, u32[]{:S(2)}) collective-permute-start(f32[40,128]{1,0:T(8,128)S(1)} %add.69), channel_id=1, source_target_pairs={{0,4},{1,5},{2,6},{3,7},{4,0},{5,1},{6,2},{7,3},{8,12},{9,13},{10,... | collective-permute-start | bytes 61448 | tf_op jit(solution)/shard_map/ppermute | solution.py:543
  39.9 4.7 %collective-permute-start.8 = (f32[40,128]{1,0:T(8,128)S(1)}, f32[40,128]{1,0:T(8,128)S(1)}, u32[]{:S(2)}, u32[]{:S(2)}) collective-permute-start(f32[40,128]{1,0:T(8,128)S(1)} %add.69), channel_id=1, source_target_pairs={{0,5},{1,4},{2,7},{3,6},{4,1},{5,0},{6,3},{7,2},{8,13},{9,12},{10,... | collective-permute-start | bytes 61448 | tf_op jit(solution)/shard_map/ppermute | solution.py:543
  41.4 3.8 %collective-permute-start.6 = (f32[40,128]{1,0:T(8,128)S(1)}, f32[40,128]{1,0:T(8,128)S(1)}, u32[]{:S(2)}, u32[]{:S(2)}) collective-permute-start(f32[40,128]{1,0:T(8,128)S(1)} %add.69), channel_id=1, source_target_pairs={{0,1},{1,0},{2,3},{3,2},{4,5},{5,4},{6,7},{7,6},{8,9},{9,8},{10,11... | collective-permute-start | bytes 61448 | tf_op jit(solution)/shard_map/ppermute | solution.py:543
  41.7 10.1 %collective-permute-start.4 = (bf16[8,128,128]{2,1,0:T(8,128)(2,1)S(1)}, bf16[8,128,128]{2,1,0:T(8,128)(2,1)S(1)}, u32[]{:S(2)}, u32[]{:S(2)}) collective-permute-start(bf16[8,128,128]{2,1,0:T(8,128)(2,1)S(1)} %get-tuple-element.104), channel_id=1, source_target_pairs={{1,0},{3,2},{5,4},{7,6},{9,8},{11,10},{13,12},{15,14},{17,16},{19,... | collective-permute-start | bytes 786440 | tf_op jit(solution)/shard_map/ppermute | solution.py:557
  45.2 3.8 %collective-permute-start.9 = (f32[40,128]{1,0:T(8,128)S(1)}, f32[40,128]{1,0:T(8,128)S(1)}, u32[]{:S(2)}, u32[]{:S(2)}) collective-permute-start(f32[40,128]{1,0:T(8,128)S(1)} %add_add_fusion), channel_id=1, source_target_pairs={{0,8},{1,9},{2,10},{3,11},{4,12},{5,13},{6,14},{7,15},{8,0},{9,1},... | collective-permute-start | bytes 61448 | tf_op jit(solution)/shard_map/ppermute | solution.py:543
  49.0 4.7 %collective-permute-start.10 = (f32[40,128]{1,0:T(8,128)S(1)}, f32[40,128]{1,0:T(8,128)S(1)}, u32[]{:S(2)}, u32[]{:S(2)}) collective-permute-start(f32[40,128]{1,0:T(8,128)S(1)} %add.73.refs_0_), channel_id=1, source_target_pairs={{0,16},{1,17},{2,18},{3,19},{4,20},{5,21},{6,22},{7,23},{8,24},{9,... | collective-permute-start | bytes 61448 | tf_op jit(solution)/shard_map/ppermute | solution.py:543
